TPU v7x, 32 devices: a whole 2x2x4 slice. The times are simulated.
32 devices in a mesh: grp: 2 (over x), scen: 16 (over z, y, core).
Axes of the slice: x: 2, y: 2, z: 4, core: 2. Of those that a mesh axis runs over, the one named last changes fastest.
Arguments:
- scenario_rows: bfloat16 [32768, 4096], P(('grp', 'scen')), parts along dimension 0, may hold values from -6 to 6
- row_weights: float32 [32768], P(('grp', 'scen')), parts along dimension 0, may hold values from 0.1 to 10
- row_counts: int32 [32], P(('grp', 'scen')), parts along dimension 0, may hold values from 1 to 1024, 10240 in all
- panel_cols: int32 [1024], P('grp'), parts along dimension 0, may hold values from 0 to 4095, as said below
- regular: float32 [512], replicated, may hold values from 0.2 to 2
- prior_schur: float32 [4096, 4096], P('scen'), as said below
Outputs:
- schur_out: float32 [8192, 4096], P(('grp', 'scen')), parts along dimension 0
- panel_factor: float32 [8192, 512], P(('grp', 'scen')), parts along dimension 0
There are 2 independent parts, one for each index of `grp`. A program takes and returns all parts, laid end to end along the dimension named above; an argument that names none is the same for every part. Nothing has to cross between parts.
Inputs may be any that keep to these rules, and one draw needn't show every extreme that they name: `panel_cols`: the 512 entries are distinct. `row_counts`: the entries of one part along grp sum to 10240. `prior_schur`: symmetric; every eigenvalue is above 0.4, so the regularized block is positive definite.
All inputs are finite; a program needn't handle non-finite values. No bound on the sum of `row_counts` on one device may be relied on, other than what follows from the above.
Results may differ from a plain program's by a relative error of at most 0.0016.
Values sent between devices are 32-bit elements; how exact they have to be, the bound alone decides.
No kernel may reach another device: no remote copies, remote signals or barrier semaphores. Data moves between devices by JAX's collectives and lax.ppermute only.
A program may use at most 128 MiB of HBM per device.

v0:
```python
import jax
import jax.numpy as jnp
from jax import lax
from jax.experimental import pallas as pl
from jax.experimental.pallas import tpu as pltpu
from jax.sharding import PartitionSpec as P

TILE = 128
GROUP = 8
HIGH = lax.Precision.HIGH
HIGHEST = lax.Precision.HIGHEST
RINGS = {8: (0, 2, 4, 6, 7, 5, 3, 1)}
VMEM_BYTES = 56 * 2**20


def row_of(values, j):
    return jnp.broadcast_to(values[j : j + 1, :], values.shape)


def invert_tile(rows):
    sub = lax.broadcasted_iota(jnp.int32, (GROUP, TILE), 0)
    lane = lax.broadcasted_iota(jnp.int32, (GROUP, TILE), 1)
    rows = list(rows)
    done = []
    for g in range(len(rows)):
        first = g * GROUP
        in_group = (lane >= first) & (lane < first + GROUP)
        own = rows[g]
        cols = [
            jnp.broadcast_to(own[:, first + k : first + k + 1], own.shape) for k in range(GROUP)
        ]
        recips, pivots, entries = [], jnp.ones_like(own), {}
        for j in range(GROUP):
            pivot = row_of(cols[j], j)
            recip = 1.0 / pivot
            recips.append(recip)
            pivots = jnp.where(sub == j, pivot, pivots)
            mult = jnp.where(sub > j, cols[j] * recip, 0.0)
            for k in range(j + 1, GROUP):
                entries[j, k] = row_of(cols[k], j)
                cols[k] = cols[k] - mult * entries[j, k]
            at = lane == first + j
            own = jnp.where(at & (sub > j), 0.0, own) - mult * jnp.where(at, 1.0, row_of(own, j))
        diag = lane == first + sub
        done.append(
            jnp.where(diag, 1.0, jnp.where(lane < first + sub, own, 0.0)) * lax.rsqrt(pivots)
        )
        spread = []
        for j in range(GROUP):
            row = jnp.where(in_group & (lane > first + j), 0.0, row_of(own, j))
            spread.append(jnp.where(lane == first + j, 1.0, row))
        for h in range(g + 1, len(rows)):
            low = rows[h]
            below = [
                jnp.broadcast_to(low[:, first + k : first + k + 1], low.shape) for k in range(GROUP)
            ]
            low = jnp.where(in_group, 0.0, low)
            for j in range(GROUP):
                mult = below[j] * recips[j]
                for k in range(j + 1, GROUP):
                    below[k] = below[k] - mult * entries[j, k]
                low = low - mult * spread[j]
            rows[h] = low
    return done


def dot_exact(left, right):
    return jnp.dot(left, right, precision=HIGHEST, preferred_element_type=jnp.float32)


def contract_exact(left, right):
    return lax.dot_general(
        left, right, (((0,), (0,)), ((), ())), precision=HIGHEST, preferred_element_type=jnp.float32
    )


def split(values):
    top = values.astype(jnp.bfloat16)
    return top, (values - top.astype(jnp.float32)).astype(jnp.bfloat16)


def dot_split(left, right):
    return sum(
        jnp.dot(a, b, preferred_element_type=jnp.float32)
        for a, b in ((left[1], right[0]), (left[0], right[1]), (left[0], right[0]))
    )


def vmem(count):
    return [pl.BlockSpec(memory_space=pltpu.VMEM)] * count


def factor_step(k, work):
    size = work.shape[0]
    at = pl.ds(k * TILE, TILE)
    tile = work[at, at]
    small = jnp.concatenate(
        invert_tile([tile[g * GROUP : (g + 1) * GROUP] for g in range(TILE // GROUP)]), axis=0
    )
    row_id = lax.broadcasted_iota(jnp.int32, (TILE, TILE), 0)
    col_id = lax.broadcasted_iota(jnp.int32, (TILE, TILE), 1)
    work[at, at] = (row_id == col_id).astype(jnp.float32)
    work[at, :] = dot_exact(small, work[at, :])
    for i in range(k + 1, size // TILE):
        to = pl.ds(i * TILE, TILE)
        lower = work[at, to]
        work[to, at] = jnp.zeros((TILE, TILE), jnp.float32)
        work[to, :] -= contract_exact(lower, work[at, :])
        work[at, to] = jnp.zeros((TILE, TILE), jnp.float32)


def factor_kernel(place_ref, mine_ref, other_ref, regular_ref, out_ref):
    chips, rows = mine_ref.shape[0], mine_ref.shape[1]
    chip, core = place_ref[0], place_ref[1]
    for ref, on_core in ((mine_ref, core), (other_ref, 1 - core)):
        for n in range(chips):
            at = (on_core * chips + lax.rem(chip + chips - n, chips)) * rows
            out_ref[pl.ds(pl.multiple_of(at, rows), rows), :] = ref[n]
    size = out_ref.shape[0]
    row_id = lax.broadcasted_iota(jnp.int32, (TILE, TILE), 0)
    col_id = lax.broadcasted_iota(jnp.int32, (TILE, TILE), 1)
    for i in range(size // TILE):
        at = pl.ds(i * TILE, TILE)
        out_ref[at, at] += jnp.where(row_id == col_id, regular_ref[:, at], 0.0)
    for k in range(size // TILE):
        factor_step(k, out_ref)


def inverse_factor(place, mine, other, regular):
    size = regular.shape[0]
    return pl.pallas_call(
        factor_kernel,
        out_shape=jax.ShapeDtypeStruct((size, size), jnp.float32),
        in_specs=[pl.BlockSpec(memory_space=pltpu.SMEM)] + vmem(3),
        out_specs=vmem(1)[0],
        cost_estimate=pl.CostEstimate(
            flops=100 * size**3, bytes_accessed=8 * size * size, transcendentals=size
        ),
        name="inverse_factor",
    )(place, mine, other, regular[None, :])


def solve_kernel(inverse_ref, first_ref, second_ref, factor_ref, weight_ref):
    inverse = inverse_ref[...]
    panel = jnp.concatenate([first_ref[...], second_ref[...]], axis=0)
    rows = dot_split(split(inverse), split(panel)).T
    factor_ref[...] = rows
    weight_ref[...] = dot_split(split(rows), split(inverse))


def solve_rows(inverse, first, second):
    half, owned = first.shape
    shape = jax.ShapeDtypeStruct((owned, 2 * half), jnp.float32)
    return pl.pallas_call(
        solve_kernel,
        out_shape=(shape, shape),
        in_specs=vmem(3),
        out_specs=vmem(2),
        cost_estimate=pl.CostEstimate(
            flops=48 * owned * half * half, bytes_accessed=32 * half * half, transcendentals=0
        ),
        name="solve_rows",
    )(inverse, first, second)


def gram_kernel(block_ref, scaled_ref, rows_ref, *refs):
    out_ref = refs[-1]
    total = jnp.dot(scaled_ref[...], rows_ref[...], preferred_element_type=jnp.float32)
    out_ref[0] = total if len(refs) == 1 else total + refs[0][0]


def gram_pieces(blocks, scaled, part, scenario_rows, owned, extra=None):
    depth = scenario_rows.shape[0]
    half = scaled.shape[0] // 2
    count = blocks.shape[0]
    piece = pl.BlockSpec((1, half, owned), lambda i, blocks: (i, 0, 0))
    more = [] if extra is None else [extra]
    return pl.pallas_call(
        gram_kernel,
        grid_spec=pltpu.PrefetchScalarGridSpec(
            num_scalar_prefetch=1,
            grid=(count,),
            in_specs=[
                pl.BlockSpec((half, depth), lambda i, blocks: (part, 0)),
                pl.BlockSpec((depth, owned), lambda i, blocks: (0, blocks[i])),
            ]
            + [piece] * len(more),
            out_specs=piece,
        ),
        out_shape=jax.ShapeDtypeStruct((count, half, owned), jnp.float32),
        cost_estimate=pl.CostEstimate(
            flops=2 * count * depth * owned * half,
            bytes_accessed=count * owned * (2 * depth + 4 * half) + 2 * depth * half,
            transcendentals=0,
        ),
        compiler_params=pltpu.CompilerParams(vmem_limit_bytes=VMEM_BYTES),
        name="gram_pieces",
    )(blocks, scaled, scenario_rows, *more)


def update_kernel(count, block_ref, weight_ref, prior_ref, *refs):
    sources, out_ref = refs[:6], refs[6]
    held, total, in_sem, prior_sem, out_sem = refs[7:]
    half, owned = held.shape[2], held.shape[3]
    fetch = pltpu.make_async_copy(prior_ref, total, prior_sem)
    fetch.start()
    loads = []
    lines = count // 4
    for n in range(count):
        way, z = n // lines, n % lines
        pair = (sources[way].at[z], sources[4 + way // 2].at[z, way % 2])
        loads.append(
            [pltpu.make_async_copy(pair[h], held.at[n, h], in_sem.at[n, h]) for h in range(2)]
        )
        for load in loads[-1]:
            load.start()
    weights = split(weight_ref[...])
    fetch.wait()
    stores = []
    for n in range(count):
        for load in loads[n]:
            load.wait()
        outer = dot_split(weights, split(held[n].reshape(2 * half, owned)))
        cols = pl.ds(pl.multiple_of(block_ref[n] * owned, owned), owned)
        total[:, cols] -= outer
        store = pltpu.make_async_copy(total.at[:, cols], out_ref.at[:, cols], out_sem.at[n])
        store.start()
        stores.append(store)
    for store in stores:
        store.wait()


def update_rows(blocks, weights, prior, sources):
    count = blocks.shape[0]
    owned, order = prior.shape
    half = weights.shape[1] // 2
    return pl.pallas_call(
        lambda *refs: update_kernel(count, *refs),
        out_shape=jax.ShapeDtypeStruct(prior.shape, jnp.float32),
        in_specs=[pl.BlockSpec(memory_space=pltpu.SMEM)]
        + vmem(1)
        + [pl.BlockSpec(memory_space=pl.ANY)] * (1 + len(sources)),
        out_specs=pl.BlockSpec(memory_space=pl.ANY),
        scratch_shapes=[
            pltpu.VMEM((count, 2, half, owned), jnp.float32),
            pltpu.VMEM(prior.shape, jnp.float32),
            pltpu.SemaphoreType.DMA((count, 2)),
            pltpu.SemaphoreType.DMA,
            pltpu.SemaphoreType.DMA((count,)),
        ],
        cost_estimate=pl.CostEstimate(
            flops=12 * owned * order * half,
            bytes_accessed=8 * owned * order + 8 * order * half,
            transcendentals=0,
        ),
        compiler_params=pltpu.CompilerParams(vmem_limit_bytes=VMEM_BYTES),
        name="update_rows",
    )(blocks, weights, prior, *sources)


def local_parts(scenario_rows, row_weights, row_counts, panel_cols, prior_schur):
    parts = lax.axis_size("scen")
    owned, order = prior_schur.shape
    depth = scenario_rows.shape[0]
    place = lax.axis_index("scen")
    live = (jnp.arange(depth, dtype=jnp.int32) < row_counts[0]).astype(jnp.float32)
    factor_w = row_weights * live * (1.0 / (depth * parts))
    pick = panel_cols[:, None] == jnp.arange(order, dtype=jnp.int32)[None, :]
    picked = lax.dot_general(
        pick.astype(jnp.bfloat16), scenario_rows, (((1,), (1,)), ((), ())),
        preferred_element_type=jnp.float32,
    )
    scaled = (picked * factor_w[None, :]).astype(jnp.bfloat16)
    picked = picked.astype(jnp.bfloat16)
    local_cols = lax.dot_general(
        pick.astype(jnp.float32), prior_schur, (((1,), (1,)), ((), ())), precision=HIGH
    )
    select = panel_cols[None, :] == place * owned + jnp.arange(owned, dtype=jnp.int32)[:, None]
    block = lax.dot_general(
        scaled, picked, (((1,), (1,)), ((), ())), preferred_element_type=jnp.float32
    ) + jnp.dot(local_cols, select.astype(jnp.float32), precision=HIGH)
    return scaled, local_cols, 0.5 * (block + block.T)


def swap_cores(values):
    parts = lax.axis_size("scen")
    return lax.ppermute(values, "scen", [(d, d ^ 1) for d in range(parts)])


def halve_block(block):
    chips = lax.axis_size("scen") // 2
    width = block.shape[0]
    core = lax.axis_index("scen") % 2
    halves = block.reshape(2, width // 2, width)
    given = lax.dynamic_index_in_dim(halves, 1 - core, 0, keepdims=False)
    kept = lax.dynamic_index_in_dim(halves, core, 0, keepdims=False)
    return (kept + swap_cores(given)).reshape(chips, -1, width)


def sum_block(block):
    parts = lax.axis_size("scen")
    chips = parts // 2
    chip = lax.axis_index("scen") // 2

    def shift(values, by):
        return lax.ppermute(values, "scen", [(d, (d + 2 * by) % parts) for d in range(parts)])

    both = halve_block(block)
    mine = lax.dynamic_index_in_dim(both, chip, 0, keepdims=False)
    for by in range(1, chips):
        mine += shift(lax.dynamic_index_in_dim(both, (chip + by) % chips, 0, keepdims=False), by)
    mine = jnp.stack([mine] + [shift(mine, by) for by in range(1, chips)])
    return mine, swap_cores(mine)


def shards_on_grid(scenario_rows, row_weights, row_counts, panel_cols, regular, prior_schur):
    parts = lax.axis_size("scen")
    chips = parts // 2
    owned = prior_schur.shape[0]
    half = panel_cols.shape[0] // 2
    place = lax.axis_index("scen")
    core, chip = place % 2, place // 2
    ring = RINGS[chips]

    scaled, local_cols, block = local_parts(
        scenario_rows, row_weights, row_counts, panel_cols, prior_schur
    )

    orders = (ring, ring[::-1])
    tables = [jnp.array(order, jnp.int32) * 2 for order in orders]
    given = [
        swap_cores(gram_pieces(tables[h] + 1 - core, scaled, h, scenario_rows, owned))
        for h in range(2)
    ]
    panel = []
    for h in range(2):
        both = gram_pieces(tables[h] + core, scaled, h, scenario_rows, owned, given[h])
        summed = lax.psum_scatter(
            both, "scen", scatter_dimension=0,
            axis_index_groups=[[2 * q + c for q in orders[h]] for c in range(2)],
        )
        panel.append(summed + local_cols[h * half : (h + 1) * half])
    block_mine, block_other = sum_block(block)

    lines = [[2 * (2 * z + y) + c for z in range(chips // 2)] for y in range(2) for c in range(2)]

    def swap_y(values):
        return lax.ppermute(values, "scen", [(d, d ^ 2) for d in range(parts)])

    second = lax.all_gather(
        jnp.stack([panel[1], swap_y(panel[1])]), "scen", axis_index_groups=lines
    )
    first = lax.all_gather(panel[0], "scen", axis_index_groups=lines)
    first = [first, swap_y(first)]
    sources = first + [swap_cores(part) for part in first] + [second, swap_cores(second)]
    z = jnp.arange(chips // 2, dtype=jnp.int32)
    blocks = jnp.concatenate(
        [2 * (2 * z + y) + c for c in (core, 1 - core) for y in (chip % 2, 1 - chip % 2)]
    )

    inverse = inverse_factor(jnp.stack([chip, core]), block_mine, block_other, regular)
    factor_rows, weights = solve_rows(inverse, *panel)
    return update_rows(blocks, weights, prior_schur, sources), factor_rows


def shards_by_groups(scenario_rows, row_weights, row_counts, panel_cols, regular, prior_schur):
    parts = lax.axis_size("scen")
    chips = parts // 2
    owned, order = prior_schur.shape
    width = panel_cols.shape[0]
    half = width // 2
    place = lax.axis_index("scen")
    core = place % 2
    same_core = [list(range(c, parts, 2)) for c in range(2)]
    scaled, local_cols, block = local_parts(
        scenario_rows, row_weights, row_counts, panel_cols, prior_schur
    )
    block = lax.psum_scatter(
        halve_block(block), "scen", scatter_dimension=0, axis_index_groups=same_core
    )
    block = lax.all_gather(block, "scen", axis_index_groups=same_core).reshape(1, half, width)
    block_other = swap_cores(block)
    gram = lax.dot_general(
        scenario_rows, scaled, (((0,), (1,)), ((), ())), preferred_element_type=jnp.float32
    ).reshape(chips, 2, owned, width)
    given = lax.dynamic_index_in_dim(gram, 1 - core, 1, keepdims=False)
    kept = lax.dynamic_index_in_dim(gram, core, 1, keepdims=False)
    gram_mine = lax.psum_scatter(
        kept + swap_cores(given), "scen", scatter_dimension=0, axis_index_groups=same_core
    )
    panel_rows = gram_mine + local_cols.T
    panel_half = lax.all_gather(panel_rows, "scen", axis_index_groups=same_core)
    panel_rest = swap_cores(panel_half)
    inverse = inverse_factor(jnp.stack([jnp.int32(0), core]), block, block_other, regular)
    factor_rows, weights = solve_rows(inverse, panel_rows.T[:half], panel_rows.T[half:])
    even = jnp.where(core == 0, panel_half, panel_rest)
    odd = jnp.where(core == 0, panel_rest, panel_half)
    panel = jnp.stack([even, odd], axis=1).reshape(order, width)
    outer = jnp.dot(weights, panel.T, precision=HIGHEST)
    return prior_schur - outer, factor_rows


def solution(mesh):
    placed = (
        P(("grp", "scen"), None),
        P(("grp", "scen")),
        P(("grp", "scen")),
        P("grp"),
        P(),
        P("scen", None),
    )
    return jax.shard_map(
        shards_on_grid if mesh.shape["scen"] // 2 in RINGS else shards_by_groups,
        mesh=mesh,
        in_specs=placed,
        out_specs=(P(("grp", "scen"), None), P(("grp", "scen"), None)),
        check_vma=False,
    )
```

profile of v0, /device:TPU:0, one launch (start us, length us, event | category | flops | bytes accessed | tf_op | source)
XLA Modules:
  0.0 258.0 jit_solution(17907779528318688159)
XLA Ops:
  7.9 1.2 broadcast_subtract_fusion.1.block_ref
  9.1 0.7 select_multiply_fusion
  9.7 8.9 %multiply_convert_fusion = (bf16[512,1024]{1,0:T(8,128)(2,1)}, f32[512,1024]{1,0:T(8,128)S(1)}) fusion(f32[1024]{0:T(1024)S(1)} %select_multiply_fusion, bf16[1024,4096]{1,0:T(8,128)(2,1)} %rows_ref.7, s32[512]{0:T(512)} %param.11), kind=kOutput, calls=%fused_computation.5 | convolution fusion | flops 4298113024 | bytes 11540480 | tf_op jit(solution)/shard_map/dot_general | solution.py:269
  18.7 8.1 %gram_pieces.4 = f32[8,256,256]{2,1,0:T(8,128)} custom-call(s32[8]{0:T(128)} %broadcast_subtract_fusion.1.block_ref, bf16[512,1024]{1,0:T(8,128)(2,1)} %get-tuple-element.17.scaled_ref, bf16[1024,4096]{1,0:T(8,128)(2,1)} %rows_ref.7), custom_call_target="tpu_custom_call" | custom-call | flops 1073741824 | bytes 6815744 | tf_op jit(solution)/shard_map/gram_pieces/pallas_call | solution.py:178
  26.8 0.5 collective-permute-start.16
  27.2 0.5 broadcast_add_fusion.1.block_ref
  27.7 3.5 %collective-permute-done.16.refs_0_ = f32[8,256,256]{2,1,0:T(8,128)S(1)} collective-permute-done((f32[8,256,256]{2,1,0:T(8,128)}, f32[8,256,256]{2,1,0:T(8,128)S(1)}, u32[]{:S(2)}, u32[]{:S(2)}) %collective-permute-start.16) | collective-permute-done | bytes 2097184 | tf_op jit(solution)/shard_map/ppermute | solution.py:287
  31.2 1.3 copy-done.3
  32.5 8.4 %gram_pieces.5 = f32[8,256,256]{2,1,0:T(8,128)} custom-call(s32[8]{0:T(128)} %broadcast_add_fusion.1.block_ref, bf16[512,1024]{1,0:T(8,128)(2,1)} %get-tuple-element.17.scaled_ref, bf16[1024,4096]{1,0:T(8,128)(2,1)} %rows_ref.7, f32[8,256,256]{2,1,0:T(8,128)} %copy-done.3), custom_call_target="tpu_custom_call" | custom-call | flops 1073741824 | bytes 6815744 | tf_op jit(solution)/shard_map/gram_pieces/pallas_call | solution.py:178
  41.0 0.6 copy-done.9
  41.6 0.5 broadcast_subtract_fusion.block_ref
  42.1 8.1 %gram_pieces.6 = f32[8,256,256]{2,1,0:T(8,128)} custom-call(s32[8]{0:T(128)} %broadcast_subtract_fusion.block_ref, bf16[512,1024]{1,0:T(8,128)(2,1)} %get-tuple-element.17.scaled_ref, bf16[1024,4096]{1,0:T(8,128)(2,1)} %rows_ref.7), custom_call_target="tpu_custom_call" | custom-call | flops 1073741824 | bytes 6815744 | tf_op jit(solution)/shard_map/gram_pieces/pallas_call | solution.py:178
  50.2 0.4 collective-permute-start.17
  50.5 0.5 broadcast_add_fusion.block_ref
  51.1 3.5 %collective-permute-done.17.refs_0_ = f32[8,256,256]{2,1,0:T(8,128)S(1)} collective-permute-done((f32[8,256,256]{2,1,0:T(8,128)}, f32[8,256,256]{2,1,0:T(8,128)S(1)}, u32[]{:S(2)}, u32[]{:S(2)}) %collective-permute-start.17) | collective-permute-done | bytes 2097184 | tf_op jit(solution)/shard_map/ppermute | solution.py:287
  54.5 1.3 copy-done.2
  55.9 8.4 %gram_pieces.7 = f32[8,256,256]{2,1,0:T(8,128)} custom-call(s32[8]{0:T(128)} %broadcast_add_fusion.block_ref, bf16[512,1024]{1,0:T(8,128)(2,1)} %get-tuple-element.17.scaled_ref, bf16[1024,4096]{1,0:T(8,128)(2,1)} %rows_ref.7, f32[8,256,256]{2,1,0:T(8,128)} %copy-done.2), custom_call_target="tpu_custom_call" | custom-call | flops 1073741824 | bytes 6815744 | tf_op jit(solution)/shard_map/gram_pieces/pallas_call | solution.py:178
  64.3 0.6 copy-done.7
  64.9 4.6 %fusion = f32[512,256]{1,0:T(8,128)S(1)} fusion(f32[256,4096]{1,0:T(8,128)} %refs_2_.1, s32[512]{0:T(512)S(1)} %copy-done.7), kind=kOutput, calls=%fused_computation.1 | convolution fusion | flops 3223322624 | bytes 4720640 | tf_op jit(solution)/shard_map/dot_general | solution.py:275
  69.6 7.2 %reduce-scatter.3.cloned.1.call-done = f32[1,256,256]{2,1,0:T(8,128)} async-done(((f32[8,256,256]{2,1,0:T(8,128)}), f32[1,256,256]{2,1,0:T(8,128)}) %reduce-scatter.3.cloned.1.call-update) | async-done | bytes 262160 | tf_op jit(solution)/shard_map/reduce_scatter | solution.py:338
  76.7 34.3 %reduce-scatter.5.cloned.1.call-done = f32[1,256,256]{2,1,0:T(8,128)} async-done(((f32[8,256,256]{2,1,0:T(8,128)}), f32[1,256,256]{2,1,0:T(8,128)}) %reduce-scatter.5.cloned.1.call-update) | async-done | bytes 262160 | tf_op jit(solution)/shard_map/reduce_scatter | solution.py:338
  111.0 1.8 slice_add_fusion
  112.9 1.5 collective-permute-start.21
  114.5 0.7 fusion.5
  115.2 4.2 %collective-permute-done.21 = f32[256,256]{1,0:T(8,128)S(1)} collective-permute-done((f32[256,256]{1,0:T(8,128)S(1)}, f32[256,256]{1,0:T(8,128)S(1)}, u32[]{:S(2)}, u32[]{:S(2)}) %collective-permute-start.21) | collective-permute-done | bytes 262176 | tf_op jit(solution)/shard_map/ppermute | solution.py:348
  119.4 0.8 pad_maximum_fusion
  120.2 1.6 convolution_add_fusion
  121.8 0.3 copy.11
  122.2 0.2 fusion.4
  122.5 0.1 collective-permute-start
  122.7 1.7 collective-permute-done
  124.4 0.1 bitcast_add_fusion.1
  124.6 1.5 collective-permute-start.1
  126.1 3.2 %collective-permute-start.7 = (f32[32,512]{1,0:T(8,128)S(1)}, f32[32,512]{1,0:T(8,128)S(1)}, u32[]{:S(2)}, u32[]{:S(2)}) collective-permute-start(f32[32,512]{1,0:T(8,128)S(1)} %get-tuple-element.11), channel_id=1, source_target_pairs={{0,14},{1,15},{2,0},{3,1},{4,2},{5,3},{6,4},{7,5},{8,6},{9,7},{10,... | collective-permute-start | bytes 196616 | tf_op jit(solution)/shard_map/ppermute | solution.py:306
  129.4 0.6 collective-permute-start.6
  129.9 2.4 collective-permute-start.4
  132.3 1.4 collective-permute-done.1
  133.7 1.3 collective-permute-start.2
  134.9 3.3 %collective-permute-done.6 = f32[32,512]{1,0:T(8,128)S(1)} collective-permute-done((f32[32,512]{1,0:T(8,128)S(1)}, f32[32,512]{1,0:T(8,128)S(1)}, u32[]{:S(2)}, u32[]{:S(2)}) %collective-permute-start.6) | collective-permute-done | bytes 65568 | tf_op jit(solution)/shard_map/ppermute | solution.py:306
  138.3 1.8 collective-permute-done.5
  140.1 11.4 %collective-permute-done.4 = f32[32,512]{1,0:T(8,128)S(1)} collective-permute-done((f32[32,512]{1,0:T(8,128)S(1)}, f32[32,512]{1,0:T(8,128)S(1)}, u32[]{:S(2)}, u32[]{:S(2)}) %collective-permute-start.4) | collective-permute-done | bytes 65568 | tf_op jit(solution)/shard_map/ppermute | solution.py:306
  151.5 0.9 collective-permute-done.3
  152.4 0.1 collective-permute-start.8
  152.5 0.1 collective-permute-start.13
  152.5 2.1 collective-permute-start.12
  154.6 5.5 %collective-permute-start.11 = (f32[32,512]{1,0:T(8,128)S(1)}, f32[32,512]{1,0:T(8,128)S(1)}, u32[]{:S(2)}, u32[]{:S(2)}) collective-permute-start(f32[32,512]{1,0:T(8,128)S(1)} %get-tuple-element.7), channel_id=1, source_target_pairs={{0,8},{1,9},{2,10},{3,11},{4,12},{5,13},{6,14},{7,15},{8,0},{9,1},... | collective-permute-start | bytes 196616 | tf_op jit(solution)/shard_map/ppermute | solution.py:306
  160.1 0.5 collective-permute-start.9
  160.7 7.6 %collective-permute-done.9 = f32[32,512]{1,0:T(8,128)S(1)} collective-permute-done((f32[32,512]{1,0:T(8,128)S(1)}, f32[32,512]{1,0:T(8,128)S(1)}, u32[]{:S(2)}, u32[]{:S(2)}) %collective-permute-start.9) | collective-permute-done | bytes 65568 | tf_op jit(solution)/shard_map/ppermute | solution.py:306
  168.3 0.7 collective-permute-start.14
  169.0 2.8 %collective-permute-done.10 = f32[32,512]{1,0:T(8,128)S(1)} collective-permute-done((f32[32,512]{1,0:T(8,128)S(1)}, f32[32,512]{1,0:T(8,128)S(1)}, u32[]{:S(2)}, u32[]{:S(2)}) %collective-permute-start.10) | collective-permute-done | bytes 65568 | tf_op jit(solution)/shard_map/ppermute | solution.py:306
  171.8 1.7 collective-permute-done.11
  173.6 0.1 collective-permute-start.18
  173.7 29.0 %all-gather.7.cloned.1.call-done = f32[8,256,256]{2,1,0:T(8,128)} async-done(((f32[2,256,256]{2,1,0:T(8,128)}), f32[8,256,256]{2,1,0:T(8,128)}) %all-gather.7.cloned.1.call-update) | async-done | bytes 2097168 | tf_op jit(solution)/shard_map/all_gather | solution.py:350
  202.7 0.6 bitcast_dynamic-update-slice_fusion.1
  203.3 0.6 bitcast_dynamic-update-slice_fusion.mine_ref
  204.0 0.5 collective-permute-start.15
  204.4 0.6 pad_add_fusion.1.place_ref
  205.0 0.7 pad_add_fusion.refs_0_
  205.8 0.5 collective-permute-start.20
  206.2 1.7 collective-permute-done.15.other_ref
  207.9 22.4 %inverse_factor.1.inverse_ref = f32[512,512]{1,0:T(8,128)} custom-call(s32[2]{0:T(128)} %pad_add_fusion.1.place_ref, f32[8,32,512]{2,1,0:T(8,128)} %bitcast_dynamic-update-slice_fusion.mine_ref, f32[8,32,512]{2,1,0:T(8,128)} %collective-permute-done.15.other_ref, f32[1,512]{1,0:T(1,128)} %bitcast.82), custom_call_target="tpu_custom_call" | custom-call | flops 13421772800 | bytes 2097152 | tf_op jit(solution)/shard_map/inverse_factor/pallas_call | solution.py:131
  230.3 4.0 %solve_rows.1 = (f32[256,512]{1,0:T(8,128)}, f32[256,512]{1,0:T(8,128)}) custom-call(f32[512,512]{1,0:T(8,128)} %inverse_factor.1.inverse_ref, f32[256,256]{1,0:T(8,128)} %get-tuple-element.9.first_ref, f32[256,256]{1,0:T(8,128)} %copy-done.5), custom_call_target="tpu_custom_call" | custom-call | flops 805306368 | bytes 2097152 | tf_op jit(solution)/shard_map/solve_rows/pallas_call | solution.py:154
  234.3 1.3 copy-done
  235.6 15.8 %update_rows.1 = f32[256,4096]{1,0:T(8,128)} custom-call(s32[16]{0:T(128)} %pad_add_fusion.refs_0_, f32[256,512]{1,0:T(8,128)} %get-tuple-element.4.refs_1_, f32[256,4096]{1,0:T(8,128)} %refs_2_.1, f32[4,256,256]{2,1,0:T(8,128)} %bitcast.79, f32[4,256,256]{2,1,0:T(8,128)} %copy-done.4, f32[4,256,256]{2,1,0:T(8,128)} %collective-permute-done.19.refs_5_, ...), custom_call_target="tpu_custom_call" | custom-call | flops 3221225472 | bytes 16777216 | tf_op jit(solution)/shard_map/update_rows/pallas_call | solution.py:237
  (52 shorter events, 0.6 us)
Async XLA Ops:
  7.2 69.6 %reduce-scatter.3.cloned.1.call-start = ((), (), s32[]{:S(2)}) async-start(), calls=%async_computation.2 | async-start | bytes 2359296 | tf_op jit(solution)/shard_map/reduce_scatter | solution.py:338
  18.7 8.6 %copy-start.10 = (s32[8]{0:T(128)S(1)}, s32[8]{0:T(128)}, u32[]{:S(2)}) copy-start(s32[8]{0:T(128)} %constant.129) | copy-start | bytes 100
  26.8 4.4 %collective-permute-start.16 = (f32[8,256,256]{2,1,0:T(8,128)}, f32[8,256,256]{2,1,0:T(8,128)S(1)}, u32[]{:S(2)}, u32[]{:S(2)}) collective-permute-start(f32[8,256,256]{2,1,0:T(8,128)} %gram_pieces.4), channel_id=1, source_target_pairs={{0,1},{1,0},{2,3},{3,2},{4,5},{5,4},{6,7},{7,6},{8,9},{9,8},{10,11... | collective-permute-start | bytes 6291464 | tf_op jit(solution)/shard_map/ppermute | solution.py:287
  31.2 1.3 copy-start.3
  40.9 0.7 copy-start.9
  40.9 70.1 %reduce-scatter.5.cloned.1.call-start = ((), (), s32[]{:S(2)}) async-start(), calls=%async_computation.3 | async-start | bytes 2359296 | tf_op jit(solution)/shard_map/reduce_scatter | solution.py:338
  42.1 8.5 %copy-start.8 = (s32[8]{0:T(128)S(1)}, s32[8]{0:T(128)}, u32[]{:S(2)}) copy-start(s32[8]{0:T(128)} %constant.131) | copy-start | bytes 100
  50.2 4.4 %collective-permute-start.17 = (f32[8,256,256]{2,1,0:T(8,128)}, f32[8,256,256]{2,1,0:T(8,128)S(1)}, u32[]{:S(2)}, u32[]{:S(2)}) collective-permute-start(f32[8,256,256]{2,1,0:T(8,128)} %gram_pieces.6), channel_id=1, source_target_pairs={{0,1},{1,0},{2,3},{3,2},{4,5},{5,4},{6,7},{7,6},{8,9},{9,8},{10,11... | collective-permute-start | bytes 6291464 | tf_op jit(solution)/shard_map/ppermute | solution.py:287
  54.5 1.3 copy-start.2
  64.3 0.7 copy-start.7
  64.3 109.3 %all-gather.5.cloned.1.call-start = ((), (), s32[]{:S(2)}) async-start(), calls=%async_computation.4 | async-start | bytes 1310720 | tf_op jit(solution)/shard_map/all_gather | solution.py:353
  69.5 44.9 %copy-start.1 = (f32[512,256]{1,0:T(8,128)}, f32[512,256]{1,0:T(8,128)S(1)}, u32[]{:S(2)}) copy-start(f32[512,256]{1,0:T(8,128)S(1)} %fusion) | copy-start | bytes 1572868
  112.8 6.5 %copy-start.5 = (f32[256,256]{1,0:T(8,128)}, f32[256,256]{1,0:T(8,128)S(1)}, u32[]{:S(2)}) copy-start(f32[256,256]{1,0:T(8,128)S(1)} %get-tuple-element.8.second_ref) | copy-start | bytes 786436
  112.9 89.8 %all-gather.7.cloned.1.call-start = ((), (), s32[]{:S(2)}) async-start(), calls=%async_computation.5 | async-start | bytes 2621440 | tf_op jit(solution)/shard_map/all_gather | solution.py:350
  112.9 6.4 %collective-permute-start.21 = (f32[256,256]{1,0:T(8,128)S(1)}, f32[256,256]{1,0:T(8,128)S(1)}, u32[]{:S(2)}, u32[]{:S(2)}) collective-permute-start(f32[256,256]{1,0:T(8,128)S(1)} %get-tuple-element.8.second_ref), channel_id=1, source_target_pairs={{0,2},{1,3},{2,0},{3,1},{4,6},{5,7},{6,4},{7,5},{8,10},{9,11},{10,... | collective-permute-start | bytes 786440 | tf_op jit(solution)/shard_map/ppermute | solution.py:348
  122.5 2.0 collective-permute-start
  124.6 9.1 %collective-permute-start.1 = (f32[32,512]{1,0:T(8,128)S(1)}, f32[32,512]{1,0:T(8,128)S(1)}, u32[]{:S(2)}, u32[]{:S(2)}) collective-permute-start(f32[32,512]{1,0:T(8,128)S(1)} %get-tuple-element.10), channel_id=1, source_target_pairs={{0,2},{1,3},{2,4},{3,5},{4,6},{5,7},{6,8},{7,9},{8,10},{9,11},{10,... | collective-permute-start | bytes 196616 | tf_op jit(solution)/shard_map/ppermute | solution.py:306
  126.1 7.6 %collective-permute-start.7 = (f32[32,512]{1,0:T(8,128)S(1)}, f32[32,512]{1,0:T(8,128)S(1)}, u32[]{:S(2)}, u32[]{:S(2)}) collective-permute-start(f32[32,512]{1,0:T(8,128)S(1)} %get-tuple-element.11), channel_id=1, source_target_pairs={{0,14},{1,15},{2,0},{3,1},{4,2},{5,3},{6,4},{7,5},{8,6},{9,7},{10,... | collective-permute-start | bytes 196616 | tf_op jit(solution)/shard_map/ppermute | solution.py:306
  129.4 8.9 %collective-permute-start.6 = (f32[32,512]{1,0:T(8,128)S(1)}, f32[32,512]{1,0:T(8,128)S(1)}, u32[]{:S(2)}, u32[]{:S(2)}) collective-permute-start(f32[32,512]{1,0:T(8,128)S(1)} %get-tuple-element.12), channel_id=1, source_target_pairs={{0,12},{1,13},{2,14},{3,15},{4,0},{5,1},{6,2},{7,3},{8,4},{9,5},{1... | collective-permute-start | bytes 196616 | tf_op jit(solution)/shard_map/ppermute | solution.py:306
  129.9 10.1 %collective-permute-start.5 = (f32[32,512]{1,0:T(8,128)S(1)}, f32[32,512]{1,0:T(8,128)S(1)}, u32[]{:S(2)}, u32[]{:S(2)}) collective-permute-start(f32[32,512]{1,0:T(8,128)S(1)} %get-tuple-element.13), channel_id=1, source_target_pairs={{0,10},{1,11},{2,12},{3,13},{4,14},{5,15},{6,0},{7,1},{8,2},{9,3},... | collective-permute-start | bytes 196616 | tf_op jit(solution)/shard_map/ppermute | solution.py:306
  129.9 21.5 %collective-permute-start.4 = (f32[32,512]{1,0:T(8,128)S(1)}, f32[32,512]{1,0:T(8,128)S(1)}, u32[]{:S(2)}, u32[]{:S(2)}) collective-permute-start(f32[32,512]{1,0:T(8,128)S(1)} %get-tuple-element.14), channel_id=1, source_target_pairs={{0,8},{1,9},{2,10},{3,11},{4,12},{5,13},{6,14},{7,15},{8,0},{9,1},... | collective-permute-start | bytes 196616 | tf_op jit(solution)/shard_map/ppermute | solution.py:306
  133.7 18.7 %collective-permute-start.3 = (f32[32,512]{1,0:T(8,128)S(1)}, f32[32,512]{1,0:T(8,128)S(1)}, u32[]{:S(2)}, u32[]{:S(2)}) collective-permute-start(f32[32,512]{1,0:T(8,128)S(1)} %get-tuple-element.15), channel_id=1, source_target_pairs={{0,6},{1,7},{2,8},{3,9},{4,10},{5,11},{6,12},{7,13},{8,14},{9,15},... | collective-permute-start | bytes 196616 | tf_op jit(solution)/shard_map/ppermute | solution.py:306
  133.7 18.7 %collective-permute-start.2 = (f32[32,512]{1,0:T(8,128)S(1)}, f32[32,512]{1,0:T(8,128)S(1)}, u32[]{:S(2)}, u32[]{:S(2)}) collective-permute-start(f32[32,512]{1,0:T(8,128)S(1)} %get-tuple-element.16), channel_id=1, source_target_pairs={{0,4},{1,5},{2,6},{3,7},{4,8},{5,9},{6,10},{7,11},{8,12},{9,13},{1... | collective-permute-start | bytes 196616 | tf_op jit(solution)/shard_map/ppermute | solution.py:306
  152.4 7.7 %collective-permute-start.8 = (f32[32,512]{1,0:T(8,128)S(1)}, f32[32,512]{1,0:T(8,128)S(1)}, u32[]{:S(2)}, u32[]{:S(2)}) collective-permute-start(f32[32,512]{1,0:T(8,128)S(1)} %get-tuple-element.7), channel_id=1, source_target_pairs={{0,2},{1,3},{2,4},{3,5},{4,6},{5,7},{6,8},{7,9},{8,10},{9,11},{10,... | collective-permute-start | bytes 196616 | tf_op jit(solution)/shard_map/ppermute | solution.py:306
  152.5 50.2 %collective-permute-start.13 = (f32[32,512]{1,0:T(8,128)S(1)}, f32[32,512]{1,0:T(8,128)S(1)}, u32[]{:S(2)}, u32[]{:S(2)}) collective-permute-start(f32[32,512]{1,0:T(8,128)S(1)} %get-tuple-element.7), channel_id=1, source_target_pairs={{0,12},{1,13},{2,14},{3,15},{4,0},{5,1},{6,2},{7,3},{8,4},{9,5},{1... | collective-permute-start | bytes 196616 | tf_op jit(solution)/shard_map/ppermute | solution.py:306
  152.5 21.1 %collective-permute-start.12 = (f32[32,512]{1,0:T(8,128)S(1)}, f32[32,512]{1,0:T(8,128)S(1)}, u32[]{:S(2)}, u32[]{:S(2)}) collective-permute-start(f32[32,512]{1,0:T(8,128)S(1)} %get-tuple-element.7), channel_id=1, source_target_pairs={{0,10},{1,11},{2,12},{3,13},{4,14},{5,15},{6,0},{7,1},{8,2},{9,3},... | collective-permute-start | bytes 196616 | tf_op jit(solution)/shard_map/ppermute | solution.py:306
  154.6 18.9 %collective-permute-start.11 = (f32[32,512]{1,0:T(8,128)S(1)}, f32[32,512]{1,0:T(8,128)S(1)}, u32[]{:S(2)}, u32[]{:S(2)}) collective-permute-start(f32[32,512]{1,0:T(8,128)S(1)} %get-tuple-element.7), channel_id=1, source_target_pairs={{0,8},{1,9},{2,10},{3,11},{4,12},{5,13},{6,14},{7,15},{8,0},{9,1},... | collective-permute-start | bytes 196616 | tf_op jit(solution)/shard_map/ppermute | solution.py:306
  160.1 11.7 %collective-permute-start.10 = (f32[32,512]{1,0:T(8,128)S(1)}, f32[32,512]{1,0:T(8,128)S(1)}, u32[]{:S(2)}, u32[]{:S(2)}) collective-permute-start(f32[32,512]{1,0:T(8,128)S(1)} %get-tuple-element.7), channel_id=1, source_target_pairs={{0,6},{1,7},{2,8},{3,9},{4,10},{5,11},{6,12},{7,13},{8,14},{9,15},... | collective-permute-start | bytes 196616 | tf_op jit(solution)/shard_map/ppermute | solution.py:306
  160.1 8.1 %collective-permute-start.9 = (f32[32,512]{1,0:T(8,128)S(1)}, f32[32,512]{1,0:T(8,128)S(1)}, u32[]{:S(2)}, u32[]{:S(2)}) collective-permute-start(f32[32,512]{1,0:T(8,128)S(1)} %get-tuple-element.7), channel_id=1, source_target_pairs={{0,4},{1,5},{2,6},{3,7},{4,8},{5,9},{6,10},{7,11},{8,12},{9,13},{1... | collective-permute-start | bytes 196616 | tf_op jit(solution)/shard_map/ppermute | solution.py:306
  168.3 35.1 %collective-permute-start.14 = (f32[32,512]{1,0:T(8,128)S(1)}, f32[32,512]{1,0:T(8,128)S(1)}, u32[]{:S(2)}, u32[]{:S(2)}) collective-permute-start(f32[32,512]{1,0:T(8,128)S(1)} %get-tuple-element.7), channel_id=1, source_target_pairs={{0,14},{1,15},{2,0},{3,1},{4,2},{5,3},{6,4},{7,5},{8,6},{9,7},{10,... | collective-permute-start | bytes 196616 | tf_op jit(solution)/shard_map/ppermute | solution.py:306
  173.6 32.2 %collective-permute-start.18 = (f32[4,256,256]{2,1,0:T(8,128)}, f32[4,256,256]{2,1,0:T(8,128)S(1)}, u32[]{:S(2)}, u32[]{:S(2)}) collective-permute-start(f32[4,256,256]{2,1,0:T(8,128)} %bitcast.77), channel_id=1, source_target_pairs={{0,2},{1,3},{2,0},{3,1},{4,6},{5,7},{6,4},{7,5},{8,10},{9,11},{10,... | collective-permute-start | bytes 3145736 | tf_op jit(solution)/shard_map/ppermute | solution.py:348
  173.7 29.0 %copy-start.6 = (f32[8,32,512]{2,1,0:T(8,128)}, f32[8,32,512]{2,1,0:T(8,128)S(1)}, u32[]{:S(2)}) copy-start(f32[8,32,512]{2,1,0:T(8,128)S(1)} %bitcast_dynamic-update-slice_fusion.2) | copy-start | bytes 1572868
  202.7 31.6 %collective-permute-start.22 = (f32[4,2,256,256]{3,2,1,0:T(8,128)}, f32[4,2,256,256]{3,2,1,0:T(8,128)S(1)}, u32[]{:S(2)}, u32[]{:S(2)}) collective-permute-start(f32[4,2,256,256]{3,2,1,0:T(8,128)} %bitcast.73), channel_id=1, source_target_pairs={{0,1},{1,0},{2,3},{3,2},{4,5},{5,4},{6,7},{7,6},{8,9},{9,8},{10,11... | collective-permute-start | bytes 6291464 | tf_op jit(solution)/shard_map/ppermute | solution.py:287
  204.0 3.9 %collective-permute-start.15 = (f32[8,32,512]{2,1,0:T(8,128)}, f32[8,32,512]{2,1,0:T(8,128)}, u32[]{:S(2)}, u32[]{:S(2)}) collective-permute-start(f32[8,32,512]{2,1,0:T(8,128)} %bitcast_dynamic-update-slice_fusion.mine_ref), channel_id=1, source_target_pairs={{0,1},{1,0},{2,3},{3,2},{4,5},{5,4},{6,7},{7,6},{8,9},{9,8},{10,11... | collective-permute-start | bytes 1572872 | tf_op jit(solution)/shard_map/ppermute | solution.py:287
  205.7 28.6 %collective-permute-start.19 = (f32[4,256,256]{2,1,0:T(8,128)}, f32[4,256,256]{2,1,0:T(8,128)}, u32[]{:S(2)}, u32[]{:S(2)}) collective-permute-start(f32[4,256,256]{2,1,0:T(8,128)} %bitcast.78), channel_id=1, source_target_pairs={{0,1},{1,0},{2,3},{3,2},{4,5},{5,4},{6,7},{7,6},{8,9},{9,8},{10,11... | collective-permute-start | bytes 3145736 | tf_op jit(solution)/shard_map/ppermute | solution.py:287
  205.8 24.5 %copy-start.4 = (f32[4,256,256]{2,1,0:T(8,128)}, f32[4,256,256]{2,1,0:T(8,128)S(1)}, u32[]{:S(2)}) copy-start(f32[4,256,256]{2,1,0:T(8,128)S(1)} %collective-permute-done.18.refs_4_) | copy-start | bytes 3145732
  205.8 28.5 %collective-permute-start.20 = (f32[4,256,256]{2,1,0:T(8,128)S(1)}, f32[4,256,256]{2,1,0:T(8,128)}, u32[]{:S(2)}, u32[]{:S(2)}) collective-permute-start(f32[4,256,256]{2,1,0:T(8,128)S(1)} %collective-permute-done.18.refs_4_), channel_id=1, source_target_pairs={{0,1},{1,0},{2,3},{3,2},{4,5},{5,4},{6,7},{7,6},{8,9},{9,8},{10,11... | collective-permute-start | bytes 3145736 | tf_op jit(solution)/shard_map/ppermute | solution.py:287
  234.3 1.3 copy-start
Sparse Core Ops, SparseCore 0:
  41.0 35.6 reduce-scatter.2
  79.0 31.9 reduce-scatter.4
  113.0 38.3 all-gather.4
  153.4 49.1 all-gather.6
where the time goes:
time: 259 us; the launch traced here: 258 us
  waiting for transfers between devices  116 us (45%)
  Pallas kernels  75.1 us (29%)
  starting transfers between devices  21.6 us (8%)
  matrix products  15.9 us (6%)
  between operations  14.8 us (6%)
  other arithmetic  7.66 us (3%)
  local copies, waits for them, and re-layouts  6.91 us (3%)
    reduce_scatter x2, waiting for transfers between devices, shards_on_grid(): lax.psum_scatter(both, 'scen', scatter_dimension=0, axis_index_groups=[[2...  41.5 us
    pallas_call x4, Pallas kernels, gram_pieces(): pl.pallas_call(gram_kernel, grid_spec=pltpu.PrefetchScalarGridSpec(num_sc...  32.9 us
    ppermute x14, waiting for transfers between devices, shift(): lax.ppermute(values, 'scen', [(d, (d + 2 * by) % parts) for d in range(pa...  31 us
    all_gather x1, waiting for transfers between devices, shards_on_grid(): lax.all_gather(jnp.stack([panel[1], swap_y(panel[1])]), 'scen', axis_inde...  29 us
    pallas_call x1, Pallas kernels, inverse_factor(): pl.pallas_call(factor_kernel, out_shape=jax.ShapeDtypeStruct((size, size)...  22.4 us
    ppermute x14, starting transfers between devices, shift(): lax.ppermute(values, 'scen', [(d, (d + 2 * by) % parts) for d in range(pa...  17.9 us
    pallas_call x1, Pallas kernels, update_rows(): pl.pallas_call(lambda *refs: update_kernel(count, *refs), out_shape=jax.S...  15.8 us
    ppermute x7, waiting for transfers between devices, swap_cores(): return lax.ppermute(values, 'scen', [(d, d ^ 1) for d in range(parts)])  10.4 us
  transfers between devices with their start and end apart: 27, of which 16 were waited for; matrix products, arithmetic and copies ran while one was open for 5% of the time, Pallas kernels for 17%

commit v1 on v0

--- a/solution.py
+++ b/solution.py
@@ -109,13 +109,12 @@
         work[at, to] = jnp.zeros((TILE, TILE), jnp.float32)
 
 
-def factor_kernel(place_ref, mine_ref, other_ref, regular_ref, out_ref):
-    chips, rows = mine_ref.shape[0], mine_ref.shape[1]
-    chip, core = place_ref[0], place_ref[1]
-    for ref, on_core in ((mine_ref, core), (other_ref, 1 - core)):
-        for n in range(chips):
-            at = (on_core * chips + lax.rem(chip + chips - n, chips)) * rows
-            out_ref[pl.ds(pl.multiple_of(at, rows), rows), :] = ref[n]
+def factor_kernel(rows_ref, mine_ref, other_ref, regular_ref, out_ref):
+    count, rows = mine_ref.shape[0], mine_ref.shape[1]
+    for n in range(2 * count):
+        ref = mine_ref if n < count else other_ref
+        at = pl.ds(pl.multiple_of(rows_ref[n] * rows, rows), rows)
+        out_ref[at, :] = ref[n % count]
     size = out_ref.shape[0]
     row_id = lax.broadcasted_iota(jnp.int32, (TILE, TILE), 0)
     col_id = lax.broadcasted_iota(jnp.int32, (TILE, TILE), 1)
@@ -126,7 +125,7 @@
         factor_step(k, out_ref)
 
 
-def inverse_factor(place, mine, other, regular):
+def inverse_factor(rows, mine, other, regular):
     size = regular.shape[0]
     return pl.pallas_call(
         factor_kernel,
@@ -137,7 +136,7 @@
             flops=100 * size**3, bytes_accessed=8 * size * size, transcendentals=size
         ),
         name="inverse_factor",
-    )(place, mine, other, regular[None, :])
+    )(rows, mine, other, regular[None, :])
 
 
 def solve_kernel(inverse_ref, first_ref, second_ref, factor_ref, weight_ref):
@@ -163,90 +162,200 @@
     )(inverse, first, second)
 
 
-def gram_kernel(block_ref, scaled_ref, rows_ref, *refs):
-    out_ref = refs[-1]
-    total = jnp.dot(scaled_ref[...], rows_ref[...], preferred_element_type=jnp.float32)
-    out_ref[0] = total if len(refs) == 1 else total + refs[0][0]
-
-
-def gram_pieces(blocks, scaled, part, scenario_rows, owned, extra=None):
-    depth = scenario_rows.shape[0]
-    half = scaled.shape[0] // 2
-    count = blocks.shape[0]
-    piece = pl.BlockSpec((1, half, owned), lambda i, blocks: (i, 0, 0))
-    more = [] if extra is None else [extra]
+def front_kernel(
+    blocks_ref, slots_ref, scalars_ref, cols_ref, weights_ref, prior_ref, rows_ref,
+    block_ref, local_ref, given_0, given_1, kept_0, kept_1,
+    pick, picked, total, sums, sems,
+):
+    step, last = pl.program_id(0), pl.num_programs(0) - 1
+    order, width = pick.shape
+    owned = prior_ref.shape[0]
+    depth = rows_ref.shape[0]
+    half = width // 2
+    tall = order // 8
+    count = blocks_ref.shape[0] // 2
+
+    @pl.when(step == 0)
+    def _():
+        picked[...] = jnp.zeros_like(picked)
+
+        @pl.loop(0, order // tall)
+        def _(n):
+            at = pl.ds(pl.multiple_of(n * tall, tall), tall)
+            ids = n * tall + lax.broadcasted_iota(jnp.int32, (tall, width), 0)
+            chosen = (ids == cols_ref[...]).astype(jnp.float32).astype(jnp.bfloat16)
+            pick[at, :] = chosen
+            for part in split(prior_ref[:, at]):
+                picked[:owned] += jnp.dot(part, chosen, preferred_element_type=jnp.float32)
+
+        local = picked[:owned].T
+        local_ref[...] = local
+        ids = scalars_ref[1] + lax.broadcasted_iota(jnp.int32, (owned, width), 0)
+        chosen = (ids == cols_ref[...]).astype(jnp.float32).astype(jnp.bfloat16)
+        sums[...] = jnp.zeros_like(sums)
+        for part in split(local):
+            sums[...] += jnp.dot(part, chosen, preferred_element_type=jnp.float32)
+
+    picked[...] = jnp.zeros_like(picked)
+
+    @pl.loop(0, order // tall)
+    def _(n):
+        at = pl.ds(pl.multiple_of(n * tall, tall), tall)
+        picked[...] += jnp.dot(rows_ref[:, at], pick[at, :], preferred_element_type=jnp.float32)
+
+    slot = step * depth + lax.broadcasted_iota(jnp.int32, (1, depth), 1)
+    live = (slot < scalars_ref[0]).astype(jnp.float32)
+    factor_w = weights_ref[...] * live * (1.0 / scalars_ref[2].astype(jnp.float32))
+    scaled = (picked[...].T * factor_w).astype(jnp.bfloat16)
+    sums[...] += jnp.dot(
+        scaled, picked[...].astype(jnp.bfloat16), preferred_element_type=jnp.float32
+    )
+
+    @pl.when(step == last)
+    def _():
+        block_ref[...] = 0.5 * (sums[...] + sums[...].T)
+
+    def stores(n):
+        on, slot = n // count, n % count
+        out = []
+        for h, (given, kept) in enumerate(((given_0, kept_0), (given_1, kept_1))):
+            for which, ref in enumerate((given, kept)):
+                out.append(
+                    (
+                        on == which,
+                        pltpu.make_async_copy(
+                            total.at[n, pl.ds(h * half, half)],
+                            ref.at[slots_ref[h * count + slot]],
+                            sems.at[n, h],
+                        ),
+                    )
+                )
+        return out
+
+    @pl.loop(0, 2 * count)
+    def _(n):
+        at = pl.ds(pl.multiple_of(blocks_ref[n] * owned, owned), owned)
+        part = jnp.dot(scaled, rows_ref[:, at], preferred_element_type=jnp.float32)
+
+        @pl.when(step == 0)
+        def _():
+            total[n] = part
+
+        @pl.when(step > 0)
+        def _():
+            total[n] += part
+
+        @pl.when(step == last)
+        def _():
+            for here, store in stores(n):
+                pl.when(here)(store.start)
+
+    @pl.when(step == last)
+    def _():
+        @pl.loop(0, 2 * count)
+        def _(n):
+            for here, store in stores(n):
+                pl.when(here)(store.wait)
+
+
+def front(blocks, slots, scalars, panel_cols, row_weights, prior, scenario_rows):
+    count = blocks.shape[0] // 2
+    depth, order = scenario_rows.shape
+    width = panel_cols.shape[0]
+    owned = prior.shape[0]
+    half = width // 2
+    tall = min(512, depth)
+    pieces = jax.ShapeDtypeStruct((count, half, owned), jnp.float32)
+    whole = lambda shape: pl.BlockSpec(shape, lambda i: (0, 0))
+    smem = pl.BlockSpec(memory_space=pltpu.SMEM)
     return pl.pallas_call(
-        gram_kernel,
-        grid_spec=pltpu.PrefetchScalarGridSpec(
-            num_scalar_prefetch=1,
-            grid=(count,),
-            in_specs=[
-                pl.BlockSpec((half, depth), lambda i, blocks: (part, 0)),
-                pl.BlockSpec((depth, owned), lambda i, blocks: (0, blocks[i])),
-            ]
-            + [piece] * len(more),
-            out_specs=piece,
-        ),
-        out_shape=jax.ShapeDtypeStruct((count, half, owned), jnp.float32),
+        front_kernel,
+        grid=(depth // tall,),
+        in_specs=[
+            smem, smem, smem, whole((1, width)),
+            pl.BlockSpec((1, tall), lambda i: (0, i)),
+            whole((owned, order)),
+            pl.BlockSpec((tall, order), lambda i: (i, 0)),
+        ],
+        out_specs=[whole((width, width)), whole((width, owned))]
+        + [pl.BlockSpec(memory_space=pl.ANY)] * 4,
+        out_shape=[
+            jax.ShapeDtypeStruct((width, width), jnp.float32),
+            jax.ShapeDtypeStruct((width, owned), jnp.float32),
+        ]
+        + [pieces] * 4,
+        scratch_shapes=[
+            pltpu.VMEM((order, width), jnp.bfloat16),
+            pltpu.VMEM((tall, width), jnp.float32),
+            pltpu.VMEM((2 * count, width, owned), jnp.float32),
+            pltpu.VMEM((width, width), jnp.float32),
+            pltpu.SemaphoreType.DMA((2 * count, 2)),
+        ],
         cost_estimate=pl.CostEstimate(
-            flops=2 * count * depth * owned * half,
-            bytes_accessed=count * owned * (2 * depth + 4 * half) + 2 * depth * half,
+            flops=4 * depth * order * width,
+            bytes_accessed=2 * depth * order + 4 * owned * order + 4 * order * width,
             transcendentals=0,
         ),
         compiler_params=pltpu.CompilerParams(vmem_limit_bytes=VMEM_BYTES),
-        name="gram_pieces",
-    )(blocks, scaled, scenario_rows, *more)
-
-
-def update_kernel(count, block_ref, weight_ref, prior_ref, *refs):
-    sources, out_ref = refs[:6], refs[6]
-    held, total, in_sem, prior_sem, out_sem = refs[7:]
+        name="front",
+    )(blocks, slots, scalars, panel_cols[None, :], row_weights[None, :], prior, scenario_rows)
+
+
+def update_kernel(count, block_ref, ring_ref, weight_ref, prior_ref, *refs):
+    sources, out_ref, scratch = refs[:-6], refs[-6], refs[-5:]
+    held, total, in_sem, prior_sem, out_sem = scratch
     half, owned = held.shape[2], held.shape[3]
     fetch = pltpu.make_async_copy(prior_ref, total, prior_sem)
     fetch.start()
+    chips = count // 2
     loads = []
-    lines = count // 4
     for n in range(count):
-        way, z = n // lines, n % lines
-        pair = (sources[way].at[z], sources[4 + way // 2].at[z, way % 2])
-        loads.append(
-            [pltpu.make_async_copy(pair[h], held.at[n, h], in_sem.at[n, h]) for h in range(2)]
-        )
-        for load in loads[-1]:
-            load.start()
+        core, slot = n // chips, n % chips
+        pieces = sources[core * (chips + 1) : (core + 1) * (chips + 1)]
+        pieces = pieces[slot : slot + 1] if slot < chips - 1 else pieces[slot:]
+        rows = half // len(pieces)
+        copies = [
+            pltpu.make_async_copy(
+                piece, held.at[n, 0, pl.ds(i * rows, rows)], in_sem.at[n, i]
+            )
+            for i, piece in enumerate(pieces)
+        ]
+        second = sources[2 * (chips + 1) + core].at[ring_ref[slot]]
+        copies.append(pltpu.make_async_copy(second, held.at[n, 1], in_sem.at[n, 2]))
+        for copy in copies:
+            copy.start()
+        loads.append(copies)
     weights = split(weight_ref[...])
     fetch.wait()
-    stores = []
     for n in range(count):
-        for load in loads[n]:
-            load.wait()
+        for copy in loads[n]:
+            copy.wait()
         outer = dot_split(weights, split(held[n].reshape(2 * half, owned)))
         cols = pl.ds(pl.multiple_of(block_ref[n] * owned, owned), owned)
         total[:, cols] -= outer
-        store = pltpu.make_async_copy(total.at[:, cols], out_ref.at[:, cols], out_sem.at[n])
-        store.start()
-        stores.append(store)
-    for store in stores:
-        store.wait()
-
-
-def update_rows(blocks, weights, prior, sources):
+    store = pltpu.make_async_copy(total, out_ref, out_sem)
+    store.start()
+    store.wait()
+
+
+def update_rows(blocks, ring, weights, prior, sources):
     count = blocks.shape[0]
     owned, order = prior.shape
     half = weights.shape[1] // 2
+    smem = pl.BlockSpec(memory_space=pltpu.SMEM)
     return pl.pallas_call(
         lambda *refs: update_kernel(count, *refs),
         out_shape=jax.ShapeDtypeStruct(prior.shape, jnp.float32),
-        in_specs=[pl.BlockSpec(memory_space=pltpu.SMEM)]
+        in_specs=[smem, smem]
         + vmem(1)
         + [pl.BlockSpec(memory_space=pl.ANY)] * (1 + len(sources)),
         out_specs=pl.BlockSpec(memory_space=pl.ANY),
         scratch_shapes=[
             pltpu.VMEM((count, 2, half, owned), jnp.float32),
             pltpu.VMEM(prior.shape, jnp.float32),
-            pltpu.SemaphoreType.DMA((count, 2)),
+            pltpu.SemaphoreType.DMA((count, 3)),
             pltpu.SemaphoreType.DMA,
-            pltpu.SemaphoreType.DMA((count,)),
+            pltpu.SemaphoreType.DMA,
         ],
         cost_estimate=pl.CostEstimate(
             flops=12 * owned * order * half,
@@ -255,7 +364,7 @@
         ),
         compiler_params=pltpu.CompilerParams(vmem_limit_bytes=VMEM_BYTES),
         name="update_rows",
-    )(blocks, weights, prior, *sources)
+    )(blocks, ring, weights, prior, *sources)
 
 
 def local_parts(scenario_rows, row_weights, row_counts, panel_cols, prior_schur):
@@ -288,79 +397,113 @@
 
 
 def halve_block(block):
-    chips = lax.axis_size("scen") // 2
     width = block.shape[0]
     core = lax.axis_index("scen") % 2
     halves = block.reshape(2, width // 2, width)
     given = lax.dynamic_index_in_dim(halves, 1 - core, 0, keepdims=False)
     kept = lax.dynamic_index_in_dim(halves, core, 0, keepdims=False)
-    return (kept + swap_cores(given)).reshape(chips, -1, width)
-
-
-def sum_block(block):
+    return kept + swap_cores(given)
+
+
+def sum_block(block, swap_y):
     parts = lax.axis_size("scen")
     chips = parts // 2
-    chip = lax.axis_index("scen") // 2
+    lines = chips // 2
+    place = lax.axis_index("scen")
+    core, y, z = place % 2, place // 2 % 2, place // 4
 
     def shift(values, by):
-        return lax.ppermute(values, "scen", [(d, (d + 2 * by) % parts) for d in range(parts)])
-
-    both = halve_block(block)
-    mine = lax.dynamic_index_in_dim(both, chip, 0, keepdims=False)
-    for by in range(1, chips):
-        mine += shift(lax.dynamic_index_in_dim(both, (chip + by) % chips, 0, keepdims=False), by)
-    mine = jnp.stack([mine] + [shift(mine, by) for by in range(1, chips)])
-    return mine, swap_cores(mine)
-
-
-def shards_on_grid(scenario_rows, row_weights, row_counts, panel_cols, regular, prior_schur):
+        return lax.ppermute(values, "scen", [(d, (d + 4 * by) % parts) for d in range(parts)])
+
+    both = halve_block(block).reshape(2, lines, -1, block.shape[0])
+    given = lax.dynamic_index_in_dim(both, 1 - y, 0, keepdims=False)
+    both = lax.dynamic_index_in_dim(both, y, 0, keepdims=False) + swap_y(given)
+    mine = lax.dynamic_index_in_dim(both, z, 0, keepdims=False)
+    mine = mine + sum(
+        shift(lax.dynamic_index_in_dim(both, (z + by) % lines, 0, keepdims=False), by)
+        for by in range(1, lines)
+    )
+    mine = jnp.stack([mine] + [shift(mine, by) for by in range(1, lines)])
+    mine = jnp.concatenate([mine, swap_y(mine)])
+    line = (z - jnp.arange(lines, dtype=jnp.int32)) % lines
+    rows = jnp.concatenate(
+        [(2 * c + w) * lines + line for c in (core, 1 - core) for w in (y, 1 - y)]
+    )
+    return rows, mine, swap_cores(mine)
+
+
+def shards_on_ring(scenario_rows, row_weights, row_counts, panel_cols, regular, prior_schur):
     parts = lax.axis_size("scen")
     chips = parts // 2
+    far = chips // 2
+    depth = scenario_rows.shape[0]
     owned = prior_schur.shape[0]
     half = panel_cols.shape[0] // 2
     place = lax.axis_index("scen")
-    core, chip = place % 2, place // 2
+    core = place % 2
     ring = RINGS[chips]
-
-    scaled, local_cols, block = local_parts(
-        scenario_rows, row_weights, row_counts, panel_cols, prior_schur
-    )
-
-    orders = (ring, ring[::-1])
-    tables = [jnp.array(order, jnp.int32) * 2 for order in orders]
-    given = [
-        swap_cores(gram_pieces(tables[h] + 1 - core, scaled, h, scenario_rows, owned))
-        for h in range(2)
-    ]
-    panel = []
-    for h in range(2):
-        both = gram_pieces(tables[h] + core, scaled, h, scenario_rows, owned, given[h])
-        summed = lax.psum_scatter(
-            both, "scen", scatter_dimension=0,
-            axis_index_groups=[[2 * q + c for q in orders[h]] for c in range(2)],
-        )
-        panel.append(summed + local_cols[h * half : (h + 1) * half])
-    block_mine, block_other = sum_block(block)
-
-    lines = [[2 * (2 * z + y) + c for z in range(chips // 2)] for y in range(2) for c in range(2)]
+    chip_at = jnp.array(ring, jnp.int32)
+    position = jnp.array([ring.index(chip) for chip in range(chips)], jnp.int32)[place // 2]
+    groups = [[2 * chip + c for chip in ring] for c in range(2)]
+
+    def step(values, way):
+        pairs = [
+            (2 * ring[q] + c, 2 * ring[(q + way) % chips] + c) for q in range(chips) for c in range(2)
+        ]
+        return lax.ppermute(values, "scen", pairs)
 
     def swap_y(values):
         return lax.ppermute(values, "scen", [(d, d ^ 2) for d in range(parts)])
 
-    second = lax.all_gather(
-        jnp.stack([panel[1], swap_y(panel[1])]), "scen", axis_index_groups=lines
-    )
-    first = lax.all_gather(panel[0], "scen", axis_index_groups=lines)
-    first = [first, swap_y(first)]
-    sources = first + [swap_cores(part) for part in first] + [second, swap_cores(second)]
-    z = jnp.arange(chips // 2, dtype=jnp.int32)
-    blocks = jnp.concatenate(
-        [2 * (2 * z + y) + c for c in (core, 1 - core) for y in (chip % 2, 1 - chip % 2)]
-    )
-
-    inverse = inverse_factor(jnp.stack([chip, core]), block_mine, block_other, regular)
-    factor_rows, weights = solve_rows(inverse, *panel)
-    return update_rows(blocks, weights, prior_schur, sources), factor_rows
+    def on_ring(offsets):
+        return (position + jnp.array(offsets, jnp.int32)) % chips
+
+    offsets = [far] + [way * d for d in range(far - 1, 0, -1) for way in (1, -1)] + [0]
+    where = on_ring(offsets)
+    blocks = jnp.concatenate([2 * chip_at[where] + c for c in (1 - core, core)])
+    slots = jnp.concatenate([jnp.arange(chips, dtype=jnp.int32), where])
+    scalars = jnp.stack([row_counts[0], place * owned, jnp.int32(depth * parts)])
+    block, local_cols, given_0, given_1, kept_0, kept_1 = front(
+        blocks, slots, scalars, panel_cols, row_weights, prior_schur, scenario_rows
+    )
+
+    summed = lax.psum_scatter(
+        kept_1 + swap_cores(given_1), "scen", scatter_dimension=0, axis_index_groups=groups
+    )
+    panel_1 = summed + local_cols[half:]
+
+    got_0 = swap_cores(given_0)
+    sides = {1: slice(0, half // 2), -1: slice(half // 2, half)}
+
+    def partial(offset):
+        n = offsets.index(offset)
+        return kept_0[n] + got_0[n]
+
+    arrived = {way: step(partial(far)[sides[way]], way) for way in (1, -1)}
+    arrived = {
+        1: jnp.pad(arrived[1], ((0, half // 2), (0, 0))),
+        -1: jnp.pad(arrived[-1], ((half // 2, 0), (0, 0))),
+    }
+    for d in range(far - 1, 0, -1):
+        arrived = {way: step(partial(way * d) + arrived[way], way) for way in (1, -1)}
+    panel_0 = partial(0) + arrived[1] + arrived[-1] + local_cols[:half]
+
+    rows, block_mine, block_other = sum_block(block, swap_y)
+
+    second = lax.all_gather(panel_1, "scen", axis_index_groups=groups)
+    first = [panel_0]
+    ahead = {1: panel_0, -1: panel_0}
+    for d in range(1, far):
+        ahead = {way: step(ahead[way], way) for way in (1, -1)}
+        first += [ahead[1], ahead[-1]]
+    first += [step(ahead[way][sides[way]], way) for way in (1, -1)]
+    sources = first + [swap_cores(piece) for piece in first] + [second, swap_cores(second)]
+    where = on_ring([0] + [-way * d for d in range(1, far) for way in (1, -1)] + [far])
+    blocks = jnp.concatenate([2 * chip_at[where] + c for c in (core, 1 - core)])
+
+    inverse = inverse_factor(rows, block_mine, block_other, regular)
+    factor_rows, weights = solve_rows(inverse, panel_0, panel_1)
+    return update_rows(blocks, where, weights, prior_schur, sources), factor_rows
 
 
 def shards_by_groups(scenario_rows, row_weights, row_counts, panel_cols, regular, prior_schur):
@@ -376,7 +519,7 @@
         scenario_rows, row_weights, row_counts, panel_cols, prior_schur
     )
     block = lax.psum_scatter(
-        halve_block(block), "scen", scatter_dimension=0, axis_index_groups=same_core
+        halve_block(block).reshape(chips, -1, width), "scen", scatter_dimension=0, axis_index_groups=same_core
     )
     block = lax.all_gather(block, "scen", axis_index_groups=same_core).reshape(1, half, width)
     block_other = swap_cores(block)
@@ -391,7 +534,7 @@
     panel_rows = gram_mine + local_cols.T
     panel_half = lax.all_gather(panel_rows, "scen", axis_index_groups=same_core)
     panel_rest = swap_cores(panel_half)
-    inverse = inverse_factor(jnp.stack([jnp.int32(0), core]), block, block_other, regular)
+    inverse = inverse_factor(jnp.stack([core, 1 - core]), block, block_other, regular)
     factor_rows, weights = solve_rows(inverse, panel_rows.T[:half], panel_rows.T[half:])
     even = jnp.where(core == 0, panel_half, panel_rest)
     odd = jnp.where(core == 0, panel_rest, panel_half)
@@ -410,7 +553,7 @@
         P("scen", None),
     )
     return jax.shard_map(
-        shards_on_grid if mesh.shape["scen"] // 2 in RINGS else shards_by_groups,
+        shards_on_ring if mesh.shape["scen"] // 2 in RINGS else shards_by_groups,
         mesh=mesh,
         in_specs=placed,
         out_specs=(P(("grp", "scen"), None), P(("grp", "scen"), None)),

time: 259 us -> 243 us (0.938)
  waiting for transfers between devices: 116 us -> 91 us
  matrix products: 15.9 us -> 0 us
  starting transfers between devices: 21.6 us -> 34.9 us
  other arithmetic: 7.66 us -> 17.3 us
  local copies, waits for them, and re-layouts: 6.91 us -> 10.3 us
    reduce_scatter x2 -> x1, waiting for transfers between devices: 41.5 us -> 0.01 us  [shards_on_ring(): lax.psum_scatter(kept_1 + swap_cores(given_1), 'scen', scatter_dimension=...]
    ppermute x14 -> x22, waiting for transfers between devices: 31 us -> 70.6 us  [the longest x16 54.5 us: step(): return lax.ppermute(values, 'scen', pairs)]
    all_gather x2 -> x1, waiting for transfers between devices: 29 us -> 0.01 us  [shards_on_ring(): second = lax.all_gather(panel_1, 'scen', axis_index_groups=groups)]
    dot_general x4 -> x0, matrix products: 15.9 us -> none  [the longest x1 8.93 us: local_parts(): lax.dot_general(pick.astype(jnp.bfloat16), scenario_rows, (((1,), (1,)),...]
    ppermute x14 -> x22, starting transfers between devices: 17.9 us -> 28.8 us  [the longest x16 21 us: step(): return lax.ppermute(values, 'scen', pairs)]
    add x7 -> x14, other arithmetic: 2.93 us -> 11.8 us  [the longest x5 5.13 us: shards_on_ring(): partial(way * d) + arrived[way]]
    ppermute x2, waiting for transfers between devices: 4.17 us -> 12.3 us  [swap_y(): return lax.ppermute(values, 'scen', [(d, d ^ 2) for d in range(parts)])]
    pallas_call x4 -> x1, Pallas kernels: 32.9 us -> 30.1 us  [front(): pl.pallas_call(front_kernel, grid=(depth // tall,), in_specs=[smem, smem,...]
  transfers between devices with their start and end apart: 27 -> 40, of which waited for: 16 -> 23; matrix products, arithmetic and copies ran while one was open for 5% -> 7% of each run, Pallas kernels for 17% -> 11%
where the time goes in v1:
time: 243 us; the launch traced here: 242 us
  waiting for transfers between devices  91 us (37%)
  Pallas kernels  73.6 us (30%)
  starting transfers between devices  34.9 us (14%)
  other arithmetic  17.3 us (7%)
  between operations  15.1 us (6%)
  local copies, waits for them, and re-layouts  10.3 us (4%)
    ppermute x16, waiting for transfers between devices, step(): return lax.ppermute(values, 'scen', pairs)  54.5 us
    pallas_call x1, Pallas kernels, front(): pl.pallas_call(front_kernel, grid=(depth // tall,), in_specs=[smem, smem,...  30.1 us
    pallas_call x1, Pallas kernels, inverse_factor(): pl.pallas_call(factor_kernel, out_shape=jax.ShapeDtypeStruct((size, size)...  22.4 us
    ppermute x16, starting transfers between devices, step(): return lax.ppermute(values, 'scen', pairs)  21 us
    pallas_call x1, Pallas kernels, update_rows(): pl.pallas_call(lambda *refs: update_kernel(count, *refs), out_shape=jax.S...  17.2 us
    ppermute x6, waiting for transfers between devices, shift(): lax.ppermute(values, 'scen', [(d, (d + 4 * by) % parts) for d in range(pa...  16.1 us
    ppermute x2, waiting for transfers between devices, swap_y(): return lax.ppermute(values, 'scen', [(d, d ^ 2) for d in range(parts)])  12.3 us
    ppermute x14, waiting for transfers between devices, swap_cores(): return lax.ppermute(values, 'scen', [(d, d ^ 1) for d in range(parts)])  8.03 us
  transfers between devices with their start and end apart: 40, of which 23 were waited for; matrix products, arithmetic and copies ran while one was open for 7% of the time, Pallas kernels for 11%

profile of v1, /device:TPU:0, one launch (start us, length us, event | category | flops | bytes accessed | tf_op | source)
XLA Modules:
  0.0 242.2 jit_solution(8768180759468332964)
XLA Ops:
  7.9 1.3 dynamic_slice.30
  9.1 1.3 compare_select_fusion
  10.4 1.3 gather_fusion.1
  12.3 0.7 pad_add_fusion.2
  13.0 30.1 %front.1 = (f32[512,512]{1,0:T(8,128)}, f32[512,256]{1,0:T(8,128)}, f32[8,256,256]{2,1,0:T(8,128)}, f32[8,256,256]{2,1,0:T(8,128)}, f32[8,256,256]{2,1,0:T(8,128)}, /*index=5*/f32[8,256,256]{2,1,0:T(8,128)}) custom-call(s32[16]{0:T(128)} %get-tuple-element.37.blocks_ref, s32[16]{0:T(128)} %get-tuple-element.38.slots_ref, s32[3]{0:T(128)} %pad_add_fusion.4.scalars_ref, ...), custom_call_target="tpu_custom_call" | custom-call | flops 8589934592 | bytes 20971520 | tf_op jit(solution)/shard_map/front/pallas_call | solution.py:271
  43.7 6.1 %collective-permute-done.19 = f32[8,256,256]{2,1,0:T(8,128)S(1)} collective-permute-done((f32[8,256,256]{2,1,0:T(8,128)}, f32[8,256,256]{2,1,0:T(8,128)S(1)}, u32[]{:S(2)}, u32[]{:S(2)}) %collective-permute-start.19) | collective-permute-done | bytes 2097184 | tf_op jit(solution)/shard_map/ppermute | solution.py:396
  49.8 3.4 %add.324 = f32[8,256,256]{2,1,0:T(8,128)} add(f32[8,256,256]{2,1,0:T(8,128)} %get-tuple-element.14, f32[8,256,256]{2,1,0:T(8,128)S(1)} %collective-permute-done.19) | non-fusion elementwise | flops 524288 | bytes 6291456 | tf_op jit(solution)/shard_map/add | solution.py:471
  53.3 1.5 copy-done.2
  54.8 1.0 slice_add_fusion.3
  55.8 3.0 %collective-permute-start.11 = (f32[128,256]{1,0:T(8,128)S(1)}, f32[128,256]{1,0:T(8,128)S(1)}, u32[]{:S(2)}, u32[]{:S(2)}) collective-permute-start(f32[128,256]{1,0:T(8,128)S(1)} %get-tuple-element.28), channel_id=1, source_target_pairs={{0,4},{1,5},{4,8},{5,9},{8,12},{9,13},{12,14},{13,15},{14,10},{15,... | collective-permute-start | bytes 393224 | tf_op jit(solution)/shard_map/ppermute | solution.py:453
  58.8 3.7 %collective-permute-done.11 = f32[128,256]{1,0:T(8,128)S(1)} collective-permute-done((f32[128,256]{1,0:T(8,128)S(1)}, f32[128,256]{1,0:T(8,128)S(1)}, u32[]{:S(2)}, u32[]{:S(2)}) %collective-permute-start.11) | collective-permute-done | bytes 131104 | tf_op jit(solution)/shard_map/ppermute | solution.py:453
  62.5 1.0 fusion.7
  63.5 1.9 collective-permute-start.12
  65.4 12.3 %collective-permute-done.12 = f32[256,256]{1,0:T(8,128)S(1)} collective-permute-done((f32[256,256]{1,0:T(8,128)S(1)}, f32[256,256]{1,0:T(8,128)S(1)}, u32[]{:S(2)}, u32[]{:S(2)}) %collective-permute-start.12) | collective-permute-done | bytes 262176 | tf_op jit(solution)/shard_map/ppermute | solution.py:453
  77.8 1.0 fusion.9
  78.8 1.2 collective-permute-start.13
  80.0 0.9 collective-permute-start.15
  80.9 6.5 %collective-permute-done.15 = f32[128,256]{1,0:T(8,128)S(1)} collective-permute-done((f32[128,256]{1,0:T(8,128)S(1)}, f32[128,256]{1,0:T(8,128)S(1)}, u32[]{:S(2)}, u32[]{:S(2)}) %collective-permute-start.15) | collective-permute-done | bytes 131104 | tf_op jit(solution)/shard_map/ppermute | solution.py:453
  87.4 5.5 %collective-permute-done.13 = f32[256,256]{1,0:T(8,128)S(1)} collective-permute-done((f32[256,256]{1,0:T(8,128)S(1)}, f32[256,256]{1,0:T(8,128)S(1)}, u32[]{:S(2)}, u32[]{:S(2)}) %collective-permute-start.13) | collective-permute-done | bytes 262176 | tf_op jit(solution)/shard_map/ppermute | solution.py:453
  92.9 1.1 fusion.11
  94.1 1.6 collective-permute-start.16
  95.6 4.8 %collective-permute-done.16 = f32[256,256]{1,0:T(8,128)S(1)} collective-permute-done((f32[256,256]{1,0:T(8,128)S(1)}, f32[256,256]{1,0:T(8,128)S(1)}, u32[]{:S(2)}, u32[]{:S(2)}) %collective-permute-start.16) | collective-permute-done | bytes 262176 | tf_op jit(solution)/shard_map/ppermute | solution.py:453
  100.5 1.0 fusion.3
  101.5 1.6 collective-permute-start.17
  103.6 4.9 %collective-permute-done.17 = f32[256,256]{1,0:T(8,128)S(1)} collective-permute-done((f32[256,256]{1,0:T(8,128)S(1)}, f32[256,256]{1,0:T(8,128)S(1)}, u32[]{:S(2)}, u32[]{:S(2)}) %collective-permute-start.17) | collective-permute-done | bytes 262176 | tf_op jit(solution)/shard_map/ppermute | solution.py:453
  108.5 1.0 fusion.5
  109.5 1.5 collective-permute-start.18
  111.1 5.0 %collective-permute-done.18 = f32[256,256]{1,0:T(8,128)} collective-permute-done((f32[256,256]{1,0:T(8,128)S(1)}, f32[256,256]{1,0:T(8,128)}, u32[]{:S(2)}, u32[]{:S(2)}) %collective-permute-start.18) | collective-permute-done | bytes 262176 | tf_op jit(solution)/shard_map/ppermute | solution.py:453
  116.1 2.2 bitcast_add_fusion.1
  118.4 1.9 collective-permute-done
  120.4 1.6 collective-permute-start.1
  122.0 8.8 %collective-permute-done.1 = f32[4,32,512]{2,1,0:T(8,128)S(1)} collective-permute-done((f32[4,32,512]{2,1,0:T(8,128)S(1)}, f32[4,32,512]{2,1,0:T(8,128)S(1)}, u32[]{:S(2)}, u32[]{:S(2)}) %collective-permute-start.1) | collective-permute-done | bytes 262176 | tf_op jit(solution)/shard_map/ppermute | solution.py:456
  130.9 1.2 collective-permute-start.3
  132.1 2.9 %collective-permute-start.4 = (f32[32,512]{1,0:T(8,128)S(1)}, f32[32,512]{1,0:T(8,128)S(1)}, u32[]{:S(2)}, u32[]{:S(2)}) collective-permute-start(f32[32,512]{1,0:T(8,128)S(1)} %get-tuple-element.31), channel_id=1, source_target_pairs={{0,12},{1,13},{2,14},{3,15},{4,0},{5,1},{6,2},{7,3},{8,4},{9,5},{1... | collective-permute-start | bytes 196616 | tf_op jit(solution)/shard_map/ppermute | solution.py:416
  135.5 3.8 %collective-permute-done.3 = f32[32,512]{1,0:T(8,128)S(1)} collective-permute-done((f32[32,512]{1,0:T(8,128)S(1)}, f32[32,512]{1,0:T(8,128)S(1)}, u32[]{:S(2)}, u32[]{:S(2)}) %collective-permute-start.3) | collective-permute-done | bytes 65568 | tf_op jit(solution)/shard_map/ppermute | solution.py:416
  139.5 4.1 %collective-permute-done.2 = f32[32,512]{1,0:T(8,128)S(1)} collective-permute-done((f32[32,512]{1,0:T(8,128)S(1)}, f32[32,512]{1,0:T(8,128)S(1)}, u32[]{:S(2)}, u32[]{:S(2)}) %collective-permute-start.2) | collective-permute-done | bytes 65568 | tf_op jit(solution)/shard_map/ppermute | solution.py:416
  143.5 0.6 constant_dynamic-update-slice_fusion.4
  144.2 1.6 collective-permute-start.6
  145.8 1.6 collective-permute-start.5
  147.3 2.5 %collective-permute-done.7 = f32[32,512]{1,0:T(8,128)S(1)} collective-permute-done((f32[32,512]{1,0:T(8,128)S(1)}, f32[32,512]{1,0:T(8,128)S(1)}, u32[]{:S(2)}, u32[]{:S(2)}) %collective-permute-start.7) | collective-permute-done | bytes 65568 | tf_op jit(solution)/shard_map/ppermute | solution.py:416
  149.8 4.8 %collective-permute-done.6 = f32[32,512]{1,0:T(8,128)S(1)} collective-permute-done((f32[32,512]{1,0:T(8,128)S(1)}, f32[32,512]{1,0:T(8,128)S(1)}, u32[]{:S(2)}, u32[]{:S(2)}) %collective-permute-start.6) | collective-permute-done | bytes 65568 | tf_op jit(solution)/shard_map/ppermute | solution.py:416
  154.6 0.8 collective-permute-done.5
  155.5 2.5 %collective-permute-start.8 = (f32[4,32,512]{2,1,0:T(8,128)S(1)}, f32[4,32,512]{2,1,0:T(8,128)S(1)}, u32[]{:S(2)}, u32[]{:S(2)}) collective-permute-start(f32[4,32,512]{2,1,0:T(8,128)S(1)} %pad_maximum_fusion), channel_id=1, source_target_pairs={{0,2},{1,3},{2,0},{3,1},{4,6},{5,7},{6,4},{7,5},{8,10},{9,11},{10,... | collective-permute-start | bytes 786440 | tf_op jit(solution)/shard_map/ppermute | solution.py:456
  158.0 0.6 constant_dynamic-update-slice_fusion.3
  159.9 2.0 collective-permute-start.20
  161.9 3.5 %collective-permute-done.8 = f32[4,32,512]{2,1,0:T(8,128)S(1)} collective-permute-done((f32[4,32,512]{2,1,0:T(8,128)S(1)}, f32[4,32,512]{2,1,0:T(8,128)S(1)}, u32[]{:S(2)}, u32[]{:S(2)}) %collective-permute-start.8) | collective-permute-done | bytes 262176 | tf_op jit(solution)/shard_map/ppermute | solution.py:456
  165.4 0.7 constant_dynamic-update-slice_fusion.mine_ref
  166.7 1.5 collective-permute-done.21.refs_6_
  168.1 2.5 %collective-permute-start.23 = (f32[256,256]{1,0:T(8,128)S(1)}, f32[256,256]{1,0:T(8,128)}, u32[]{:S(2)}, u32[]{:S(2)}) collective-permute-start(f32[256,256]{1,0:T(8,128)S(1)} %collective-permute-done.21.refs_6_), channel_id=1, source_target_pairs={{0,2},{1,3},{4,0},{5,1},{8,4},{9,5},{12,8},{13,9},{14,12},{15,13},... | collective-permute-start | bytes 786440 | tf_op jit(solution)/shard_map/ppermute | solution.py:453
  170.6 1.1 compare_select_fusion.1
  171.7 0.6 gather_fusion
  173.1 2.0 collective-permute-done.23.refs_8_
  175.0 2.1 collective-permute-start.25
  177.2 4.7 %collective-permute-done.25.refs_10_ = f32[256,256]{1,0:T(8,128)S(1)} collective-permute-done((f32[256,256]{1,0:T(8,128)}, f32[256,256]{1,0:T(8,128)S(1)}, u32[]{:S(2)}, u32[]{:S(2)}) %collective-permute-start.25) | collective-permute-done | bytes 262176 | tf_op jit(solution)/shard_map/ppermute | solution.py:453
  181.9 1.9 collective-permute-done.24.refs_9_
  183.8 0.7 collective-permute-start.27
  184.5 1.4 collective-permute-start.26
  187.1 0.7 copy-done.10
  187.8 0.7 copy-done.11
  188.5 1.3 collective-permute-done.27.refs_12_
  190.3 22.4 %inverse_factor.1.inverse_ref = f32[512,512]{1,0:T(8,128)} custom-call(s32[16]{0:T(128)} %pad_add_fusion.1.rows_ref, f32[8,32,512]{2,1,0:T(8,128)} %constant_dynamic-update-slice_fusion.mine_ref, f32[8,32,512]{2,1,0:T(8,128)} %collective-permute-done.9.other_ref, f32[1,512]{1,0:T(1,128)} %bitcast.83), custom_call_target="tpu_custom_call" | custom-call | flops 13421772800 | bytes 2097152 | tf_op jit(solution)/shard_map/inverse_factor/pallas_call | solution.py:130
  212.7 4.0 %solve_rows.1 = (f32[256,512]{1,0:T(8,128)}, f32[256,512]{1,0:T(8,128)}) custom-call(f32[512,512]{1,0:T(8,128)} %inverse_factor.1.inverse_ref, f32[256,256]{1,0:T(8,128)} %copy-done.3, f32[256,256]{1,0:T(8,128)} %get-tuple-element.26.second_ref), custom_call_target="tpu_custom_call" | custom-call | flops 805306368 | bytes 2097152 | tf_op jit(solution)/shard_map/solve_rows/pallas_call | solution.py:153
  216.8 1.3 copy-done.1
  218.1 17.2 %update_rows.1 = f32[256,4096]{1,0:T(8,128)} custom-call(s32[16]{0:T(128)} %pad_add_fusion.refs_0_, s32[8]{0:T(128)} %get-tuple-element.23.refs_1_, f32[256,512]{1,0:T(8,128)} %get-tuple-element.16.refs_2_, f32[256,4096]{1,0:T(8,128)} %refs_3_.1, f32[256,256]{1,0:T(8,128)} %copy-done.3, f32[256,256]{1,0:T(8,128)} %copy-done.8, f32[256,256]{1,0:T(8,128)} %copy-done.7, ...), custom_call_target="tpu_custom_call" | custom-call | flops 3221225472 | bytes 16777216 | tf_op jit(solution)/shard_map/update_rows/pallas_call | solution.py:346
  (88 shorter events, 7.0 us)
Async XLA Ops:
  7.2 108.9 %reduce-scatter.2.cloned.1.call-start = ((), (), s32[]{:S(2)}) async-start(), calls=%async_computation.1 | async-start | bytes 2359296 | tf_op jit(solution)/shard_map/reduce_scatter | solution.py:470
  43.1 6.7 %collective-permute-start.19 = (f32[8,256,256]{2,1,0:T(8,128)}, f32[8,256,256]{2,1,0:T(8,128)S(1)}, u32[]{:S(2)}, u32[]{:S(2)}) collective-permute-start(f32[8,256,256]{2,1,0:T(8,128)} %get-tuple-element.15), channel_id=1, source_target_pairs={{0,1},{1,0},{2,3},{3,2},{4,5},{5,4},{6,7},{7,6},{8,9},{9,8},{10,11... | collective-permute-start | bytes 6291464 | tf_op jit(solution)/shard_map/ppermute | solution.py:396
  43.6 9.7 %collective-permute-start.10 = (f32[8,256,256]{2,1,0:T(8,128)}, f32[8,256,256]{2,1,0:T(8,128)}, u32[]{:S(2)}, u32[]{:S(2)}) collective-permute-start(f32[8,256,256]{2,1,0:T(8,128)} %get-tuple-element.12), channel_id=1, source_target_pairs={{0,1},{1,0},{2,3},{3,2},{4,5},{5,4},{6,7},{7,6},{8,9},{9,8},{10,11... | collective-permute-start | bytes 6291464 | tf_op jit(solution)/shard_map/ppermute | solution.py:396
  53.2 1.6 copy-start.2
  53.2 118.5 %all-gather.3.cloned.1.call-start = ((), (), s32[]{:S(2)}) async-start(), calls=%async_computation.2 | async-start | bytes 2359296 | tf_op jit(solution)/shard_map/all_gather | solution.py:493
  55.8 6.7 %collective-permute-start.11 = (f32[128,256]{1,0:T(8,128)S(1)}, f32[128,256]{1,0:T(8,128)S(1)}, u32[]{:S(2)}, u32[]{:S(2)}) collective-permute-start(f32[128,256]{1,0:T(8,128)S(1)} %get-tuple-element.28), channel_id=1, source_target_pairs={{0,4},{1,5},{4,8},{5,9},{8,12},{9,13},{12,14},{13,15},{14,10},{15,... | collective-permute-start | bytes 393224 | tf_op jit(solution)/shard_map/ppermute | solution.py:453
  63.5 14.2 %collective-permute-start.12 = (f32[256,256]{1,0:T(8,128)S(1)}, f32[256,256]{1,0:T(8,128)S(1)}, u32[]{:S(2)}, u32[]{:S(2)}) collective-permute-start(f32[256,256]{1,0:T(8,128)S(1)} %fusion.7), channel_id=1, source_target_pairs={{0,4},{1,5},{4,8},{5,9},{8,12},{9,13},{12,14},{13,15},{14,10},{15,... | collective-permute-start | bytes 786440 | tf_op jit(solution)/shard_map/ppermute | solution.py:453
  78.8 14.2 %collective-permute-start.13 = (f32[256,256]{1,0:T(8,128)S(1)}, f32[256,256]{1,0:T(8,128)S(1)}, u32[]{:S(2)}, u32[]{:S(2)}) collective-permute-start(f32[256,256]{1,0:T(8,128)S(1)} %fusion.9), channel_id=1, source_target_pairs={{0,4},{1,5},{4,8},{5,9},{8,12},{9,13},{12,14},{13,15},{14,10},{15,... | collective-permute-start | bytes 786440 | tf_op jit(solution)/shard_map/ppermute | solution.py:453
  80.0 7.4 %collective-permute-start.15 = (f32[128,256]{1,0:T(8,128)S(1)}, f32[128,256]{1,0:T(8,128)S(1)}, u32[]{:S(2)}, u32[]{:S(2)}) collective-permute-start(f32[128,256]{1,0:T(8,128)S(1)} %get-tuple-element.29), channel_id=1, source_target_pairs={{0,2},{1,3},{4,0},{5,1},{8,4},{9,5},{12,8},{13,9},{14,12},{15,13},... | collective-permute-start | bytes 393224 | tf_op jit(solution)/shard_map/ppermute | solution.py:453
  94.1 6.4 %collective-permute-start.16 = (f32[256,256]{1,0:T(8,128)S(1)}, f32[256,256]{1,0:T(8,128)S(1)}, u32[]{:S(2)}, u32[]{:S(2)}) collective-permute-start(f32[256,256]{1,0:T(8,128)S(1)} %get-tuple-element.25), channel_id=1, source_target_pairs={{0,2},{1,3},{4,0},{5,1},{8,4},{9,5},{12,8},{13,9},{14,12},{15,13},... | collective-permute-start | bytes 786440 | tf_op jit(solution)/shard_map/ppermute | solution.py:453
  101.5 16.8 %copy-start.4 = (f32[512,512]{1,0:T(8,128)S(1)}, f32[512,512]{1,0:T(8,128)}, u32[]{:S(2)}) copy-start(f32[512,512]{1,0:T(8,128)} %get-tuple-element.10) | copy-start | bytes 3145732
  101.5 7.0 %collective-permute-start.17 = (f32[256,256]{1,0:T(8,128)S(1)}, f32[256,256]{1,0:T(8,128)S(1)}, u32[]{:S(2)}, u32[]{:S(2)}) collective-permute-start(f32[256,256]{1,0:T(8,128)S(1)} %fusion.3), channel_id=1, source_target_pairs={{0,2},{1,3},{4,0},{5,1},{8,4},{9,5},{12,8},{13,9},{14,12},{15,13},... | collective-permute-start | bytes 786440 | tf_op jit(solution)/shard_map/ppermute | solution.py:453
  103.1 8.0 %collective-permute-start.14 = (f32[256,256]{1,0:T(8,128)S(1)}, f32[256,256]{1,0:T(8,128)}, u32[]{:S(2)}, u32[]{:S(2)}) collective-permute-start(f32[256,256]{1,0:T(8,128)S(1)} %get-tuple-element.24), channel_id=1, source_target_pairs={{0,4},{1,5},{4,8},{5,9},{8,12},{9,13},{12,14},{13,15},{14,10},{15,... | collective-permute-start | bytes 786440 | tf_op jit(solution)/shard_map/ppermute | solution.py:453
  109.5 6.5 %collective-permute-start.18 = (f32[256,256]{1,0:T(8,128)S(1)}, f32[256,256]{1,0:T(8,128)}, u32[]{:S(2)}, u32[]{:S(2)}) collective-permute-start(f32[256,256]{1,0:T(8,128)S(1)} %fusion.5), channel_id=1, source_target_pairs={{0,2},{1,3},{4,0},{5,1},{8,4},{9,5},{12,8},{13,9},{14,12},{15,13},... | collective-permute-start | bytes 786440 | tf_op jit(solution)/shard_map/ppermute | solution.py:453
  118.2 47.9 %copy-start.3 = (f32[256,256]{1,0:T(8,128)}, f32[256,256]{1,0:T(8,128)S(1)}, u32[]{:S(2)}) copy-start(f32[256,256]{1,0:T(8,128)S(1)} %get-tuple-element.27.first_ref.refs_4_) | copy-start | bytes 786436
  118.3 2.0 collective-permute-start
  120.4 50.2 %copy-start.13 = (s32[8]{0:T(128)S(1)}, s32[8]{0:T(128)}, u32[]{:S(2)}) copy-start(s32[8]{0:T(128)} %constant.138.clone) | copy-start | bytes 100
  120.4 51.3 %copy-start = (s32[8]{0:T(128)S(1)}, s32[8]{0:T(128)}, u32[]{:S(2)}) copy-start(s32[8]{0:T(128)} %constant.135.clone) | copy-start | bytes 100
  120.4 10.4 %collective-permute-start.1 = (f32[4,32,512]{2,1,0:T(8,128)S(1)}, f32[4,32,512]{2,1,0:T(8,128)S(1)}, u32[]{:S(2)}, u32[]{:S(2)}) collective-permute-start(f32[4,32,512]{2,1,0:T(8,128)S(1)} %dynamic-slice_bitcast_fusion.1), channel_id=1, source_target_pairs={{0,2},{1,3},{2,0},{3,1},{4,6},{5,7},{6,4},{7,5},{8,10},{9,11},{10,... | collective-permute-start | bytes 786440 | tf_op jit(solution)/shard_map/ppermute | solution.py:456
  130.9 8.5 %collective-permute-start.3 = (f32[32,512]{1,0:T(8,128)S(1)}, f32[32,512]{1,0:T(8,128)S(1)}, u32[]{:S(2)}, u32[]{:S(2)}) collective-permute-start(f32[32,512]{1,0:T(8,128)S(1)} %get-tuple-element.30), channel_id=1, source_target_pairs={{0,8},{1,9},{2,10},{3,11},{4,12},{5,13},{6,14},{7,15},{8,0},{9,1},... | collective-permute-start | bytes 196616 | tf_op jit(solution)/shard_map/ppermute | solution.py:416
  132.1 7.3 %collective-permute-start.4 = (f32[32,512]{1,0:T(8,128)S(1)}, f32[32,512]{1,0:T(8,128)S(1)}, u32[]{:S(2)}, u32[]{:S(2)}) collective-permute-start(f32[32,512]{1,0:T(8,128)S(1)} %get-tuple-element.31), channel_id=1, source_target_pairs={{0,12},{1,13},{2,14},{3,15},{4,0},{5,1},{6,2},{7,3},{8,4},{9,5},{1... | collective-permute-start | bytes 196616 | tf_op jit(solution)/shard_map/ppermute | solution.py:416
  135.0 8.5 %collective-permute-start.2 = (f32[32,512]{1,0:T(8,128)S(1)}, f32[32,512]{1,0:T(8,128)S(1)}, u32[]{:S(2)}, u32[]{:S(2)}) collective-permute-start(f32[32,512]{1,0:T(8,128)S(1)} %get-tuple-element.32), channel_id=1, source_target_pairs={{0,4},{1,5},{2,6},{3,7},{4,8},{5,9},{6,10},{7,11},{8,12},{9,13},{1... | collective-permute-start | bytes 196616 | tf_op jit(solution)/shard_map/ppermute | solution.py:416
  144.2 5.7 %collective-permute-start.7 = (f32[32,512]{1,0:T(8,128)S(1)}, f32[32,512]{1,0:T(8,128)S(1)}, u32[]{:S(2)}, u32[]{:S(2)}) collective-permute-start(f32[32,512]{1,0:T(8,128)S(1)} %get-tuple-element.19), channel_id=1, source_target_pairs={{0,12},{1,13},{2,14},{3,15},{4,0},{5,1},{6,2},{7,3},{8,4},{9,5},{1... | collective-permute-start | bytes 196616 | tf_op jit(solution)/shard_map/ppermute | solution.py:416
  144.2 10.5 %collective-permute-start.6 = (f32[32,512]{1,0:T(8,128)S(1)}, f32[32,512]{1,0:T(8,128)S(1)}, u32[]{:S(2)}, u32[]{:S(2)}) collective-permute-start(f32[32,512]{1,0:T(8,128)S(1)} %get-tuple-element.19), channel_id=1, source_target_pairs={{0,8},{1,9},{2,10},{3,11},{4,12},{5,13},{6,14},{7,15},{8,0},{9,1},... | collective-permute-start | bytes 196616 | tf_op jit(solution)/shard_map/ppermute | solution.py:416
  145.8 9.7 %collective-permute-start.5 = (f32[32,512]{1,0:T(8,128)S(1)}, f32[32,512]{1,0:T(8,128)S(1)}, u32[]{:S(2)}, u32[]{:S(2)}) collective-permute-start(f32[32,512]{1,0:T(8,128)S(1)} %get-tuple-element.19), channel_id=1, source_target_pairs={{0,4},{1,5},{2,6},{3,7},{4,8},{5,9},{6,10},{7,11},{8,12},{9,13},{1... | collective-permute-start | bytes 196616 | tf_op jit(solution)/shard_map/ppermute | solution.py:416
  155.5 9.9 %collective-permute-start.8 = (f32[4,32,512]{2,1,0:T(8,128)S(1)}, f32[4,32,512]{2,1,0:T(8,128)S(1)}, u32[]{:S(2)}, u32[]{:S(2)}) collective-permute-start(f32[4,32,512]{2,1,0:T(8,128)S(1)} %pad_maximum_fusion), channel_id=1, source_target_pairs={{0,2},{1,3},{2,0},{3,1},{4,6},{5,7},{6,4},{7,5},{8,10},{9,11},{10,... | collective-permute-start | bytes 786440 | tf_op jit(solution)/shard_map/ppermute | solution.py:456
  159.9 8.2 %collective-permute-start.21 = (f32[256,256]{1,0:T(8,128)S(1)}, f32[256,256]{1,0:T(8,128)S(1)}, u32[]{:S(2)}, u32[]{:S(2)}) collective-permute-start(f32[256,256]{1,0:T(8,128)S(1)} %get-tuple-element.27.first_ref.refs_4_), channel_id=1, source_target_pairs={{0,2},{1,3},{4,0},{5,1},{8,4},{9,5},{12,8},{13,9},{14,12},{15,13},... | collective-permute-start | bytes 786440 | tf_op jit(solution)/shard_map/ppermute | solution.py:453
  159.9 10.7 %collective-permute-start.20 = (f32[256,256]{1,0:T(8,128)S(1)}, f32[256,256]{1,0:T(8,128)S(1)}, u32[]{:S(2)}, u32[]{:S(2)}) collective-permute-start(f32[256,256]{1,0:T(8,128)S(1)} %get-tuple-element.27.first_ref.refs_4_), channel_id=1, source_target_pairs={{0,4},{1,5},{4,8},{5,9},{8,12},{9,13},{12,14},{13,15},{14,10},{15,... | collective-permute-start | bytes 786440 | tf_op jit(solution)/shard_map/ppermute | solution.py:453
  166.1 6.2 %collective-permute-start.9 = (f32[8,32,512]{2,1,0:T(8,128)}, f32[8,32,512]{2,1,0:T(8,128)}, u32[]{:S(2)}, u32[]{:S(2)}) collective-permute-start(f32[8,32,512]{2,1,0:T(8,128)} %constant_dynamic-update-slice_fusion.mine_ref), channel_id=1, source_target_pairs={{0,1},{1,0},{2,3},{3,2},{4,5},{5,4},{6,7},{7,6},{8,9},{9,8},{10,11... | collective-permute-start | bytes 1572872 | tf_op jit(solution)/shard_map/ppermute | solution.py:396
  166.2 6.8 %collective-permute-start.28 = (f32[256,256]{1,0:T(8,128)S(1)}, f32[256,256]{1,0:T(8,128)S(1)}, u32[]{:S(2)}, u32[]{:S(2)}) collective-permute-start(f32[256,256]{1,0:T(8,128)S(1)} %get-tuple-element.27.first_ref.refs_4_), channel_id=1, source_target_pairs={{0,1},{1,0},{2,3},{3,2},{4,5},{5,4},{6,7},{7,6},{8,9},{9,8},{10,11... | collective-permute-start | bytes 786440 | tf_op jit(solution)/shard_map/ppermute | solution.py:396
  168.1 44.6 %copy-start.7 = (f32[256,256]{1,0:T(8,128)}, f32[256,256]{1,0:T(8,128)S(1)}, u32[]{:S(2)}) copy-start(f32[256,256]{1,0:T(8,128)S(1)} %collective-permute-done.21.refs_6_) | copy-start | bytes 786436
  168.1 6.9 %collective-permute-start.23 = (f32[256,256]{1,0:T(8,128)S(1)}, f32[256,256]{1,0:T(8,128)}, u32[]{:S(2)}, u32[]{:S(2)}) collective-permute-start(f32[256,256]{1,0:T(8,128)S(1)} %collective-permute-done.21.refs_6_), channel_id=1, source_target_pairs={{0,2},{1,3},{4,0},{5,1},{8,4},{9,5},{12,8},{13,9},{14,12},{15,13},... | collective-permute-start | bytes 786440 | tf_op jit(solution)/shard_map/ppermute | solution.py:453
  170.6 42.1 %copy-start.8 = (f32[256,256]{1,0:T(8,128)}, f32[256,256]{1,0:T(8,128)S(1)}, u32[]{:S(2)}) copy-start(f32[256,256]{1,0:T(8,128)S(1)} %collective-permute-done.20.refs_5_) | copy-start | bytes 786436
  170.6 6.6 %collective-permute-start.22 = (f32[256,256]{1,0:T(8,128)S(1)}, f32[256,256]{1,0:T(8,128)}, u32[]{:S(2)}, u32[]{:S(2)}) collective-permute-start(f32[256,256]{1,0:T(8,128)S(1)} %collective-permute-done.20.refs_5_), channel_id=1, source_target_pairs={{0,4},{1,5},{4,8},{5,9},{8,12},{9,13},{12,14},{13,15},{14,10},{15,... | collective-permute-start | bytes 786440 | tf_op jit(solution)/shard_map/ppermute | solution.py:453
  171.7 45.0 %collective-permute-start.37 = (f32[8,256,256]{2,1,0:T(8,128)}, f32[8,256,256]{2,1,0:T(8,128)S(1)}, u32[]{:S(2)}, u32[]{:S(2)}) collective-permute-start(f32[8,256,256]{2,1,0:T(8,128)} %bitcast.71), channel_id=1, source_target_pairs={{0,1},{1,0},{2,3},{3,2},{4,5},{5,4},{6,7},{7,6},{8,9},{9,8},{10,11... | collective-permute-start | bytes 6291464 | tf_op jit(solution)/shard_map/ppermute | solution.py:396
  172.4 11.4 %collective-permute-start.30 = (f32[256,256]{1,0:T(8,128)S(1)}, f32[256,256]{1,0:T(8,128)}, u32[]{:S(2)}, u32[]{:S(2)}) collective-permute-start(f32[256,256]{1,0:T(8,128)S(1)} %collective-permute-done.21.refs_6_), channel_id=1, source_target_pairs={{0,1},{1,0},{2,3},{3,2},{4,5},{5,4},{6,7},{7,6},{8,9},{9,8},{10,11... | collective-permute-start | bytes 786440 | tf_op jit(solution)/shard_map/ppermute | solution.py:396
  173.0 39.7 %copy-start.9 = (f32[256,256]{1,0:T(8,128)}, f32[256,256]{1,0:T(8,128)S(1)}, u32[]{:S(2)}) copy-start(f32[256,256]{1,0:T(8,128)S(1)} %collective-permute-done.28.refs_13_) | copy-start | bytes 786436
  173.0 11.6 %collective-permute-start.29 = (f32[256,256]{1,0:T(8,128)S(1)}, f32[256,256]{1,0:T(8,128)}, u32[]{:S(2)}, u32[]{:S(2)}) collective-permute-start(f32[256,256]{1,0:T(8,128)S(1)} %collective-permute-done.20.refs_5_), channel_id=1, source_target_pairs={{0,1},{1,0},{2,3},{3,2},{4,5},{5,4},{6,7},{7,6},{8,9},{9,8},{10,11... | collective-permute-start | bytes 786440 | tf_op jit(solution)/shard_map/ppermute | solution.py:396
  175.0 6.9 %collective-permute-start.25 = (f32[256,256]{1,0:T(8,128)}, f32[256,256]{1,0:T(8,128)S(1)}, u32[]{:S(2)}, u32[]{:S(2)}) collective-permute-start(f32[256,256]{1,0:T(8,128)} %collective-permute-done.23.refs_8_), channel_id=1, source_target_pairs={{0,2},{1,3},{4,0},{5,1},{8,4},{9,5},{12,8},{13,9},{14,12},{15,13},... | collective-permute-start | bytes 786440 | tf_op jit(solution)/shard_map/ppermute | solution.py:453
  177.2 6.6 %collective-permute-start.24 = (f32[256,256]{1,0:T(8,128)}, f32[256,256]{1,0:T(8,128)S(1)}, u32[]{:S(2)}, u32[]{:S(2)}) collective-permute-start(f32[256,256]{1,0:T(8,128)} %collective-permute-done.22.refs_7_), channel_id=1, source_target_pairs={{0,4},{1,5},{4,8},{5,9},{8,12},{9,13},{12,14},{13,15},{14,10},{15,... | collective-permute-start | bytes 786440 | tf_op jit(solution)/shard_map/ppermute | solution.py:453
  181.9 30.8 %copy-start.5 = (f32[256,256]{1,0:T(8,128)}, f32[256,256]{1,0:T(8,128)S(1)}, u32[]{:S(2)}) copy-start(f32[256,256]{1,0:T(8,128)S(1)} %collective-permute-done.25.refs_10_) | copy-start | bytes 786436
  181.9 5.2 %collective-permute-start.32 = (f32[256,256]{1,0:T(8,128)}, f32[256,256]{1,0:T(8,128)S(1)}, u32[]{:S(2)}, u32[]{:S(2)}) collective-permute-start(f32[256,256]{1,0:T(8,128)} %collective-permute-done.23.refs_8_), channel_id=1, source_target_pairs={{0,1},{1,0},{2,3},{3,2},{4,5},{5,4},{6,7},{7,6},{8,9},{9,8},{10,11... | collective-permute-start | bytes 786440 | tf_op jit(solution)/shard_map/ppermute | solution.py:396
  183.8 28.9 %copy-start.6 = (f32[256,256]{1,0:T(8,128)}, f32[256,256]{1,0:T(8,128)S(1)}, u32[]{:S(2)}) copy-start(f32[256,256]{1,0:T(8,128)S(1)} %collective-permute-done.24.refs_9_) | copy-start | bytes 786436
  183.8 4.0 %collective-permute-start.31 = (f32[256,256]{1,0:T(8,128)}, f32[256,256]{1,0:T(8,128)S(1)}, u32[]{:S(2)}, u32[]{:S(2)}) collective-permute-start(f32[256,256]{1,0:T(8,128)} %collective-permute-done.22.refs_7_), channel_id=1, source_target_pairs={{0,1},{1,0},{2,3},{3,2},{4,5},{5,4},{6,7},{7,6},{8,9},{9,8},{10,11... | collective-permute-start | bytes 786440 | tf_op jit(solution)/shard_map/ppermute | solution.py:396
  183.8 6.0 %collective-permute-start.27 = (f32[128,256]{1,0:T(8,128)S(1)}, f32[128,256]{1,0:T(8,128)S(1)}, u32[]{:S(2)}, u32[]{:S(2)}) collective-permute-start(f32[128,256]{1,0:T(8,128)S(1)} %slice.113), channel_id=1, source_target_pairs={{0,2},{1,3},{4,0},{5,1},{8,4},{9,5},{12,8},{13,9},{14,12},{15,13},... | collective-permute-start | bytes 393224 | tf_op jit(solution)/shard_map/ppermute | solution.py:453
  184.5 5.6 %collective-permute-start.26 = (f32[128,256]{1,0:T(8,128)S(1)}, f32[128,256]{1,0:T(8,128)}, u32[]{:S(2)}, u32[]{:S(2)}) collective-permute-start(f32[128,256]{1,0:T(8,128)S(1)} %slice.112), channel_id=1, source_target_pairs={{0,4},{1,5},{4,8},{5,9},{8,12},{9,13},{12,14},{13,15},{14,10},{15,... | collective-permute-start | bytes 393224 | tf_op jit(solution)/shard_map/ppermute | solution.py:453
  187.1 0.7 copy-start.10
  187.1 29.6 %collective-permute-start.34 = (f32[256,256]{1,0:T(8,128)S(1)}, f32[256,256]{1,0:T(8,128)}, u32[]{:S(2)}, u32[]{:S(2)}) collective-permute-start(f32[256,256]{1,0:T(8,128)S(1)} %collective-permute-done.25.refs_10_), channel_id=1, source_target_pairs={{0,1},{1,0},{2,3},{3,2},{4,5},{5,4},{6,7},{7,6},{8,9},{9,8},{10,11... | collective-permute-start | bytes 786440 | tf_op jit(solution)/shard_map/ppermute | solution.py:396
  187.8 0.7 copy-start.11
  188.5 28.2 %collective-permute-start.33 = (f32[256,256]{1,0:T(8,128)S(1)}, f32[256,256]{1,0:T(8,128)}, u32[]{:S(2)}, u32[]{:S(2)}) collective-permute-start(f32[256,256]{1,0:T(8,128)S(1)} %collective-permute-done.24.refs_9_), channel_id=1, source_target_pairs={{0,1},{1,0},{2,3},{3,2},{4,5},{5,4},{6,7},{7,6},{8,9},{9,8},{10,11... | collective-permute-start | bytes 786440 | tf_op jit(solution)/shard_map/ppermute | solution.py:396
  189.8 22.9 %copy-start.12 = (f32[128,256]{1,0:T(8,128)}, f32[128,256]{1,0:T(8,128)S(1)}, u32[]{:S(2)}) copy-start(f32[128,256]{1,0:T(8,128)S(1)} %collective-permute-done.27.refs_12_) | copy-start | bytes 393220
  189.8 26.9 %collective-permute-start.36 = (f32[128,256]{1,0:T(8,128)S(1)}, f32[128,256]{1,0:T(8,128)}, u32[]{:S(2)}, u32[]{:S(2)}) collective-permute-start(f32[128,256]{1,0:T(8,128)S(1)} %collective-permute-done.27.refs_12_), channel_id=1, source_target_pairs={{0,1},{1,0},{2,3},{3,2},{4,5},{5,4},{6,7},{7,6},{8,9},{9,8},{10,11... | collective-permute-start | bytes 393224 | tf_op jit(solution)/shard_map/ppermute | solution.py:396
  190.2 26.6 %collective-permute-start.35 = (f32[128,256]{1,0:T(8,128)}, f32[128,256]{1,0:T(8,128)}, u32[]{:S(2)}, u32[]{:S(2)}) collective-permute-start(f32[128,256]{1,0:T(8,128)} %collective-permute-done.26.refs_11_), channel_id=1, source_target_pairs={{0,1},{1,0},{2,3},{3,2},{4,5},{5,4},{6,7},{7,6},{8,9},{9,8},{10,11... | collective-permute-start | bytes 393224 | tf_op jit(solution)/shard_map/ppermute | solution.py:396
  216.8 1.3 copy-start.1
Sparse Core Ops, SparseCore 0:
  53.3 44.1 reduce-scatter.1
  118.4 43.8 all-gather.2

commit v2 on v1

--- a/solution.py
+++ b/solution.py
@@ -109,11 +109,12 @@
         work[at, to] = jnp.zeros((TILE, TILE), jnp.float32)
 
 
-def factor_kernel(rows_ref, mine_ref, other_ref, regular_ref, out_ref):
+def factor_first(table_ref, mine_ref, other_ref, regular_ref, out_ref):
     count, rows = mine_ref.shape[0], mine_ref.shape[1]
+    place = lax.axis_index("scen")
     for n in range(2 * count):
         ref = mine_ref if n < count else other_ref
-        at = pl.ds(pl.multiple_of(rows_ref[n] * rows, rows), rows)
+        at = pl.ds(pl.multiple_of(table_ref[2 * count * place + n] * rows, rows), rows)
         out_ref[at, :] = ref[n % count]
     size = out_ref.shape[0]
     row_id = lax.broadcasted_iota(jnp.int32, (TILE, TILE), 0)
@@ -121,22 +122,38 @@
     for i in range(size // TILE):
         at = pl.ds(i * TILE, TILE)
         out_ref[at, at] += jnp.where(row_id == col_id, regular_ref[:, at], 0.0)
-    for k in range(size // TILE):
-        factor_step(k, out_ref)
-
-
-def inverse_factor(rows, mine, other, regular):
+    factor_step(0, out_ref)
+
+
+def factor_next(k, work_ref, out_ref):
+    out_ref[...] = work_ref[...]
+    factor_step(k, out_ref)
+
+
+def factor_stages(table, mine, other, regular):
     size = regular.shape[0]
-    return pl.pallas_call(
-        factor_kernel,
+    settings = dict(
         out_shape=jax.ShapeDtypeStruct((size, size), jnp.float32),
-        in_specs=[pl.BlockSpec(memory_space=pltpu.SMEM)] + vmem(3),
         out_specs=vmem(1)[0],
         cost_estimate=pl.CostEstimate(
-            flops=100 * size**3, bytes_accessed=8 * size * size, transcendentals=size
+            flops=50 * size**3, bytes_accessed=8 * size * size, transcendentals=size
         ),
-        name="inverse_factor",
-    )(rows, mine, other, regular[None, :])
+    )
+    first = lambda work: pl.pallas_call(
+        factor_first,
+        in_specs=[pl.BlockSpec(memory_space=pltpu.SMEM)] + vmem(3),
+        name="factor_0",
+        **settings,
+    )(table, mine, other, regular[None, :])
+    return [first] + [
+        pl.pallas_call(
+            lambda work_ref, out_ref, k=k: factor_next(k, work_ref, out_ref),
+            in_specs=vmem(1),
+            name=f"factor_{k}",
+            **settings,
+        )
+        for k in range(1, size // TILE)
+    ]
 
 
 def solve_kernel(inverse_ref, first_ref, second_ref, factor_ref, weight_ref):
@@ -163,17 +180,22 @@
 
 
 def front_kernel(
-    blocks_ref, slots_ref, scalars_ref, cols_ref, weights_ref, prior_ref, rows_ref,
-    block_ref, local_ref, given_0, given_1, kept_0, kept_1,
+    table_ref, counts_ref, cols_ref, weights_ref, prior_ref, rows_ref,
+    block_ref, local_0, local_1, given_0, given_1, kept_0, kept_1,
     pick, picked, total, sums, sems,
 ):
     step, last = pl.program_id(0), pl.num_programs(0) - 1
+    place, parts = lax.axis_index("scen"), lax.axis_size("scen")
     order, width = pick.shape
     owned = prior_ref.shape[0]
     depth = rows_ref.shape[0]
     half = width // 2
-    tall = order // 8
-    count = blocks_ref.shape[0] // 2
+    tall = order // 4
+    count = given_0.shape[0]
+    wide = 4
+
+    def entry(kind, n):
+        return table_ref[4 * count * place + kind * 2 * count + n]
 
     @pl.when(step == 0)
     def _():
@@ -185,16 +207,17 @@
             ids = n * tall + lax.broadcasted_iota(jnp.int32, (tall, width), 0)
             chosen = (ids == cols_ref[...]).astype(jnp.float32).astype(jnp.bfloat16)
             pick[at, :] = chosen
-            for part in split(prior_ref[:, at]):
-                picked[:owned] += jnp.dot(part, chosen, preferred_element_type=jnp.float32)
-
-        local = picked[:owned].T
-        local_ref[...] = local
-        ids = scalars_ref[1] + lax.broadcasted_iota(jnp.int32, (owned, width), 0)
+            both = jnp.concatenate(split(prior_ref[:, at]), axis=0)
+            picked[...] += jnp.dot(both, chosen, preferred_element_type=jnp.float32)
+
+        local = (picked[:owned] + picked[owned : 2 * owned]).T
+        local_0[...] = local[:half]
+        local_1[...] = local[half:]
+        ids = place * owned + lax.broadcasted_iota(jnp.int32, (owned, width), 0)
         chosen = (ids == cols_ref[...]).astype(jnp.float32).astype(jnp.bfloat16)
-        sums[...] = jnp.zeros_like(sums)
-        for part in split(local):
-            sums[...] += jnp.dot(part, chosen, preferred_element_type=jnp.float32)
+        sums[...] = sum(
+            jnp.dot(part, chosen, preferred_element_type=jnp.float32) for part in split(local)
+        )
 
     picked[...] = jnp.zeros_like(picked)
 
@@ -204,8 +227,8 @@
         picked[...] += jnp.dot(rows_ref[:, at], pick[at, :], preferred_element_type=jnp.float32)
 
     slot = step * depth + lax.broadcasted_iota(jnp.int32, (1, depth), 1)
-    live = (slot < scalars_ref[0]).astype(jnp.float32)
-    factor_w = weights_ref[...] * live * (1.0 / scalars_ref[2].astype(jnp.float32))
+    live = (slot < counts_ref[0]).astype(jnp.float32)
+    factor_w = weights_ref[...] * live * (1.0 / (depth * pl.num_programs(0) * parts))
     scaled = (picked[...].T * factor_w).astype(jnp.bfloat16)
     sums[...] += jnp.dot(
         scaled, picked[...].astype(jnp.bfloat16), preferred_element_type=jnp.float32
@@ -215,75 +238,79 @@
     def _():
         block_ref[...] = 0.5 * (sums[...] + sums[...].T)
 
-    def stores(n):
-        on, slot = n // count, n % count
-        out = []
-        for h, (given, kept) in enumerate(((given_0, kept_0), (given_1, kept_1))):
-            for which, ref in enumerate((given, kept)):
-                out.append(
-                    (
-                        on == which,
-                        pltpu.make_async_copy(
-                            total.at[n, pl.ds(h * half, half)],
-                            ref.at[slots_ref[h * count + slot]],
-                            sems.at[n, h],
-                        ),
-                    )
-                )
-        return out
-
-    @pl.loop(0, 2 * count)
-    def _(n):
-        at = pl.ds(pl.multiple_of(blocks_ref[n] * owned, owned), owned)
-        part = jnp.dot(scaled, rows_ref[:, at], preferred_element_type=jnp.float32)
-
-        @pl.when(step == 0)
-        def _():
-            total[n] = part
-
-        @pl.when(step > 0)
-        def _():
-            total[n] += part
-
-        @pl.when(step == last)
-        def _():
-            for here, store in stores(n):
-                pl.when(here)(store.start)
+    def stores(n, which):
+        refs = ((given_0, given_1), (kept_0, kept_1))[which]
+        for h, ref in enumerate(refs):
+            yield pltpu.make_async_copy(
+                total.at[n, pl.ds(h * half, half)],
+                ref.at[entry(1, h * count + lax.rem(n, count))],
+                sems.at[n, h],
+            )
+
+    def each(action):
+        for which in range(2):
+
+            @pl.loop(which * count, (which + 1) * count)
+            def _(n):
+                for store in stores(n, which):
+                    action(store)
+
+    for which in range(2):
+
+        @pl.loop(0, count // wide)
+        def _(m):
+            first = which * count + m * wide
+            columns = [
+                rows_ref[:, pl.ds(pl.multiple_of(entry(0, first + i) * owned, owned), owned)]
+                for i in range(wide)
+            ]
+            part = jnp.dot(
+                scaled, jnp.concatenate(columns, axis=1), preferred_element_type=jnp.float32
+            )
+
+            @pl.when(step == 0)
+            def _():
+                for i in range(wide):
+                    total[first + i] = part[:, i * owned : (i + 1) * owned]
+
+            @pl.when(step > 0)
+            def _():
+                for i in range(wide):
+                    total[first + i] += part[:, i * owned : (i + 1) * owned]
+
+            @pl.when(step == last)
+            def _():
+                for i in range(wide):
+                    for store in stores(first + i, which):
+                        store.start()
 
     @pl.when(step == last)
     def _():
-        @pl.loop(0, 2 * count)
-        def _(n):
-            for here, store in stores(n):
-                pl.when(here)(store.wait)
-
-
-def front(blocks, slots, scalars, panel_cols, row_weights, prior, scenario_rows):
-    count = blocks.shape[0] // 2
+        each(lambda store: store.wait())
+
+
+def front(table, count, row_counts, panel_cols, row_weights, prior, scenario_rows):
     depth, order = scenario_rows.shape
     width = panel_cols.shape[0]
     owned = prior.shape[0]
     half = width // 2
-    tall = min(512, depth)
+    tall = 512
     pieces = jax.ShapeDtypeStruct((count, half, owned), jnp.float32)
+    local = jax.ShapeDtypeStruct((half, owned), jnp.float32)
     whole = lambda shape: pl.BlockSpec(shape, lambda i: (0, 0))
     smem = pl.BlockSpec(memory_space=pltpu.SMEM)
     return pl.pallas_call(
         front_kernel,
         grid=(depth // tall,),
         in_specs=[
-            smem, smem, smem, whole((1, width)),
+            smem, smem, whole((1, width)),
             pl.BlockSpec((1, tall), lambda i: (0, i)),
             whole((owned, order)),
             pl.BlockSpec((tall, order), lambda i: (i, 0)),
         ],
-        out_specs=[whole((width, width)), whole((width, owned))]
+        out_specs=[whole((width, width)), whole((half, owned)), whole((half, owned))]
         + [pl.BlockSpec(memory_space=pl.ANY)] * 4,
-        out_shape=[
-            jax.ShapeDtypeStruct((width, width), jnp.float32),
-            jax.ShapeDtypeStruct((width, owned), jnp.float32),
-        ]
-        + [pieces] * 4,
+        out_shape=[jax.ShapeDtypeStruct((width, width), jnp.float32), local, local] + [pieces] * 4,
         scratch_shapes=[
             pltpu.VMEM((order, width), jnp.bfloat16),
             pltpu.VMEM((tall, width), jnp.float32),
@@ -298,16 +325,21 @@
         ),
         compiler_params=pltpu.CompilerParams(vmem_limit_bytes=VMEM_BYTES),
         name="front",
-    )(blocks, slots, scalars, panel_cols[None, :], row_weights[None, :], prior, scenario_rows)
-
-
-def update_kernel(count, block_ref, ring_ref, weight_ref, prior_ref, *refs):
-    sources, out_ref, scratch = refs[:-6], refs[-6], refs[-5:]
-    held, total, in_sem, prior_sem, out_sem = scratch
+    )(table, row_counts, panel_cols[None, :], row_weights[None, :], prior, scenario_rows)
+
+
+def update_kernel(count, table_ref, weight_ref, prior_ref, *refs):
+    sources, out_ref, scratch = refs[:-7], refs[-7], refs[-6:]
+    held, before, total, in_sem, prior_sem, out_sem = scratch
+    place = lax.axis_index("scen")
     half, owned = held.shape[2], held.shape[3]
-    fetch = pltpu.make_async_copy(prior_ref, total, prior_sem)
-    fetch.start()
     chips = count // 2
+    wide = 4
+
+    def entry(n):
+        return table_ref[(count + chips) * place + n]
+
+    fetch = pltpu.make_async_copy(prior_ref, before, prior_sem)
     loads = []
     for n in range(count):
         core, slot = n // chips, n % chips
@@ -320,38 +352,43 @@
             )
             for i, piece in enumerate(pieces)
         ]
-        second = sources[2 * (chips + 1) + core].at[ring_ref[slot]]
+        second = sources[2 * (chips + 1) + core].at[entry(count + slot)]
         copies.append(pltpu.make_async_copy(second, held.at[n, 1], in_sem.at[n, 2]))
         for copy in copies:
             copy.start()
         loads.append(copies)
+        if n == wide - 1:
+            fetch.start()
     weights = split(weight_ref[...])
-    fetch.wait()
-    for n in range(count):
-        for copy in loads[n]:
-            copy.wait()
-        outer = dot_split(weights, split(held[n].reshape(2 * half, owned)))
-        cols = pl.ds(pl.multiple_of(block_ref[n] * owned, owned), owned)
-        total[:, cols] -= outer
+    for first in range(0, count, wide):
+        for n in range(first, first + wide):
+            for copy in loads[n]:
+                copy.wait()
+        panel = [held[n].reshape(2 * half, owned) for n in range(first, first + wide)]
+        outer = dot_split(weights, split(jnp.concatenate(panel, axis=1)))
+        if first == 0:
+            fetch.wait()
+        for i in range(wide):
+            cols = pl.ds(pl.multiple_of(entry(first + i) * owned, owned), owned)
+            total[:, cols] = before[:, cols] - outer[:, i * owned : (i + 1) * owned]
     store = pltpu.make_async_copy(total, out_ref, out_sem)
     store.start()
     store.wait()
 
 
-def update_rows(blocks, ring, weights, prior, sources):
-    count = blocks.shape[0]
+def update_rows(table, count, weights, prior, sources):
     owned, order = prior.shape
     half = weights.shape[1] // 2
-    smem = pl.BlockSpec(memory_space=pltpu.SMEM)
     return pl.pallas_call(
         lambda *refs: update_kernel(count, *refs),
         out_shape=jax.ShapeDtypeStruct(prior.shape, jnp.float32),
-        in_specs=[smem, smem]
+        in_specs=[pl.BlockSpec(memory_space=pltpu.SMEM)]
         + vmem(1)
         + [pl.BlockSpec(memory_space=pl.ANY)] * (1 + len(sources)),
         out_specs=pl.BlockSpec(memory_space=pl.ANY),
         scratch_shapes=[
             pltpu.VMEM((count, 2, half, owned), jnp.float32),
+            pltpu.VMEM(prior.shape, jnp.float32),
             pltpu.VMEM(prior.shape, jnp.float32),
             pltpu.SemaphoreType.DMA((count, 3)),
             pltpu.SemaphoreType.DMA,
@@ -364,7 +401,7 @@
         ),
         compiler_params=pltpu.CompilerParams(vmem_limit_bytes=VMEM_BYTES),
         name="update_rows",
-    )(blocks, ring, weights, prior, *sources)
+    )(table, weights, prior, *sources)
 
 
 def local_parts(scenario_rows, row_weights, row_counts, panel_cols, prior_schur):
@@ -405,46 +442,41 @@
     return kept + swap_cores(given)
 
 
-def sum_block(block, swap_y):
-    parts = lax.axis_size("scen")
-    chips = parts // 2
-    lines = chips // 2
-    place = lax.axis_index("scen")
-    core, y, z = place % 2, place // 2 % 2, place // 4
-
-    def shift(values, by):
-        return lax.ppermute(values, "scen", [(d, (d + 4 * by) % parts) for d in range(parts)])
-
-    both = halve_block(block).reshape(2, lines, -1, block.shape[0])
-    given = lax.dynamic_index_in_dim(both, 1 - y, 0, keepdims=False)
-    both = lax.dynamic_index_in_dim(both, y, 0, keepdims=False) + swap_y(given)
-    mine = lax.dynamic_index_in_dim(both, z, 0, keepdims=False)
-    mine = mine + sum(
-        shift(lax.dynamic_index_in_dim(both, (z + by) % lines, 0, keepdims=False), by)
-        for by in range(1, lines)
-    )
-    mine = jnp.stack([mine] + [shift(mine, by) for by in range(1, lines)])
-    mine = jnp.concatenate([mine, swap_y(mine)])
-    line = (z - jnp.arange(lines, dtype=jnp.int32)) % lines
-    rows = jnp.concatenate(
-        [(2 * c + w) * lines + line for c in (core, 1 - core) for w in (y, 1 - y)]
-    )
-    return rows, mine, swap_cores(mine)
+def tables(chips):
+    ring, far, lines = RINGS[chips], chips // 2, chips // 2
+    offsets = work_offsets(far)
+    back = [0] + [-way * d for d in range(1, far) for way in (1, -1)] + [far]
+    fronts, updates, factors = [], [], []
+    for place in range(2 * chips):
+        chip, core = place // 2, place % 2
+        z, y, at = chip // 2, chip % 2, ring.index(chip)
+        where = [(at + offset) % chips for offset in offsets]
+        fronts += [2 * ring[q] + c for c in (1 - core, core) for q in where]
+        fronts += list(range(chips)) + where
+        where = [(at + offset) % chips for offset in back]
+        updates += [2 * ring[q] + c for c in (core, 1 - core) for q in where] + where
+        factors += [
+            (2 * c + w) * lines + (z - by) % lines
+            for c in (core, 1 - core) for w in (y, 1 - y) for by in range(lines)
+        ]
+    return [jnp.array(table, jnp.int32) for table in (fronts, updates, factors)]
+
+
+def work_offsets(far):
+    return [far] + [way * d for d in range(far - 1, 0, -1) for way in (1, -1)] + [0]
 
 
 def shards_on_ring(scenario_rows, row_weights, row_counts, panel_cols, regular, prior_schur):
     parts = lax.axis_size("scen")
     chips = parts // 2
-    far = chips // 2
-    depth = scenario_rows.shape[0]
-    owned = prior_schur.shape[0]
+    far = lines = chips // 2
     half = panel_cols.shape[0] // 2
     place = lax.axis_index("scen")
-    core = place % 2
+    y, z = place // 2 % 2, place // 4
     ring = RINGS[chips]
-    chip_at = jnp.array(ring, jnp.int32)
-    position = jnp.array([ring.index(chip) for chip in range(chips)], jnp.int32)[place // 2]
     groups = [[2 * chip + c for chip in ring] for c in range(2)]
+    offsets = work_offsets(far)
+    front_table, update_table, factor_table = tables(chips)
 
     def step(values, way):
         pairs = [
@@ -455,22 +487,24 @@
     def swap_y(values):
         return lax.ppermute(values, "scen", [(d, d ^ 2) for d in range(parts)])
 
-    def on_ring(offsets):
-        return (position + jnp.array(offsets, jnp.int32)) % chips
-
-    offsets = [far] + [way * d for d in range(far - 1, 0, -1) for way in (1, -1)] + [0]
-    where = on_ring(offsets)
-    blocks = jnp.concatenate([2 * chip_at[where] + c for c in (1 - core, core)])
-    slots = jnp.concatenate([jnp.arange(chips, dtype=jnp.int32), where])
-    scalars = jnp.stack([row_counts[0], place * owned, jnp.int32(depth * parts)])
-    block, local_cols, given_0, given_1, kept_0, kept_1 = front(
-        blocks, slots, scalars, panel_cols, row_weights, prior_schur, scenario_rows
-    )
-
+    def shift(values, by):
+        return lax.ppermute(values, "scen", [(d, (d + 4 * by) % parts) for d in range(parts)])
+
+    def slab(values, at):
+        return lax.dynamic_index_in_dim(values, at, 0, keepdims=False)
+
+    together = lax.optimization_barrier
+
+    block, local_0, local_1, given_0, given_1, kept_0, kept_1 = front(
+        front_table, chips, row_counts, panel_cols, row_weights, prior_schur, scenario_rows
+    )
+
+    got_1 = swap_cores(given_1)
+    got_1, given_0 = together((got_1, given_0))
     summed = lax.psum_scatter(
-        kept_1 + swap_cores(given_1), "scen", scatter_dimension=0, axis_index_groups=groups
-    )
-    panel_1 = summed + local_cols[half:]
+        kept_1 + got_1, "scen", scatter_dimension=0, axis_index_groups=groups
+    )
+    panel_1 = summed + local_1
 
     got_0 = swap_cores(given_0)
     sides = {1: slice(0, half // 2), -1: slice(half // 2, half)}
@@ -479,31 +513,57 @@
         n = offsets.index(offset)
         return kept_0[n] + got_0[n]
 
-    arrived = {way: step(partial(far)[sides[way]], way) for way in (1, -1)}
-    arrived = {
-        1: jnp.pad(arrived[1], ((0, half // 2), (0, 0))),
-        -1: jnp.pad(arrived[-1], ((half // 2, 0), (0, 0))),
-    }
+    block = halve_block(block).reshape(2, lines, -1, block.shape[0])
+    ahead = [partial(far)[sides[way]] for way in (1, -1)]
+    ahead, beside = together((ahead, slab(block, 1 - y)))
+    ahead, beside = together(([step(ahead[0], 1), step(ahead[1], -1)], swap_y(beside)))
+    arrived = [
+        jnp.pad(ahead[0], ((0, half // 2), (0, 0))),
+        jnp.pad(ahead[1], ((half // 2, 0), (0, 0))),
+    ]
+
+    block = slab(block, y) + beside
+    beside = [slab(block, (z + by) % lines) for by in range(1, lines)]
     for d in range(far - 1, 0, -1):
-        arrived = {way: step(partial(way * d) + arrived[way], way) for way in (1, -1)}
-    panel_0 = partial(0) + arrived[1] + arrived[-1] + local_cols[:half]
-
-    rows, block_mine, block_other = sum_block(block, swap_y)
+        ahead = [partial(way * d) + arrived[n] for n, way in enumerate((1, -1))]
+        ahead, beside = together((ahead, beside))
+        arrived = [step(ahead[0], 1), step(ahead[1], -1)]
+        if d == far - 1:
+            beside = [shift(beside[by - 1], by) for by in range(1, lines)]
+        elif d == far - 2:
+            beside = [shift(beside, by) for by in range(1, lines)]
+        else:
+            beside = swap_y(beside)
+        arrived, beside = together((arrived, beside))
+        if d == far - 1:
+            mine = beside = sum(beside) + slab(block, z)
+        elif d == far - 2:
+            near = beside = jnp.stack([mine] + beside)
+        else:
+            block = jnp.concatenate([near, beside])
+    panel_0 = partial(0) + arrived[0] + arrived[1] + local_0
+    stages = factor_stages(factor_table, block, swap_cores(block), regular)
 
     second = lax.all_gather(panel_1, "scen", axis_index_groups=groups)
     first = [panel_0]
-    ahead = {1: panel_0, -1: panel_0}
-    for d in range(1, far):
-        ahead = {way: step(ahead[way], way) for way in (1, -1)}
-        first += [ahead[1], ahead[-1]]
-    first += [step(ahead[way][sides[way]], way) for way in (1, -1)]
+    ahead = [panel_0, panel_0]
+    work = None
+    for d in range(1, far + 1):
+        if d == far:
+            ahead = [ahead[n][sides[way]] for n, way in enumerate((1, -1))]
+        if d > 1:
+            ahead, work = together((ahead, work))
+        ahead, work = together(
+            ([step(ahead[0], 1), step(ahead[1], -1)], stages[d - 1](work))
+        )
+        first += ahead
+    inverse = work
+    for stage in stages[far:]:
+        inverse = stage(inverse)
     sources = first + [swap_cores(piece) for piece in first] + [second, swap_cores(second)]
-    where = on_ring([0] + [-way * d for d in range(1, far) for way in (1, -1)] + [far])
-    blocks = jnp.concatenate([2 * chip_at[where] + c for c in (core, 1 - core)])
-
-    inverse = inverse_factor(rows, block_mine, block_other, regular)
+
     factor_rows, weights = solve_rows(inverse, panel_0, panel_1)
-    return update_rows(blocks, where, weights, prior_schur, sources), factor_rows
+    return update_rows(update_table, parts, weights, prior_schur, sources), factor_rows
 
 
 def shards_by_groups(scenario_rows, row_weights, row_counts, panel_cols, regular, prior_schur):
@@ -534,7 +594,10 @@
     panel_rows = gram_mine + local_cols.T
     panel_half = lax.all_gather(panel_rows, "scen", axis_index_groups=same_core)
     panel_rest = swap_cores(panel_half)
-    inverse = inverse_factor(jnp.stack([core, 1 - core]), block, block_other, regular)
+    table = jnp.array([c ^ (d % 2) for d in range(parts) for c in range(2)], jnp.int32)
+    inverse = None
+    for stage in factor_stages(table, block, block_other, regular):
+        inverse = stage(inverse)
     factor_rows, weights = solve_rows(inverse, panel_rows.T[:half], panel_rows.T[half:])
     even = jnp.where(core == 0, panel_half, panel_rest)
     odd = jnp.where(core == 0, panel_rest, panel_half)

time: 243 us -> 219 us (0.901)
  waiting for transfers between devices: 91 us -> 84.3 us
  local copies, waits for them, and re-layouts: 10.3 us -> 5.24 us
  other arithmetic: 17.3 us -> 12.5 us
  Pallas kernels: 73.6 us -> 69.3 us
    ppermute x16, waiting for transfers between devices: 54.5 us -> 31 us  [step(): return lax.ppermute(values, 'scen', pairs)]
    ppermute x6, waiting for transfers between devices: 16.1 us -> 30.2 us  [shift(): lax.ppermute(values, 'scen', [(d, (d + 4 * by) % parts) for d in range(pa...]
    reduce_scatter x1, waiting for transfers between devices: 0.01 us -> 13.4 us  [shards_on_ring(): lax.psum_scatter(kept_1 + got_1, 'scen', scatter_dimension=0, axis_index_...]
    ppermute x2, waiting for transfers between devices: 12.3 us -> 2.75 us  [swap_y(): return lax.ppermute(values, 'scen', [(d, d ^ 2) for d in range(parts)])]
    pallas_call x1 -> x4, Pallas kernels: 22.4 us -> 29.4 us  [the longest x3 21.6 us: shards_on_ring(): stages[d - 1](work)]
    pallas_call x1, Pallas kernels: 30.1 us -> 24.4 us  [front(): pl.pallas_call(front_kernel, grid=(depth // tall,), in_specs=[smem, smem,...]
    pallas_call x1, Pallas kernels: 17.2 us -> 11.6 us  [update_rows(): pl.pallas_call(lambda *refs: update_kernel(count, *refs), out_shape=jax.S...]
    ppermute x16, starting transfers between devices: 21 us -> 16.6 us  [step(): return lax.ppermute(values, 'scen', pairs)]
  transfers between devices with their start and end apart: 40 -> 40, of which waited for: 23 -> 15; matrix products, arithmetic and copies ran while one was open for 7% -> 5% of each run, Pallas kernels for 11% -> 15%
where the time goes in v2:
time: 219 us
  waiting for transfers between devices  84.3 us (38%)
  Pallas kernels  69.3 us (32%)
  starting transfers between devices  32.5 us (15%)
  between operations  15 us (7%)
  other arithmetic  12.5 us (6%)
  local copies, waits for them, and re-layouts  5.24 us (2%)
    ppermute x16, waiting for transfers between devices, step(): return lax.ppermute(values, 'scen', pairs)  31 us
    ppermute x6, waiting for transfers between devices, shift(): lax.ppermute(values, 'scen', [(d, (d + 4 * by) % parts) for d in range(pa...  30.2 us
    pallas_call x1, Pallas kernels, front(): pl.pallas_call(front_kernel, grid=(depth // tall,), in_specs=[smem, smem,...  24.4 us
    pallas_call x3, Pallas kernels, shards_on_ring(): stages[d - 1](work)  21.6 us
    ppermute x16, starting transfers between devices, step(): return lax.ppermute(values, 'scen', pairs)  16.6 us
    reduce_scatter x1, waiting for transfers between devices, shards_on_ring(): lax.psum_scatter(kept_1 + got_1, 'scen', scatter_dimension=0, axis_index_...  13.4 us
    pallas_call x1, Pallas kernels, update_rows(): pl.pallas_call(lambda *refs: update_kernel(count, *refs), out_shape=jax.S...  11.6 us
    ppermute x6, starting transfers between devices, shift(): lax.ppermute(values, 'scen', [(d, (d + 4 * by) % parts) for d in range(pa...  9.15 us
  transfers between devices with their start and end apart: 40, of which 15 were waited for; matrix products, arithmetic and copies ran while one was open for 5% of the time, Pallas kernels for 15%

profile of v2, /device:TPU:0, one launch (start us, length us, event | category | flops | bytes accessed | tf_op | source)
XLA Modules:
  0.0 218.8 jit_solution(12604280222225926818)
XLA Ops:
  7.9 24.4 %front.1 = (f32[512,512]{1,0:T(8,128)}, f32[256,256]{1,0:T(8,128)}, f32[256,256]{1,0:T(8,128)}, f32[8,256,256]{2,1,0:T(8,128)}, f32[8,256,256]{2,1,0:T(8,128)}, ...) custom-call(s32[512]{0:T(512)} %constant.93.clone.table_ref, s32[1]{0:T(128)S(6)} %copy.15.counts_ref, s32[1,512]{1,0:T(1,128)} %bitcast.80, ...), custom_call_target="tpu_custom_call" | custom-call | flops 8589934592 | bytes 20971520 | tf_op jit(solution)/shard_map/front/pallas_call | solution.py:302
  32.2 0.5 collective-permute-start
  32.8 4.0 %collective-permute-done = f32[8,256,256]{2,1,0:T(8,128)S(1)} collective-permute-done((f32[8,256,256]{2,1,0:T(8,128)}, f32[8,256,256]{2,1,0:T(8,128)S(1)}, u32[]{:S(2)}, u32[]{:S(2)}) %collective-permute-start) | collective-permute-done | bytes 2097184 | tf_op jit(solution)/shard_map/ppermute | solution.py:433
  36.8 3.2 %add.202 = f32[8,256,256]{2,1,0:T(8,128)} add(f32[8,256,256]{2,1,0:T(8,128)} %get-tuple-element.111, f32[8,256,256]{2,1,0:T(8,128)S(1)} %collective-permute-done) | non-fusion elementwise | flops 524288 | bytes 6291456 | tf_op jit(solution)/shard_map/add | solution.py:505
  40.1 0.4 collective-permute-start.1
  40.5 0.7 copy-done.3
  41.2 0.8 dynamic-slice_bitcast_fusion
  42.1 0.4 collective-permute-start.2
  42.4 2.8 %collective-permute-done.2 = f32[256,512]{1,0:T(8,128)S(1)} collective-permute-done((f32[256,512]{1,0:T(8,128)}, f32[256,512]{1,0:T(8,128)S(1)}, u32[]{:S(2)}, u32[]{:S(2)}) %collective-permute-start.2) | collective-permute-done | bytes 524320 | tf_op jit(solution)/shard_map/ppermute | solution.py:433
  45.3 1.1 bitcast_add_fusion
  46.4 1.0 slice_add_fusion.3
  47.4 0.7 slice_bitcast_fusion
  48.2 2.9 %collective-permute-start.5 = (f32[4,32,512]{2,1,0:T(8,128)S(1)}, f32[4,32,512]{2,1,0:T(8,128)S(1)}, u32[]{:S(2)}, u32[]{:S(2)}) collective-permute-start(f32[4,32,512]{2,1,0:T(8,128)S(1)} %dynamic-slice_bitcast_fusion.1), channel_id=1, source_target_pairs={{0,2},{1,3},{2,0},{3,1},{4,6},{5,7},{6,4},{7,5},{8,10},{9,11},{10,... | collective-permute-start | bytes 786440 | tf_op jit(solution)/shard_map/ppermute | solution.py:488
  51.0 1.6 collective-permute-start.3
  52.6 0.5 collective-permute-start.4
  53.1 16.0 %collective-permute-done.3 = f32[128,256]{1,0:T(8,128)S(1)} collective-permute-done((f32[128,256]{1,0:T(8,128)}, f32[128,256]{1,0:T(8,128)S(1)}, u32[]{:S(2)}, u32[]{:S(2)}) %collective-permute-start.3) | collective-permute-done | bytes 131104 | tf_op jit(solution)/shard_map/ppermute | solution.py:485
  69.1 13.4 %reduce-scatter.2.cloned.1.call-done = f32[1,256,256]{2,1,0:T(8,128)} async-done(((f32[8,256,256]{2,1,0:T(8,128)}), f32[1,256,256]{2,1,0:T(8,128)}) %reduce-scatter.2.cloned.1.call-update) | async-done | bytes 262160 | tf_op jit(solution)/shard_map/reduce_scatter | solution.py:504
  82.5 1.7 bitcast_add_fusion.1.second_ref
  84.3 0.7 dynamic-slice_bitcast_fusion.2
  84.9 1.1 fusion.5
  86.1 1.2 collective-permute-start.6
  87.3 0.9 collective-permute-start.7
  88.2 1.1 collective-permute-start.8
  89.3 1.5 collective-permute-start.9
  90.8 1.8 collective-permute-start.10
  92.7 9.7 %collective-permute-done.8 = f32[32,512]{1,0:T(8,128)S(1)} collective-permute-done((f32[32,512]{1,0:T(8,128)}, f32[32,512]{1,0:T(8,128)S(1)}, u32[]{:S(2)}, u32[]{:S(2)}) %collective-permute-start.8) | collective-permute-done | bytes 65568 | tf_op jit(solution)/shard_map/ppermute | solution.py:491
  102.4 2.6 %collective-permute-done.9 = f32[32,512]{1,0:T(8,128)S(1)} collective-permute-done((f32[32,512]{1,0:T(8,128)}, f32[32,512]{1,0:T(8,128)S(1)}, u32[]{:S(2)}, u32[]{:S(2)}) %collective-permute-start.9) | collective-permute-done | bytes 65568 | tf_op jit(solution)/shard_map/ppermute | solution.py:491
  104.9 1.2 collective-permute-done.10
  106.2 0.9 constant_dynamic-update-slice_fusion.4
  107.0 1.1 fusion.3
  108.2 2.3 %collective-permute-start.11 = (f32[256,256]{1,0:T(8,128)S(1)}, f32[256,256]{1,0:T(8,128)S(1)}, u32[]{:S(2)}, u32[]{:S(2)}) collective-permute-start(f32[256,256]{1,0:T(8,128)S(1)} %get-tuple-element.83), channel_id=1, source_target_pairs={{0,4},{1,5},{4,8},{5,9},{8,12},{9,13},{12,14},{13,15},{14,10},{15,... | collective-permute-start | bytes 786440 | tf_op jit(solution)/shard_map/ppermute | solution.py:485
  110.5 4.1 %collective-permute-start.15 = (f32[32,512]{1,0:T(8,128)S(1)}, f32[32,512]{1,0:T(8,128)S(1)}, u32[]{:S(2)}, u32[]{:S(2)}) collective-permute-start(f32[32,512]{1,0:T(8,128)S(1)} %get-tuple-element.85), channel_id=1, source_target_pairs={{0,12},{1,13},{2,14},{3,15},{4,0},{5,1},{6,2},{7,3},{8,4},{9,5},{1... | collective-permute-start | bytes 196616 | tf_op jit(solution)/shard_map/ppermute | solution.py:491
  114.6 0.6 collective-permute-start.13
  115.1 9.2 %collective-permute-done.15 = f32[32,512]{1,0:T(8,128)S(1)} collective-permute-done((f32[32,512]{1,0:T(8,128)S(1)}, f32[32,512]{1,0:T(8,128)S(1)}, u32[]{:S(2)}, u32[]{:S(2)}) %collective-permute-start.15) | collective-permute-done | bytes 65568 | tf_op jit(solution)/shard_map/ppermute | solution.py:491
  124.3 7.5 %collective-permute-done.14 = f32[32,512]{1,0:T(8,128)S(1)} collective-permute-done((f32[32,512]{1,0:T(8,128)S(1)}, f32[32,512]{1,0:T(8,128)S(1)}, u32[]{:S(2)}, u32[]{:S(2)}) %collective-permute-start.14) | collective-permute-done | bytes 65568 | tf_op jit(solution)/shard_map/ppermute | solution.py:491
  131.9 1.1 fusion.1
  133.1 2.0 collective-permute-start.17
  135.2 4.3 %collective-permute-done.16 = f32[256,256]{1,0:T(8,128)S(1)} collective-permute-done((f32[256,256]{1,0:T(8,128)S(1)}, f32[256,256]{1,0:T(8,128)S(1)}, u32[]{:S(2)}, u32[]{:S(2)}) %collective-permute-start.16) | collective-permute-done | bytes 262176 | tf_op jit(solution)/shard_map/ppermute | solution.py:485
  139.5 2.7 %collective-permute-done.18 = f32[4,32,512]{2,1,0:T(8,128)S(1)} collective-permute-done((f32[4,32,512]{2,1,0:T(8,128)S(1)}, f32[4,32,512]{2,1,0:T(8,128)S(1)}, u32[]{:S(2)}, u32[]{:S(2)}) %collective-permute-start.18) | collective-permute-done | bytes 262176 | tf_op jit(solution)/shard_map/ppermute | solution.py:488
  142.4 1.1 fusion.15.first_ref.refs_3_
  143.6 2.1 collective-permute-start.20
  145.7 0.8 copy-done.16
  146.5 7.8 %factor_0.1.work_ref = f32[512,512]{1,0:T(8,128)} custom-call(s32[256]{0:T(256)} %constant.95.clone.table_ref, f32[8,32,512]{2,1,0:T(8,128)} %copy-done.15, f32[8,32,512]{2,1,0:T(8,128)} %copy-done.16, f32[1,512]{1,0:T(1,128)} %bitcast.81), custom_call_target="tpu_custom_call" | custom-call | flops 6710886400 | bytes 2097152 | tf_op jit(solution)/shard_map/factor_0/pallas_call | solution.py:142
  154.3 2.1 collective-permute-start.23
  156.4 7.5 %factor_1.1.work_ref = f32[512,512]{1,0:T(8,128)} custom-call(f32[512,512]{1,0:T(8,128)} %factor_0.1.work_ref), custom_call_target="tpu_custom_call" | custom-call | flops 6710886400 | bytes 2097152 | tf_op jit(solution)/shard_map/factor_1/pallas_call | solution.py:557
  164.0 0.6 collective-permute-start.28
  164.5 0.1 collective-permute-start.29
  164.6 0.4 collective-permute-start.30
  165.1 7.8 %collective-permute-done.24.refs_8_ = f32[256,256]{1,0:T(8,128)S(1)} collective-permute-done((f32[256,256]{1,0:T(8,128)S(1)}, f32[256,256]{1,0:T(8,128)S(1)}, u32[]{:S(2)}, u32[]{:S(2)}) %collective-permute-start.24) | collective-permute-done | bytes 262176 | tf_op jit(solution)/shard_map/ppermute | solution.py:485
  172.9 1.7 collective-permute-start.25
  174.6 7.2 %factor_2.1.work_ref = f32[512,512]{1,0:T(8,128)} custom-call(f32[512,512]{1,0:T(8,128)} %factor_1.1.work_ref), custom_call_target="tpu_custom_call" | custom-call | flops 6710886400 | bytes 2097152 | tf_op jit(solution)/shard_map/factor_2/pallas_call | solution.py:557
  181.9 0.3 collective-permute-start.26
  182.3 1.7 collective-permute-start.27
  184.0 0.5 collective-permute-start.32
  184.5 2.4 %collective-permute-done.26.refs_10_ = f32[128,256]{1,0:T(8,128)S(1)} collective-permute-done((f32[128,256]{1,0:T(8,128)S(1)}, f32[128,256]{1,0:T(8,128)S(1)}, u32[]{:S(2)}, u32[]{:S(2)}) %collective-permute-start.26) | collective-permute-done | bytes 131104 | tf_op jit(solution)/shard_map/ppermute | solution.py:485
  186.9 0.4 collective-permute-done.27.refs_11_
  187.3 0.1 collective-permute-start.34
  187.5 6.9 %factor_3.1.inverse_ref = f32[512,512]{1,0:T(8,128)} custom-call(f32[512,512]{1,0:T(8,128)} %factor_2.1.work_ref), custom_call_target="tpu_custom_call" | custom-call | flops 6710886400 | bytes 2097152 | tf_op jit(solution)/shard_map/factor_3/pallas_call | solution.py:557
  194.3 0.5 collective-permute-start.35
  194.8 0.1 collective-permute-start.36
  194.9 4.0 %solve_rows.1 = (f32[256,512]{1,0:T(8,128)}, f32[256,512]{1,0:T(8,128)}) custom-call(f32[512,512]{1,0:T(8,128)} %factor_3.1.inverse_ref, f32[256,256]{1,0:T(8,128)} %copy-done.2, f32[256,256]{1,0:T(8,128)} %bitcast_add_fusion.1.second_ref), custom_call_target="tpu_custom_call" | custom-call | flops 805306368 | bytes 2097152 | tf_op jit(solution)/shard_map/solve_rows/pallas_call | solution.py:170
  199.0 0.6 copy-done.11
  199.7 0.7 copy-done
  200.4 11.6 %update_rows.1 = f32[256,4096]{1,0:T(8,128)} custom-call(s32[384]{0:T(512)} %constant.94.clone.refs_0_, f32[256,512]{1,0:T(8,128)} %get-tuple-element.114.refs_1_, f32[256,4096]{1,0:T(8,128)} %refs_2_.1, f32[256,256]{1,0:T(8,128)} %copy-done.2, f32[256,256]{1,0:T(8,128)} %copy-done.7, f32[256,256]{1,0:T(8,128)} %copy-done.6, f32[256,256]{1,0:T(8,128)} %copy-done.8, ...), custom_call_target="tpu_custom_call" | custom-call | flops 3221225472 | bytes 16777216 | tf_op jit(solution)/shard_map/update_rows/pallas_call | solution.py:382
  (80 shorter events, 0.7 us)
Async XLA Ops:
  7.2 75.4 %reduce-scatter.2.cloned.1.call-start = ((), (), s32[]{:S(2)}) async-start(), calls=%async_computation.1 | async-start | bytes 2359296 | tf_op jit(solution)/shard_map/reduce_scatter | solution.py:504
  32.2 4.5 %collective-permute-start = (f32[8,256,256]{2,1,0:T(8,128)}, f32[8,256,256]{2,1,0:T(8,128)S(1)}, u32[]{:S(2)}, u32[]{:S(2)}) collective-permute-start(f32[8,256,256]{2,1,0:T(8,128)} %get-tuple-element.63), channel_id=1, source_target_pairs={{0,1},{1,0},{2,3},{3,2},{4,5},{5,4},{6,7},{7,6},{8,9},{9,8},{10,11... | collective-permute-start | bytes 6291464 | tf_op jit(solution)/shard_map/ppermute | solution.py:433
  40.0 1.2 copy-start.3
  40.0 6.4 %copy-start.1 = (f32[8,256,256]{2,1,0:T(8,128)S(1)}, f32[8,256,256]{2,1,0:T(8,128)}, u32[]{:S(2)}) copy-start(f32[8,256,256]{2,1,0:T(8,128)} %get-tuple-element.62) | copy-start | bytes 6291460
  40.0 116.4 %all-gather.3.cloned.1.call-start = ((), (), s32[]{:S(2)}) async-start(), calls=%async_computation.2 | async-start | bytes 2359296 | tf_op jit(solution)/shard_map/all_gather | solution.py:547
  40.1 6.3 %collective-permute-start.1 = (f32[8,256,256]{2,1,0:T(8,128)}, f32[8,256,256]{2,1,0:T(8,128)}, u32[]{:S(2)}, u32[]{:S(2)}) collective-permute-start(f32[8,256,256]{2,1,0:T(8,128)} %get-tuple-element.65), channel_id=1, source_target_pairs={{0,1},{1,0},{2,3},{3,2},{4,5},{5,4},{6,7},{7,6},{8,9},{9,8},{10,11... | collective-permute-start | bytes 6291464 | tf_op jit(solution)/shard_map/ppermute | solution.py:433
  42.1 3.2 %collective-permute-start.2 = (f32[256,512]{1,0:T(8,128)}, f32[256,512]{1,0:T(8,128)S(1)}, u32[]{:S(2)}, u32[]{:S(2)}) collective-permute-start(f32[256,512]{1,0:T(8,128)} %dynamic-slice_bitcast_fusion), channel_id=1, source_target_pairs={{0,1},{1,0},{2,3},{3,2},{4,5},{5,4},{6,7},{7,6},{8,9},{9,8},{10,11... | collective-permute-start | bytes 1572872 | tf_op jit(solution)/shard_map/ppermute | solution.py:433
  42.4 40.1 %copy-start.12 = (f32[256,256]{1,0:T(8,128)S(1)}, f32[256,256]{1,0:T(8,128)}, u32[]{:S(2)}) copy-start(f32[256,256]{1,0:T(8,128)} %get-tuple-element.113) | copy-start | bytes 786436
  48.2 20.9 %collective-permute-start.5 = (f32[4,32,512]{2,1,0:T(8,128)S(1)}, f32[4,32,512]{2,1,0:T(8,128)S(1)}, u32[]{:S(2)}, u32[]{:S(2)}) collective-permute-start(f32[4,32,512]{2,1,0:T(8,128)S(1)} %dynamic-slice_bitcast_fusion.1), channel_id=1, source_target_pairs={{0,2},{1,3},{2,0},{3,1},{4,6},{5,7},{6,4},{7,5},{8,10},{9,11},{10,... | collective-permute-start | bytes 786440 | tf_op jit(solution)/shard_map/ppermute | solution.py:488
  51.0 18.0 %collective-permute-start.3 = (f32[128,256]{1,0:T(8,128)}, f32[128,256]{1,0:T(8,128)S(1)}, u32[]{:S(2)}, u32[]{:S(2)}) collective-permute-start(f32[128,256]{1,0:T(8,128)} %get-tuple-element.67), channel_id=1, source_target_pairs={{0,4},{1,5},{4,8},{5,9},{8,12},{9,13},{12,14},{13,15},{14,10},{15,... | collective-permute-start | bytes 393224 | tf_op jit(solution)/shard_map/ppermute | solution.py:485
  52.6 16.5 %collective-permute-start.4 = (f32[128,256]{1,0:T(8,128)}, f32[128,256]{1,0:T(8,128)}, u32[]{:S(2)}, u32[]{:S(2)}) collective-permute-start(f32[128,256]{1,0:T(8,128)} %get-tuple-element.68), channel_id=1, source_target_pairs={{0,2},{1,3},{4,0},{5,1},{8,4},{9,5},{12,8},{13,9},{14,12},{15,13},... | collective-permute-start | bytes 393224 | tf_op jit(solution)/shard_map/ppermute | solution.py:485
  86.1 20.1 %collective-permute-start.6 = (f32[256,256]{1,0:T(8,128)S(1)}, f32[256,256]{1,0:T(8,128)S(1)}, u32[]{:S(2)}, u32[]{:S(2)}) collective-permute-start(f32[256,256]{1,0:T(8,128)S(1)} %get-tuple-element.73), channel_id=1, source_target_pairs={{0,4},{1,5},{4,8},{5,9},{8,12},{9,13},{12,14},{13,15},{14,10},{15,... | collective-permute-start | bytes 786440 | tf_op jit(solution)/shard_map/ppermute | solution.py:485
  87.3 18.9 %collective-permute-start.7 = (f32[256,256]{1,0:T(8,128)S(1)}, f32[256,256]{1,0:T(8,128)S(1)}, u32[]{:S(2)}, u32[]{:S(2)}) collective-permute-start(f32[256,256]{1,0:T(8,128)S(1)} %get-tuple-element.74), channel_id=1, source_target_pairs={{0,2},{1,3},{4,0},{5,1},{8,4},{9,5},{12,8},{13,9},{14,12},{15,13},... | collective-permute-start | bytes 786440 | tf_op jit(solution)/shard_map/ppermute | solution.py:485
  88.2 14.2 %collective-permute-start.8 = (f32[32,512]{1,0:T(8,128)}, f32[32,512]{1,0:T(8,128)S(1)}, u32[]{:S(2)}, u32[]{:S(2)}) collective-permute-start(f32[32,512]{1,0:T(8,128)} %get-tuple-element.75), channel_id=1, source_target_pairs={{0,4},{1,5},{2,6},{3,7},{4,8},{5,9},{6,10},{7,11},{8,12},{9,13},{1... | collective-permute-start | bytes 196616 | tf_op jit(solution)/shard_map/ppermute | solution.py:491
  89.3 15.6 %collective-permute-start.9 = (f32[32,512]{1,0:T(8,128)}, f32[32,512]{1,0:T(8,128)S(1)}, u32[]{:S(2)}, u32[]{:S(2)}) collective-permute-start(f32[32,512]{1,0:T(8,128)} %get-tuple-element.76), channel_id=1, source_target_pairs={{0,8},{1,9},{2,10},{3,11},{4,12},{5,13},{6,14},{7,15},{8,0},{9,1},... | collective-permute-start | bytes 196616 | tf_op jit(solution)/shard_map/ppermute | solution.py:491
  90.8 15.4 %collective-permute-start.10 = (f32[32,512]{1,0:T(8,128)}, f32[32,512]{1,0:T(8,128)}, u32[]{:S(2)}, u32[]{:S(2)}) collective-permute-start(f32[32,512]{1,0:T(8,128)} %get-tuple-element.77), channel_id=1, source_target_pairs={{0,12},{1,13},{2,14},{3,15},{4,0},{5,1},{6,2},{7,3},{8,4},{9,5},{1... | collective-permute-start | bytes 196616 | tf_op jit(solution)/shard_map/ppermute | solution.py:491
  108.2 34.2 %copy-start.13 = (f32[256,256]{1,0:T(8,128)S(1)}, f32[256,256]{1,0:T(8,128)}, u32[]{:S(2)}) copy-start(f32[256,256]{1,0:T(8,128)} %get-tuple-element.96) | copy-start | bytes 786436
  108.2 23.7 %collective-permute-start.11 = (f32[256,256]{1,0:T(8,128)S(1)}, f32[256,256]{1,0:T(8,128)S(1)}, u32[]{:S(2)}, u32[]{:S(2)}) collective-permute-start(f32[256,256]{1,0:T(8,128)S(1)} %get-tuple-element.83), channel_id=1, source_target_pairs={{0,4},{1,5},{4,8},{5,9},{8,12},{9,13},{12,14},{13,15},{14,10},{15,... | collective-permute-start | bytes 786440 | tf_op jit(solution)/shard_map/ppermute | solution.py:485
  110.5 21.4 %collective-permute-start.12 = (f32[256,256]{1,0:T(8,128)S(1)}, f32[256,256]{1,0:T(8,128)S(1)}, u32[]{:S(2)}, u32[]{:S(2)}) collective-permute-start(f32[256,256]{1,0:T(8,128)S(1)} %get-tuple-element.84), channel_id=1, source_target_pairs={{0,2},{1,3},{4,0},{5,1},{8,4},{9,5},{12,8},{13,9},{14,12},{15,13},... | collective-permute-start | bytes 786440 | tf_op jit(solution)/shard_map/ppermute | solution.py:485
  110.5 13.9 %collective-permute-start.15 = (f32[32,512]{1,0:T(8,128)S(1)}, f32[32,512]{1,0:T(8,128)S(1)}, u32[]{:S(2)}, u32[]{:S(2)}) collective-permute-start(f32[32,512]{1,0:T(8,128)S(1)} %get-tuple-element.85), channel_id=1, source_target_pairs={{0,12},{1,13},{2,14},{3,15},{4,0},{5,1},{6,2},{7,3},{8,4},{9,5},{1... | collective-permute-start | bytes 196616 | tf_op jit(solution)/shard_map/ppermute | solution.py:491
  114.6 17.3 %collective-permute-start.14 = (f32[32,512]{1,0:T(8,128)S(1)}, f32[32,512]{1,0:T(8,128)S(1)}, u32[]{:S(2)}, u32[]{:S(2)}) collective-permute-start(f32[32,512]{1,0:T(8,128)S(1)} %get-tuple-element.85), channel_id=1, source_target_pairs={{0,8},{1,9},{2,10},{3,11},{4,12},{5,13},{6,14},{7,15},{8,0},{9,1},... | collective-permute-start | bytes 196616 | tf_op jit(solution)/shard_map/ppermute | solution.py:491
  114.6 17.3 %collective-permute-start.13 = (f32[32,512]{1,0:T(8,128)S(1)}, f32[32,512]{1,0:T(8,128)S(1)}, u32[]{:S(2)}, u32[]{:S(2)}) collective-permute-start(f32[32,512]{1,0:T(8,128)S(1)} %get-tuple-element.85), channel_id=1, source_target_pairs={{0,4},{1,5},{2,6},{3,7},{4,8},{5,9},{6,10},{7,11},{8,12},{9,13},{1... | collective-permute-start | bytes 196616 | tf_op jit(solution)/shard_map/ppermute | solution.py:491
  133.1 6.4 %collective-permute-start.16 = (f32[256,256]{1,0:T(8,128)S(1)}, f32[256,256]{1,0:T(8,128)S(1)}, u32[]{:S(2)}, u32[]{:S(2)}) collective-permute-start(f32[256,256]{1,0:T(8,128)S(1)} %get-tuple-element.91), channel_id=1, source_target_pairs={{0,4},{1,5},{4,8},{5,9},{8,12},{9,13},{12,14},{13,15},{14,10},{15,... | collective-permute-start | bytes 786440 | tf_op jit(solution)/shard_map/ppermute | solution.py:485
  133.1 6.4 %collective-permute-start.17 = (f32[256,256]{1,0:T(8,128)S(1)}, f32[256,256]{1,0:T(8,128)S(1)}, u32[]{:S(2)}, u32[]{:S(2)}) collective-permute-start(f32[256,256]{1,0:T(8,128)S(1)} %get-tuple-element.92), channel_id=1, source_target_pairs={{0,2},{1,3},{4,0},{5,1},{8,4},{9,5},{12,8},{13,9},{14,12},{15,13},... | collective-permute-start | bytes 786440 | tf_op jit(solution)/shard_map/ppermute | solution.py:485
  135.1 7.2 %collective-permute-start.18 = (f32[4,32,512]{2,1,0:T(8,128)S(1)}, f32[4,32,512]{2,1,0:T(8,128)S(1)}, u32[]{:S(2)}, u32[]{:S(2)}) collective-permute-start(f32[4,32,512]{2,1,0:T(8,128)S(1)} %pad_maximum_fusion), channel_id=1, source_target_pairs={{0,2},{1,3},{2,0},{3,1},{4,6},{5,7},{6,4},{7,5},{8,10},{9,11},{10,... | collective-permute-start | bytes 786440 | tf_op jit(solution)/shard_map/ppermute | solution.py:488
  142.3 1.2 copy-start.15
  142.3 3.4 %collective-permute-start.21 = (f32[8,32,512]{2,1,0:T(8,128)S(1)}, f32[8,32,512]{2,1,0:T(8,128)S(1)}, u32[]{:S(2)}, u32[]{:S(2)}) collective-permute-start(f32[8,32,512]{2,1,0:T(8,128)S(1)} %constant_dynamic-update-slice_fusion.mine_ref), channel_id=1, source_target_pairs={{0,1},{1,0},{2,3},{3,2},{4,5},{5,4},{6,7},{7,6},{8,9},{9,8},{10,11... | collective-permute-start | bytes 1572872 | tf_op jit(solution)/shard_map/ppermute | solution.py:433
  143.6 20.4 %copy-start.2 = (f32[256,256]{1,0:T(8,128)}, f32[256,256]{1,0:T(8,128)S(1)}, u32[]{:S(2)}) copy-start(f32[256,256]{1,0:T(8,128)S(1)} %fusion.15.first_ref.refs_3_) | copy-start | bytes 786436
  143.6 10.7 %collective-permute-start.20 = (f32[256,256]{1,0:T(8,128)S(1)}, f32[256,256]{1,0:T(8,128)S(1)}, u32[]{:S(2)}, u32[]{:S(2)}) collective-permute-start(f32[256,256]{1,0:T(8,128)S(1)} %fusion.15.first_ref.refs_3_), channel_id=1, source_target_pairs={{0,2},{1,3},{4,0},{5,1},{8,4},{9,5},{12,8},{13,9},{14,12},{15,13},... | collective-permute-start | bytes 786440 | tf_op jit(solution)/shard_map/ppermute | solution.py:485
  145.7 8.6 %collective-permute-start.19 = (f32[256,256]{1,0:T(8,128)S(1)}, f32[256,256]{1,0:T(8,128)S(1)}, u32[]{:S(2)}, u32[]{:S(2)}) collective-permute-start(f32[256,256]{1,0:T(8,128)S(1)} %fusion.15.first_ref.refs_3_), channel_id=1, source_target_pairs={{0,4},{1,5},{4,8},{5,9},{8,12},{9,13},{12,14},{13,15},{14,10},{15,... | collective-permute-start | bytes 786440 | tf_op jit(solution)/shard_map/ppermute | solution.py:485
  145.7 0.8 copy-start.16
  154.2 10.4 %copy-start.6 = (f32[256,256]{1,0:T(8,128)}, f32[256,256]{1,0:T(8,128)S(1)}, u32[]{:S(2)}) copy-start(f32[256,256]{1,0:T(8,128)S(1)} %collective-permute-done.20.refs_5_) | copy-start | bytes 786436
  154.2 10.3 %copy-start.7 = (f32[256,256]{1,0:T(8,128)}, f32[256,256]{1,0:T(8,128)S(1)}, u32[]{:S(2)}) copy-start(f32[256,256]{1,0:T(8,128)S(1)} %collective-permute-done.19.refs_4_) | copy-start | bytes 786436
  154.3 9.6 %collective-permute-start.22 = (f32[256,256]{1,0:T(8,128)S(1)}, f32[256,256]{1,0:T(8,128)S(1)}, u32[]{:S(2)}, u32[]{:S(2)}) collective-permute-start(f32[256,256]{1,0:T(8,128)S(1)} %collective-permute-done.19.refs_4_), channel_id=1, source_target_pairs={{0,4},{1,5},{4,8},{5,9},{8,12},{9,13},{12,14},{13,15},{14,10},{15,... | collective-permute-start | bytes 786440 | tf_op jit(solution)/shard_map/ppermute | solution.py:485
  154.3 9.6 %collective-permute-start.23 = (f32[256,256]{1,0:T(8,128)S(1)}, f32[256,256]{1,0:T(8,128)}, u32[]{:S(2)}, u32[]{:S(2)}) collective-permute-start(f32[256,256]{1,0:T(8,128)S(1)} %collective-permute-done.20.refs_5_), channel_id=1, source_target_pairs={{0,2},{1,3},{4,0},{5,1},{8,4},{9,5},{12,8},{13,9},{14,12},{15,13},... | collective-permute-start | bytes 786440 | tf_op jit(solution)/shard_map/ppermute | solution.py:485
  156.4 42.6 %collective-permute-start.37 = (f32[8,256,256]{2,1,0:T(8,128)}, f32[8,256,256]{2,1,0:T(8,128)S(1)}, u32[]{:S(2)}, u32[]{:S(2)}) collective-permute-start(f32[8,256,256]{2,1,0:T(8,128)} %bitcast.69), channel_id=1, source_target_pairs={{0,1},{1,0},{2,3},{3,2},{4,5},{5,4},{6,7},{7,6},{8,9},{9,8},{10,11... | collective-permute-start | bytes 6291464 | tf_op jit(solution)/shard_map/ppermute | solution.py:433
  163.9 1.2 copy-start.8
  163.9 9.0 %collective-permute-start.24 = (f32[256,256]{1,0:T(8,128)S(1)}, f32[256,256]{1,0:T(8,128)S(1)}, u32[]{:S(2)}, u32[]{:S(2)}) collective-permute-start(f32[256,256]{1,0:T(8,128)S(1)} %collective-permute-done.22.refs_6_), channel_id=1, source_target_pairs={{0,4},{1,5},{4,8},{5,9},{8,12},{9,13},{12,14},{13,15},{14,10},{15,... | collective-permute-start | bytes 786440 | tf_op jit(solution)/shard_map/ppermute | solution.py:485
  164.0 18.3 %collective-permute-start.28 = (f32[256,256]{1,0:T(8,128)S(1)}, f32[256,256]{1,0:T(8,128)}, u32[]{:S(2)}, u32[]{:S(2)}) collective-permute-start(f32[256,256]{1,0:T(8,128)S(1)} %fusion.15.first_ref.refs_3_), channel_id=1, source_target_pairs={{0,1},{1,0},{2,3},{3,2},{4,5},{5,4},{6,7},{7,6},{8,9},{9,8},{10,11... | collective-permute-start | bytes 786440 | tf_op jit(solution)/shard_map/ppermute | solution.py:433
  164.5 19.5 %collective-permute-start.29 = (f32[256,256]{1,0:T(8,128)S(1)}, f32[256,256]{1,0:T(8,128)}, u32[]{:S(2)}, u32[]{:S(2)}) collective-permute-start(f32[256,256]{1,0:T(8,128)S(1)} %collective-permute-done.19.refs_4_), channel_id=1, source_target_pairs={{0,1},{1,0},{2,3},{3,2},{4,5},{5,4},{6,7},{7,6},{8,9},{9,8},{10,11... | collective-permute-start | bytes 786440 | tf_op jit(solution)/shard_map/ppermute | solution.py:433
  164.6 19.4 %collective-permute-start.30 = (f32[256,256]{1,0:T(8,128)S(1)}, f32[256,256]{1,0:T(8,128)}, u32[]{:S(2)}, u32[]{:S(2)}) collective-permute-start(f32[256,256]{1,0:T(8,128)S(1)} %collective-permute-done.20.refs_5_), channel_id=1, source_target_pairs={{0,1},{1,0},{2,3},{3,2},{4,5},{5,4},{6,7},{7,6},{8,9},{9,8},{10,11... | collective-permute-start | bytes 786440 | tf_op jit(solution)/shard_map/ppermute | solution.py:433
  172.9 14.1 %copy-start.4 = (f32[256,256]{1,0:T(8,128)}, f32[256,256]{1,0:T(8,128)S(1)}, u32[]{:S(2)}) copy-start(f32[256,256]{1,0:T(8,128)S(1)} %collective-permute-done.24.refs_8_) | copy-start | bytes 786436
  172.9 9.0 %collective-permute-start.25 = (f32[256,256]{1,0:T(8,128)}, f32[256,256]{1,0:T(8,128)S(1)}, u32[]{:S(2)}, u32[]{:S(2)}) collective-permute-start(f32[256,256]{1,0:T(8,128)} %collective-permute-done.23.refs_7_), channel_id=1, source_target_pairs={{0,2},{1,3},{4,0},{5,1},{8,4},{9,5},{12,8},{13,9},{14,12},{15,13},... | collective-permute-start | bytes 786440 | tf_op jit(solution)/shard_map/ppermute | solution.py:485
  181.9 12.4 %copy-start.5 = (f32[256,256]{1,0:T(8,128)}, f32[256,256]{1,0:T(8,128)S(1)}, u32[]{:S(2)}) copy-start(f32[256,256]{1,0:T(8,128)S(1)} %collective-permute-done.25.refs_9_) | copy-start | bytes 786436
  181.9 5.0 %collective-permute-start.26 = (f32[128,256]{1,0:T(8,128)S(1)}, f32[128,256]{1,0:T(8,128)S(1)}, u32[]{:S(2)}, u32[]{:S(2)}) collective-permute-start(f32[128,256]{1,0:T(8,128)S(1)} %slice.88), channel_id=1, source_target_pairs={{0,4},{1,5},{4,8},{5,9},{8,12},{9,13},{12,14},{13,15},{14,10},{15,... | collective-permute-start | bytes 393224 | tf_op jit(solution)/shard_map/ppermute | solution.py:485
  182.3 5.1 %collective-permute-start.27 = (f32[128,256]{1,0:T(8,128)S(1)}, f32[128,256]{1,0:T(8,128)}, u32[]{:S(2)}, u32[]{:S(2)}) collective-permute-start(f32[128,256]{1,0:T(8,128)S(1)} %slice.89), channel_id=1, source_target_pairs={{0,2},{1,3},{4,0},{5,1},{8,4},{9,5},{12,8},{13,9},{14,12},{15,13},... | collective-permute-start | bytes 393224 | tf_op jit(solution)/shard_map/ppermute | solution.py:485
  184.0 10.3 %collective-permute-start.31 = (f32[256,256]{1,0:T(8,128)}, f32[256,256]{1,0:T(8,128)S(1)}, u32[]{:S(2)}, u32[]{:S(2)}) collective-permute-start(f32[256,256]{1,0:T(8,128)} %copy-done.8), channel_id=1, source_target_pairs={{0,1},{1,0},{2,3},{3,2},{4,5},{5,4},{6,7},{7,6},{8,9},{9,8},{10,11... | collective-permute-start | bytes 786440 | tf_op jit(solution)/shard_map/ppermute | solution.py:433
  184.0 10.8 %collective-permute-start.32 = (f32[256,256]{1,0:T(8,128)}, f32[256,256]{1,0:T(8,128)S(1)}, u32[]{:S(2)}, u32[]{:S(2)}) collective-permute-start(f32[256,256]{1,0:T(8,128)} %collective-permute-done.23.refs_7_), channel_id=1, source_target_pairs={{0,1},{1,0},{2,3},{3,2},{4,5},{5,4},{6,7},{7,6},{8,9},{9,8},{10,11... | collective-permute-start | bytes 786440 | tf_op jit(solution)/shard_map/ppermute | solution.py:433
  186.9 7.4 %copy-start.14 = (f32[128,256]{1,0:T(8,128)}, f32[128,256]{1,0:T(8,128)S(1)}, u32[]{:S(2)}) copy-start(f32[128,256]{1,0:T(8,128)S(1)} %collective-permute-done.26.refs_10_) | copy-start | bytes 393220
  186.9 12.0 %collective-permute-start.33 = (f32[256,256]{1,0:T(8,128)S(1)}, f32[256,256]{1,0:T(8,128)S(1)}, u32[]{:S(2)}, u32[]{:S(2)}) collective-permute-start(f32[256,256]{1,0:T(8,128)S(1)} %collective-permute-done.24.refs_8_), channel_id=1, source_target_pairs={{0,1},{1,0},{2,3},{3,2},{4,5},{5,4},{6,7},{7,6},{8,9},{9,8},{10,11... | collective-permute-start | bytes 786440 | tf_op jit(solution)/shard_map/ppermute | solution.py:433
  187.3 11.6 %collective-permute-start.34 = (f32[256,256]{1,0:T(8,128)S(1)}, f32[256,256]{1,0:T(8,128)}, u32[]{:S(2)}, u32[]{:S(2)}) collective-permute-start(f32[256,256]{1,0:T(8,128)S(1)} %collective-permute-done.25.refs_9_), channel_id=1, source_target_pairs={{0,1},{1,0},{2,3},{3,2},{4,5},{5,4},{6,7},{7,6},{8,9},{9,8},{10,11... | collective-permute-start | bytes 786440 | tf_op jit(solution)/shard_map/ppermute | solution.py:433
  194.3 4.7 %copy-start.9 = (f32[256,256]{1,0:T(8,128)}, f32[256,256]{1,0:T(8,128)S(1)}, u32[]{:S(2)}) copy-start(f32[256,256]{1,0:T(8,128)S(1)} %collective-permute-done.31.refs_15_) | copy-start | bytes 786436
  194.3 4.6 %collective-permute-start.35 = (f32[128,256]{1,0:T(8,128)S(1)}, f32[128,256]{1,0:T(8,128)}, u32[]{:S(2)}, u32[]{:S(2)}) collective-permute-start(f32[128,256]{1,0:T(8,128)S(1)} %collective-permute-done.26.refs_10_), channel_id=1, source_target_pairs={{0,1},{1,0},{2,3},{3,2},{4,5},{5,4},{6,7},{7,6},{8,9},{9,8},{10,11... | collective-permute-start | bytes 393224 | tf_op jit(solution)/shard_map/ppermute | solution.py:433
  194.8 4.2 %copy-start.10 = (f32[256,256]{1,0:T(8,128)}, f32[256,256]{1,0:T(8,128)S(1)}, u32[]{:S(2)}) copy-start(f32[256,256]{1,0:T(8,128)S(1)} %collective-permute-done.32.refs_16_) | copy-start | bytes 786436
  194.8 4.2 %collective-permute-start.36 = (f32[128,256]{1,0:T(8,128)}, f32[128,256]{1,0:T(8,128)}, u32[]{:S(2)}, u32[]{:S(2)}) collective-permute-start(f32[128,256]{1,0:T(8,128)} %collective-permute-done.27.refs_11_), channel_id=1, source_target_pairs={{0,1},{1,0},{2,3},{3,2},{4,5},{5,4},{6,7},{7,6},{8,9},{9,8},{10,11... | collective-permute-start | bytes 393224 | tf_op jit(solution)/shard_map/ppermute | solution.py:433
  198.9 0.7 copy-start.11
  199.0 1.4 copy-start
Sparse Core Ops, SparseCore 0:
  40.1 42.3 reduce-scatter.1
  84.4 43.4 all-gather.2

commit v3 on v2

--- a/solution.py
+++ b/solution.py
@@ -179,15 +179,20 @@
     )(inverse, first, second)
 
 
+def chosen_rows(first, count, cols):
+    ids = first + lax.broadcasted_iota(jnp.int32, (count, cols.shape[1]), 0)
+    return (ids == cols).astype(jnp.float32).astype(jnp.bfloat16)
+
+
 def front_kernel(
-    table_ref, counts_ref, cols_ref, weights_ref, prior_ref, rows_ref,
-    block_ref, local_0, local_1, given_0, given_1, kept_0, kept_1,
-    pick, picked, total, sums, sems,
+    table_ref, counts_ref, cols_ref, weights_ref, rows_ref,
+    block_ref, given_0, given_1, kept_0, kept_1,
+    pick, picked, total, sems,
 ):
     step, last = pl.program_id(0), pl.num_programs(0) - 1
     place, parts = lax.axis_index("scen"), lax.axis_size("scen")
     order, width = pick.shape
-    owned = prior_ref.shape[0]
+    owned = total.shape[2]
     depth = rows_ref.shape[0]
     half = width // 2
     tall = order // 4
@@ -199,25 +204,12 @@
 
     @pl.when(step == 0)
     def _():
-        picked[...] = jnp.zeros_like(picked)
+        block_ref[...] = jnp.zeros_like(block_ref)
 
         @pl.loop(0, order // tall)
         def _(n):
             at = pl.ds(pl.multiple_of(n * tall, tall), tall)
-            ids = n * tall + lax.broadcasted_iota(jnp.int32, (tall, width), 0)
-            chosen = (ids == cols_ref[...]).astype(jnp.float32).astype(jnp.bfloat16)
-            pick[at, :] = chosen
-            both = jnp.concatenate(split(prior_ref[:, at]), axis=0)
-            picked[...] += jnp.dot(both, chosen, preferred_element_type=jnp.float32)
-
-        local = (picked[:owned] + picked[owned : 2 * owned]).T
-        local_0[...] = local[:half]
-        local_1[...] = local[half:]
-        ids = place * owned + lax.broadcasted_iota(jnp.int32, (owned, width), 0)
-        chosen = (ids == cols_ref[...]).astype(jnp.float32).astype(jnp.bfloat16)
-        sums[...] = sum(
-            jnp.dot(part, chosen, preferred_element_type=jnp.float32) for part in split(local)
-        )
+            pick[at, :] = chosen_rows(n * tall, tall, cols_ref[...])
 
     picked[...] = jnp.zeros_like(picked)
 
@@ -230,13 +222,9 @@
     live = (slot < counts_ref[0]).astype(jnp.float32)
     factor_w = weights_ref[...] * live * (1.0 / (depth * pl.num_programs(0) * parts))
     scaled = (picked[...].T * factor_w).astype(jnp.bfloat16)
-    sums[...] += jnp.dot(
+    block_ref[...] += jnp.dot(
         scaled, picked[...].astype(jnp.bfloat16), preferred_element_type=jnp.float32
     )
-
-    @pl.when(step == last)
-    def _():
-        block_ref[...] = 0.5 * (sums[...] + sums[...].T)
 
     def stores(n, which):
         refs = ((given_0, given_1), (kept_0, kept_1))[which]
@@ -289,14 +277,12 @@
         each(lambda store: store.wait())
 
 
-def front(table, count, row_counts, panel_cols, row_weights, prior, scenario_rows):
+def front(table, count, owned, row_counts, panel_cols, row_weights, scenario_rows):
     depth, order = scenario_rows.shape
     width = panel_cols.shape[0]
-    owned = prior.shape[0]
     half = width // 2
     tall = 512
     pieces = jax.ShapeDtypeStruct((count, half, owned), jnp.float32)
-    local = jax.ShapeDtypeStruct((half, owned), jnp.float32)
     whole = lambda shape: pl.BlockSpec(shape, lambda i: (0, 0))
     smem = pl.BlockSpec(memory_space=pltpu.SMEM)
     return pl.pallas_call(
@@ -305,27 +291,72 @@
         in_specs=[
             smem, smem, whole((1, width)),
             pl.BlockSpec((1, tall), lambda i: (0, i)),
-            whole((owned, order)),
             pl.BlockSpec((tall, order), lambda i: (i, 0)),
         ],
-        out_specs=[whole((width, width)), whole((half, owned)), whole((half, owned))]
-        + [pl.BlockSpec(memory_space=pl.ANY)] * 4,
-        out_shape=[jax.ShapeDtypeStruct((width, width), jnp.float32), local, local] + [pieces] * 4,
+        out_specs=[whole((width, width))] + [pl.BlockSpec(memory_space=pl.ANY)] * 4,
+        out_shape=[jax.ShapeDtypeStruct((width, width), jnp.float32)] + [pieces] * 4,
         scratch_shapes=[
             pltpu.VMEM((order, width), jnp.bfloat16),
             pltpu.VMEM((tall, width), jnp.float32),
             pltpu.VMEM((2 * count, width, owned), jnp.float32),
-            pltpu.VMEM((width, width), jnp.float32),
             pltpu.SemaphoreType.DMA((2 * count, 2)),
         ],
         cost_estimate=pl.CostEstimate(
             flops=4 * depth * order * width,
-            bytes_accessed=2 * depth * order + 4 * owned * order + 4 * order * width,
+            bytes_accessed=2 * depth * order + 4 * order * width,
             transcendentals=0,
         ),
         compiler_params=pltpu.CompilerParams(vmem_limit_bytes=VMEM_BYTES),
         name="front",
-    )(table, row_counts, panel_cols[None, :], row_weights[None, :], prior, scenario_rows)
+    )(table, row_counts, panel_cols[None, :], row_weights[None, :], scenario_rows)
+
+
+def prior_kernel(cols_ref, prior_ref, gram_ref, local_0, local_1, given_ref, kept_ref, picked):
+    place = lax.axis_index("scen")
+    core = lax.rem(place, 2)
+    owned, order = prior_ref.shape
+    width = cols_ref.shape[1]
+    half = width // 2
+    tall = order // 4
+    picked[...] = jnp.zeros_like(picked)
+
+    @pl.loop(0, order // tall)
+    def _(n):
+        at = pl.ds(pl.multiple_of(n * tall, tall), tall)
+        both = jnp.concatenate(split(prior_ref[:, at]), axis=0)
+        chosen = chosen_rows(n * tall, tall, cols_ref[...])
+        picked[...] += jnp.dot(both, chosen, preferred_element_type=jnp.float32)
+
+    local = (picked[:owned] + picked[owned:]).T
+    local_0[...] = local[:half]
+    local_1[...] = local[half:]
+    chosen = chosen_rows(place * owned, owned, cols_ref[...])
+    block = gram_ref[...] + sum(
+        jnp.dot(part, chosen, preferred_element_type=jnp.float32) for part in split(local)
+    )
+    block = 0.5 * (block + block.T)
+    kept_ref[...] = jnp.where(core == 0, block[:half], block[half:])
+    given_ref[...] = jnp.where(core == 0, block[half:], block[:half])
+
+
+def prior_parts(panel_cols, prior, gram):
+    owned, order = prior.shape
+    width = panel_cols.shape[0]
+    half = width // 2
+    local = jax.ShapeDtypeStruct((half, owned), jnp.float32)
+    rows = jax.ShapeDtypeStruct((half, width), jnp.float32)
+    return pl.pallas_call(
+        prior_kernel,
+        out_shape=[local, local, rows, rows],
+        in_specs=vmem(3),
+        out_specs=vmem(4),
+        scratch_shapes=[pltpu.VMEM((2 * owned, width), jnp.float32)],
+        cost_estimate=pl.CostEstimate(
+            flops=4 * owned * order * width, bytes_accessed=4 * owned * order, transcendentals=0
+        ),
+        compiler_params=pltpu.CompilerParams(vmem_limit_bytes=VMEM_BYTES),
+        name="prior_parts",
+    )(panel_cols[None, :], prior, gram)
 
 
 def update_kernel(count, table_ref, weight_ref, prior_ref, *refs):
@@ -456,8 +487,8 @@
         where = [(at + offset) % chips for offset in back]
         updates += [2 * ring[q] + c for c in (core, 1 - core) for q in where] + where
         factors += [
-            (2 * c + w) * lines + (z - by) % lines
-            for c in (core, 1 - core) for w in (y, 1 - y) for by in range(lines)
+            (2 * c + w) * lines + (z ^ by)
+            for c in (core, 1 - core) for w in (y, 1 - y) for by in (0, 2, 1, 3)
         ]
     return [jnp.array(table, jnp.int32) for table in (fronts, updates, factors)]
 
@@ -484,65 +515,62 @@
         ]
         return lax.ppermute(values, "scen", pairs)
 
-    def swap_y(values):
-        return lax.ppermute(values, "scen", [(d, d ^ 2) for d in range(parts)])
-
-    def shift(values, by):
-        return lax.ppermute(values, "scen", [(d, (d + 4 * by) % parts) for d in range(parts)])
+    def swap(values, bit):
+        return lax.ppermute(values, "scen", [(d, d ^ bit) for d in range(parts)])
 
     def slab(values, at):
         return lax.dynamic_index_in_dim(values, at, 0, keepdims=False)
 
     together = lax.optimization_barrier
 
-    block, local_0, local_1, given_0, given_1, kept_0, kept_1 = front(
-        front_table, chips, row_counts, panel_cols, row_weights, prior_schur, scenario_rows
-    )
-
-    got_1 = swap_cores(given_1)
+    gram, given_0, given_1, kept_0, kept_1 = front(
+        front_table, chips, prior_schur.shape[0], row_counts, panel_cols, row_weights, scenario_rows
+    )
+
+    got_1 = swap(given_1, 1)
     got_1, given_0 = together((got_1, given_0))
     summed = lax.psum_scatter(
         kept_1 + got_1, "scen", scatter_dimension=0, axis_index_groups=groups
     )
-    panel_1 = summed + local_1
-
-    got_0 = swap_cores(given_0)
+    got_0 = swap(given_0, 1)
+
+    local_0, local_1, block_given, block_kept = prior_parts(panel_cols, prior_schur, gram)
+    block = (block_kept + swap(block_given, 1)).reshape(2, lines, -1, 2 * half)
+    block = slab(block, y) + swap(slab(block, 1 - y), 2)
+    low, high = z % 2, z // 2
+    block = block.reshape(2, 2, -1, 2 * half)
+    pairs = lax.dynamic_index_in_dim(block, low, 1, keepdims=False)
+    pairs = pairs + swap(lax.dynamic_index_in_dim(block, 1 - low, 1, keepdims=False), 4)
+    moves = [8, 8, 4, 2]
+    beside = slab(pairs, 1 - high)
+
     sides = {1: slice(0, half // 2), -1: slice(half // 2, half)}
 
     def partial(offset):
         n = offsets.index(offset)
         return kept_0[n] + got_0[n]
 
-    block = halve_block(block).reshape(2, lines, -1, block.shape[0])
-    ahead = [partial(far)[sides[way]] for way in (1, -1)]
-    ahead, beside = together((ahead, slab(block, 1 - y)))
-    ahead, beside = together(([step(ahead[0], 1), step(ahead[1], -1)], swap_y(beside)))
-    arrived = [
-        jnp.pad(ahead[0], ((0, half // 2), (0, 0))),
-        jnp.pad(ahead[1], ((half // 2, 0), (0, 0))),
-    ]
-
-    block = slab(block, y) + beside
-    beside = [slab(block, (z + by) % lines) for by in range(1, lines)]
-    for d in range(far - 1, 0, -1):
-        ahead = [partial(way * d) + arrived[n] for n, way in enumerate((1, -1))]
+    arrived = None
+    for d in range(far, 0, -1):
+        if d == far:
+            ahead = [partial(far)[sides[way]] for way in (1, -1)]
+        else:
+            ahead = [partial(way * d) + arrived[n] for n, way in enumerate((1, -1))]
         ahead, beside = together((ahead, beside))
-        arrived = [step(ahead[0], 1), step(ahead[1], -1)]
-        if d == far - 1:
-            beside = [shift(beside[by - 1], by) for by in range(1, lines)]
-        elif d == far - 2:
-            beside = [shift(beside, by) for by in range(1, lines)]
+        moved = swap(beside, moves[far - d])
+        arrived, moved = together(([step(ahead[0], 1), step(ahead[1], -1)], moved))
+        if d == far:
+            arrived = [
+                jnp.pad(arrived[0], ((0, half // 2), (0, 0))),
+                jnp.pad(arrived[1], ((half // 2, 0), (0, 0))),
+            ]
+            beside = (slab(pairs, high) + moved)[None]
         else:
-            beside = swap_y(beside)
-        arrived, beside = together((arrived, beside))
-        if d == far - 1:
-            mine = beside = sum(beside) + slab(block, z)
-        elif d == far - 2:
-            near = beside = jnp.stack([mine] + beside)
-        else:
-            block = jnp.concatenate([near, beside])
+            beside = jnp.concatenate([beside, moved])
+    arrived, summed = together((arrived, summed))
     panel_0 = partial(0) + arrived[0] + arrived[1] + local_0
-    stages = factor_stages(factor_table, block, swap_cores(block), regular)
+    panel_1 = summed + local_1
+    stages = factor_stages(factor_table, beside, swap(beside, 1), regular)
 
     second = lax.all_gather(panel_1, "scen", axis_index_groups=groups)
     first = [panel_0]
@@ -560,7 +588,7 @@
     inverse = work
     for stage in stages[far:]:
         inverse = stage(inverse)
-    sources = first + [swap_cores(piece) for piece in first] + [second, swap_cores(second)]
+    sources = first + [swap(piece, 1) for piece in first] + [second, swap(second, 1)]
 
     factor_rows, weights = solve_rows(inverse, panel_0, panel_1)
     return update_rows(update_table, parts, weights, prior_schur, sources), factor_rows

time: 219 us -> 218 us (level)
  starting transfers between devices: 32.5 us -> 25 us
  waiting for transfers between devices: 84.3 us -> 91.5 us
  Pallas kernels: 69.3 us -> 72.2 us
  other arithmetic: 12.5 us -> 10.2 us
    all_gather x1, waiting for transfers between devices: 0.01 us -> 19.5 us  [shards_on_ring(): second = lax.all_gather(panel_1, 'scen', axis_index_groups=groups)]
    reduce_scatter x1, waiting for transfers between devices: 13.4 us -> 0.01 us  [shards_on_ring(): lax.psum_scatter(kept_1 + got_1, 'scen', scatter_dimension=0, axis_index_...]
    ppermute x22 -> x20, waiting for transfers between devices: 39.9 us -> 50.3 us  [swap(): return lax.ppermute(values, 'scen', [(d, d ^ bit) for d in range(parts)])]
    ppermute x16, waiting for transfers between devices: 31 us -> 21.6 us  [step(): return lax.ppermute(values, 'scen', pairs)]
    pallas_call x0 -> x1, Pallas kernels: none -> 7.38 us  [prior_parts(): pl.pallas_call(prior_kernel, out_shape=[local, local, rows, rows], in_spe...]
    ppermute x22 -> x20, starting transfers between devices: 15.8 us -> 8.92 us  [swap(): return lax.ppermute(values, 'scen', [(d, d ^ bit) for d in range(parts)])]
    pallas_call x1, Pallas kernels: 24.4 us -> 19.9 us  [front(): pl.pallas_call(front_kernel, grid=(depth // tall,), in_specs=[smem, smem,...]
  transfers between devices with their start and end apart: 40 -> 38, of which waited for: 15 -> 16; matrix products, arithmetic and copies ran while one was open for 5% -> 4% of each run, Pallas kernels for 15% -> 19%
where the time goes in v3:
time: 218 us; the launch traced here: 217 us
  waiting for transfers between devices  91.5 us (42%)
  Pallas kernels  72.2 us (33%)
  starting transfers between devices  25 us (11%)
  between operations  15.1 us (7%)
  other arithmetic  10.2 us (5%)
  local copies, waits for them, and re-layouts  3.17 us (1%)
    ppermute x20, waiting for transfers between devices, swap(): return lax.ppermute(values, 'scen', [(d, d ^ bit) for d in range(parts)])  50.3 us
    ppermute x16, waiting for transfers between devices, step(): return lax.ppermute(values, 'scen', pairs)  21.6 us
    pallas_call x3, Pallas kernels, shards_on_ring(): stages[d - 1](work)  21.6 us
    pallas_call x1, Pallas kernels, front(): pl.pallas_call(front_kernel, grid=(depth // tall,), in_specs=[smem, smem,...  19.9 us
    all_gather x1, waiting for transfers between devices, shards_on_ring(): second = lax.all_gather(panel_1, 'scen', axis_index_groups=groups)  19.5 us
    ppermute x16, starting transfers between devices, step(): return lax.ppermute(values, 'scen', pairs)  16 us
    pallas_call x1, Pallas kernels, update_rows(): pl.pallas_call(lambda *refs: update_kernel(count, *refs), out_shape=jax.S...  11.6 us
    ppermute x20, starting transfers between devices, swap(): return lax.ppermute(values, 'scen', [(d, d ^ bit) for d in range(parts)])  8.92 us
  transfers between devices with their start and end apart: 38, of which 16 were waited for; matrix products, arithmetic and copies ran while one was open for 4% of the time, Pallas kernels for 19%

profile of v3, /device:TPU:0, one launch (start us, length us, event | category | flops | bytes accessed | tf_op | source)
XLA Modules:
  0.0 217.2 jit_solution(11131762435527964834)
XLA Ops:
  7.9 19.9 %front.1 = (f32[512,512]{1,0:T(8,128)}, f32[8,256,256]{2,1,0:T(8,128)}, f32[8,256,256]{2,1,0:T(8,128)}, f32[8,256,256]{2,1,0:T(8,128)}, f32[8,256,256]{2,1,0:T(8,128)}) custom-call(s32[512]{0:T(512)} %constant.80.clone.table_ref, s32[1]{0:T(128)S(6)} %copy.12.counts_ref, s32[1,512]{1,0:T(1,128)} %bitcast.67, f32[1,1024]{1,0:T(1,128)} %bitcast.66, ...), custom_call_target="tpu_custom_call" | custom-call | flops 8589934592 | bytes 16777216 | tf_op jit(solution)/shard_map/front/pallas_call | solution.py:288
  27.7 0.6 collective-permute-start
  28.3 4.0 %collective-permute-done = f32[8,256,256]{2,1,0:T(8,128)S(1)} collective-permute-done((f32[8,256,256]{2,1,0:T(8,128)}, f32[8,256,256]{2,1,0:T(8,128)S(1)}, u32[]{:S(2)}, u32[]{:S(2)}) %collective-permute-start) | collective-permute-done | bytes 2097184 | tf_op jit(solution)/shard_map/ppermute | solution.py:519
  32.3 0.4 collective-permute-start.1
  32.7 7.4 %prior_parts.1 = (f32[256,256]{1,0:T(8,128)}, f32[256,256]{1,0:T(8,128)}, f32[256,512]{1,0:T(8,128)}, f32[256,512]{1,0:T(8,128)}) custom-call(s32[1,512]{1,0:T(1,128)} %bitcast.68, f32[256,4096]{1,0:T(8,128)} %refs_2_.1, f32[512,512]{1,0:T(8,128)} %get-tuple-element.65.gram_ref), custom_call_target="tpu_custom_call" | custom-call | flops 2147483648 | bytes 4194304 | tf_op jit(solution)/shard_map/prior_parts/pallas_call | solution.py:348
  40.1 0.1 collective-permute-start.2
  40.2 1.6 add.165
  42.0 0.2 collective-permute-done.2
  42.2 0.8 copy-done.7
  43.0 1.1 add.141
  44.1 2.9 %collective-permute-start.3 = (f32[4,32,512]{2,1,0:T(8,128)S(1)}, f32[4,32,512]{2,1,0:T(8,128)S(1)}, u32[]{:S(2)}, u32[]{:S(2)}) collective-permute-start(f32[4,32,512]{2,1,0:T(8,128)S(1)} %dynamic-slice_bitcast_fusion), channel_id=1, source_target_pairs={{0,2},{1,3},{2,0},{3,1},{4,6},{5,7},{6,4},{7,5},{8,10},{9,11},{10,... | collective-permute-start | bytes 786440 | tf_op jit(solution)/shard_map/ppermute | solution.py:519
  47.0 9.0 %collective-permute-done.3 = f32[4,32,512]{2,1,0:T(8,128)S(1)} collective-permute-done((f32[4,32,512]{2,1,0:T(8,128)S(1)}, f32[4,32,512]{2,1,0:T(8,128)S(1)}, u32[]{:S(2)}, u32[]{:S(2)}) %collective-permute-start.3) | collective-permute-done | bytes 262176 | tf_op jit(solution)/shard_map/ppermute | solution.py:519
  56.1 0.1 collective-permute-start.4
  56.2 8.0 %collective-permute-done.4 = f32[2,32,512]{2,1,0:T(8,128)S(1)} collective-permute-done((f32[2,32,512]{2,1,0:T(8,128)S(1)}, f32[2,32,512]{2,1,0:T(8,128)S(1)}, u32[]{:S(2)}, u32[]{:S(2)}) %collective-permute-start.4) | collective-permute-done | bytes 131104 | tf_op jit(solution)/shard_map/ppermute | solution.py:519
  64.3 1.0 slice_add_fusion.3
  65.3 0.3 collective-permute-start.5
  65.6 2.2 %collective-permute-start.6 = (f32[128,256]{1,0:T(8,128)S(1)}, f32[128,256]{1,0:T(8,128)S(1)}, u32[]{:S(2)}, u32[]{:S(2)}) collective-permute-start(f32[128,256]{1,0:T(8,128)S(1)} %get-tuple-element.69), channel_id=1, source_target_pairs={{0,2},{1,3},{4,0},{5,1},{8,4},{9,5},{12,8},{13,9},{14,12},{15,13},... | collective-permute-start | bytes 393224 | tf_op jit(solution)/shard_map/ppermute | solution.py:516
  67.8 1.8 collective-permute-start.7
  69.6 10.4 %collective-permute-done.7 = f32[32,512]{1,0:T(8,128)S(1)} collective-permute-done((f32[32,512]{1,0:T(8,128)S(1)}, f32[32,512]{1,0:T(8,128)S(1)}, u32[]{:S(2)}, u32[]{:S(2)}) %collective-permute-start.7) | collective-permute-done | bytes 65568 | tf_op jit(solution)/shard_map/ppermute | solution.py:519
  80.0 1.1 fusion.5
  81.2 2.0 collective-permute-start.9
  83.2 8.6 %collective-permute-done.10 = f32[1,32,512]{2,1,0:T(8,128)S(1)} collective-permute-done((f32[1,32,512]{2,1,0:T(8,128)S(1)}, f32[1,32,512]{2,1,0:T(8,128)S(1)}, u32[]{:S(2)}, u32[]{:S(2)}) %collective-permute-start.10) | collective-permute-done | bytes 65568 | tf_op jit(solution)/shard_map/ppermute | solution.py:519
  91.9 1.2 fusion.3
  93.1 2.0 collective-permute-start.12
  95.2 7.1 %collective-permute-done.13 = f32[2,32,512]{2,1,0:T(8,128)S(1)} collective-permute-done((f32[2,32,512]{2,1,0:T(8,128)S(1)}, f32[2,32,512]{2,1,0:T(8,128)S(1)}, u32[]{:S(2)}, u32[]{:S(2)}) %collective-permute-start.13) | collective-permute-done | bytes 131104 | tf_op jit(solution)/shard_map/ppermute | solution.py:519
  102.4 1.2 fusion.1
  103.5 0.3 collective-permute-start.14
  103.8 1.8 collective-permute-start.15
  105.6 1.1 collective-permute-start.16
  106.7 5.1 %collective-permute-done.14 = f32[256,256]{1,0:T(8,128)S(1)} collective-permute-done((f32[256,256]{1,0:T(8,128)S(1)}, f32[256,256]{1,0:T(8,128)S(1)}, u32[]{:S(2)}, u32[]{:S(2)}) %collective-permute-start.14) | collective-permute-done | bytes 262176 | tf_op jit(solution)/shard_map/ppermute | solution.py:516
  111.8 2.8 %collective-permute-done.16 = f32[4,32,512]{2,1,0:T(8,128)S(1)} collective-permute-done((f32[4,32,512]{2,1,0:T(8,128)S(1)}, f32[4,32,512]{2,1,0:T(8,128)S(1)}, u32[]{:S(2)}, u32[]{:S(2)}) %collective-permute-start.16) | collective-permute-done | bytes 262176 | tf_op jit(solution)/shard_map/ppermute | solution.py:519
  114.6 1.7 add.169.second_ref
  116.4 0.1 collective-permute-start.19
  116.5 1.2 fusion.15.first_ref.refs_3_
  117.7 1.8 collective-permute-start.18
  119.6 0.3 collective-permute-start.17
  119.9 0.8 copy-done.18
  120.6 7.8 %factor_0.1.work_ref = f32[512,512]{1,0:T(8,128)} custom-call(s32[256]{0:T(256)} %constant.82.clone.table_ref, f32[8,32,512]{2,1,0:T(8,128)} %copy-done.17, f32[8,32,512]{2,1,0:T(8,128)} %copy-done.18, f32[1,512]{1,0:T(1,128)} %bitcast.69), custom_call_target="tpu_custom_call" | custom-call | flops 6710886400 | bytes 2097152 | tf_op jit(solution)/shard_map/factor_0/pallas_call | solution.py:142
  128.4 2.8 %collective-permute-done.18.refs_5_ = f32[256,256]{1,0:T(8,128)S(1)} collective-permute-done((f32[256,256]{1,0:T(8,128)S(1)}, f32[256,256]{1,0:T(8,128)S(1)}, u32[]{:S(2)}, u32[]{:S(2)}) %collective-permute-start.18) | collective-permute-done | bytes 262176 | tf_op jit(solution)/shard_map/ppermute | solution.py:516
  131.2 2.3 %collective-permute-done.17.refs_4_ = f32[256,256]{1,0:T(8,128)S(1)} collective-permute-done((f32[256,256]{1,0:T(8,128)S(1)}, f32[256,256]{1,0:T(8,128)S(1)}, u32[]{:S(2)}, u32[]{:S(2)}) %collective-permute-start.17) | collective-permute-done | bytes 262176 | tf_op jit(solution)/shard_map/ppermute | solution.py:516
  133.5 0.3 collective-permute-start.20
  133.8 1.7 collective-permute-start.21
  135.5 19.5 %all-gather.3.cloned.1.call-done = f32[2048,256]{1,0:T(8,128)} async-done(((f32[256,256]{1,0:T(8,128)}), f32[2048,256]{1,0:T(8,128)}) %all-gather.3.cloned.1.call-update) | async-done | bytes 2097168 | tf_op jit(solution)/shard_map/all_gather | solution.py:575
  155.0 7.5 %factor_1.1.work_ref = f32[512,512]{1,0:T(8,128)} custom-call(f32[512,512]{1,0:T(8,128)} %factor_0.1.work_ref), custom_call_target="tpu_custom_call" | custom-call | flops 6710886400 | bytes 2097152 | tf_op jit(solution)/shard_map/factor_1/pallas_call | solution.py:585
  162.5 0.6 collective-permute-start.22
  163.1 0.2 collective-permute-start.26
  163.4 0.3 collective-permute-start.27
  163.6 0.2 collective-permute-start.28
  163.9 7.4 %collective-permute-done.22.refs_8_ = f32[256,256]{1,0:T(8,128)S(1)} collective-permute-done((f32[256,256]{1,0:T(8,128)S(1)}, f32[256,256]{1,0:T(8,128)S(1)}, u32[]{:S(2)}, u32[]{:S(2)}) %collective-permute-start.22) | collective-permute-done | bytes 262176 | tf_op jit(solution)/shard_map/ppermute | solution.py:516
  171.3 0.5 collective-permute-start.23
  171.8 7.3 %factor_2.1.work_ref = f32[512,512]{1,0:T(8,128)} custom-call(f32[512,512]{1,0:T(8,128)} %factor_1.1.work_ref), custom_call_target="tpu_custom_call" | custom-call | flops 6710886400 | bytes 2097152 | tf_op jit(solution)/shard_map/factor_2/pallas_call | solution.py:585
  179.1 0.4 collective-permute-done.23.refs_9_
  179.5 1.2 collective-permute-start.24
  180.7 0.9 collective-permute-start.25
  181.6 0.5 collective-permute-start.30
  182.1 2.4 %collective-permute-done.24.refs_10_ = f32[128,256]{1,0:T(8,128)S(1)} collective-permute-done((f32[128,256]{1,0:T(8,128)S(1)}, f32[128,256]{1,0:T(8,128)S(1)}, u32[]{:S(2)}, u32[]{:S(2)}) %collective-permute-start.24) | collective-permute-done | bytes 131104 | tf_op jit(solution)/shard_map/ppermute | solution.py:516
  184.5 1.2 collective-permute-done.25.refs_11_
  185.7 6.9 %factor_3.1.inverse_ref = f32[512,512]{1,0:T(8,128)} custom-call(f32[512,512]{1,0:T(8,128)} %factor_2.1.work_ref), custom_call_target="tpu_custom_call" | custom-call | flops 6710886400 | bytes 2097152 | tf_op jit(solution)/shard_map/factor_3/pallas_call | solution.py:585
  192.6 0.6 collective-permute-start.33
  193.2 0.1 collective-permute-start.34
  193.3 4.0 %solve_rows.1 = (f32[256,512]{1,0:T(8,128)}, f32[256,512]{1,0:T(8,128)}) custom-call(f32[512,512]{1,0:T(8,128)} %factor_3.1.inverse_ref, f32[256,256]{1,0:T(8,128)} %copy-done.3, f32[256,256]{1,0:T(8,128)} %add.169.second_ref), custom_call_target="tpu_custom_call" | custom-call | flops 805306368 | bytes 2097152 | tf_op jit(solution)/shard_map/solve_rows/pallas_call | solution.py:170
  197.4 0.6 copy-done.13
  198.1 0.7 copy-done
  198.8 11.6 %update_rows.1 = f32[256,4096]{1,0:T(8,128)} custom-call(s32[384]{0:T(512)} %constant.81.clone.refs_0_, f32[256,512]{1,0:T(8,128)} %get-tuple-element.112.refs_1_, f32[256,4096]{1,0:T(8,128)} %refs_2_.1, f32[256,256]{1,0:T(8,128)} %copy-done.3, f32[256,256]{1,0:T(8,128)} %copy-done.9, f32[256,256]{1,0:T(8,128)} %copy-done.8, f32[256,256]{1,0:T(8,128)} %copy-done.10, ...), custom_call_target="tpu_custom_call" | custom-call | flops 3221225472 | bytes 16777216 | tf_op jit(solution)/shard_map/update_rows/pallas_call | solution.py:413
  (81 shorter events, 0.7 us)
Async XLA Ops:
  7.2 107.5 %reduce-scatter.2.cloned.1.call-start = ((), (), s32[]{:S(2)}) async-start(), calls=%async_computation.1 | async-start | bytes 2359296 | tf_op jit(solution)/shard_map/reduce_scatter | solution.py:532
  27.7 4.6 %collective-permute-start = (f32[8,256,256]{2,1,0:T(8,128)}, f32[8,256,256]{2,1,0:T(8,128)S(1)}, u32[]{:S(2)}, u32[]{:S(2)}) collective-permute-start(f32[8,256,256]{2,1,0:T(8,128)} %get-tuple-element.62), channel_id=1, source_target_pairs={{0,1},{1,0},{2,3},{3,2},{4,5},{5,4},{6,7},{7,6},{8,9},{9,8},{10,11... | collective-permute-start | bytes 6291464 | tf_op jit(solution)/shard_map/ppermute | solution.py:519
  32.3 32.0 %collective-permute-start.1 = (f32[8,256,256]{2,1,0:T(8,128)}, f32[8,256,256]{2,1,0:T(8,128)}, u32[]{:S(2)}, u32[]{:S(2)}) collective-permute-start(f32[8,256,256]{2,1,0:T(8,128)} %get-tuple-element.64), channel_id=1, source_target_pairs={{0,1},{1,0},{2,3},{3,2},{4,5},{5,4},{6,7},{7,6},{8,9},{9,8},{10,11... | collective-permute-start | bytes 6291464 | tf_op jit(solution)/shard_map/ppermute | solution.py:519
  32.7 7.5 %copy-start.1 = (f32[8,256,256]{2,1,0:T(8,128)S(1)}, f32[8,256,256]{2,1,0:T(8,128)}, u32[]{:S(2)}) copy-start(f32[8,256,256]{2,1,0:T(8,128)} %get-tuple-element.91) | copy-start | bytes 6291460
  40.1 2.1 collective-permute-start.2
  41.8 1.1 copy-start.6
  41.9 22.4 %copy-start.2 = (f32[8,256,256]{2,1,0:T(8,128)S(1)}, f32[8,256,256]{2,1,0:T(8,128)}, u32[]{:S(2)}) copy-start(f32[8,256,256]{2,1,0:T(8,128)} %get-tuple-element.61) | copy-start | bytes 6291460
  41.9 113.1 %all-gather.3.cloned.1.call-start = ((), (), s32[]{:S(2)}) async-start(), calls=%async_computation.2 | async-start | bytes 2359296 | tf_op jit(solution)/shard_map/all_gather | solution.py:575
  42.2 0.8 copy-start.7
  44.1 11.9 %collective-permute-start.3 = (f32[4,32,512]{2,1,0:T(8,128)S(1)}, f32[4,32,512]{2,1,0:T(8,128)S(1)}, u32[]{:S(2)}, u32[]{:S(2)}) collective-permute-start(f32[4,32,512]{2,1,0:T(8,128)S(1)} %dynamic-slice_bitcast_fusion), channel_id=1, source_target_pairs={{0,2},{1,3},{2,0},{3,1},{4,6},{5,7},{6,4},{7,5},{8,10},{9,11},{10,... | collective-permute-start | bytes 786440 | tf_op jit(solution)/shard_map/ppermute | solution.py:519
  56.1 8.1 %collective-permute-start.4 = (f32[2,32,512]{2,1,0:T(8,128)S(1)}, f32[2,32,512]{2,1,0:T(8,128)S(1)}, u32[]{:S(2)}, u32[]{:S(2)}) collective-permute-start(f32[2,32,512]{2,1,0:T(8,128)S(1)} %dynamic-slice_bitcast_fusion.1), channel_id=1, source_target_pairs={{0,4},{1,5},{2,6},{3,7},{4,0},{5,1},{6,2},{7,3},{8,12},{9,13},{10,... | collective-permute-start | bytes 393224 | tf_op jit(solution)/shard_map/ppermute | solution.py:519
  65.3 14.7 %collective-permute-start.5 = (f32[128,256]{1,0:T(8,128)S(1)}, f32[128,256]{1,0:T(8,128)S(1)}, u32[]{:S(2)}, u32[]{:S(2)}) collective-permute-start(f32[128,256]{1,0:T(8,128)S(1)} %get-tuple-element.68), channel_id=1, source_target_pairs={{0,4},{1,5},{4,8},{5,9},{8,12},{9,13},{12,14},{13,15},{14,10},{15,... | collective-permute-start | bytes 393224 | tf_op jit(solution)/shard_map/ppermute | solution.py:516
  65.6 14.4 %collective-permute-start.6 = (f32[128,256]{1,0:T(8,128)S(1)}, f32[128,256]{1,0:T(8,128)S(1)}, u32[]{:S(2)}, u32[]{:S(2)}) collective-permute-start(f32[128,256]{1,0:T(8,128)S(1)} %get-tuple-element.69), channel_id=1, source_target_pairs={{0,2},{1,3},{4,0},{5,1},{8,4},{9,5},{12,8},{13,9},{14,12},{15,13},... | collective-permute-start | bytes 393224 | tf_op jit(solution)/shard_map/ppermute | solution.py:516
  67.8 12.2 %collective-permute-start.7 = (f32[32,512]{1,0:T(8,128)S(1)}, f32[32,512]{1,0:T(8,128)S(1)}, u32[]{:S(2)}, u32[]{:S(2)}) collective-permute-start(f32[32,512]{1,0:T(8,128)S(1)} %dynamic-slice_bitcast_fusion.2), channel_id=1, source_target_pairs={{0,8},{1,9},{2,10},{3,11},{4,12},{5,13},{6,14},{7,15},{8,0},{9,1},... | collective-permute-start | bytes 196616 | tf_op jit(solution)/shard_map/ppermute | solution.py:519
  81.1 10.7 %collective-permute-start.8 = (f32[256,256]{1,0:T(8,128)S(1)}, f32[256,256]{1,0:T(8,128)S(1)}, u32[]{:S(2)}, u32[]{:S(2)}) collective-permute-start(f32[256,256]{1,0:T(8,128)S(1)} %get-tuple-element.74), channel_id=1, source_target_pairs={{0,4},{1,5},{4,8},{5,9},{8,12},{9,13},{12,14},{13,15},{14,10},{15,... | collective-permute-start | bytes 786440 | tf_op jit(solution)/shard_map/ppermute | solution.py:516
  81.2 10.7 %collective-permute-start.9 = (f32[256,256]{1,0:T(8,128)S(1)}, f32[256,256]{1,0:T(8,128)S(1)}, u32[]{:S(2)}, u32[]{:S(2)}) collective-permute-start(f32[256,256]{1,0:T(8,128)S(1)} %get-tuple-element.75), channel_id=1, source_target_pairs={{0,2},{1,3},{4,0},{5,1},{8,4},{9,5},{12,8},{13,9},{14,12},{15,13},... | collective-permute-start | bytes 786440 | tf_op jit(solution)/shard_map/ppermute | solution.py:516
  83.2 8.6 %collective-permute-start.10 = (f32[1,32,512]{2,1,0:T(8,128)S(1)}, f32[1,32,512]{2,1,0:T(8,128)S(1)}, u32[]{:S(2)}, u32[]{:S(2)}) collective-permute-start(f32[1,32,512]{2,1,0:T(8,128)S(1)} %fusion.16), channel_id=1, source_target_pairs={{0,8},{1,9},{2,10},{3,11},{4,12},{5,13},{6,14},{7,15},{8,0},{9,1},... | collective-permute-start | bytes 196616 | tf_op jit(solution)/shard_map/ppermute | solution.py:519
  91.9 22.8 %copy-start.14 = (f32[256,256]{1,0:T(8,128)S(1)}, f32[256,256]{1,0:T(8,128)}, u32[]{:S(2)}) copy-start(f32[256,256]{1,0:T(8,128)} %get-tuple-element.111) | copy-start | bytes 786436
  93.0 9.3 %collective-permute-start.11 = (f32[256,256]{1,0:T(8,128)S(1)}, f32[256,256]{1,0:T(8,128)S(1)}, u32[]{:S(2)}, u32[]{:S(2)}) collective-permute-start(f32[256,256]{1,0:T(8,128)S(1)} %get-tuple-element.80), channel_id=1, source_target_pairs={{0,4},{1,5},{4,8},{5,9},{8,12},{9,13},{12,14},{13,15},{14,10},{15,... | collective-permute-start | bytes 786440 | tf_op jit(solution)/shard_map/ppermute | solution.py:516
  93.1 9.2 %collective-permute-start.12 = (f32[256,256]{1,0:T(8,128)S(1)}, f32[256,256]{1,0:T(8,128)S(1)}, u32[]{:S(2)}, u32[]{:S(2)}) collective-permute-start(f32[256,256]{1,0:T(8,128)S(1)} %get-tuple-element.81), channel_id=1, source_target_pairs={{0,2},{1,3},{4,0},{5,1},{8,4},{9,5},{12,8},{13,9},{14,12},{15,13},... | collective-permute-start | bytes 786440 | tf_op jit(solution)/shard_map/ppermute | solution.py:516
  95.1 7.2 %collective-permute-start.13 = (f32[2,32,512]{2,1,0:T(8,128)S(1)}, f32[2,32,512]{2,1,0:T(8,128)S(1)}, u32[]{:S(2)}, u32[]{:S(2)}) collective-permute-start(f32[2,32,512]{2,1,0:T(8,128)S(1)} %pad_maximum_fusion.1), channel_id=1, source_target_pairs={{0,4},{1,5},{2,6},{3,7},{4,0},{5,1},{6,2},{7,3},{8,12},{9,13},{10,... | collective-permute-start | bytes 393224 | tf_op jit(solution)/shard_map/ppermute | solution.py:519
  102.3 14.2 %copy-start.15 = (f32[256,256]{1,0:T(8,128)S(1)}, f32[256,256]{1,0:T(8,128)}, u32[]{:S(2)}) copy-start(f32[256,256]{1,0:T(8,128)} %get-tuple-element.95) | copy-start | bytes 786436
  103.5 8.3 %collective-permute-start.14 = (f32[256,256]{1,0:T(8,128)S(1)}, f32[256,256]{1,0:T(8,128)S(1)}, u32[]{:S(2)}, u32[]{:S(2)}) collective-permute-start(f32[256,256]{1,0:T(8,128)S(1)} %get-tuple-element.86), channel_id=1, source_target_pairs={{0,4},{1,5},{4,8},{5,9},{8,12},{9,13},{12,14},{13,15},{14,10},{15,... | collective-permute-start | bytes 786440 | tf_op jit(solution)/shard_map/ppermute | solution.py:516
  103.8 8.0 %collective-permute-start.15 = (f32[256,256]{1,0:T(8,128)S(1)}, f32[256,256]{1,0:T(8,128)}, u32[]{:S(2)}, u32[]{:S(2)}) collective-permute-start(f32[256,256]{1,0:T(8,128)S(1)} %get-tuple-element.87), channel_id=1, source_target_pairs={{0,2},{1,3},{4,0},{5,1},{8,4},{9,5},{12,8},{13,9},{14,12},{15,13},... | collective-permute-start | bytes 786440 | tf_op jit(solution)/shard_map/ppermute | solution.py:516
  105.6 9.0 %collective-permute-start.16 = (f32[4,32,512]{2,1,0:T(8,128)S(1)}, f32[4,32,512]{2,1,0:T(8,128)S(1)}, u32[]{:S(2)}, u32[]{:S(2)}) collective-permute-start(f32[4,32,512]{2,1,0:T(8,128)S(1)} %pad_maximum_fusion), channel_id=1, source_target_pairs={{0,2},{1,3},{2,0},{3,1},{4,6},{5,7},{6,4},{7,5},{8,10},{9,11},{10,... | collective-permute-start | bytes 786440 | tf_op jit(solution)/shard_map/ppermute | solution.py:519
  116.4 1.3 copy-start.17
  116.4 3.4 %collective-permute-start.19 = (f32[8,32,512]{2,1,0:T(8,128)S(1)}, f32[8,32,512]{2,1,0:T(8,128)S(1)}, u32[]{:S(2)}, u32[]{:S(2)}) collective-permute-start(f32[8,32,512]{2,1,0:T(8,128)S(1)} %constant_dynamic-update-slice_fusion.mine_ref), channel_id=1, source_target_pairs={{0,1},{1,0},{2,3},{3,2},{4,5},{5,4},{6,7},{7,6},{8,9},{9,8},{10,11... | collective-permute-start | bytes 1572872 | tf_op jit(solution)/shard_map/ppermute | solution.py:519
  117.7 45.4 %copy-start.3 = (f32[256,256]{1,0:T(8,128)}, f32[256,256]{1,0:T(8,128)S(1)}, u32[]{:S(2)}) copy-start(f32[256,256]{1,0:T(8,128)S(1)} %fusion.15.first_ref.refs_3_) | copy-start | bytes 786436
  117.7 13.4 %collective-permute-start.18 = (f32[256,256]{1,0:T(8,128)S(1)}, f32[256,256]{1,0:T(8,128)S(1)}, u32[]{:S(2)}, u32[]{:S(2)}) collective-permute-start(f32[256,256]{1,0:T(8,128)S(1)} %fusion.15.first_ref.refs_3_), channel_id=1, source_target_pairs={{0,2},{1,3},{4,0},{5,1},{8,4},{9,5},{12,8},{13,9},{14,12},{15,13},... | collective-permute-start | bytes 786440 | tf_op jit(solution)/shard_map/ppermute | solution.py:516
  119.6 13.9 %collective-permute-start.17 = (f32[256,256]{1,0:T(8,128)S(1)}, f32[256,256]{1,0:T(8,128)S(1)}, u32[]{:S(2)}, u32[]{:S(2)}) collective-permute-start(f32[256,256]{1,0:T(8,128)S(1)} %fusion.15.first_ref.refs_3_), channel_id=1, source_target_pairs={{0,4},{1,5},{4,8},{5,9},{8,12},{9,13},{12,14},{13,15},{14,10},{15,... | collective-permute-start | bytes 786440 | tf_op jit(solution)/shard_map/ppermute | solution.py:516
  119.9 0.8 copy-start.18
  131.2 32.5 %copy-start.8 = (f32[256,256]{1,0:T(8,128)}, f32[256,256]{1,0:T(8,128)S(1)}, u32[]{:S(2)}) copy-start(f32[256,256]{1,0:T(8,128)S(1)} %collective-permute-done.18.refs_5_) | copy-start | bytes 786436
  133.5 29.9 %copy-start.9 = (f32[256,256]{1,0:T(8,128)}, f32[256,256]{1,0:T(8,128)S(1)}, u32[]{:S(2)}) copy-start(f32[256,256]{1,0:T(8,128)S(1)} %collective-permute-done.17.refs_4_) | copy-start | bytes 786436
  133.5 29.0 %collective-permute-start.20 = (f32[256,256]{1,0:T(8,128)S(1)}, f32[256,256]{1,0:T(8,128)S(1)}, u32[]{:S(2)}, u32[]{:S(2)}) collective-permute-start(f32[256,256]{1,0:T(8,128)S(1)} %collective-permute-done.17.refs_4_), channel_id=1, source_target_pairs={{0,4},{1,5},{4,8},{5,9},{8,12},{9,13},{12,14},{13,15},{14,10},{15,... | collective-permute-start | bytes 786440 | tf_op jit(solution)/shard_map/ppermute | solution.py:516
  133.8 28.8 %collective-permute-start.21 = (f32[256,256]{1,0:T(8,128)S(1)}, f32[256,256]{1,0:T(8,128)}, u32[]{:S(2)}, u32[]{:S(2)}) collective-permute-start(f32[256,256]{1,0:T(8,128)S(1)} %collective-permute-done.18.refs_5_), channel_id=1, source_target_pairs={{0,2},{1,3},{4,0},{5,1},{8,4},{9,5},{12,8},{13,9},{14,12},{15,13},... | collective-permute-start | bytes 786440 | tf_op jit(solution)/shard_map/ppermute | solution.py:516
  155.0 42.3 %collective-permute-start.35 = (f32[8,256,256]{2,1,0:T(8,128)}, f32[8,256,256]{2,1,0:T(8,128)S(1)}, u32[]{:S(2)}, u32[]{:S(2)}) collective-permute-start(f32[8,256,256]{2,1,0:T(8,128)} %bitcast.59), channel_id=1, source_target_pairs={{0,1},{1,0},{2,3},{3,2},{4,5},{5,4},{6,7},{7,6},{8,9},{9,8},{10,11... | collective-permute-start | bytes 6291464 | tf_op jit(solution)/shard_map/ppermute | solution.py:519
  162.5 1.4 copy-start.10
  162.5 8.8 %collective-permute-start.22 = (f32[256,256]{1,0:T(8,128)S(1)}, f32[256,256]{1,0:T(8,128)S(1)}, u32[]{:S(2)}, u32[]{:S(2)}) collective-permute-start(f32[256,256]{1,0:T(8,128)S(1)} %collective-permute-done.20.refs_6_), channel_id=1, source_target_pairs={{0,4},{1,5},{4,8},{5,9},{8,12},{9,13},{12,14},{13,15},{14,10},{15,... | collective-permute-start | bytes 786440 | tf_op jit(solution)/shard_map/ppermute | solution.py:516
  163.1 17.5 %collective-permute-start.26 = (f32[256,256]{1,0:T(8,128)S(1)}, f32[256,256]{1,0:T(8,128)}, u32[]{:S(2)}, u32[]{:S(2)}) collective-permute-start(f32[256,256]{1,0:T(8,128)S(1)} %fusion.15.first_ref.refs_3_), channel_id=1, source_target_pairs={{0,1},{1,0},{2,3},{3,2},{4,5},{5,4},{6,7},{7,6},{8,9},{9,8},{10,11... | collective-permute-start | bytes 786440 | tf_op jit(solution)/shard_map/ppermute | solution.py:519
  163.4 18.2 %collective-permute-start.27 = (f32[256,256]{1,0:T(8,128)S(1)}, f32[256,256]{1,0:T(8,128)}, u32[]{:S(2)}, u32[]{:S(2)}) collective-permute-start(f32[256,256]{1,0:T(8,128)S(1)} %collective-permute-done.17.refs_4_), channel_id=1, source_target_pairs={{0,1},{1,0},{2,3},{3,2},{4,5},{5,4},{6,7},{7,6},{8,9},{9,8},{10,11... | collective-permute-start | bytes 786440 | tf_op jit(solution)/shard_map/ppermute | solution.py:519
  163.6 17.9 %collective-permute-start.28 = (f32[256,256]{1,0:T(8,128)S(1)}, f32[256,256]{1,0:T(8,128)}, u32[]{:S(2)}, u32[]{:S(2)}) collective-permute-start(f32[256,256]{1,0:T(8,128)S(1)} %collective-permute-done.18.refs_5_), channel_id=1, source_target_pairs={{0,1},{1,0},{2,3},{3,2},{4,5},{5,4},{6,7},{7,6},{8,9},{9,8},{10,11... | collective-permute-start | bytes 786440 | tf_op jit(solution)/shard_map/ppermute | solution.py:519
  171.3 13.2 %copy-start.4 = (f32[256,256]{1,0:T(8,128)}, f32[256,256]{1,0:T(8,128)S(1)}, u32[]{:S(2)}) copy-start(f32[256,256]{1,0:T(8,128)S(1)} %collective-permute-done.22.refs_8_) | copy-start | bytes 786436
  171.3 8.1 %collective-permute-start.23 = (f32[256,256]{1,0:T(8,128)}, f32[256,256]{1,0:T(8,128)S(1)}, u32[]{:S(2)}, u32[]{:S(2)}) collective-permute-start(f32[256,256]{1,0:T(8,128)} %collective-permute-done.21.refs_7_), channel_id=1, source_target_pairs={{0,2},{1,3},{4,0},{5,1},{8,4},{9,5},{12,8},{13,9},{14,12},{15,13},... | collective-permute-start | bytes 786440 | tf_op jit(solution)/shard_map/ppermute | solution.py:516
  179.4 13.2 %copy-start.5 = (f32[256,256]{1,0:T(8,128)}, f32[256,256]{1,0:T(8,128)S(1)}, u32[]{:S(2)}) copy-start(f32[256,256]{1,0:T(8,128)S(1)} %collective-permute-done.23.refs_9_) | copy-start | bytes 786436
  179.5 5.0 %collective-permute-start.24 = (f32[128,256]{1,0:T(8,128)S(1)}, f32[128,256]{1,0:T(8,128)S(1)}, u32[]{:S(2)}, u32[]{:S(2)}) collective-permute-start(f32[128,256]{1,0:T(8,128)S(1)} %slice.88), channel_id=1, source_target_pairs={{0,4},{1,5},{4,8},{5,9},{8,12},{9,13},{12,14},{13,15},{14,10},{15,... | collective-permute-start | bytes 393224 | tf_op jit(solution)/shard_map/ppermute | solution.py:516
  180.7 5.1 %collective-permute-start.25 = (f32[128,256]{1,0:T(8,128)S(1)}, f32[128,256]{1,0:T(8,128)}, u32[]{:S(2)}, u32[]{:S(2)}) collective-permute-start(f32[128,256]{1,0:T(8,128)S(1)} %slice.89), channel_id=1, source_target_pairs={{0,2},{1,3},{4,0},{5,1},{8,4},{9,5},{12,8},{13,9},{14,12},{15,13},... | collective-permute-start | bytes 393224 | tf_op jit(solution)/shard_map/ppermute | solution.py:516
  181.6 11.1 %collective-permute-start.29 = (f32[256,256]{1,0:T(8,128)}, f32[256,256]{1,0:T(8,128)S(1)}, u32[]{:S(2)}, u32[]{:S(2)}) collective-permute-start(f32[256,256]{1,0:T(8,128)} %copy-done.10), channel_id=1, source_target_pairs={{0,1},{1,0},{2,3},{3,2},{4,5},{5,4},{6,7},{7,6},{8,9},{9,8},{10,11... | collective-permute-start | bytes 786440 | tf_op jit(solution)/shard_map/ppermute | solution.py:519
  181.6 11.6 %collective-permute-start.30 = (f32[256,256]{1,0:T(8,128)}, f32[256,256]{1,0:T(8,128)S(1)}, u32[]{:S(2)}, u32[]{:S(2)}) collective-permute-start(f32[256,256]{1,0:T(8,128)} %collective-permute-done.21.refs_7_), channel_id=1, source_target_pairs={{0,1},{1,0},{2,3},{3,2},{4,5},{5,4},{6,7},{7,6},{8,9},{9,8},{10,11... | collective-permute-start | bytes 786440 | tf_op jit(solution)/shard_map/ppermute | solution.py:519
  184.5 8.1 %copy-start.16 = (f32[128,256]{1,0:T(8,128)}, f32[128,256]{1,0:T(8,128)S(1)}, u32[]{:S(2)}) copy-start(f32[128,256]{1,0:T(8,128)S(1)} %collective-permute-done.24.refs_10_) | copy-start | bytes 393220
  184.5 12.8 %collective-permute-start.31 = (f32[256,256]{1,0:T(8,128)S(1)}, f32[256,256]{1,0:T(8,128)S(1)}, u32[]{:S(2)}, u32[]{:S(2)}) collective-permute-start(f32[256,256]{1,0:T(8,128)S(1)} %collective-permute-done.22.refs_8_), channel_id=1, source_target_pairs={{0,1},{1,0},{2,3},{3,2},{4,5},{5,4},{6,7},{7,6},{8,9},{9,8},{10,11... | collective-permute-start | bytes 786440 | tf_op jit(solution)/shard_map/ppermute | solution.py:519
  185.7 11.6 %collective-permute-start.32 = (f32[256,256]{1,0:T(8,128)S(1)}, f32[256,256]{1,0:T(8,128)}, u32[]{:S(2)}, u32[]{:S(2)}) collective-permute-start(f32[256,256]{1,0:T(8,128)S(1)} %collective-permute-done.23.refs_9_), channel_id=1, source_target_pairs={{0,1},{1,0},{2,3},{3,2},{4,5},{5,4},{6,7},{7,6},{8,9},{9,8},{10,11... | collective-permute-start | bytes 786440 | tf_op jit(solution)/shard_map/ppermute | solution.py:519
  192.6 4.8 %copy-start.11 = (f32[256,256]{1,0:T(8,128)}, f32[256,256]{1,0:T(8,128)S(1)}, u32[]{:S(2)}) copy-start(f32[256,256]{1,0:T(8,128)S(1)} %collective-permute-done.29.refs_15_) | copy-start | bytes 786436
  192.6 4.7 %collective-permute-start.33 = (f32[128,256]{1,0:T(8,128)S(1)}, f32[128,256]{1,0:T(8,128)}, u32[]{:S(2)}, u32[]{:S(2)}) collective-permute-start(f32[128,256]{1,0:T(8,128)S(1)} %collective-permute-done.24.refs_10_), channel_id=1, source_target_pairs={{0,1},{1,0},{2,3},{3,2},{4,5},{5,4},{6,7},{7,6},{8,9},{9,8},{10,11... | collective-permute-start | bytes 393224 | tf_op jit(solution)/shard_map/ppermute | solution.py:519
  193.2 4.2 %copy-start.12 = (f32[256,256]{1,0:T(8,128)}, f32[256,256]{1,0:T(8,128)S(1)}, u32[]{:S(2)}) copy-start(f32[256,256]{1,0:T(8,128)S(1)} %collective-permute-done.30.refs_16_) | copy-start | bytes 786436
  193.2 4.1 %collective-permute-start.34 = (f32[128,256]{1,0:T(8,128)}, f32[128,256]{1,0:T(8,128)}, u32[]{:S(2)}, u32[]{:S(2)}) collective-permute-start(f32[128,256]{1,0:T(8,128)} %collective-permute-done.25.refs_11_), channel_id=1, source_target_pairs={{0,1},{1,0},{2,3},{3,2},{4,5},{5,4},{6,7},{7,6},{8,9},{9,8},{10,11... | collective-permute-start | bytes 393224 | tf_op jit(solution)/shard_map/ppermute | solution.py:519
  197.3 0.7 copy-start.13
  197.4 1.4 copy-start
Sparse Core Ops, SparseCore 0:
  42.0 43.8 reduce-scatter.1
  116.5 38.5 all-gather.2

commit v4 on v3

--- a/solution.py
+++ b/solution.py
@@ -109,13 +109,13 @@
         work[at, to] = jnp.zeros((TILE, TILE), jnp.float32)
 
 
-def factor_first(table_ref, mine_ref, other_ref, regular_ref, out_ref):
-    count, rows = mine_ref.shape[0], mine_ref.shape[1]
+def factor_first(table_ref, regular_ref, *refs):
+    parts, out_ref = refs[:-1], refs[-1]
+    count, rows = parts[0].shape[0], parts[0].shape[1]
     place = lax.axis_index("scen")
-    for n in range(2 * count):
-        ref = mine_ref if n < count else other_ref
-        at = pl.ds(pl.multiple_of(table_ref[2 * count * place + n] * rows, rows), rows)
-        out_ref[at, :] = ref[n % count]
+    for n in range(len(parts) * count):
+        row = table_ref[len(parts) * count * place + n]
+        out_ref[pl.ds(pl.multiple_of(row * rows, rows), rows), :] = parts[n // count][n % count]
     size = out_ref.shape[0]
     row_id = lax.broadcasted_iota(jnp.int32, (TILE, TILE), 0)
     col_id = lax.broadcasted_iota(jnp.int32, (TILE, TILE), 1)
@@ -130,7 +130,7 @@
     factor_step(k, out_ref)
 
 
-def factor_stages(table, mine, other, regular):
+def factor_stages(table, parts, regular):
     size = regular.shape[0]
     settings = dict(
         out_shape=jax.ShapeDtypeStruct((size, size), jnp.float32),
@@ -141,10 +141,10 @@
     )
     first = lambda work: pl.pallas_call(
         factor_first,
-        in_specs=[pl.BlockSpec(memory_space=pltpu.SMEM)] + vmem(3),
+        in_specs=[pl.BlockSpec(memory_space=pltpu.SMEM)] + vmem(1 + len(parts)),
         name="factor_0",
         **settings,
-    )(table, mine, other, regular[None, :])
+    )(table, regular[None, :], *parts)
     return [first] + [
         pl.pallas_call(
             lambda work_ref, out_ref, k=k: factor_next(k, work_ref, out_ref),
@@ -184,23 +184,11 @@
     return (ids == cols).astype(jnp.float32).astype(jnp.bfloat16)
 
 
-def front_kernel(
-    table_ref, counts_ref, cols_ref, weights_ref, rows_ref,
-    block_ref, given_0, given_1, kept_0, kept_1,
-    pick, picked, total, sems,
-):
-    step, last = pl.program_id(0), pl.num_programs(0) - 1
-    place, parts = lax.axis_index("scen"), lax.axis_size("scen")
+def pick_kernel(counts_ref, cols_ref, weights_ref, rows_ref, scaled_ref, block_ref, pick, picked):
+    step, parts = pl.program_id(0), lax.axis_size("scen")
     order, width = pick.shape
-    owned = total.shape[2]
     depth = rows_ref.shape[0]
-    half = width // 2
     tall = order // 4
-    count = given_0.shape[0]
-    wide = 4
-
-    def entry(kind, n):
-        return table_ref[4 * count * place + kind * 2 * count + n]
 
     @pl.when(step == 0)
     def _():
@@ -222,93 +210,120 @@
     live = (slot < counts_ref[0]).astype(jnp.float32)
     factor_w = weights_ref[...] * live * (1.0 / (depth * pl.num_programs(0) * parts))
     scaled = (picked[...].T * factor_w).astype(jnp.bfloat16)
+    scaled_ref[...] = scaled
     block_ref[...] += jnp.dot(
         scaled, picked[...].astype(jnp.bfloat16), preferred_element_type=jnp.float32
     )
 
-    def stores(n, which):
-        refs = ((given_0, given_1), (kept_0, kept_1))[which]
-        for h, ref in enumerate(refs):
+
+def pick_columns(row_counts, panel_cols, row_weights, scenario_rows):
+    depth, order = scenario_rows.shape
+    width = panel_cols.shape[0]
+    tall = 512
+    whole = lambda shape: pl.BlockSpec(shape, lambda i: (0, 0))
+    return pl.pallas_call(
+        pick_kernel,
+        grid=(depth // tall,),
+        in_specs=[
+            pl.BlockSpec(memory_space=pltpu.SMEM),
+            whole((1, width)),
+            pl.BlockSpec((1, tall), lambda i: (0, i)),
+            pl.BlockSpec((tall, order), lambda i: (i, 0)),
+        ],
+        out_specs=[pl.BlockSpec((width, tall), lambda i: (0, i)), whole((width, width))],
+        out_shape=[
+            jax.ShapeDtypeStruct((width, depth), jnp.bfloat16),
+            jax.ShapeDtypeStruct((width, width), jnp.float32),
+        ],
+        scratch_shapes=[
+            pltpu.VMEM((order, width), jnp.bfloat16),
+            pltpu.VMEM((tall, width), jnp.float32),
+        ],
+        cost_estimate=pl.CostEstimate(
+            flops=3 * depth * order * width, bytes_accessed=2 * depth * order, transcendentals=0
+        ),
+        compiler_params=pltpu.CompilerParams(vmem_limit_bytes=VMEM_BYTES),
+        name="pick_columns",
+    )(row_counts, panel_cols[None, :], row_weights[None, :], scenario_rows)
+
+
+def gram_kernel(which, table_ref, scaled_ref, rows_ref, first_ref, second_ref, total, sems):
+    step, last = pl.program_id(0), pl.num_programs(0) - 1
+    count, width, owned = total.shape
+    half = width // 2
+    wide = 4
+    base = 4 * count * lax.axis_index("scen")
+
+    def stores(n):
+        for h, ref in enumerate((first_ref, second_ref)):
             yield pltpu.make_async_copy(
                 total.at[n, pl.ds(h * half, half)],
-                ref.at[entry(1, h * count + lax.rem(n, count))],
+                ref.at[table_ref[base + 2 * count + h * count + n]],
                 sems.at[n, h],
             )
 
-    def each(action):
-        for which in range(2):
-
-            @pl.loop(which * count, (which + 1) * count)
-            def _(n):
-                for store in stores(n, which):
-                    action(store)
-
-    for which in range(2):
-
-        @pl.loop(0, count // wide)
-        def _(m):
-            first = which * count + m * wide
-            columns = [
-                rows_ref[:, pl.ds(pl.multiple_of(entry(0, first + i) * owned, owned), owned)]
-                for i in range(wide)
-            ]
-            part = jnp.dot(
-                scaled, jnp.concatenate(columns, axis=1), preferred_element_type=jnp.float32
-            )
-
-            @pl.when(step == 0)
-            def _():
-                for i in range(wide):
-                    total[first + i] = part[:, i * owned : (i + 1) * owned]
-
-            @pl.when(step > 0)
-            def _():
-                for i in range(wide):
-                    total[first + i] += part[:, i * owned : (i + 1) * owned]
-
-            @pl.when(step == last)
-            def _():
-                for i in range(wide):
-                    for store in stores(first + i, which):
-                        store.start()
+    for first in range(0, count, wide):
+        columns = [
+            pl.multiple_of(table_ref[base + which * count + n] * owned, owned)
+            for n in range(first, first + wide)
+        ]
+        part = jnp.dot(
+            scaled_ref[...],
+            jnp.concatenate([rows_ref[:, pl.ds(at, owned)] for at in columns], axis=1),
+            preferred_element_type=jnp.float32,
+        )
+
+        @pl.when(step == 0)
+        def _():
+            for i in range(wide):
+                total[first + i] = part[:, i * owned : (i + 1) * owned]
+
+        @pl.when(step > 0)
+        def _():
+            for i in range(wide):
+                total[first + i] += part[:, i * owned : (i + 1) * owned]
+
+        @pl.when(step == last)
+        def _():
+            for n in range(first, first + wide):
+                for store in stores(n):
+                    store.start()
 
     @pl.when(step == last)
     def _():
-        each(lambda store: store.wait())
-
-
-def front(table, count, owned, row_counts, panel_cols, row_weights, scenario_rows):
+        for n in range(count):
+            for store in stores(n):
+                store.wait()
+
+
+def gram_blocks(which, table, count, owned, scaled, scenario_rows):
     depth, order = scenario_rows.shape
-    width = panel_cols.shape[0]
+    width = scaled.shape[0]
     half = width // 2
     tall = 512
     pieces = jax.ShapeDtypeStruct((count, half, owned), jnp.float32)
-    whole = lambda shape: pl.BlockSpec(shape, lambda i: (0, 0))
-    smem = pl.BlockSpec(memory_space=pltpu.SMEM)
     return pl.pallas_call(
-        front_kernel,
+        lambda *refs: gram_kernel(which, *refs),
         grid=(depth // tall,),
         in_specs=[
-            smem, smem, whole((1, width)),
-            pl.BlockSpec((1, tall), lambda i: (0, i)),
+            pl.BlockSpec(memory_space=pltpu.SMEM),
+            pl.BlockSpec((width, tall), lambda i: (0, i)),
             pl.BlockSpec((tall, order), lambda i: (i, 0)),
         ],
-        out_specs=[whole((width, width))] + [pl.BlockSpec(memory_space=pl.ANY)] * 4,
-        out_shape=[jax.ShapeDtypeStruct((width, width), jnp.float32)] + [pieces] * 4,
+        out_specs=[pl.BlockSpec(memory_space=pl.ANY)] * 2,
+        out_shape=[pieces] * 2,
         scratch_shapes=[
-            pltpu.VMEM((order, width), jnp.bfloat16),
-            pltpu.VMEM((tall, width), jnp.float32),
-            pltpu.VMEM((2 * count, width, owned), jnp.float32),
-            pltpu.SemaphoreType.DMA((2 * count, 2)),
+            pltpu.VMEM((count, width, owned), jnp.float32),
+            pltpu.SemaphoreType.DMA((count, 2)),
         ],
         cost_estimate=pl.CostEstimate(
-            flops=4 * depth * order * width,
-            bytes_accessed=2 * depth * order + 4 * order * width,
+            flops=depth * order * width,
+            bytes_accessed=2 * depth * order + 2 * order * width,
             transcendentals=0,
         ),
         compiler_params=pltpu.CompilerParams(vmem_limit_bytes=VMEM_BYTES),
-        name="front",
-    )(table, row_counts, panel_cols[None, :], row_weights[None, :], scenario_rows)
+        name=("gram_other", "gram_mine")[which],
+    )(table, scaled, scenario_rows)
 
 
 def prior_kernel(cols_ref, prior_ref, gram_ref, local_0, local_1, given_ref, kept_ref, picked):
@@ -487,8 +502,8 @@
         where = [(at + offset) % chips for offset in back]
         updates += [2 * ring[q] + c for c in (core, 1 - core) for q in where] + where
         factors += [
-            (2 * c + w) * lines + (z ^ by)
-            for c in (core, 1 - core) for w in (y, 1 - y) for by in (0, 2, 1, 3)
+            (2 * c + w) * lines + (z - by) % lines
+            for c in (core, 1 - core) for w in (y, 1 - y) for by in range(lines)
         ]
     return [jnp.array(table, jnp.int32) for table in (fronts, updates, factors)]
 
@@ -523,26 +538,25 @@
 
     together = lax.optimization_barrier
 
-    gram, given_0, given_1, kept_0, kept_1 = front(
-        front_table, chips, prior_schur.shape[0], row_counts, panel_cols, row_weights, scenario_rows
-    )
-
-    got_1 = swap(given_1, 1)
-    got_1, given_0 = together((got_1, given_0))
+    def shift(values, by):
+        return lax.ppermute(values, "scen", [(d, (d + 4 * by) % parts) for d in range(parts)])
+
+    scaled, gram = pick_columns(row_counts, panel_cols, row_weights, scenario_rows)
+    local_0, local_1, block_given, block_kept = prior_parts(panel_cols, prior_schur, gram)
+    owned = prior_schur.shape[0]
+    block_given, block_kept, scaled = together((block_given, block_kept, scaled))
+    block_got = swap(block_given, 1)
+    given_0, given_1 = gram_blocks(0, front_table, chips, owned, scaled, scenario_rows)
+    block_got, given_0, given_1 = together((block_got, given_0, given_1))
+    block = (block_kept + block_got).reshape(2, lines, -1, 2 * half)
+    beside, given_0, given_1, scaled = together((slab(block, 1 - y), given_0, given_1, scaled))
+    beside, got_1, got_0 = swap(beside, 2), swap(given_1, 1), swap(given_0, 1)
+    kept_0, kept_1 = gram_blocks(1, front_table, chips, owned, scaled, scenario_rows)
+    beside, got_0, got_1, kept_0, kept_1 = together((beside, got_0, got_1, kept_0, kept_1))
+
     summed = lax.psum_scatter(
         kept_1 + got_1, "scen", scatter_dimension=0, axis_index_groups=groups
     )
-    got_0 = swap(given_0, 1)
-
-    local_0, local_1, block_given, block_kept = prior_parts(panel_cols, prior_schur, gram)
-    block = (block_kept + swap(block_given, 1)).reshape(2, lines, -1, 2 * half)
-    block = slab(block, y) + swap(slab(block, 1 - y), 2)
-    low, high = z % 2, z // 2
-    block = block.reshape(2, 2, -1, 2 * half)
-    pairs = lax.dynamic_index_in_dim(block, low, 1, keepdims=False)
-    pairs = pairs + swap(lax.dynamic_index_in_dim(block, 1 - low, 1, keepdims=False), 4)
-    moves = [8, 8, 4, 2]
-    beside = slab(pairs, 1 - high)
 
     sides = {1: slice(0, half // 2), -1: slice(half // 2, half)}
 
@@ -550,6 +564,8 @@
         n = offsets.index(offset)
         return kept_0[n] + got_0[n]
 
+    block = slab(block, y) + beside
+    beside = [slab(block, (z + by) % lines) for by in range(1, lines)]
     arrived = None
     for d in range(far, 0, -1):
         if d == far:
@@ -557,40 +573,47 @@
         else:
             ahead = [partial(way * d) + arrived[n] for n, way in enumerate((1, -1))]
         ahead, beside = together((ahead, beside))
-        moved = swap(beside, moves[far - d])
-        arrived, moved = together(([step(ahead[0], 1), step(ahead[1], -1)], moved))
+        arrived = [step(ahead[0], 1), step(ahead[1], -1)]
+        if d == far:
+            beside = [shift(beside[by - 1], by) for by in range(1, lines)]
+        elif d == far - 1:
+            beside = [beside] + [shift(beside, by) for by in range(1, lines)]
+        elif d == far - 2:
+            beside = [beside] + [swap(beside, bit) for bit in (2, 1, 3)]
+        else:
+            beside = stages[0](None)
+        arrived, beside = together((arrived, beside))
         if d == far:
             arrived = [
                 jnp.pad(arrived[0], ((0, half // 2), (0, 0))),
                 jnp.pad(arrived[1], ((half // 2, 0), (0, 0))),
             ]
-            beside = (slab(pairs, high) + moved)[None]
-        else:
-            beside = jnp.concatenate([beside, moved])
-    arrived, summed = together((arrived, summed))
+            beside = sum(beside) + slab(block, z)
+        elif d == far - 1:
+            beside = jnp.stack(beside)
+        elif d == far - 2:
+            stages = factor_stages(factor_table, beside, regular)
+    work = beside
+    arrived, summed, work = together((arrived, summed, work))
     panel_0 = partial(0) + arrived[0] + arrived[1] + local_0
     panel_1 = summed + local_1
-    stages = factor_stages(factor_table, beside, swap(beside, 1), regular)
 
     second = lax.all_gather(panel_1, "scen", axis_index_groups=groups)
     first = [panel_0]
     ahead = [panel_0, panel_0]
-    work = None
     for d in range(1, far + 1):
         if d == far:
             ahead = [ahead[n][sides[way]] for n, way in enumerate((1, -1))]
-        if d > 1:
-            ahead, work = together((ahead, work))
-        ahead, work = together(
-            ([step(ahead[0], 1), step(ahead[1], -1)], stages[d - 1](work))
-        )
+        ahead, work = together((ahead, work))
+        ahead = [step(ahead[0], 1), step(ahead[1], -1)]
+        work = stages[d](work) if d < len(stages) else solve_rows(work, panel_0, panel_1)
+        ahead, work = together((ahead, work))
         first += ahead
-    inverse = work
-    for stage in stages[far:]:
-        inverse = stage(inverse)
+    ahead, second = together((ahead, second))
+    first[-2:] = ahead
     sources = first + [swap(piece, 1) for piece in first] + [second, swap(second, 1)]
 
-    factor_rows, weights = solve_rows(inverse, panel_0, panel_1)
+    factor_rows, weights = work
     return update_rows(update_table, parts, weights, prior_schur, sources), factor_rows
 
 
@@ -624,7 +647,7 @@
     panel_rest = swap_cores(panel_half)
     table = jnp.array([c ^ (d % 2) for d in range(parts) for c in range(2)], jnp.int32)
     inverse = None
-    for stage in factor_stages(table, block, block_other, regular):
+    for stage in factor_stages(table, [block, block_other], regular):
         inverse = stage(inverse)
     factor_rows, weights = solve_rows(inverse, panel_rows.T[:half], panel_rows.T[half:])
     even = jnp.where(core == 0, panel_half, panel_rest)

time: 218 us -> 198 us (0.908)
  waiting for transfers between devices: 91.5 us -> 53.8 us
  starting transfers between devices: 25 us -> 37.1 us
  Pallas kernels: 72.2 us -> 79 us
    ppermute x20 -> x17, waiting for transfers between devices: 50.3 us -> 13.7 us  [swap(): return lax.ppermute(values, 'scen', [(d, d ^ bit) for d in range(parts)])]
    ppermute x0 -> x6, waiting for transfers between devices: none -> 25.6 us  [shift(): lax.ppermute(values, 'scen', [(d, (d + 4 * by) % parts) for d in range(pa...]
    all_gather x1, waiting for transfers between devices: 19.5 us -> 0.02 us  [shards_on_ring(): second = lax.all_gather(panel_1, 'scen', axis_index_groups=groups)]
    ppermute x0 -> x6, starting transfers between devices: none -> 10.1 us  [shift(): lax.ppermute(values, 'scen', [(d, (d + 4 * by) % parts) for d in range(pa...]
    ppermute x16, waiting for transfers between devices: 21.6 us -> 14.5 us  [step(): return lax.ppermute(values, 'scen', pairs)]
    pallas_call x4 -> x6, Pallas kernels: 41.5 us -> 48.4 us  [the longest x3 21.6 us: shards_on_ring(): stages[d](work)]
    ppermute x16, starting transfers between devices: 16 us -> 18.4 us  [step(): return lax.ppermute(values, 'scen', pairs)]
    ppermute x20 -> x17, starting transfers between devices: 8.92 us -> 8.5 us  [swap(): return lax.ppermute(values, 'scen', [(d, d ^ bit) for d in range(parts)])]
  transfers between devices with their start and end apart: 38 -> 41, of which waited for: 16 -> 18; matrix products, arithmetic and copies ran while one was open for 4% -> 2% of each run, Pallas kernels for 19% -> 25%
where the time goes in v4:
time: 198 us
  Pallas kernels  79 us (40%)
  waiting for transfers between devices  53.8 us (27%)
  starting transfers between devices  37.1 us (19%)
  between operations  15.2 us (8%)
  other arithmetic  9.11 us (5%)
  local copies, waits for them, and re-layouts  3.41 us (2%)
    ppermute x6, waiting for transfers between devices, shift(): lax.ppermute(values, 'scen', [(d, (d + 4 * by) % parts) for d in range(pa...  25.6 us
    pallas_call x3, Pallas kernels, shards_on_ring(): stages[d](work)  21.6 us
    ppermute x16, starting transfers between devices, step(): return lax.ppermute(values, 'scen', pairs)  18.4 us
    pallas_call x2, Pallas kernels, gram_blocks(): pl.pallas_call(lambda *refs: gram_kernel(which, *refs), grid=(depth // ta...  15.7 us
    ppermute x16, waiting for transfers between devices, step(): return lax.ppermute(values, 'scen', pairs)  14.5 us
    ppermute x17, waiting for transfers between devices, swap(): return lax.ppermute(values, 'scen', [(d, d ^ bit) for d in range(parts)])  13.7 us
    pallas_call x1, Pallas kernels, update_rows(): pl.pallas_call(lambda *refs: update_kernel(count, *refs), out_shape=jax.S...  11.6 us
    pallas_call x1, Pallas kernels, pick_columns(): pl.pallas_call(pick_kernel, grid=(depth // tall,), in_specs=[pl.BlockSpec...  11 us
  transfers between devices with their start and end apart: 41, of which 18 were waited for; matrix products, arithmetic and copies ran while one was open for 2% of the time, Pallas kernels for 25%

profile of v4, /device:TPU:0, one launch (start us, length us, event | category | flops | bytes accessed | tf_op | source)
XLA Modules:
  0.0 197.6 jit_solution(12391492922303939865)
XLA Ops:
  7.9 11.0 %pick_columns.1 = (bf16[512,1024]{1,0:T(8,128)(2,1)}, f32[512,512]{1,0:T(8,128)}) custom-call(s32[1]{0:T(128)S(6)} %copy.11.counts_ref, s32[1,512]{1,0:T(1,128)} %bitcast.54, f32[1,1024]{1,0:T(1,128)} %bitcast.53, bf16[1024,4096]{1,0:T(8,128)(2,1)} %refs_2_.4), custom_call_target="tpu_custom_call" | custom-call | flops 6442450944 | bytes 8388608 | tf_op jit(solution)/shard_map/pick_columns/pallas_call | solution.py:224
  18.9 7.2 %prior_parts.1 = (f32[256,256]{1,0:T(8,128)}, f32[256,256]{1,0:T(8,128)}, f32[256,512]{1,0:T(8,128)}, f32[256,512]{1,0:T(8,128)}) custom-call(s32[1,512]{1,0:T(1,128)} %bitcast.55, f32[256,4096]{1,0:T(8,128)} %refs_2_.5, f32[512,512]{1,0:T(8,128)} %get-tuple-element.92.gram_ref), custom_call_target="tpu_custom_call" | custom-call | flops 2147483648 | bytes 4194304 | tf_op jit(solution)/shard_map/prior_parts/pallas_call | solution.py:363
  26.1 0.4 collective-permute-start
  26.5 7.9 %gram_other.1 = (f32[8,256,256]{2,1,0:T(8,128)}, f32[8,256,256]{2,1,0:T(8,128)}) custom-call(s32[512]{0:T(512)} %constant.82.clone.refs_0_, bf16[512,1024]{1,0:T(8,128)(2,1)} %get-tuple-element.107.refs_1_, bf16[1024,4096]{1,0:T(8,128)(2,1)} %refs_2_.4), custom_call_target="tpu_custom_call" | custom-call | flops 2147483648 | bytes 12582912 | tf_op jit(solution)/shard_map/gram_other/pallas_call | solution.py:305
  34.7 1.3 copy-done.25
  36.0 3.0 %collective-permute-start.1 = (f32[4,32,512]{2,1,0:T(8,128)S(1)}, f32[4,32,512]{2,1,0:T(8,128)S(1)}, u32[]{:S(2)}, u32[]{:S(2)}) collective-permute-start(f32[4,32,512]{2,1,0:T(8,128)S(1)} %dynamic-slice_bitcast_fusion), channel_id=1, source_target_pairs={{0,2},{1,3},{2,0},{3,1},{4,6},{5,7},{6,4},{7,5},{8,10},{9,11},{10,... | collective-permute-start | bytes 786440 | tf_op jit(solution)/shard_map/ppermute | solution.py:534
  39.0 7.9 %gram_mine.1 = (f32[8,256,256]{2,1,0:T(8,128)}, f32[8,256,256]{2,1,0:T(8,128)}) custom-call(s32[512]{0:T(512)} %constant.82.clone.refs_0_, bf16[512,1024]{1,0:T(8,128)(2,1)} %get-tuple-element.107.refs_1_, bf16[1024,4096]{1,0:T(8,128)(2,1)} %refs_2_.4), custom_call_target="tpu_custom_call" | custom-call | flops 2147483648 | bytes 12582912 | tf_op jit(solution)/shard_map/gram_mine/pallas_call | solution.py:305
  46.9 3.2 %add.185 = f32[8,256,256]{2,1,0:T(8,128)} add(f32[8,256,256]{2,1,0:T(8,128)} %get-tuple-element.145, f32[8,256,256]{2,1,0:T(8,128)S(1)} %collective-permute-done.3) | non-fusion elementwise | flops 524288 | bytes 6291456 | tf_op jit(solution)/shard_map/add | solution.py:558
  50.3 1.0 slice_add_fusion
  51.3 1.6 collective-permute-start.4
  53.0 0.4 collective-permute-start.5
  53.4 1.6 collective-permute-start.6
  55.0 2.5 %collective-permute-start.7 = (f32[32,512]{1,0:T(8,128)S(1)}, f32[32,512]{1,0:T(8,128)S(1)}, u32[]{:S(2)}, u32[]{:S(2)}) collective-permute-start(f32[32,512]{1,0:T(8,128)S(1)} %get-tuple-element.116), channel_id=1, source_target_pairs={{0,8},{1,9},{2,10},{3,11},{4,12},{5,13},{6,14},{7,15},{8,0},{9,1},... | collective-permute-start | bytes 196616 | tf_op jit(solution)/shard_map/ppermute | solution.py:542
  57.5 1.4 collective-permute-start.8
  58.9 6.0 %collective-permute-done.6 = f32[32,512]{1,0:T(8,128)S(1)} collective-permute-done((f32[32,512]{1,0:T(8,128)S(1)}, f32[32,512]{1,0:T(8,128)S(1)}, u32[]{:S(2)}, u32[]{:S(2)}) %collective-permute-start.6) | collective-permute-done | bytes 65568 | tf_op jit(solution)/shard_map/ppermute | solution.py:542
  64.9 1.3 collective-permute-done.7
  66.2 1.1 bitcast_add_fusion.2
  67.3 3.0 %collective-permute-start.9 = (f32[256,256]{1,0:T(8,128)S(1)}, f32[256,256]{1,0:T(8,128)S(1)}, u32[]{:S(2)}, u32[]{:S(2)}) collective-permute-start(f32[256,256]{1,0:T(8,128)S(1)} %get-tuple-element.123), channel_id=1, source_target_pairs={{0,4},{1,5},{4,8},{5,9},{8,12},{9,13},{12,14},{13,15},{14,10},{15,... | collective-permute-start | bytes 786440 | tf_op jit(solution)/shard_map/ppermute | solution.py:531
  70.3 2.1 %collective-permute-start.13 = (f32[32,512]{1,0:T(8,128)S(1)}, f32[32,512]{1,0:T(8,128)S(1)}, u32[]{:S(2)}, u32[]{:S(2)}) collective-permute-start(f32[32,512]{1,0:T(8,128)S(1)} %bitcast_add_fusion.8), channel_id=1, source_target_pairs={{0,12},{1,13},{2,14},{3,15},{4,0},{5,1},{6,2},{7,3},{8,4},{9,5},{1... | collective-permute-start | bytes 196616 | tf_op jit(solution)/shard_map/ppermute | solution.py:542
  72.4 1.4 collective-permute-start.12
  73.8 1.1 collective-permute-start.11
  74.9 10.3 %collective-permute-done.13 = f32[32,512]{1,0:T(8,128)S(1)} collective-permute-done((f32[32,512]{1,0:T(8,128)S(1)}, f32[32,512]{1,0:T(8,128)S(1)}, u32[]{:S(2)}, u32[]{:S(2)}) %collective-permute-start.13) | collective-permute-done | bytes 65568 | tf_op jit(solution)/shard_map/ppermute | solution.py:542
  85.2 8.0 %collective-permute-done.12 = f32[32,512]{1,0:T(8,128)S(1)} collective-permute-done((f32[32,512]{1,0:T(8,128)S(1)}, f32[32,512]{1,0:T(8,128)S(1)}, u32[]{:S(2)}, u32[]{:S(2)}) %collective-permute-start.12) | collective-permute-done | bytes 65568 | tf_op jit(solution)/shard_map/ppermute | solution.py:542
  93.4 2.0 %collective-permute-start.15 = (f32[256,256]{1,0:T(8,128)S(1)}, f32[256,256]{1,0:T(8,128)S(1)}, u32[]{:S(2)}, u32[]{:S(2)}) collective-permute-start(f32[256,256]{1,0:T(8,128)S(1)} %get-tuple-element.133), channel_id=1, source_target_pairs={{0,2},{1,3},{4,0},{5,1},{8,4},{9,5},{12,8},{13,9},{14,12},{15,13},... | collective-permute-start | bytes 786440 | tf_op jit(solution)/shard_map/ppermute | solution.py:531
  95.4 0.1 collective-permute-start.17
  95.6 2.0 %collective-permute-start.16 = (f32[4,32,512]{2,1,0:T(8,128)S(1)}, f32[4,32,512]{2,1,0:T(8,128)}, u32[]{:S(2)}, u32[]{:S(2)}) collective-permute-start(f32[4,32,512]{2,1,0:T(8,128)S(1)} %pad_maximum_fusion.refs_0_), channel_id=1, source_target_pairs={{0,2},{1,3},{2,0},{3,1},{4,6},{5,7},{6,4},{7,5},{8,10},{9,11},{10,... | collective-permute-start | bytes 786440 | tf_op jit(solution)/shard_map/ppermute | solution.py:534
  97.6 3.5 %collective-permute-done.14 = f32[256,256]{1,0:T(8,128)S(1)} collective-permute-done((f32[256,256]{1,0:T(8,128)S(1)}, f32[256,256]{1,0:T(8,128)S(1)}, u32[]{:S(2)}, u32[]{:S(2)}) %collective-permute-start.14) | collective-permute-done | bytes 262176 | tf_op jit(solution)/shard_map/ppermute | solution.py:531
  101.1 1.0 collective-permute-done.15
  102.1 5.1 %collective-permute-done.18.refs_3_ = f32[4,32,512]{2,1,0:T(8,128)S(1)} collective-permute-done((f32[4,32,512]{2,1,0:T(8,128)S(1)}, f32[4,32,512]{2,1,0:T(8,128)S(1)}, u32[]{:S(2)}, u32[]{:S(2)}) %collective-permute-start.18) | collective-permute-done | bytes 262176 | tf_op jit(solution)/shard_map/ppermute | solution.py:534
  107.2 3.9 %collective-permute-done.16.refs_1_ = f32[4,32,512]{2,1,0:T(8,128)} collective-permute-done((f32[4,32,512]{2,1,0:T(8,128)S(1)}, f32[4,32,512]{2,1,0:T(8,128)}, u32[]{:S(2)}, u32[]{:S(2)}) %collective-permute-start.16) | collective-permute-done | bytes 262176 | tf_op jit(solution)/shard_map/ppermute | solution.py:534
  111.1 0.8 bitcast_add_fusion
  112.0 2.0 %collective-permute-start.20 = (f32[256,256]{1,0:T(8,128)S(1)}, f32[256,256]{1,0:T(8,128)S(1)}, u32[]{:S(2)}, u32[]{:S(2)}) collective-permute-start(f32[256,256]{1,0:T(8,128)S(1)} %get-tuple-element.142), channel_id=1, source_target_pairs={{0,2},{1,3},{4,0},{5,1},{8,4},{9,5},{12,8},{13,9},{14,12},{15,13},... | collective-permute-start | bytes 786440 | tf_op jit(solution)/shard_map/ppermute | solution.py:531
  114.0 7.9 %factor_0.1.work_ref = f32[512,512]{1,0:T(8,128)} custom-call(s32[256]{0:T(256)} %constant.84.clone.table_ref, f32[1,512]{1,0:T(1,128)} %bitcast.56, f32[4,32,512]{2,1,0:T(8,128)} %copy-done.19, f32[4,32,512]{2,1,0:T(8,128)} %collective-permute-done.16.refs_1_, f32[4,32,512]{2,1,0:T(8,128)} %copy-done.27, f32[4,32,512]{2,1,0:T(8,128)} %copy-done.26), custom_call_target="tpu_custom_call" | custom-call | flops 6710886400 | bytes 2097152 | tf_op jit(solution)/shard_map/factor_0/pallas_call | solution.py:142
  121.9 1.7 add.189.second_ref
  123.6 1.0 fusion.1.first_ref.refs_3_
  124.8 2.0 %collective-permute-start.22 = (f32[256,256]{1,0:T(8,128)S(1)}, f32[256,256]{1,0:T(8,128)S(1)}, u32[]{:S(2)}, u32[]{:S(2)}) collective-permute-start(f32[256,256]{1,0:T(8,128)S(1)} %fusion.1.first_ref.refs_3_), channel_id=1, source_target_pairs={{0,2},{1,3},{4,0},{5,1},{8,4},{9,5},{12,8},{13,9},{14,12},{15,13},... | collective-permute-start | bytes 786440 | tf_op jit(solution)/shard_map/ppermute | solution.py:531
  126.8 7.5 %factor_1.1.work_ref = f32[512,512]{1,0:T(8,128)} custom-call(f32[512,512]{1,0:T(8,128)} %factor_0.1.work_ref), custom_call_target="tpu_custom_call" | custom-call | flops 6710886400 | bytes 2097152 | tf_op jit(solution)/shard_map/factor_1/pallas_call | solution.py:609
  134.3 2.5 %collective-permute-done.22.refs_5_ = f32[256,256]{1,0:T(8,128)S(1)} collective-permute-done((f32[256,256]{1,0:T(8,128)S(1)}, f32[256,256]{1,0:T(8,128)S(1)}, u32[]{:S(2)}, u32[]{:S(2)}) %collective-permute-start.22) | collective-permute-done | bytes 262176 | tf_op jit(solution)/shard_map/ppermute | solution.py:531
  136.7 2.5 %collective-permute-start.24 = (f32[256,256]{1,0:T(8,128)S(1)}, f32[256,256]{1,0:T(8,128)S(1)}, u32[]{:S(2)}, u32[]{:S(2)}) collective-permute-start(f32[256,256]{1,0:T(8,128)S(1)} %collective-permute-done.22.refs_5_), channel_id=1, source_target_pairs={{0,2},{1,3},{4,0},{5,1},{8,4},{9,5},{12,8},{13,9},{14,12},{15,13},... | collective-permute-start | bytes 786440 | tf_op jit(solution)/shard_map/ppermute | solution.py:531
  139.2 7.3 %factor_2.1.work_ref = f32[512,512]{1,0:T(8,128)} custom-call(f32[512,512]{1,0:T(8,128)} %factor_1.1.work_ref), custom_call_target="tpu_custom_call" | custom-call | flops 6710886400 | bytes 2097152 | tf_op jit(solution)/shard_map/factor_2/pallas_call | solution.py:609
  146.5 3.9 %collective-permute-done.23.refs_6_ = f32[256,256]{1,0:T(8,128)S(1)} collective-permute-done((f32[256,256]{1,0:T(8,128)S(1)}, f32[256,256]{1,0:T(8,128)S(1)}, u32[]{:S(2)}, u32[]{:S(2)}) %collective-permute-start.23) | collective-permute-done | bytes 262176 | tf_op jit(solution)/shard_map/ppermute | solution.py:531
  150.4 0.2 collective-permute-done.24.refs_7_
  150.6 2.5 %collective-permute-start.26 = (f32[256,256]{1,0:T(8,128)S(1)}, f32[256,256]{1,0:T(8,128)S(1)}, u32[]{:S(2)}, u32[]{:S(2)}) collective-permute-start(f32[256,256]{1,0:T(8,128)S(1)} %collective-permute-done.24.refs_7_), channel_id=1, source_target_pairs={{0,2},{1,3},{4,0},{5,1},{8,4},{9,5},{12,8},{13,9},{14,12},{15,13},... | collective-permute-start | bytes 786440 | tf_op jit(solution)/shard_map/ppermute | solution.py:531
  153.0 6.9 %factor_3.1.inverse_ref = f32[512,512]{1,0:T(8,128)} custom-call(f32[512,512]{1,0:T(8,128)} %factor_2.1.work_ref), custom_call_target="tpu_custom_call" | custom-call | flops 6710886400 | bytes 2097152 | tf_op jit(solution)/shard_map/factor_3/pallas_call | solution.py:609
  159.9 3.5 %collective-permute-done.25.refs_8_ = f32[256,256]{1,0:T(8,128)S(1)} collective-permute-done((f32[256,256]{1,0:T(8,128)S(1)}, f32[256,256]{1,0:T(8,128)S(1)}, u32[]{:S(2)}, u32[]{:S(2)}) %collective-permute-start.25) | collective-permute-done | bytes 262176 | tf_op jit(solution)/shard_map/ppermute | solution.py:531
  163.4 0.4 collective-permute-start.27
  163.9 1.8 collective-permute-start.28
  165.6 4.0 %solve_rows.1 = (f32[256,512]{1,0:T(8,128)}, f32[256,512]{1,0:T(8,128)}) custom-call(f32[512,512]{1,0:T(8,128)} %factor_3.1.inverse_ref, f32[256,256]{1,0:T(8,128)} %copy-done.2, f32[256,256]{1,0:T(8,128)} %add.189.second_ref), custom_call_target="tpu_custom_call" | custom-call | flops 805306368 | bytes 2097152 | tf_op jit(solution)/shard_map/solve_rows/pallas_call | solution.py:170
  169.8 0.5 collective-permute-start.29
  170.4 0.4 collective-permute-start.31
  170.9 3.0 %collective-permute-done.29.refs_12_ = f32[256,256]{1,0:T(8,128)S(1)} collective-permute-done((f32[256,256]{1,0:T(8,128)S(1)}, f32[256,256]{1,0:T(8,128)S(1)}, u32[]{:S(2)}, u32[]{:S(2)}) %collective-permute-start.29) | collective-permute-done | bytes 262176 | tf_op jit(solution)/shard_map/ppermute | solution.py:534
  174.0 0.4 collective-permute-start.33
  174.3 0.4 collective-permute-start.34
  174.7 0.4 collective-permute-start.35
  175.1 0.4 collective-permute-start.36
  175.5 0.4 collective-permute-done.33.refs_16_
  175.8 0.1 collective-permute-start.37
  176.0 0.2 collective-permute-done.34.refs_17_
  176.2 0.4 collective-permute-done.35.refs_18_
  176.6 0.2 collective-permute-done.36.refs_19_
  176.8 0.4 collective-permute-done.37.refs_20_
  177.4 0.4 copy-done.24
  177.8 1.4 copy-done
  179.2 11.6 %update_rows.1 = f32[256,4096]{1,0:T(8,128)} custom-call(s32[384]{0:T(512)} %constant.83.clone.refs_0_, f32[256,512]{1,0:T(8,128)} %get-tuple-element.171.refs_1_, f32[256,4096]{1,0:T(8,128)} %refs_2_.5, f32[256,256]{1,0:T(8,128)} %copy-done.2, f32[256,256]{1,0:T(8,128)} %copy-done.7, f32[256,256]{1,0:T(8,128)} %copy-done.8, f32[256,256]{1,0:T(8,128)} %copy-done.9, ...), custom_call_target="tpu_custom_call" | custom-call | flops 3221225472 | bytes 16777216 | tf_op jit(solution)/shard_map/update_rows/pallas_call | solution.py:428
  (102 shorter events, 1.3 us)
Async XLA Ops:
  7.2 114.7 %reduce-scatter.2.cloned.1.call-start = ((), (), s32[]{:S(2)}) async-start(), calls=%async_computation.1 | async-start | bytes 2359296 | tf_op jit(solution)/shard_map/reduce_scatter | solution.py:557
  26.1 8.3 %collective-permute-start = (f32[256,512]{1,0:T(8,128)}, f32[256,512]{1,0:T(8,128)S(1)}, u32[]{:S(2)}, u32[]{:S(2)}) collective-permute-start(f32[256,512]{1,0:T(8,128)} %get-tuple-element.97), channel_id=1, source_target_pairs={{0,1},{1,0},{2,3},{3,2},{4,5},{5,4},{6,7},{7,6},{8,9},{9,8},{10,11... | collective-permute-start | bytes 1572872 | tf_op jit(solution)/shard_map/ppermute | solution.py:534
  26.5 7.9 %copy-start.6 = (f32[256,512]{1,0:T(8,128)S(1)}, f32[256,512]{1,0:T(8,128)}, u32[]{:S(2)}) copy-start(f32[256,512]{1,0:T(8,128)} %get-tuple-element.96) | copy-start | bytes 1572868
  34.4 1.6 copy-start.25
  34.5 12.3 %collective-permute-start.2 = (f32[8,256,256]{2,1,0:T(8,128)}, f32[8,256,256]{2,1,0:T(8,128)S(1)}, u32[]{:S(2)}, u32[]{:S(2)}) collective-permute-start(f32[8,256,256]{2,1,0:T(8,128)} %get-tuple-element.105), channel_id=1, source_target_pairs={{0,1},{1,0},{2,3},{3,2},{4,5},{5,4},{6,7},{7,6},{8,9},{9,8},{10,11... | collective-permute-start | bytes 6291464 | tf_op jit(solution)/shard_map/ppermute | solution.py:534
  36.0 10.9 %collective-permute-start.3 = (f32[8,256,256]{2,1,0:T(8,128)S(1)}, f32[8,256,256]{2,1,0:T(8,128)S(1)}, u32[]{:S(2)}, u32[]{:S(2)}) collective-permute-start(f32[8,256,256]{2,1,0:T(8,128)S(1)} %copy-done.25), channel_id=1, source_target_pairs={{0,1},{1,0},{2,3},{3,2},{4,5},{5,4},{6,7},{7,6},{8,9},{9,8},{10,11... | collective-permute-start | bytes 6291464 | tf_op jit(solution)/shard_map/ppermute | solution.py:534
  36.0 10.8 %collective-permute-start.1 = (f32[4,32,512]{2,1,0:T(8,128)S(1)}, f32[4,32,512]{2,1,0:T(8,128)S(1)}, u32[]{:S(2)}, u32[]{:S(2)}) collective-permute-start(f32[4,32,512]{2,1,0:T(8,128)S(1)} %dynamic-slice_bitcast_fusion), channel_id=1, source_target_pairs={{0,2},{1,3},{2,0},{3,1},{4,6},{5,7},{6,4},{7,5},{8,10},{9,11},{10,... | collective-permute-start | bytes 786440 | tf_op jit(solution)/shard_map/ppermute | solution.py:534
  50.1 119.6 %all-gather.3.cloned.1.call-start = ((), (), s32[]{:S(2)}) async-start(), calls=%async_computation.2 | async-start | bytes 2359296 | tf_op jit(solution)/shard_map/all_gather | solution.py:601
  51.3 14.9 %collective-permute-start.4 = (f32[128,256]{1,0:T(8,128)S(1)}, f32[128,256]{1,0:T(8,128)S(1)}, u32[]{:S(2)}, u32[]{:S(2)}) collective-permute-start(f32[128,256]{1,0:T(8,128)S(1)} %get-tuple-element.113), channel_id=1, source_target_pairs={{0,4},{1,5},{4,8},{5,9},{8,12},{9,13},{12,14},{13,15},{14,10},{15,... | collective-permute-start | bytes 393224 | tf_op jit(solution)/shard_map/ppermute | solution.py:531
  53.0 13.2 %collective-permute-start.5 = (f32[128,256]{1,0:T(8,128)S(1)}, f32[128,256]{1,0:T(8,128)S(1)}, u32[]{:S(2)}, u32[]{:S(2)}) collective-permute-start(f32[128,256]{1,0:T(8,128)S(1)} %get-tuple-element.114), channel_id=1, source_target_pairs={{0,2},{1,3},{4,0},{5,1},{8,4},{9,5},{12,8},{13,9},{14,12},{15,13},... | collective-permute-start | bytes 393224 | tf_op jit(solution)/shard_map/ppermute | solution.py:531
  53.4 11.5 %collective-permute-start.6 = (f32[32,512]{1,0:T(8,128)S(1)}, f32[32,512]{1,0:T(8,128)S(1)}, u32[]{:S(2)}, u32[]{:S(2)}) collective-permute-start(f32[32,512]{1,0:T(8,128)S(1)} %get-tuple-element.115), channel_id=1, source_target_pairs={{0,4},{1,5},{2,6},{3,7},{4,8},{5,9},{6,10},{7,11},{8,12},{9,13},{1... | collective-permute-start | bytes 196616 | tf_op jit(solution)/shard_map/ppermute | solution.py:542
  55.0 11.2 %collective-permute-start.7 = (f32[32,512]{1,0:T(8,128)S(1)}, f32[32,512]{1,0:T(8,128)S(1)}, u32[]{:S(2)}, u32[]{:S(2)}) collective-permute-start(f32[32,512]{1,0:T(8,128)S(1)} %get-tuple-element.116), channel_id=1, source_target_pairs={{0,8},{1,9},{2,10},{3,11},{4,12},{5,13},{6,14},{7,15},{8,0},{9,1},... | collective-permute-start | bytes 196616 | tf_op jit(solution)/shard_map/ppermute | solution.py:542
  57.5 8.7 %collective-permute-start.8 = (f32[32,512]{1,0:T(8,128)S(1)}, f32[32,512]{1,0:T(8,128)S(1)}, u32[]{:S(2)}, u32[]{:S(2)}) collective-permute-start(f32[32,512]{1,0:T(8,128)S(1)} %get-tuple-element.117), channel_id=1, source_target_pairs={{0,12},{1,13},{2,14},{3,15},{4,0},{5,1},{6,2},{7,3},{8,4},{9,5},{1... | collective-permute-start | bytes 196616 | tf_op jit(solution)/shard_map/ppermute | solution.py:542
  58.9 34.4 %copy-start.1 = (f32[8,256,256]{2,1,0:T(8,128)S(1)}, f32[8,256,256]{2,1,0:T(8,128)}, u32[]{:S(2)}) copy-start(f32[8,256,256]{2,1,0:T(8,128)} %get-tuple-element.110) | copy-start | bytes 6291460
  67.3 25.9 %collective-permute-start.9 = (f32[256,256]{1,0:T(8,128)S(1)}, f32[256,256]{1,0:T(8,128)S(1)}, u32[]{:S(2)}, u32[]{:S(2)}) collective-permute-start(f32[256,256]{1,0:T(8,128)S(1)} %get-tuple-element.123), channel_id=1, source_target_pairs={{0,4},{1,5},{4,8},{5,9},{8,12},{9,13},{12,14},{13,15},{14,10},{15,... | collective-permute-start | bytes 786440 | tf_op jit(solution)/shard_map/ppermute | solution.py:531
  70.3 22.9 %collective-permute-start.10 = (f32[256,256]{1,0:T(8,128)S(1)}, f32[256,256]{1,0:T(8,128)S(1)}, u32[]{:S(2)}, u32[]{:S(2)}) collective-permute-start(f32[256,256]{1,0:T(8,128)S(1)} %get-tuple-element.124), channel_id=1, source_target_pairs={{0,2},{1,3},{4,0},{5,1},{8,4},{9,5},{12,8},{13,9},{14,12},{15,13},... | collective-permute-start | bytes 786440 | tf_op jit(solution)/shard_map/ppermute | solution.py:531
  70.3 14.9 %collective-permute-start.13 = (f32[32,512]{1,0:T(8,128)S(1)}, f32[32,512]{1,0:T(8,128)S(1)}, u32[]{:S(2)}, u32[]{:S(2)}) collective-permute-start(f32[32,512]{1,0:T(8,128)S(1)} %bitcast_add_fusion.8), channel_id=1, source_target_pairs={{0,12},{1,13},{2,14},{3,15},{4,0},{5,1},{6,2},{7,3},{8,4},{9,5},{1... | collective-permute-start | bytes 196616 | tf_op jit(solution)/shard_map/ppermute | solution.py:542
  72.4 20.8 %collective-permute-start.12 = (f32[32,512]{1,0:T(8,128)S(1)}, f32[32,512]{1,0:T(8,128)S(1)}, u32[]{:S(2)}, u32[]{:S(2)}) collective-permute-start(f32[32,512]{1,0:T(8,128)S(1)} %bitcast_add_fusion.8), channel_id=1, source_target_pairs={{0,8},{1,9},{2,10},{3,11},{4,12},{5,13},{6,14},{7,15},{8,0},{9,1},... | collective-permute-start | bytes 196616 | tf_op jit(solution)/shard_map/ppermute | solution.py:542
  73.8 19.4 %collective-permute-start.11 = (f32[32,512]{1,0:T(8,128)S(1)}, f32[32,512]{1,0:T(8,128)S(1)}, u32[]{:S(2)}, u32[]{:S(2)}) collective-permute-start(f32[32,512]{1,0:T(8,128)S(1)} %bitcast_add_fusion.8), channel_id=1, source_target_pairs={{0,4},{1,5},{2,6},{3,7},{4,8},{5,9},{6,10},{7,11},{8,12},{9,13},{1... | collective-permute-start | bytes 196616 | tf_op jit(solution)/shard_map/ppermute | solution.py:542
  93.2 18.7 %copy-start.19 = (f32[4,32,512]{2,1,0:T(8,128)}, f32[4,32,512]{2,1,0:T(8,128)S(1)}, u32[]{:S(2)}) copy-start(f32[4,32,512]{2,1,0:T(8,128)S(1)} %pad_maximum_fusion.refs_0_) | copy-start | bytes 786436
  93.4 7.7 %collective-permute-start.14 = (f32[256,256]{1,0:T(8,128)S(1)}, f32[256,256]{1,0:T(8,128)S(1)}, u32[]{:S(2)}, u32[]{:S(2)}) collective-permute-start(f32[256,256]{1,0:T(8,128)S(1)} %get-tuple-element.132), channel_id=1, source_target_pairs={{0,4},{1,5},{4,8},{5,9},{8,12},{9,13},{12,14},{13,15},{14,10},{15,... | collective-permute-start | bytes 786440 | tf_op jit(solution)/shard_map/ppermute | solution.py:531
  93.4 8.6 %collective-permute-start.15 = (f32[256,256]{1,0:T(8,128)S(1)}, f32[256,256]{1,0:T(8,128)S(1)}, u32[]{:S(2)}, u32[]{:S(2)}) collective-permute-start(f32[256,256]{1,0:T(8,128)S(1)} %get-tuple-element.133), channel_id=1, source_target_pairs={{0,2},{1,3},{4,0},{5,1},{8,4},{9,5},{12,8},{13,9},{14,12},{15,13},... | collective-permute-start | bytes 786440 | tf_op jit(solution)/shard_map/ppermute | solution.py:531
  95.4 11.8 %collective-permute-start.18 = (f32[4,32,512]{2,1,0:T(8,128)S(1)}, f32[4,32,512]{2,1,0:T(8,128)S(1)}, u32[]{:S(2)}, u32[]{:S(2)}) collective-permute-start(f32[4,32,512]{2,1,0:T(8,128)S(1)} %pad_maximum_fusion.refs_0_), channel_id=1, source_target_pairs={{0,3},{1,2},{2,1},{3,0},{4,7},{5,6},{6,5},{7,4},{8,11},{9,10},{10,... | collective-permute-start | bytes 786440 | tf_op jit(solution)/shard_map/ppermute | solution.py:534
  95.4 11.8 %collective-permute-start.17 = (f32[4,32,512]{2,1,0:T(8,128)S(1)}, f32[4,32,512]{2,1,0:T(8,128)S(1)}, u32[]{:S(2)}, u32[]{:S(2)}) collective-permute-start(f32[4,32,512]{2,1,0:T(8,128)S(1)} %pad_maximum_fusion.refs_0_), channel_id=1, source_target_pairs={{0,1},{1,0},{2,3},{3,2},{4,5},{5,4},{6,7},{7,6},{8,9},{9,8},{10,11... | collective-permute-start | bytes 786440 | tf_op jit(solution)/shard_map/ppermute | solution.py:534
  95.6 15.5 %collective-permute-start.16 = (f32[4,32,512]{2,1,0:T(8,128)S(1)}, f32[4,32,512]{2,1,0:T(8,128)}, u32[]{:S(2)}, u32[]{:S(2)}) collective-permute-start(f32[4,32,512]{2,1,0:T(8,128)S(1)} %pad_maximum_fusion.refs_0_), channel_id=1, source_target_pairs={{0,2},{1,3},{2,0},{3,1},{4,6},{5,7},{6,4},{7,5},{8,10},{9,11},{10,... | collective-permute-start | bytes 786440 | tf_op jit(solution)/shard_map/ppermute | solution.py:534
  107.2 6.8 %copy-start.26 = (f32[4,32,512]{2,1,0:T(8,128)}, f32[4,32,512]{2,1,0:T(8,128)S(1)}, u32[]{:S(2)}) copy-start(f32[4,32,512]{2,1,0:T(8,128)S(1)} %collective-permute-done.18.refs_3_) | copy-start | bytes 786436
  107.2 6.8 %copy-start.27 = (f32[4,32,512]{2,1,0:T(8,128)}, f32[4,32,512]{2,1,0:T(8,128)S(1)}, u32[]{:S(2)}) copy-start(f32[4,32,512]{2,1,0:T(8,128)S(1)} %collective-permute-done.17.refs_2_) | copy-start | bytes 786436
  112.0 9.9 %collective-permute-start.19 = (f32[256,256]{1,0:T(8,128)}, f32[256,256]{1,0:T(8,128)S(1)}, u32[]{:S(2)}, u32[]{:S(2)}) collective-permute-start(f32[256,256]{1,0:T(8,128)} %get-tuple-element.141), channel_id=1, source_target_pairs={{0,4},{1,5},{4,8},{5,9},{8,12},{9,13},{12,14},{13,15},{14,10},{15,... | collective-permute-start | bytes 786440 | tf_op jit(solution)/shard_map/ppermute | solution.py:531
  112.0 9.9 %collective-permute-start.20 = (f32[256,256]{1,0:T(8,128)S(1)}, f32[256,256]{1,0:T(8,128)S(1)}, u32[]{:S(2)}, u32[]{:S(2)}) collective-permute-start(f32[256,256]{1,0:T(8,128)S(1)} %get-tuple-element.142), channel_id=1, source_target_pairs={{0,2},{1,3},{4,0},{5,1},{8,4},{9,5},{12,8},{13,9},{14,12},{15,13},... | collective-permute-start | bytes 786440 | tf_op jit(solution)/shard_map/ppermute | solution.py:531
  114.0 7.9 %copy-start.18 = (f32[256,256]{1,0:T(8,128)S(1)}, f32[256,256]{1,0:T(8,128)}, u32[]{:S(2)}) copy-start(f32[256,256]{1,0:T(8,128)} %get-tuple-element.168) | copy-start | bytes 786436
  114.0 9.6 %copy-start.20 = (f32[256,256]{1,0:T(8,128)S(1)}, f32[256,256]{1,0:T(8,128)}, u32[]{:S(2)}) copy-start(f32[256,256]{1,0:T(8,128)} %get-tuple-element.150) | copy-start | bytes 786436
  124.7 9.6 %copy-start.2 = (f32[256,256]{1,0:T(8,128)}, f32[256,256]{1,0:T(8,128)S(1)}, u32[]{:S(2)}) copy-start(f32[256,256]{1,0:T(8,128)S(1)} %fusion.1.first_ref.refs_3_) | copy-start | bytes 786436
  124.7 9.6 %collective-permute-start.21 = (f32[256,256]{1,0:T(8,128)S(1)}, f32[256,256]{1,0:T(8,128)S(1)}, u32[]{:S(2)}, u32[]{:S(2)}) collective-permute-start(f32[256,256]{1,0:T(8,128)S(1)} %fusion.1.first_ref.refs_3_), channel_id=1, source_target_pairs={{0,4},{1,5},{4,8},{5,9},{8,12},{9,13},{12,14},{13,15},{14,10},{15,... | collective-permute-start | bytes 786440 | tf_op jit(solution)/shard_map/ppermute | solution.py:531
  124.8 12.0 %collective-permute-start.22 = (f32[256,256]{1,0:T(8,128)S(1)}, f32[256,256]{1,0:T(8,128)S(1)}, u32[]{:S(2)}, u32[]{:S(2)}) collective-permute-start(f32[256,256]{1,0:T(8,128)S(1)} %fusion.1.first_ref.refs_3_), channel_id=1, source_target_pairs={{0,2},{1,3},{4,0},{5,1},{8,4},{9,5},{12,8},{13,9},{14,12},{15,13},... | collective-permute-start | bytes 786440 | tf_op jit(solution)/shard_map/ppermute | solution.py:531
  134.3 36.1 %copy-start.7 = (f32[256,256]{1,0:T(8,128)}, f32[256,256]{1,0:T(8,128)S(1)}, u32[]{:S(2)}) copy-start(f32[256,256]{1,0:T(8,128)S(1)} %collective-permute-done.21.refs_4_) | copy-start | bytes 786436
  136.7 33.7 %copy-start.8 = (f32[256,256]{1,0:T(8,128)}, f32[256,256]{1,0:T(8,128)S(1)}, u32[]{:S(2)}) copy-start(f32[256,256]{1,0:T(8,128)S(1)} %collective-permute-done.22.refs_5_) | copy-start | bytes 786436
  136.7 13.7 %collective-permute-start.23 = (f32[256,256]{1,0:T(8,128)S(1)}, f32[256,256]{1,0:T(8,128)S(1)}, u32[]{:S(2)}, u32[]{:S(2)}) collective-permute-start(f32[256,256]{1,0:T(8,128)S(1)} %collective-permute-done.21.refs_4_), channel_id=1, source_target_pairs={{0,4},{1,5},{4,8},{5,9},{8,12},{9,13},{12,14},{13,15},{14,10},{15,... | collective-permute-start | bytes 786440 | tf_op jit(solution)/shard_map/ppermute | solution.py:531
  136.7 13.8 %collective-permute-start.24 = (f32[256,256]{1,0:T(8,128)S(1)}, f32[256,256]{1,0:T(8,128)S(1)}, u32[]{:S(2)}, u32[]{:S(2)}) collective-permute-start(f32[256,256]{1,0:T(8,128)S(1)} %collective-permute-done.22.refs_5_), channel_id=1, source_target_pairs={{0,2},{1,3},{4,0},{5,1},{8,4},{9,5},{12,8},{13,9},{14,12},{15,13},... | collective-permute-start | bytes 786440 | tf_op jit(solution)/shard_map/ppermute | solution.py:531
  150.4 20.4 %copy-start.9 = (f32[256,256]{1,0:T(8,128)}, f32[256,256]{1,0:T(8,128)S(1)}, u32[]{:S(2)}) copy-start(f32[256,256]{1,0:T(8,128)S(1)} %collective-permute-done.23.refs_6_) | copy-start | bytes 786436
  150.6 23.4 %copy-start.10 = (f32[256,256]{1,0:T(8,128)}, f32[256,256]{1,0:T(8,128)S(1)}, u32[]{:S(2)}) copy-start(f32[256,256]{1,0:T(8,128)S(1)} %collective-permute-done.24.refs_7_) | copy-start | bytes 786436
  150.6 12.8 %collective-permute-start.25 = (f32[256,256]{1,0:T(8,128)S(1)}, f32[256,256]{1,0:T(8,128)S(1)}, u32[]{:S(2)}, u32[]{:S(2)}) collective-permute-start(f32[256,256]{1,0:T(8,128)S(1)} %collective-permute-done.23.refs_6_), channel_id=1, source_target_pairs={{0,4},{1,5},{4,8},{5,9},{8,12},{9,13},{12,14},{13,15},{14,10},{15,... | collective-permute-start | bytes 786440 | tf_op jit(solution)/shard_map/ppermute | solution.py:531
  150.6 12.8 %collective-permute-start.26 = (f32[256,256]{1,0:T(8,128)S(1)}, f32[256,256]{1,0:T(8,128)S(1)}, u32[]{:S(2)}, u32[]{:S(2)}) collective-permute-start(f32[256,256]{1,0:T(8,128)S(1)} %collective-permute-done.24.refs_7_), channel_id=1, source_target_pairs={{0,2},{1,3},{4,0},{5,1},{8,4},{9,5},{12,8},{13,9},{14,12},{15,13},... | collective-permute-start | bytes 786440 | tf_op jit(solution)/shard_map/ppermute | solution.py:531
  159.9 9.9 %copy-start.3 = (f32[256,256]{1,0:T(8,128)S(1)}, f32[256,256]{1,0:T(8,128)}, u32[]{:S(2)}) copy-start(f32[256,256]{1,0:T(8,128)} %copy-done.2) | copy-start | bytes 786436
  163.4 13.8 %copy-start.4 = (f32[256,256]{1,0:T(8,128)}, f32[256,256]{1,0:T(8,128)S(1)}, u32[]{:S(2)}) copy-start(f32[256,256]{1,0:T(8,128)S(1)} %collective-permute-done.25.refs_8_) | copy-start | bytes 786436
  163.4 13.8 %copy-start.5 = (f32[256,256]{1,0:T(8,128)}, f32[256,256]{1,0:T(8,128)S(1)}, u32[]{:S(2)}) copy-start(f32[256,256]{1,0:T(8,128)S(1)} %collective-permute-done.26.refs_9_) | copy-start | bytes 786436
  163.4 6.3 %collective-permute-start.27 = (f32[128,256]{1,0:T(8,128)S(1)}, f32[128,256]{1,0:T(8,128)S(1)}, u32[]{:S(2)}, u32[]{:S(2)}) collective-permute-start(f32[128,256]{1,0:T(8,128)S(1)} %slice.88), channel_id=1, source_target_pairs={{0,4},{1,5},{4,8},{5,9},{8,12},{9,13},{12,14},{13,15},{14,10},{15,... | collective-permute-start | bytes 393224 | tf_op jit(solution)/shard_map/ppermute | solution.py:531
  163.9 5.8 %collective-permute-start.28 = (f32[128,256]{1,0:T(8,128)S(1)}, f32[128,256]{1,0:T(8,128)S(1)}, u32[]{:S(2)}, u32[]{:S(2)}) collective-permute-start(f32[128,256]{1,0:T(8,128)S(1)} %slice.89), channel_id=1, source_target_pairs={{0,2},{1,3},{4,0},{5,1},{8,4},{9,5},{12,8},{13,9},{14,12},{15,13},... | collective-permute-start | bytes 393224 | tf_op jit(solution)/shard_map/ppermute | solution.py:531
  169.7 7.5 %copy-start.21 = (f32[128,256]{1,0:T(8,128)}, f32[128,256]{1,0:T(8,128)S(1)}, u32[]{:S(2)}) copy-start(f32[128,256]{1,0:T(8,128)S(1)} %collective-permute-done.27.refs_10_) | copy-start | bytes 393220
  169.7 7.5 %copy-start.22 = (f32[128,256]{1,0:T(8,128)}, f32[128,256]{1,0:T(8,128)S(1)}, u32[]{:S(2)}) copy-start(f32[128,256]{1,0:T(8,128)S(1)} %collective-permute-done.28.refs_11_) | copy-start | bytes 393220
  169.7 7.5 %collective-permute-start.38 = (f32[8,256,256]{2,1,0:T(8,128)}, f32[8,256,256]{2,1,0:T(8,128)S(1)}, u32[]{:S(2)}, u32[]{:S(2)}) collective-permute-start(f32[8,256,256]{2,1,0:T(8,128)} %bitcast.44), channel_id=1, source_target_pairs={{0,1},{1,0},{2,3},{3,2},{4,5},{5,4},{6,7},{7,6},{8,9},{9,8},{10,11... | collective-permute-start | bytes 6291464 | tf_op jit(solution)/shard_map/ppermute | solution.py:534
  169.8 4.1 %collective-permute-start.29 = (f32[256,256]{1,0:T(8,128)S(1)}, f32[256,256]{1,0:T(8,128)S(1)}, u32[]{:S(2)}, u32[]{:S(2)}) collective-permute-start(f32[256,256]{1,0:T(8,128)S(1)} %copy-done.3), channel_id=1, source_target_pairs={{0,1},{1,0},{2,3},{3,2},{4,5},{5,4},{6,7},{7,6},{8,9},{9,8},{10,11... | collective-permute-start | bytes 786440 | tf_op jit(solution)/shard_map/ppermute | solution.py:534
  170.3 4.0 %collective-permute-start.30 = (f32[256,256]{1,0:T(8,128)S(1)}, f32[256,256]{1,0:T(8,128)S(1)}, u32[]{:S(2)}, u32[]{:S(2)}) collective-permute-start(f32[256,256]{1,0:T(8,128)S(1)} %collective-permute-done.21.refs_4_), channel_id=1, source_target_pairs={{0,1},{1,0},{2,3},{3,2},{4,5},{5,4},{6,7},{7,6},{8,9},{9,8},{10,11... | collective-permute-start | bytes 786440 | tf_op jit(solution)/shard_map/ppermute | solution.py:534
  170.4 4.3 %collective-permute-start.31 = (f32[256,256]{1,0:T(8,128)S(1)}, f32[256,256]{1,0:T(8,128)S(1)}, u32[]{:S(2)}, u32[]{:S(2)}) collective-permute-start(f32[256,256]{1,0:T(8,128)S(1)} %collective-permute-done.22.refs_5_), channel_id=1, source_target_pairs={{0,1},{1,0},{2,3},{3,2},{4,5},{5,4},{6,7},{7,6},{8,9},{9,8},{10,11... | collective-permute-start | bytes 786440 | tf_op jit(solution)/shard_map/ppermute | solution.py:534
  170.8 4.3 %collective-permute-start.32 = (f32[256,256]{1,0:T(8,128)S(1)}, f32[256,256]{1,0:T(8,128)S(1)}, u32[]{:S(2)}, u32[]{:S(2)}) collective-permute-start(f32[256,256]{1,0:T(8,128)S(1)} %collective-permute-done.23.refs_6_), channel_id=1, source_target_pairs={{0,1},{1,0},{2,3},{3,2},{4,5},{5,4},{6,7},{7,6},{8,9},{9,8},{10,11... | collective-permute-start | bytes 786440 | tf_op jit(solution)/shard_map/ppermute | solution.py:534
  174.0 3.3 %copy-start.11 = (f32[256,256]{1,0:T(8,128)}, f32[256,256]{1,0:T(8,128)S(1)}, u32[]{:S(2)}) copy-start(f32[256,256]{1,0:T(8,128)S(1)} %collective-permute-done.29.refs_12_) | copy-start | bytes 786436
  174.0 1.9 collective-permute-start.33
  174.3 2.9 %copy-start.12 = (f32[256,256]{1,0:T(8,128)}, f32[256,256]{1,0:T(8,128)S(1)}, u32[]{:S(2)}) copy-start(f32[256,256]{1,0:T(8,128)S(1)} %collective-permute-done.30.refs_13_) | copy-start | bytes 786436
  174.3 1.9 collective-permute-start.34
  174.7 2.5 %copy-start.13 = (f32[256,256]{1,0:T(8,128)}, f32[256,256]{1,0:T(8,128)S(1)}, u32[]{:S(2)}) copy-start(f32[256,256]{1,0:T(8,128)S(1)} %collective-permute-done.31.refs_14_) | copy-start | bytes 786436
  174.7 1.9 collective-permute-start.35
  175.1 2.2 %copy-start.14 = (f32[256,256]{1,0:T(8,128)}, f32[256,256]{1,0:T(8,128)S(1)}, u32[]{:S(2)}) copy-start(f32[256,256]{1,0:T(8,128)S(1)} %collective-permute-done.32.refs_15_) | copy-start | bytes 786436
  175.1 1.7 collective-permute-start.36
  175.8 1.4 copy-start.15
  175.8 1.3 collective-permute-start.37
  (5 other events, 4.4 us)
Sparse Core Ops, SparseCore 0:
  50.2 47.0 reduce-scatter.1
  123.8 39.7 all-gather.2

commit v5 on v3

--- a/solution.py
+++ b/solution.py
@@ -109,13 +109,14 @@
         work[at, to] = jnp.zeros((TILE, TILE), jnp.float32)
 
 
-def factor_first(table_ref, mine_ref, other_ref, regular_ref, out_ref):
-    count, rows = mine_ref.shape[0], mine_ref.shape[1]
+def factor_first(table_ref, regular_ref, *refs):
+    parts, out_ref, packed = refs[:-2], refs[-2], refs[-1]
+    count, rows = parts[0].shape[0], parts[0].shape[1]
     place = lax.axis_index("scen")
-    for n in range(2 * count):
-        ref = mine_ref if n < count else other_ref
-        at = pl.ds(pl.multiple_of(table_ref[2 * count * place + n] * rows, rows), rows)
-        out_ref[at, :] = ref[n % count]
+    for n in range(len(parts) * count):
+        row = table_ref[len(parts) * count * place + n]
+        packed[pl.ds(pl.multiple_of(row * rows, rows), rows), :] = parts[n // count][n % count]
+    unpack(packed, out_ref)
     size = out_ref.shape[0]
     row_id = lax.broadcasted_iota(jnp.int32, (TILE, TILE), 0)
     col_id = lax.broadcasted_iota(jnp.int32, (TILE, TILE), 1)
@@ -130,7 +131,7 @@
     factor_step(k, out_ref)
 
 
-def factor_stages(table, mine, other, regular):
+def factor_stages(table, parts, regular):
     size = regular.shape[0]
     settings = dict(
         out_shape=jax.ShapeDtypeStruct((size, size), jnp.float32),
@@ -141,10 +142,11 @@
     )
     first = lambda work: pl.pallas_call(
         factor_first,
-        in_specs=[pl.BlockSpec(memory_space=pltpu.SMEM)] + vmem(3),
+        in_specs=[pl.BlockSpec(memory_space=pltpu.SMEM)] + vmem(1 + len(parts)),
+        scratch_shapes=[pltpu.VMEM((2 * TILE, 5 * TILE), jnp.float32)],
         name="factor_0",
         **settings,
-    )(table, mine, other, regular[None, :])
+    )(table, regular[None, :], *parts)
     return [first] + [
         pl.pallas_call(
             lambda work_ref, out_ref, k=k: factor_next(k, work_ref, out_ref),
@@ -177,6 +179,22 @@
         ),
         name="solve_rows",
     )(inverse, first, second)
+
+
+def pack(block):
+    near = jnp.concatenate([block[:TILE, :TILE], block[3 * TILE :]], axis=1)
+    far = jnp.concatenate([block[TILE : 2 * TILE, : 2 * TILE], block[2 * TILE : 3 * TILE, : 3 * TILE]], axis=1)
+    return near, far
+
+
+def unpack(packed, out):
+    starts = {0: (0, 0), 1: (1, 0), 2: (1, 2), 3: (0, 1)}
+    for i, (half, first) in starts.items():
+        for j in range(i + 1):
+            tile = packed[pl.ds(half * TILE, TILE), pl.ds((first + j) * TILE, TILE)]
+            out[pl.ds(i * TILE, TILE), pl.ds(j * TILE, TILE)] = tile
+            if j < i:
+                out[pl.ds(j * TILE, TILE), pl.ds(i * TILE, TILE)] = tile.T
 
 
 def chosen_rows(first, count, cols):
@@ -334,9 +352,9 @@
     block = gram_ref[...] + sum(
         jnp.dot(part, chosen, preferred_element_type=jnp.float32) for part in split(local)
     )
-    block = 0.5 * (block + block.T)
-    kept_ref[...] = jnp.where(core == 0, block[:half], block[half:])
-    given_ref[...] = jnp.where(core == 0, block[half:], block[:half])
+    near, far = pack(0.5 * (block + block.T))
+    kept_ref[...] = jnp.where(core == 0, near, far)
+    given_ref[...] = jnp.where(core == 0, far, near)
 
 
 def prior_parts(panel_cols, prior, gram):
@@ -344,7 +362,7 @@
     width = panel_cols.shape[0]
     half = width // 2
     local = jax.ShapeDtypeStruct((half, owned), jnp.float32)
-    rows = jax.ShapeDtypeStruct((half, width), jnp.float32)
+    rows = jax.ShapeDtypeStruct((TILE, 5 * TILE), jnp.float32)
     return pl.pallas_call(
         prior_kernel,
         out_shape=[local, local, rows, rows],
@@ -465,9 +483,8 @@
 
 
 def halve_block(block):
-    width = block.shape[0]
     core = lax.axis_index("scen") % 2
-    halves = block.reshape(2, width // 2, width)
+    halves = jnp.stack(pack(block))
     given = lax.dynamic_index_in_dim(halves, 1 - core, 0, keepdims=False)
     kept = lax.dynamic_index_in_dim(halves, core, 0, keepdims=False)
     return kept + swap_cores(given)
@@ -487,8 +504,8 @@
         where = [(at + offset) % chips for offset in back]
         updates += [2 * ring[q] + c for c in (core, 1 - core) for q in where] + where
         factors += [
-            (2 * c + w) * lines + (z ^ by)
-            for c in (core, 1 - core) for w in (y, 1 - y) for by in (0, 2, 1, 3)
+            (2 * c + w) * lines + (z - by) % lines
+            for c in (core, 1 - core) for w in (y, 1 - y) for by in range(lines)
         ]
     return [jnp.array(table, jnp.int32) for table in (fronts, updates, factors)]
 
@@ -523,26 +540,20 @@
 
     together = lax.optimization_barrier
 
+    def shift(values, by):
+        return lax.ppermute(values, "scen", [(d, (d + 4 * by) % parts) for d in range(parts)])
+
     gram, given_0, given_1, kept_0, kept_1 = front(
         front_table, chips, prior_schur.shape[0], row_counts, panel_cols, row_weights, scenario_rows
     )
-
-    got_1 = swap(given_1, 1)
-    got_1, given_0 = together((got_1, given_0))
+    got_1, got_0 = swap(given_1, 1), swap(given_0, 1)
+    local_0, local_1, block_given, block_kept = prior_parts(panel_cols, prior_schur, gram)
+    got_0, got_1, block_given, block_kept = together((got_0, got_1, block_given, block_kept))
+    block = (block_kept + swap(block_given, 1)).reshape(2, lines, -1, block_kept.shape[1])
+
     summed = lax.psum_scatter(
         kept_1 + got_1, "scen", scatter_dimension=0, axis_index_groups=groups
     )
-    got_0 = swap(given_0, 1)
-
-    local_0, local_1, block_given, block_kept = prior_parts(panel_cols, prior_schur, gram)
-    block = (block_kept + swap(block_given, 1)).reshape(2, lines, -1, 2 * half)
-    block = slab(block, y) + swap(slab(block, 1 - y), 2)
-    low, high = z % 2, z // 2
-    block = block.reshape(2, 2, -1, 2 * half)
-    pairs = lax.dynamic_index_in_dim(block, low, 1, keepdims=False)
-    pairs = pairs + swap(lax.dynamic_index_in_dim(block, 1 - low, 1, keepdims=False), 4)
-    moves = [8, 8, 4, 2]
-    beside = slab(pairs, 1 - high)
 
     sides = {1: slice(0, half // 2), -1: slice(half // 2, half)}
 
@@ -550,6 +561,7 @@
         n = offsets.index(offset)
         return kept_0[n] + got_0[n]
 
+    beside = slab(block, 1 - y)
     arrived = None
     for d in range(far, 0, -1):
         if d == far:
@@ -557,20 +569,31 @@
         else:
             ahead = [partial(way * d) + arrived[n] for n, way in enumerate((1, -1))]
         ahead, beside = together((ahead, beside))
-        moved = swap(beside, moves[far - d])
-        arrived, moved = together(([step(ahead[0], 1), step(ahead[1], -1)], moved))
+        arrived = [step(ahead[0], 1), step(ahead[1], -1)]
+        if d == far:
+            beside = swap(beside, 2)
+        elif d == far - 1:
+            beside = [shift(beside[by - 1], by) for by in range(1, lines)]
+        elif d == far - 2:
+            beside = [beside] + [shift(beside, by) for by in range(1, lines)]
+        else:
+            beside = [beside] + [swap(beside, bit) for bit in (2, 1, 3)]
+        arrived, beside = together((arrived, beside))
         if d == far:
             arrived = [
                 jnp.pad(arrived[0], ((0, half // 2), (0, 0))),
                 jnp.pad(arrived[1], ((half // 2, 0), (0, 0))),
             ]
-            beside = (slab(pairs, high) + moved)[None]
-        else:
-            beside = jnp.concatenate([beside, moved])
+            block = slab(block, y) + beside
+            beside = [slab(block, (z + by) % lines) for by in range(1, lines)]
+        elif d == far - 1:
+            beside = sum(beside) + slab(block, z)
+        elif d == far - 2:
+            beside = jnp.stack(beside)
     arrived, summed = together((arrived, summed))
+    stages = factor_stages(factor_table, beside, regular)
     panel_0 = partial(0) + arrived[0] + arrived[1] + local_0
     panel_1 = summed + local_1
-    stages = factor_stages(factor_table, beside, swap(beside, 1), regular)
 
     second = lax.all_gather(panel_1, "scen", axis_index_groups=groups)
     first = [panel_0]
@@ -581,16 +604,16 @@
             ahead = [ahead[n][sides[way]] for n, way in enumerate((1, -1))]
         if d > 1:
             ahead, work = together((ahead, work))
-        ahead, work = together(
-            ([step(ahead[0], 1), step(ahead[1], -1)], stages[d - 1](work))
-        )
+        ahead = [step(ahead[0], 1), step(ahead[1], -1)]
+        ahead, work = together((ahead, stages[d - 1](work)))
         first += ahead
-    inverse = work
+    ahead, second = together((ahead, second))
+    first[-2:] = ahead
+    sources = first + [swap(piece, 1) for piece in first] + [second, swap(second, 1)]
+
     for stage in stages[far:]:
-        inverse = stage(inverse)
-    sources = first + [swap(piece, 1) for piece in first] + [second, swap(second, 1)]
-
-    factor_rows, weights = solve_rows(inverse, panel_0, panel_1)
+        work = stage(work)
+    factor_rows, weights = solve_rows(work, panel_0, panel_1)
     return update_rows(update_table, parts, weights, prior_schur, sources), factor_rows
 
 
@@ -607,9 +630,9 @@
         scenario_rows, row_weights, row_counts, panel_cols, prior_schur
     )
     block = lax.psum_scatter(
-        halve_block(block).reshape(chips, -1, width), "scen", scatter_dimension=0, axis_index_groups=same_core
-    )
-    block = lax.all_gather(block, "scen", axis_index_groups=same_core).reshape(1, half, width)
+        halve_block(block).reshape(chips, -1, 5 * TILE), "scen", scatter_dimension=0, axis_index_groups=same_core
+    )
+    block = lax.all_gather(block, "scen", axis_index_groups=same_core).reshape(1, TILE, 5 * TILE)
     block_other = swap_cores(block)
     gram = lax.dot_general(
         scenario_rows, scaled, (((0,), (1,)), ((), ())), preferred_element_type=jnp.float32
@@ -624,7 +647,7 @@
     panel_rest = swap_cores(panel_half)
     table = jnp.array([c ^ (d % 2) for d in range(parts) for c in range(2)], jnp.int32)
     inverse = None
-    for stage in factor_stages(table, block, block_other, regular):
+    for stage in factor_stages(table, [block, block_other], regular):
         inverse = stage(inverse)
     factor_rows, weights = solve_rows(inverse, panel_rows.T[:half], panel_rows.T[half:])
     even = jnp.where(core == 0, panel_half, panel_rest)

time: 218 us -> 190 us (0.87)
  waiting for transfers between devices: 91.5 us -> 52.4 us
  starting transfers between devices: 25 us -> 35.7 us
  local copies, waits for them, and re-layouts: 3.17 us -> 5.53 us
    ppermute x20 -> x17, waiting for transfers between devices: 50.3 us -> 13.1 us  [swap(): return lax.ppermute(values, 'scen', [(d, d ^ bit) for d in range(parts)])]
    all_gather x1, waiting for transfers between devices: 19.5 us -> 0.02 us  [shards_on_ring(): second = lax.all_gather(panel_1, 'scen', axis_index_groups=groups)]
    ppermute x0 -> x6, waiting for transfers between devices: none -> 18.3 us  [shift(): lax.ppermute(values, 'scen', [(d, (d + 4 * by) % parts) for d in range(pa...]
    ppermute x0 -> x6, starting transfers between devices: none -> 9.77 us  [shift(): lax.ppermute(values, 'scen', [(d, (d + 4 * by) % parts) for d in range(pa...]
    unnamed x39 -> x54, local copies, waits for them, and re-layouts: 3.05 us -> 4.84 us
    ppermute x20 -> x17, starting transfers between devices: 8.92 us -> 8.81 us  [swap(): return lax.ppermute(values, 'scen', [(d, d ^ bit) for d in range(parts)])]
  transfers between devices with their start and end apart: 38 -> 41, of which waited for: 16 -> 14; matrix products, arithmetic and copies ran while one was open for 4% -> 3% of each run, Pallas kernels for 19% -> 21%
where the time goes in v5:
time: 190 us
  Pallas kernels  71.9 us (38%)
  waiting for transfers between devices  52.4 us (28%)
  starting transfers between devices  35.7 us (19%)
  between operations  15.1 us (8%)
  other arithmetic  8.92 us (5%)
  local copies, waits for them, and re-layouts  5.53 us (3%)
    pallas_call x3, Pallas kernels, shards_on_ring(): ahead, work = together((ahead, stages[d - 1](work)))  21.7 us
    ppermute x16, waiting for transfers between devices, step(): return lax.ppermute(values, 'scen', pairs)  20.9 us
    pallas_call x1, Pallas kernels, front(): pl.pallas_call(front_kernel, grid=(depth // tall,), in_specs=[smem, smem,...  19.9 us
    ppermute x6, waiting for transfers between devices, shift(): lax.ppermute(values, 'scen', [(d, (d + 4 * by) % parts) for d in range(pa...  18.3 us
    ppermute x16, starting transfers between devices, step(): return lax.ppermute(values, 'scen', pairs)  17 us
    ppermute x17, waiting for transfers between devices, swap(): return lax.ppermute(values, 'scen', [(d, d ^ bit) for d in range(parts)])  13.1 us
    pallas_call x1, Pallas kernels, update_rows(): pl.pallas_call(lambda *refs: update_kernel(count, *refs), out_shape=jax.S...  11.6 us
    ppermute x6, starting transfers between devices, shift(): lax.ppermute(values, 'scen', [(d, (d + 4 * by) % parts) for d in range(pa...  9.77 us
  transfers between devices with their start and end apart: 41, of which 14 were waited for; matrix products, arithmetic and copies ran while one was open for 3% of the time, Pallas kernels for 21%

profile of v5, /device:TPU:0, one launch (start us, length us, event | category | flops | bytes accessed | tf_op | source)
XLA Modules:
  0.0 189.6 jit_solution(869309323643113813)
XLA Ops:
  7.9 19.9 %front.1 = (f32[512,512]{1,0:T(8,128)}, f32[8,256,256]{2,1,0:T(8,128)}, f32[8,256,256]{2,1,0:T(8,128)}, f32[8,256,256]{2,1,0:T(8,128)}, f32[8,256,256]{2,1,0:T(8,128)}) custom-call(s32[512]{0:T(512)} %constant.82.clone.table_ref, s32[1]{0:T(128)S(6)} %copy.11.counts_ref, s32[1,512]{1,0:T(1,128)} %bitcast.54, f32[1,1024]{1,0:T(1,128)} %bitcast.53, ...), custom_call_target="tpu_custom_call" | custom-call | flops 8589934592 | bytes 16777216 | tf_op jit(solution)/shard_map/front/pallas_call | solution.py:306
  27.8 0.6 collective-permute-start
  28.4 7.1 %prior_parts.1 = (f32[256,256]{1,0:T(8,128)}, f32[256,256]{1,0:T(8,128)}, f32[128,640]{1,0:T(8,128)}, f32[128,640]{1,0:T(8,128)}) custom-call(s32[1,512]{1,0:T(1,128)} %bitcast.55, f32[256,4096]{1,0:T(8,128)} %refs_2_.1, f32[512,512]{1,0:T(8,128)} %get-tuple-element.79.gram_ref), custom_call_target="tpu_custom_call" | custom-call | flops 2147483648 | bytes 4194304 | tf_op jit(solution)/shard_map/prior_parts/pallas_call | solution.py:366
  35.5 1.3 copy-done.3
  36.8 1.6 add.185
  38.6 0.5 collective-permute-start.2
  39.1 1.0 copy-done.2
  40.0 1.0 slice_add_fusion
  41.1 3.0 %collective-permute-start.5 = (f32[4,16,640]{2,1,0:T(8,128)S(1)}, f32[4,16,640]{2,1,0:T(8,128)S(1)}, u32[]{:S(2)}, u32[]{:S(2)}) collective-permute-start(f32[4,16,640]{2,1,0:T(8,128)S(1)} %dynamic-slice_bitcast_fusion), channel_id=1, source_target_pairs={{0,2},{1,3},{2,0},{3,1},{4,6},{5,7},{6,4},{7,5},{8,10},{9,11},{10,... | collective-permute-start | bytes 491528 | tf_op jit(solution)/shard_map/ppermute | solution.py:536
  44.1 1.6 collective-permute-start.3
  45.7 0.4 collective-permute-start.4
  46.2 7.8 %collective-permute-done.3 = f32[128,256]{1,0:T(8,128)S(1)} collective-permute-done((f32[128,256]{1,0:T(8,128)S(1)}, f32[128,256]{1,0:T(8,128)S(1)}, u32[]{:S(2)}, u32[]{:S(2)}) %collective-permute-start.3) | collective-permute-done | bytes 131104 | tf_op jit(solution)/shard_map/ppermute | solution.py:533
  54.0 1.0 collective-permute-done.4
  55.0 0.6 dynamic-slice_bitcast_fusion.1
  55.6 1.1 bitcast_add_fusion.2
  56.9 2.5 %collective-permute-start.7 = (f32[256,256]{1,0:T(8,128)S(1)}, f32[256,256]{1,0:T(8,128)S(1)}, u32[]{:S(2)}, u32[]{:S(2)}) collective-permute-start(f32[256,256]{1,0:T(8,128)S(1)} %get-tuple-element.92), channel_id=1, source_target_pairs={{0,2},{1,3},{4,0},{5,1},{8,4},{9,5},{12,8},{13,9},{14,12},{15,13},... | collective-permute-start | bytes 786440 | tf_op jit(solution)/shard_map/ppermute | solution.py:533
  59.4 4.1 %collective-permute-start.9 = (f32[16,640]{1,0:T(8,128)S(1)}, f32[16,640]{1,0:T(8,128)S(1)}, u32[]{:S(2)}, u32[]{:S(2)}) collective-permute-start(f32[16,640]{1,0:T(8,128)S(1)} %get-tuple-element.94), channel_id=1, source_target_pairs={{0,8},{1,9},{2,10},{3,11},{4,12},{5,13},{6,14},{7,15},{8,0},{9,1},... | collective-permute-start | bytes 122888 | tf_op jit(solution)/shard_map/ppermute | solution.py:544
  63.5 0.4 collective-permute-start.10
  63.9 13.4 %collective-permute-done.8 = f32[16,640]{1,0:T(8,128)S(1)} collective-permute-done((f32[16,640]{1,0:T(8,128)}, f32[16,640]{1,0:T(8,128)S(1)}, u32[]{:S(2)}, u32[]{:S(2)}) %collective-permute-start.8) | collective-permute-done | bytes 40992 | tf_op jit(solution)/shard_map/ppermute | solution.py:544
  77.4 1.2 bitcast_add_fusion.1
  78.6 1.9 %collective-permute-start.11 = (f32[256,256]{1,0:T(8,128)S(1)}, f32[256,256]{1,0:T(8,128)S(1)}, u32[]{:S(2)}, u32[]{:S(2)}) collective-permute-start(f32[256,256]{1,0:T(8,128)S(1)} %get-tuple-element.101), channel_id=1, source_target_pairs={{0,4},{1,5},{4,8},{5,9},{8,12},{9,13},{12,14},{13,15},{14,10},{15,... | collective-permute-start | bytes 786440 | tf_op jit(solution)/shard_map/ppermute | solution.py:533
  80.5 0.2 collective-permute-start.12
  80.6 2.7 %collective-permute-start.15 = (f32[16,640]{1,0:T(8,128)S(1)}, f32[16,640]{1,0:T(8,128)S(1)}, u32[]{:S(2)}, u32[]{:S(2)}) collective-permute-start(f32[16,640]{1,0:T(8,128)S(1)} %bitcast_add_fusion.8), channel_id=1, source_target_pairs={{0,12},{1,13},{2,14},{3,15},{4,0},{5,1},{6,2},{7,3},{8,4},{9,5},{1... | collective-permute-start | bytes 122888 | tf_op jit(solution)/shard_map/ppermute | solution.py:544
  83.3 0.7 collective-permute-start.14
  84.0 1.9 collective-permute-start.13
  85.8 2.4 %collective-permute-done.15 = f32[16,640]{1,0:T(8,128)S(1)} collective-permute-done((f32[16,640]{1,0:T(8,128)S(1)}, f32[16,640]{1,0:T(8,128)S(1)}, u32[]{:S(2)}, u32[]{:S(2)}) %collective-permute-start.15) | collective-permute-done | bytes 40992 | tf_op jit(solution)/shard_map/ppermute | solution.py:544
  88.2 2.6 %collective-permute-done.14 = f32[16,640]{1,0:T(8,128)S(1)} collective-permute-done((f32[16,640]{1,0:T(8,128)S(1)}, f32[16,640]{1,0:T(8,128)S(1)}, u32[]{:S(2)}, u32[]{:S(2)}) %collective-permute-start.14) | collective-permute-done | bytes 40992 | tf_op jit(solution)/shard_map/ppermute | solution.py:544
  90.8 1.2 bitcast_add_fusion
  92.1 1.9 %collective-permute-start.17 = (f32[256,256]{1,0:T(8,128)S(1)}, f32[256,256]{1,0:T(8,128)S(1)}, u32[]{:S(2)}, u32[]{:S(2)}) collective-permute-start(f32[256,256]{1,0:T(8,128)S(1)} %get-tuple-element.111), channel_id=1, source_target_pairs={{0,2},{1,3},{4,0},{5,1},{8,4},{9,5},{12,8},{13,9},{14,12},{15,13},... | collective-permute-start | bytes 786440 | tf_op jit(solution)/shard_map/ppermute | solution.py:533
  94.1 0.9 collective-permute-start.19
  95.0 1.2 collective-permute-start.18
  96.2 7.0 %collective-permute-done.20.refs_3_ = f32[4,16,640]{2,1,0:T(8,128)S(1)} collective-permute-done((f32[4,16,640]{2,1,0:T(8,128)S(1)}, f32[4,16,640]{2,1,0:T(8,128)S(1)}, u32[]{:S(2)}, u32[]{:S(2)}) %collective-permute-start.20) | collective-permute-done | bytes 163872 | tf_op jit(solution)/shard_map/ppermute | solution.py:536
  103.3 2.2 %collective-permute-done.18.refs_1_ = f32[4,16,640]{2,1,0:T(8,128)S(1)} collective-permute-done((f32[4,16,640]{2,1,0:T(8,128)S(1)}, f32[4,16,640]{2,1,0:T(8,128)S(1)}, u32[]{:S(2)}, u32[]{:S(2)}) %collective-permute-start.18) | collective-permute-done | bytes 163872 | tf_op jit(solution)/shard_map/ppermute | solution.py:536
  105.5 0.6 copy-done.26
  106.1 1.7 add.189.second_ref
  107.9 1.0 fusion.1.first_ref.refs_3_
  108.9 2.1 %collective-permute-start.22 = (f32[256,256]{1,0:T(8,128)S(1)}, f32[256,256]{1,0:T(8,128)S(1)}, u32[]{:S(2)}, u32[]{:S(2)}) collective-permute-start(f32[256,256]{1,0:T(8,128)S(1)} %fusion.1.first_ref.refs_3_), channel_id=1, source_target_pairs={{0,2},{1,3},{4,0},{5,1},{8,4},{9,5},{12,8},{13,9},{14,12},{15,13},... | collective-permute-start | bytes 786440 | tf_op jit(solution)/shard_map/ppermute | solution.py:533
  111.0 7.7 %factor_0.1.work_ref = f32[512,512]{1,0:T(8,128)} custom-call(s32[256]{0:T(256)} %constant.84.clone.table_ref, f32[1,512]{1,0:T(1,128)} %bitcast.56, f32[4,16,640]{2,1,0:T(8,128)} %copy-done.21, f32[4,16,640]{2,1,0:T(8,128)} %copy-done.26, f32[4,16,640]{2,1,0:T(8,128)} %copy-done.25, f32[4,16,640]{2,1,0:T(8,128)} %copy-done.24), custom_call_target="tpu_custom_call" | custom-call | flops 6710886400 | bytes 2097152 | tf_op jit(solution)/shard_map/factor_0/pallas_call | solution.py:143
  118.7 1.6 collective-permute-done.22.refs_5_
  120.3 3.5 %collective-permute-done.21.refs_4_ = f32[256,256]{1,0:T(8,128)S(1)} collective-permute-done((f32[256,256]{1,0:T(8,128)S(1)}, f32[256,256]{1,0:T(8,128)S(1)}, u32[]{:S(2)}, u32[]{:S(2)}) %collective-permute-start.21) | collective-permute-done | bytes 262176 | tf_op jit(solution)/shard_map/ppermute | solution.py:533
  123.9 1.9 %collective-permute-start.24 = (f32[256,256]{1,0:T(8,128)S(1)}, f32[256,256]{1,0:T(8,128)S(1)}, u32[]{:S(2)}, u32[]{:S(2)}) collective-permute-start(f32[256,256]{1,0:T(8,128)S(1)} %collective-permute-done.22.refs_5_), channel_id=1, source_target_pairs={{0,2},{1,3},{4,0},{5,1},{8,4},{9,5},{12,8},{13,9},{14,12},{15,13},... | collective-permute-start | bytes 786440 | tf_op jit(solution)/shard_map/ppermute | solution.py:533
  125.8 7.5 %factor_1.1.work_ref = f32[512,512]{1,0:T(8,128)} custom-call(f32[512,512]{1,0:T(8,128)} %factor_0.1.work_ref), custom_call_target="tpu_custom_call" | custom-call | flops 6710886400 | bytes 2097152 | tf_op jit(solution)/shard_map/factor_1/pallas_call | solution.py:608
  133.3 4.3 %collective-permute-done.23.refs_6_ = f32[256,256]{1,0:T(8,128)S(1)} collective-permute-done((f32[256,256]{1,0:T(8,128)S(1)}, f32[256,256]{1,0:T(8,128)S(1)}, u32[]{:S(2)}, u32[]{:S(2)}) %collective-permute-start.23) | collective-permute-done | bytes 262176 | tf_op jit(solution)/shard_map/ppermute | solution.py:533
  137.7 2.0 %collective-permute-start.26 = (f32[256,256]{1,0:T(8,128)S(1)}, f32[256,256]{1,0:T(8,128)S(1)}, u32[]{:S(2)}, u32[]{:S(2)}) collective-permute-start(f32[256,256]{1,0:T(8,128)S(1)} %collective-permute-done.24.refs_7_), channel_id=1, source_target_pairs={{0,2},{1,3},{4,0},{5,1},{8,4},{9,5},{12,8},{13,9},{14,12},{15,13},... | collective-permute-start | bytes 786440 | tf_op jit(solution)/shard_map/ppermute | solution.py:533
  139.7 7.3 %factor_2.1.work_ref = f32[512,512]{1,0:T(8,128)} custom-call(f32[512,512]{1,0:T(8,128)} %factor_1.1.work_ref), custom_call_target="tpu_custom_call" | custom-call | flops 6710886400 | bytes 2097152 | tf_op jit(solution)/shard_map/factor_2/pallas_call | solution.py:608
  146.9 2.7 %collective-permute-done.25.refs_8_ = f32[256,256]{1,0:T(8,128)S(1)} collective-permute-done((f32[256,256]{1,0:T(8,128)S(1)}, f32[256,256]{1,0:T(8,128)S(1)}, u32[]{:S(2)}, u32[]{:S(2)}) %collective-permute-start.25) | collective-permute-done | bytes 262176 | tf_op jit(solution)/shard_map/ppermute | solution.py:533
  149.7 0.4 collective-permute-start.27
  150.1 1.7 collective-permute-start.28
  151.8 6.9 %factor_3.1.inverse_ref = f32[512,512]{1,0:T(8,128)} custom-call(f32[512,512]{1,0:T(8,128)} %factor_2.1.work_ref), custom_call_target="tpu_custom_call" | custom-call | flops 6710886400 | bytes 2097152 | tf_op jit(solution)/shard_map/factor_3/pallas_call | solution.py:608
  158.8 0.5 collective-permute-start.29
  159.4 0.4 collective-permute-start.31
  159.9 3.4 %collective-permute-done.29.refs_12_ = f32[256,256]{1,0:T(8,128)S(1)} collective-permute-done((f32[256,256]{1,0:T(8,128)S(1)}, f32[256,256]{1,0:T(8,128)S(1)}, u32[]{:S(2)}, u32[]{:S(2)}) %collective-permute-start.29) | collective-permute-done | bytes 262176 | tf_op jit(solution)/shard_map/ppermute | solution.py:536
  163.3 0.4 collective-permute-start.33
  163.7 0.4 collective-permute-start.34
  164.1 0.4 collective-permute-start.35
  164.4 0.2 collective-permute-done.32.refs_15_
  164.6 0.1 collective-permute-start.36
  164.8 0.3 collective-permute-done.33.refs_16_
  165.1 0.3 copy-done.15
  165.4 0.1 collective-permute-start.37
  165.5 4.0 %solve_rows.1 = (f32[256,512]{1,0:T(8,128)}, f32[256,512]{1,0:T(8,128)}) custom-call(f32[512,512]{1,0:T(8,128)} %factor_3.1.inverse_ref, f32[256,256]{1,0:T(8,128)} %copy-done.4, f32[256,256]{1,0:T(8,128)} %add.189.second_ref), custom_call_target="tpu_custom_call" | custom-call | flops 805306368 | bytes 2097152 | tf_op jit(solution)/shard_map/solve_rows/pallas_call | solution.py:172
  169.6 0.6 copy-done.17
  170.4 0.8 copy-done
  171.2 11.6 %update_rows.1 = f32[256,4096]{1,0:T(8,128)} custom-call(s32[384]{0:T(512)} %constant.83.clone.refs_0_, f32[256,512]{1,0:T(8,128)} %get-tuple-element.139.refs_1_, f32[256,4096]{1,0:T(8,128)} %refs_2_.1, f32[256,256]{1,0:T(8,128)} %copy-done.4, f32[256,256]{1,0:T(8,128)} %copy-done.9, f32[256,256]{1,0:T(8,128)} %copy-done.8, f32[256,256]{1,0:T(8,128)} %copy-done.10, ...), custom_call_target="tpu_custom_call" | custom-call | flops 3221225472 | bytes 16777216 | tf_op jit(solution)/shard_map/update_rows/pallas_call | solution.py:431
  (98 shorter events, 1.3 us)
Async XLA Ops:
  7.2 99.0 %reduce-scatter.2.cloned.1.call-start = ((), (), s32[]{:S(2)}) async-start(), calls=%async_computation.1 | async-start | bytes 2359296 | tf_op jit(solution)/shard_map/reduce_scatter | solution.py:554
  27.8 7.7 %collective-permute-start = (f32[8,256,256]{2,1,0:T(8,128)}, f32[8,256,256]{2,1,0:T(8,128)S(1)}, u32[]{:S(2)}, u32[]{:S(2)}) collective-permute-start(f32[8,256,256]{2,1,0:T(8,128)} %get-tuple-element.77), channel_id=1, source_target_pairs={{0,1},{1,0},{2,3},{3,2},{4,5},{5,4},{6,7},{7,6},{8,9},{9,8},{10,11... | collective-permute-start | bytes 6291464 | tf_op jit(solution)/shard_map/ppermute | solution.py:536
  28.3 7.1 %collective-permute-start.1 = (f32[8,256,256]{2,1,0:T(8,128)}, f32[8,256,256]{2,1,0:T(8,128)S(1)}, u32[]{:S(2)}, u32[]{:S(2)}) collective-permute-start(f32[8,256,256]{2,1,0:T(8,128)} %get-tuple-element.78), channel_id=1, source_target_pairs={{0,1},{1,0},{2,3},{3,2},{4,5},{5,4},{6,7},{7,6},{8,9},{9,8},{10,11... | collective-permute-start | bytes 6291464 | tf_op jit(solution)/shard_map/ppermute | solution.py:536
  28.4 8.4 %copy-start.1 = (f32[8,256,256]{2,1,0:T(8,128)S(1)}, f32[8,256,256]{2,1,0:T(8,128)}, u32[]{:S(2)}) copy-start(f32[8,256,256]{2,1,0:T(8,128)} %get-tuple-element.115) | copy-start | bytes 6291460
  35.5 1.3 copy-start.3
  36.8 1.7 copy-start.23
  38.4 1.6 copy-start.2
  38.4 2.6 %copy-start.7 = (f32[128,640]{1,0:T(8,128)S(1)}, f32[128,640]{1,0:T(8,128)}, u32[]{:S(2)}) copy-start(f32[128,640]{1,0:T(8,128)} %get-tuple-element.83) | copy-start | bytes 983044
  38.5 120.2 %all-gather.3.cloned.1.call-start = ((), (), s32[]{:S(2)}) async-start(), calls=%async_computation.2 | async-start | bytes 2359296 | tf_op jit(solution)/shard_map/all_gather | solution.py:598
  38.6 2.5 %collective-permute-start.2 = (f32[128,640]{1,0:T(8,128)S(1)}, f32[128,640]{1,0:T(8,128)S(1)}, u32[]{:S(2)}, u32[]{:S(2)}) collective-permute-start(f32[128,640]{1,0:T(8,128)S(1)} %copy-done.23), channel_id=1, source_target_pairs={{0,1},{1,0},{2,3},{3,2},{4,5},{5,4},{6,7},{7,6},{8,9},{9,8},{10,11... | collective-permute-start | bytes 983048 | tf_op jit(solution)/shard_map/ppermute | solution.py:536
  41.1 13.8 %collective-permute-start.5 = (f32[4,16,640]{2,1,0:T(8,128)S(1)}, f32[4,16,640]{2,1,0:T(8,128)S(1)}, u32[]{:S(2)}, u32[]{:S(2)}) collective-permute-start(f32[4,16,640]{2,1,0:T(8,128)S(1)} %dynamic-slice_bitcast_fusion), channel_id=1, source_target_pairs={{0,2},{1,3},{2,0},{3,1},{4,6},{5,7},{6,4},{7,5},{8,10},{9,11},{10,... | collective-permute-start | bytes 491528 | tf_op jit(solution)/shard_map/ppermute | solution.py:536
  44.1 9.8 %collective-permute-start.3 = (f32[128,256]{1,0:T(8,128)S(1)}, f32[128,256]{1,0:T(8,128)S(1)}, u32[]{:S(2)}, u32[]{:S(2)}) collective-permute-start(f32[128,256]{1,0:T(8,128)S(1)} %get-tuple-element.85), channel_id=1, source_target_pairs={{0,4},{1,5},{4,8},{5,9},{8,12},{9,13},{12,14},{13,15},{14,10},{15,... | collective-permute-start | bytes 393224 | tf_op jit(solution)/shard_map/ppermute | solution.py:533
  45.7 9.2 %collective-permute-start.4 = (f32[128,256]{1,0:T(8,128)S(1)}, f32[128,256]{1,0:T(8,128)S(1)}, u32[]{:S(2)}, u32[]{:S(2)}) collective-permute-start(f32[128,256]{1,0:T(8,128)S(1)} %get-tuple-element.86), channel_id=1, source_target_pairs={{0,2},{1,3},{4,0},{5,1},{8,4},{9,5},{12,8},{13,9},{14,12},{15,13},... | collective-permute-start | bytes 393224 | tf_op jit(solution)/shard_map/ppermute | solution.py:533
  56.7 20.6 %collective-permute-start.6 = (f32[256,256]{1,0:T(8,128)S(1)}, f32[256,256]{1,0:T(8,128)S(1)}, u32[]{:S(2)}, u32[]{:S(2)}) collective-permute-start(f32[256,256]{1,0:T(8,128)S(1)} %get-tuple-element.91), channel_id=1, source_target_pairs={{0,4},{1,5},{4,8},{5,9},{8,12},{9,13},{12,14},{13,15},{14,10},{15,... | collective-permute-start | bytes 786440 | tf_op jit(solution)/shard_map/ppermute | solution.py:533
  56.9 20.4 %collective-permute-start.7 = (f32[256,256]{1,0:T(8,128)S(1)}, f32[256,256]{1,0:T(8,128)S(1)}, u32[]{:S(2)}, u32[]{:S(2)}) collective-permute-start(f32[256,256]{1,0:T(8,128)S(1)} %get-tuple-element.92), channel_id=1, source_target_pairs={{0,2},{1,3},{4,0},{5,1},{8,4},{9,5},{12,8},{13,9},{14,12},{15,13},... | collective-permute-start | bytes 786440 | tf_op jit(solution)/shard_map/ppermute | solution.py:533
  59.3 18.0 %collective-permute-start.8 = (f32[16,640]{1,0:T(8,128)}, f32[16,640]{1,0:T(8,128)S(1)}, u32[]{:S(2)}, u32[]{:S(2)}) collective-permute-start(f32[16,640]{1,0:T(8,128)} %get-tuple-element.93), channel_id=1, source_target_pairs={{0,4},{1,5},{2,6},{3,7},{4,8},{5,9},{6,10},{7,11},{8,12},{9,13},{1... | collective-permute-start | bytes 122888 | tf_op jit(solution)/shard_map/ppermute | solution.py:544
  59.4 18.0 %collective-permute-start.9 = (f32[16,640]{1,0:T(8,128)S(1)}, f32[16,640]{1,0:T(8,128)S(1)}, u32[]{:S(2)}, u32[]{:S(2)}) collective-permute-start(f32[16,640]{1,0:T(8,128)S(1)} %get-tuple-element.94), channel_id=1, source_target_pairs={{0,8},{1,9},{2,10},{3,11},{4,12},{5,13},{6,14},{7,15},{8,0},{9,1},... | collective-permute-start | bytes 122888 | tf_op jit(solution)/shard_map/ppermute | solution.py:544
  63.5 13.8 %collective-permute-start.10 = (f32[16,640]{1,0:T(8,128)S(1)}, f32[16,640]{1,0:T(8,128)S(1)}, u32[]{:S(2)}, u32[]{:S(2)}) collective-permute-start(f32[16,640]{1,0:T(8,128)S(1)} %get-tuple-element.95), channel_id=1, source_target_pairs={{0,12},{1,13},{2,14},{3,15},{4,0},{5,1},{6,2},{7,3},{8,4},{9,5},{1... | collective-permute-start | bytes 122888 | tf_op jit(solution)/shard_map/ppermute | solution.py:544
  77.3 28.8 %copy-start.19 = (f32[256,256]{1,0:T(8,128)S(1)}, f32[256,256]{1,0:T(8,128)}, u32[]{:S(2)}) copy-start(f32[256,256]{1,0:T(8,128)} %get-tuple-element.138) | copy-start | bytes 786436
  78.5 29.3 %copy-start.20 = (f32[256,256]{1,0:T(8,128)S(1)}, f32[256,256]{1,0:T(8,128)}, u32[]{:S(2)}) copy-start(f32[256,256]{1,0:T(8,128)} %get-tuple-element.119) | copy-start | bytes 786436
  78.6 12.2 %collective-permute-start.11 = (f32[256,256]{1,0:T(8,128)S(1)}, f32[256,256]{1,0:T(8,128)S(1)}, u32[]{:S(2)}, u32[]{:S(2)}) collective-permute-start(f32[256,256]{1,0:T(8,128)S(1)} %get-tuple-element.101), channel_id=1, source_target_pairs={{0,4},{1,5},{4,8},{5,9},{8,12},{9,13},{12,14},{13,15},{14,10},{15,... | collective-permute-start | bytes 786440 | tf_op jit(solution)/shard_map/ppermute | solution.py:533
  80.5 10.3 %collective-permute-start.12 = (f32[256,256]{1,0:T(8,128)S(1)}, f32[256,256]{1,0:T(8,128)S(1)}, u32[]{:S(2)}, u32[]{:S(2)}) collective-permute-start(f32[256,256]{1,0:T(8,128)S(1)} %get-tuple-element.102), channel_id=1, source_target_pairs={{0,2},{1,3},{4,0},{5,1},{8,4},{9,5},{12,8},{13,9},{14,12},{15,13},... | collective-permute-start | bytes 786440 | tf_op jit(solution)/shard_map/ppermute | solution.py:533
  80.6 7.5 %collective-permute-start.15 = (f32[16,640]{1,0:T(8,128)S(1)}, f32[16,640]{1,0:T(8,128)S(1)}, u32[]{:S(2)}, u32[]{:S(2)}) collective-permute-start(f32[16,640]{1,0:T(8,128)S(1)} %bitcast_add_fusion.8), channel_id=1, source_target_pairs={{0,12},{1,13},{2,14},{3,15},{4,0},{5,1},{6,2},{7,3},{8,4},{9,5},{1... | collective-permute-start | bytes 122888 | tf_op jit(solution)/shard_map/ppermute | solution.py:544
  83.3 7.5 %collective-permute-start.14 = (f32[16,640]{1,0:T(8,128)S(1)}, f32[16,640]{1,0:T(8,128)S(1)}, u32[]{:S(2)}, u32[]{:S(2)}) collective-permute-start(f32[16,640]{1,0:T(8,128)S(1)} %bitcast_add_fusion.8), channel_id=1, source_target_pairs={{0,8},{1,9},{2,10},{3,11},{4,12},{5,13},{6,14},{7,15},{8,0},{9,1},... | collective-permute-start | bytes 122888 | tf_op jit(solution)/shard_map/ppermute | solution.py:544
  84.0 6.8 %collective-permute-start.13 = (f32[16,640]{1,0:T(8,128)S(1)}, f32[16,640]{1,0:T(8,128)S(1)}, u32[]{:S(2)}, u32[]{:S(2)}) collective-permute-start(f32[16,640]{1,0:T(8,128)S(1)} %bitcast_add_fusion.8), channel_id=1, source_target_pairs={{0,4},{1,5},{2,6},{3,7},{4,8},{5,9},{6,10},{7,11},{8,12},{9,13},{1... | collective-permute-start | bytes 122888 | tf_op jit(solution)/shard_map/ppermute | solution.py:544
  90.8 14.7 %copy-start.21 = (f32[4,16,640]{2,1,0:T(8,128)}, f32[4,16,640]{2,1,0:T(8,128)S(1)}, u32[]{:S(2)}) copy-start(f32[4,16,640]{2,1,0:T(8,128)S(1)} %pad_maximum_fusion.refs_0_) | copy-start | bytes 491524
  92.0 13.5 %collective-permute-start.16 = (f32[256,256]{1,0:T(8,128)S(1)}, f32[256,256]{1,0:T(8,128)S(1)}, u32[]{:S(2)}, u32[]{:S(2)}) collective-permute-start(f32[256,256]{1,0:T(8,128)S(1)} %get-tuple-element.110), channel_id=1, source_target_pairs={{0,4},{1,5},{4,8},{5,9},{8,12},{9,13},{12,14},{13,15},{14,10},{15,... | collective-permute-start | bytes 786440 | tf_op jit(solution)/shard_map/ppermute | solution.py:533
  92.1 14.0 %collective-permute-start.17 = (f32[256,256]{1,0:T(8,128)S(1)}, f32[256,256]{1,0:T(8,128)S(1)}, u32[]{:S(2)}, u32[]{:S(2)}) collective-permute-start(f32[256,256]{1,0:T(8,128)S(1)} %get-tuple-element.111), channel_id=1, source_target_pairs={{0,2},{1,3},{4,0},{5,1},{8,4},{9,5},{12,8},{13,9},{14,12},{15,13},... | collective-permute-start | bytes 786440 | tf_op jit(solution)/shard_map/ppermute | solution.py:533
  94.1 9.2 %collective-permute-start.20 = (f32[4,16,640]{2,1,0:T(8,128)S(1)}, f32[4,16,640]{2,1,0:T(8,128)S(1)}, u32[]{:S(2)}, u32[]{:S(2)}) collective-permute-start(f32[4,16,640]{2,1,0:T(8,128)S(1)} %pad_maximum_fusion.refs_0_), channel_id=1, source_target_pairs={{0,3},{1,2},{2,1},{3,0},{4,7},{5,6},{6,5},{7,4},{8,11},{9,10},{10,... | collective-permute-start | bytes 491528 | tf_op jit(solution)/shard_map/ppermute | solution.py:536
  94.1 9.2 %collective-permute-start.19 = (f32[4,16,640]{2,1,0:T(8,128)S(1)}, f32[4,16,640]{2,1,0:T(8,128)S(1)}, u32[]{:S(2)}, u32[]{:S(2)}) collective-permute-start(f32[4,16,640]{2,1,0:T(8,128)S(1)} %pad_maximum_fusion.refs_0_), channel_id=1, source_target_pairs={{0,1},{1,0},{2,3},{3,2},{4,5},{5,4},{6,7},{7,6},{8,9},{9,8},{10,11... | collective-permute-start | bytes 491528 | tf_op jit(solution)/shard_map/ppermute | solution.py:536
  95.0 10.5 %collective-permute-start.18 = (f32[4,16,640]{2,1,0:T(8,128)S(1)}, f32[4,16,640]{2,1,0:T(8,128)S(1)}, u32[]{:S(2)}, u32[]{:S(2)}) collective-permute-start(f32[4,16,640]{2,1,0:T(8,128)S(1)} %pad_maximum_fusion.refs_0_), channel_id=1, source_target_pairs={{0,2},{1,3},{2,0},{3,1},{4,6},{5,7},{6,4},{7,5},{8,10},{9,11},{10,... | collective-permute-start | bytes 491528 | tf_op jit(solution)/shard_map/ppermute | solution.py:536
  103.3 2.2 %copy-start.24 = (f32[4,16,640]{2,1,0:T(8,128)}, f32[4,16,640]{2,1,0:T(8,128)S(1)}, u32[]{:S(2)}) copy-start(f32[4,16,640]{2,1,0:T(8,128)S(1)} %collective-permute-done.20.refs_3_) | copy-start | bytes 491524
  103.3 2.2 %copy-start.25 = (f32[4,16,640]{2,1,0:T(8,128)}, f32[4,16,640]{2,1,0:T(8,128)S(1)}, u32[]{:S(2)}) copy-start(f32[4,16,640]{2,1,0:T(8,128)S(1)} %collective-permute-done.19.refs_2_) | copy-start | bytes 491524
  108.9 49.9 %copy-start.4 = (f32[256,256]{1,0:T(8,128)}, f32[256,256]{1,0:T(8,128)S(1)}, u32[]{:S(2)}) copy-start(f32[256,256]{1,0:T(8,128)S(1)} %fusion.1.first_ref.refs_3_) | copy-start | bytes 786436
  108.9 11.4 %collective-permute-start.22 = (f32[256,256]{1,0:T(8,128)S(1)}, f32[256,256]{1,0:T(8,128)S(1)}, u32[]{:S(2)}, u32[]{:S(2)}) collective-permute-start(f32[256,256]{1,0:T(8,128)S(1)} %fusion.1.first_ref.refs_3_), channel_id=1, source_target_pairs={{0,2},{1,3},{4,0},{5,1},{8,4},{9,5},{12,8},{13,9},{14,12},{15,13},... | collective-permute-start | bytes 786440 | tf_op jit(solution)/shard_map/ppermute | solution.py:533
  111.0 12.8 %collective-permute-start.21 = (f32[256,256]{1,0:T(8,128)S(1)}, f32[256,256]{1,0:T(8,128)S(1)}, u32[]{:S(2)}, u32[]{:S(2)}) collective-permute-start(f32[256,256]{1,0:T(8,128)S(1)} %fusion.1.first_ref.refs_3_), channel_id=1, source_target_pairs={{0,4},{1,5},{4,8},{5,9},{8,12},{9,13},{12,14},{13,15},{14,10},{15,... | collective-permute-start | bytes 786440 | tf_op jit(solution)/shard_map/ppermute | solution.py:533
  120.3 39.1 %copy-start.8 = (f32[256,256]{1,0:T(8,128)}, f32[256,256]{1,0:T(8,128)S(1)}, u32[]{:S(2)}) copy-start(f32[256,256]{1,0:T(8,128)S(1)} %collective-permute-done.22.refs_5_) | copy-start | bytes 786436
  123.8 35.5 %copy-start.9 = (f32[256,256]{1,0:T(8,128)}, f32[256,256]{1,0:T(8,128)S(1)}, u32[]{:S(2)}) copy-start(f32[256,256]{1,0:T(8,128)S(1)} %collective-permute-done.21.refs_4_) | copy-start | bytes 786436
  123.8 13.8 %collective-permute-start.23 = (f32[256,256]{1,0:T(8,128)S(1)}, f32[256,256]{1,0:T(8,128)S(1)}, u32[]{:S(2)}, u32[]{:S(2)}) collective-permute-start(f32[256,256]{1,0:T(8,128)S(1)} %collective-permute-done.21.refs_4_), channel_id=1, source_target_pairs={{0,4},{1,5},{4,8},{5,9},{8,12},{9,13},{12,14},{13,15},{14,10},{15,... | collective-permute-start | bytes 786440 | tf_op jit(solution)/shard_map/ppermute | solution.py:533
  123.9 13.7 %collective-permute-start.24 = (f32[256,256]{1,0:T(8,128)S(1)}, f32[256,256]{1,0:T(8,128)S(1)}, u32[]{:S(2)}, u32[]{:S(2)}) collective-permute-start(f32[256,256]{1,0:T(8,128)S(1)} %collective-permute-done.22.refs_5_), channel_id=1, source_target_pairs={{0,2},{1,3},{4,0},{5,1},{8,4},{9,5},{12,8},{13,9},{14,12},{15,13},... | collective-permute-start | bytes 786440 | tf_op jit(solution)/shard_map/ppermute | solution.py:533
  137.6 9.3 %copy-start.10 = (f32[256,256]{1,0:T(8,128)}, f32[256,256]{1,0:T(8,128)S(1)}, u32[]{:S(2)}) copy-start(f32[256,256]{1,0:T(8,128)S(1)} %collective-permute-done.23.refs_6_) | copy-start | bytes 786436
  137.6 9.3 %copy-start.11 = (f32[256,256]{1,0:T(8,128)}, f32[256,256]{1,0:T(8,128)S(1)}, u32[]{:S(2)}) copy-start(f32[256,256]{1,0:T(8,128)S(1)} %collective-permute-done.24.refs_7_) | copy-start | bytes 786436
  137.6 12.1 %collective-permute-start.25 = (f32[256,256]{1,0:T(8,128)S(1)}, f32[256,256]{1,0:T(8,128)S(1)}, u32[]{:S(2)}, u32[]{:S(2)}) collective-permute-start(f32[256,256]{1,0:T(8,128)S(1)} %collective-permute-done.23.refs_6_), channel_id=1, source_target_pairs={{0,4},{1,5},{4,8},{5,9},{8,12},{9,13},{12,14},{13,15},{14,10},{15,... | collective-permute-start | bytes 786440 | tf_op jit(solution)/shard_map/ppermute | solution.py:533
  137.7 12.0 %collective-permute-start.26 = (f32[256,256]{1,0:T(8,128)S(1)}, f32[256,256]{1,0:T(8,128)S(1)}, u32[]{:S(2)}, u32[]{:S(2)}) collective-permute-start(f32[256,256]{1,0:T(8,128)S(1)} %collective-permute-done.24.refs_7_), channel_id=1, source_target_pairs={{0,2},{1,3},{4,0},{5,1},{8,4},{9,5},{12,8},{13,9},{14,12},{15,13},... | collective-permute-start | bytes 786440 | tf_op jit(solution)/shard_map/ppermute | solution.py:533
  149.7 14.0 %copy-start.5 = (f32[256,256]{1,0:T(8,128)}, f32[256,256]{1,0:T(8,128)S(1)}, u32[]{:S(2)}) copy-start(f32[256,256]{1,0:T(8,128)S(1)} %collective-permute-done.25.refs_8_) | copy-start | bytes 786436
  149.7 14.4 %copy-start.6 = (f32[256,256]{1,0:T(8,128)}, f32[256,256]{1,0:T(8,128)S(1)}, u32[]{:S(2)}) copy-start(f32[256,256]{1,0:T(8,128)S(1)} %collective-permute-done.26.refs_9_) | copy-start | bytes 786436
  149.7 9.0 %collective-permute-start.27 = (f32[128,256]{1,0:T(8,128)S(1)}, f32[128,256]{1,0:T(8,128)S(1)}, u32[]{:S(2)}, u32[]{:S(2)}) collective-permute-start(f32[128,256]{1,0:T(8,128)S(1)} %slice.88), channel_id=1, source_target_pairs={{0,4},{1,5},{4,8},{5,9},{8,12},{9,13},{12,14},{13,15},{14,10},{15,... | collective-permute-start | bytes 393224 | tf_op jit(solution)/shard_map/ppermute | solution.py:533
  150.1 8.5 %collective-permute-start.28 = (f32[128,256]{1,0:T(8,128)S(1)}, f32[128,256]{1,0:T(8,128)}, u32[]{:S(2)}, u32[]{:S(2)}) collective-permute-start(f32[128,256]{1,0:T(8,128)S(1)} %slice.89), channel_id=1, source_target_pairs={{0,2},{1,3},{4,0},{5,1},{8,4},{9,5},{12,8},{13,9},{14,12},{15,13},... | collective-permute-start | bytes 393224 | tf_op jit(solution)/shard_map/ppermute | solution.py:533
  158.7 11.0 %copy-start.22 = (f32[128,256]{1,0:T(8,128)}, f32[128,256]{1,0:T(8,128)S(1)}, u32[]{:S(2)}) copy-start(f32[128,256]{1,0:T(8,128)S(1)} %collective-permute-done.27.refs_10_) | copy-start | bytes 393220
  158.7 10.9 %collective-permute-start.38 = (f32[8,256,256]{2,1,0:T(8,128)}, f32[8,256,256]{2,1,0:T(8,128)S(1)}, u32[]{:S(2)}, u32[]{:S(2)}) collective-permute-start(f32[8,256,256]{2,1,0:T(8,128)} %bitcast.44), channel_id=1, source_target_pairs={{0,1},{1,0},{2,3},{3,2},{4,5},{5,4},{6,7},{7,6},{8,9},{9,8},{10,11... | collective-permute-start | bytes 6291464 | tf_op jit(solution)/shard_map/ppermute | solution.py:536
  158.8 4.5 %collective-permute-start.29 = (f32[256,256]{1,0:T(8,128)S(1)}, f32[256,256]{1,0:T(8,128)S(1)}, u32[]{:S(2)}, u32[]{:S(2)}) collective-permute-start(f32[256,256]{1,0:T(8,128)S(1)} %fusion.1.first_ref.refs_3_), channel_id=1, source_target_pairs={{0,1},{1,0},{2,3},{3,2},{4,5},{5,4},{6,7},{7,6},{8,9},{9,8},{10,11... | collective-permute-start | bytes 786440 | tf_op jit(solution)/shard_map/ppermute | solution.py:536
  159.3 4.4 %collective-permute-start.30 = (f32[256,256]{1,0:T(8,128)S(1)}, f32[256,256]{1,0:T(8,128)S(1)}, u32[]{:S(2)}, u32[]{:S(2)}) collective-permute-start(f32[256,256]{1,0:T(8,128)S(1)} %collective-permute-done.21.refs_4_), channel_id=1, source_target_pairs={{0,1},{1,0},{2,3},{3,2},{4,5},{5,4},{6,7},{7,6},{8,9},{9,8},{10,11... | collective-permute-start | bytes 786440 | tf_op jit(solution)/shard_map/ppermute | solution.py:536
  159.4 4.7 %collective-permute-start.31 = (f32[256,256]{1,0:T(8,128)S(1)}, f32[256,256]{1,0:T(8,128)S(1)}, u32[]{:S(2)}, u32[]{:S(2)}) collective-permute-start(f32[256,256]{1,0:T(8,128)S(1)} %collective-permute-done.22.refs_5_), channel_id=1, source_target_pairs={{0,1},{1,0},{2,3},{3,2},{4,5},{5,4},{6,7},{7,6},{8,9},{9,8},{10,11... | collective-permute-start | bytes 786440 | tf_op jit(solution)/shard_map/ppermute | solution.py:536
  159.8 4.8 %collective-permute-start.32 = (f32[256,256]{1,0:T(8,128)}, f32[256,256]{1,0:T(8,128)S(1)}, u32[]{:S(2)}, u32[]{:S(2)}) collective-permute-start(f32[256,256]{1,0:T(8,128)} %copy-done.10), channel_id=1, source_target_pairs={{0,1},{1,0},{2,3},{3,2},{4,5},{5,4},{6,7},{7,6},{8,9},{9,8},{10,11... | collective-permute-start | bytes 786440 | tf_op jit(solution)/shard_map/ppermute | solution.py:536
  163.3 1.1 copy-start.12
  163.3 1.7 collective-permute-start.33
  163.7 0.9 copy-start.13
  163.7 5.9 %collective-permute-start.34 = (f32[256,256]{1,0:T(8,128)S(1)}, f32[256,256]{1,0:T(8,128)S(1)}, u32[]{:S(2)}, u32[]{:S(2)}) collective-permute-start(f32[256,256]{1,0:T(8,128)S(1)} %collective-permute-done.25.refs_8_), channel_id=1, source_target_pairs={{0,1},{1,0},{2,3},{3,2},{4,5},{5,4},{6,7},{7,6},{8,9},{9,8},{10,11... | collective-permute-start | bytes 786440 | tf_op jit(solution)/shard_map/ppermute | solution.py:536
  164.1 5.5 %collective-permute-start.35 = (f32[256,256]{1,0:T(8,128)S(1)}, f32[256,256]{1,0:T(8,128)S(1)}, u32[]{:S(2)}, u32[]{:S(2)}) collective-permute-start(f32[256,256]{1,0:T(8,128)S(1)} %collective-permute-done.26.refs_9_), channel_id=1, source_target_pairs={{0,1},{1,0},{2,3},{3,2},{4,5},{5,4},{6,7},{7,6},{8,9},{9,8},{10,11... | collective-permute-start | bytes 786440 | tf_op jit(solution)/shard_map/ppermute | solution.py:536
  164.6 4.9 %collective-permute-start.36 = (f32[128,256]{1,0:T(8,128)S(1)}, f32[128,256]{1,0:T(8,128)}, u32[]{:S(2)}, u32[]{:S(2)}) collective-permute-start(f32[128,256]{1,0:T(8,128)S(1)} %collective-permute-done.27.refs_10_), channel_id=1, source_target_pairs={{0,1},{1,0},{2,3},{3,2},{4,5},{5,4},{6,7},{7,6},{8,9},{9,8},{10,11... | collective-permute-start | bytes 393224 | tf_op jit(solution)/shard_map/ppermute | solution.py:536
  165.4 4.3 %copy-start.16 = (f32[256,256]{1,0:T(8,128)}, f32[256,256]{1,0:T(8,128)S(1)}, u32[]{:S(2)}) copy-start(f32[256,256]{1,0:T(8,128)S(1)} %collective-permute-done.33.refs_16_) | copy-start | bytes 786436
  165.4 4.2 %collective-permute-start.37 = (f32[128,256]{1,0:T(8,128)}, f32[128,256]{1,0:T(8,128)}, u32[]{:S(2)}, u32[]{:S(2)}) collective-permute-start(f32[128,256]{1,0:T(8,128)} %collective-permute-done.28.refs_11_), channel_id=1, source_target_pairs={{0,1},{1,0},{2,3},{3,2},{4,5},{5,4},{6,7},{7,6},{8,9},{9,8},{10,11... | collective-permute-start | bytes 393224 | tf_op jit(solution)/shard_map/ppermute | solution.py:536
  169.6 0.8 copy-start.18
  169.6 1.5 copy-start
  (4 other events, 2.8 us)
Sparse Core Ops, SparseCore 0:
  38.6 44.4 reduce-scatter.1
  108.0 41.0 all-gather.2

commit v6 on v5

--- a/solution.py
+++ b/solution.py
@@ -158,27 +158,26 @@
     ]
 
 
-def solve_kernel(inverse_ref, first_ref, second_ref, factor_ref, weight_ref):
+def solve_kernel(inverse_ref, panel_ref, factor_ref, weight_ref):
     inverse = inverse_ref[...]
-    panel = jnp.concatenate([first_ref[...], second_ref[...]], axis=0)
-    rows = dot_split(split(inverse), split(panel)).T
+    rows = dot_split(split(inverse), split(panel_ref[...])).T
     factor_ref[...] = rows
     weight_ref[...] = dot_split(split(rows), split(inverse))
 
 
-def solve_rows(inverse, first, second):
-    half, owned = first.shape
-    shape = jax.ShapeDtypeStruct((owned, 2 * half), jnp.float32)
+def solve_rows(inverse, panel):
+    width, owned = panel.shape
+    shape = jax.ShapeDtypeStruct((owned, width), jnp.float32)
     return pl.pallas_call(
         solve_kernel,
         out_shape=(shape, shape),
-        in_specs=vmem(3),
+        in_specs=vmem(2),
         out_specs=vmem(2),
         cost_estimate=pl.CostEstimate(
-            flops=48 * owned * half * half, bytes_accessed=32 * half * half, transcendentals=0
+            flops=12 * owned * width * width, bytes_accessed=8 * width * width, transcendentals=0
         ),
         name="solve_rows",
-    )(inverse, first, second)
+    )(inverse, panel)
 
 
 def pack(block):
@@ -202,27 +201,23 @@
     return (ids == cols).astype(jnp.float32).astype(jnp.bfloat16)
 
 
-def front_kernel(
-    table_ref, counts_ref, cols_ref, weights_ref, rows_ref,
-    block_ref, given_0, given_1, kept_0, kept_1,
-    pick, picked, total, sems,
+def pick_kernel(
+    counts_ref, cols_ref, weights_ref, prior_ref, rows_ref,
+    scaled_ref, local_ref, given_ref, kept_ref,
+    pick, picked, block, held, prior_sem,
 ):
     step, last = pl.program_id(0), pl.num_programs(0) - 1
     place, parts = lax.axis_index("scen"), lax.axis_size("scen")
     order, width = pick.shape
-    owned = total.shape[2]
     depth = rows_ref.shape[0]
-    half = width // 2
+    owned = held.shape[0]
     tall = order // 4
-    count = given_0.shape[0]
-    wide = 4
-
-    def entry(kind, n):
-        return table_ref[4 * count * place + kind * 2 * count + n]
+    fetch = pltpu.make_async_copy(prior_ref, held, prior_sem)
 
     @pl.when(step == 0)
     def _():
-        block_ref[...] = jnp.zeros_like(block_ref)
+        fetch.start()
+        block[...] = jnp.zeros_like(block)
 
         @pl.loop(0, order // tall)
         def _(n):
@@ -240,26 +235,90 @@
     live = (slot < counts_ref[0]).astype(jnp.float32)
     factor_w = weights_ref[...] * live * (1.0 / (depth * pl.num_programs(0) * parts))
     scaled = (picked[...].T * factor_w).astype(jnp.bfloat16)
-    block_ref[...] += jnp.dot(
+    scaled_ref[...] = scaled
+    block[...] += jnp.dot(
         scaled, picked[...].astype(jnp.bfloat16), preferred_element_type=jnp.float32
     )
+
+    @pl.when(step == last)
+    def _():
+        fetch.wait()
+        picked[...] = jnp.zeros_like(picked)
+
+        @pl.loop(0, order // tall)
+        def _(n):
+            at = pl.ds(pl.multiple_of(n * tall, tall), tall)
+            both = jnp.concatenate(split(held[:, at]), axis=0)
+            picked[...] += jnp.dot(both, pick[at, :], preferred_element_type=jnp.float32)
+
+        local = (picked[:owned] + picked[owned : 2 * owned]).T
+        local_ref[...] = local
+        chosen = chosen_rows(place * owned, owned, cols_ref[...])
+        total = block[...] + sum(
+            jnp.dot(part, chosen, preferred_element_type=jnp.float32) for part in split(local)
+        )
+        near, far = pack(0.5 * (total + total.T))
+        core = lax.rem(place, 2)
+        kept_ref[...] = jnp.where(core == 0, near, far)
+        given_ref[...] = jnp.where(core == 0, far, near)
+
+
+def pick_columns(row_counts, panel_cols, row_weights, prior, scenario_rows):
+    depth, order = scenario_rows.shape
+    width = panel_cols.shape[0]
+    owned = prior.shape[0]
+    tall = 512
+    rows = jax.ShapeDtypeStruct((TILE, 5 * TILE), jnp.float32)
+    whole = lambda shape: pl.BlockSpec(shape, lambda i: (0, 0))
+    return pl.pallas_call(
+        pick_kernel,
+        grid=(depth // tall,),
+        in_specs=[
+            pl.BlockSpec(memory_space=pltpu.SMEM),
+            whole((1, width)),
+            pl.BlockSpec((1, tall), lambda i: (0, i)),
+            pl.BlockSpec(memory_space=pl.ANY),
+            pl.BlockSpec((tall, order), lambda i: (i, 0)),
+        ],
+        out_specs=[pl.BlockSpec((width, tall), lambda i: (0, i)), whole((width, owned))]
+        + [whole(rows.shape)] * 2,
+        out_shape=[
+            jax.ShapeDtypeStruct((width, depth), jnp.bfloat16),
+            jax.ShapeDtypeStruct((width, owned), jnp.float32),
+            rows,
+            rows,
+        ],
+        scratch_shapes=[
+            pltpu.VMEM((order, width), jnp.bfloat16),
+            pltpu.VMEM((tall, width), jnp.float32),
+            pltpu.VMEM((width, width), jnp.float32),
+            pltpu.VMEM(prior.shape, jnp.float32),
+            pltpu.SemaphoreType.DMA,
+        ],
+        cost_estimate=pl.CostEstimate(
+            flops=3 * depth * order * width,
+            bytes_accessed=2 * depth * order + 4 * owned * order,
+            transcendentals=0,
+        ),
+        compiler_params=pltpu.CompilerParams(vmem_limit_bytes=VMEM_BYTES),
+        name="pick_columns",
+    )(row_counts, panel_cols[None, :], row_weights[None, :], prior, scenario_rows)
+
+
+def gram_kernel(
+    table_ref, scaled_ref, rows_ref, given_0, given_1, kept_0, kept_1, total, sems
+):
+    step, last = pl.program_id(0), pl.num_programs(0) - 1
+    count, cut = given_0.shape[0], given_0.shape[1]
+    width, owned = total.shape[1], total.shape[2]
+    wide = 4
+    base = 4 * count * lax.axis_index("scen")
 
     def stores(n, which):
         refs = ((given_0, given_1), (kept_0, kept_1))[which]
-        for h, ref in enumerate(refs):
-            yield pltpu.make_async_copy(
-                total.at[n, pl.ds(h * half, half)],
-                ref.at[entry(1, h * count + lax.rem(n, count))],
-                sems.at[n, h],
-            )
-
-    def each(action):
-        for which in range(2):
-
-            @pl.loop(which * count, (which + 1) * count)
-            def _(n):
-                for store in stores(n, which):
-                    action(store)
+        for h, (ref, rows) in enumerate(zip(refs, (pl.ds(0, cut), pl.ds(cut, width - cut)))):
+            slot = table_ref[base + 2 * count + h * count + lax.rem(n, count)]
+            yield pltpu.make_async_copy(total.at[n, rows], ref.at[slot], sems.at[n, h])
 
     for which in range(2):
 
@@ -267,11 +326,12 @@
         def _(m):
             first = which * count + m * wide
             columns = [
-                rows_ref[:, pl.ds(pl.multiple_of(entry(0, first + i) * owned, owned), owned)]
-                for i in range(wide)
+                pl.multiple_of(table_ref[base + first + i] * owned, owned) for i in range(wide)
             ]
             part = jnp.dot(
-                scaled, jnp.concatenate(columns, axis=1), preferred_element_type=jnp.float32
+                scaled_ref[...],
+                jnp.concatenate([rows_ref[:, pl.ds(at, owned)] for at in columns], axis=1),
+                preferred_element_type=jnp.float32,
             )
 
             @pl.when(step == 0)
@@ -292,101 +352,52 @@
 
     @pl.when(step == last)
     def _():
-        each(lambda store: store.wait())
-
-
-def front(table, count, owned, row_counts, panel_cols, row_weights, scenario_rows):
+        for which in range(2):
+
+            @pl.loop(which * count, (which + 1) * count)
+            def _(n):
+                for store in stores(n, which):
+                    store.wait()
+
+
+def gram_blocks(table, count, cut, owned, scaled, scenario_rows):
     depth, order = scenario_rows.shape
-    width = panel_cols.shape[0]
-    half = width // 2
+    width = scaled.shape[0]
     tall = 512
-    pieces = jax.ShapeDtypeStruct((count, half, owned), jnp.float32)
-    whole = lambda shape: pl.BlockSpec(shape, lambda i: (0, 0))
-    smem = pl.BlockSpec(memory_space=pltpu.SMEM)
+    shapes = [
+        jax.ShapeDtypeStruct((count, rows, owned), jnp.float32) for rows in (cut, width - cut)
+    ]
     return pl.pallas_call(
-        front_kernel,
+        gram_kernel,
         grid=(depth // tall,),
         in_specs=[
-            smem, smem, whole((1, width)),
-            pl.BlockSpec((1, tall), lambda i: (0, i)),
+            pl.BlockSpec(memory_space=pltpu.SMEM),
+            pl.BlockSpec((width, tall), lambda i: (0, i)),
             pl.BlockSpec((tall, order), lambda i: (i, 0)),
         ],
-        out_specs=[whole((width, width))] + [pl.BlockSpec(memory_space=pl.ANY)] * 4,
-        out_shape=[jax.ShapeDtypeStruct((width, width), jnp.float32)] + [pieces] * 4,
+        out_specs=[pl.BlockSpec(memory_space=pl.ANY)] * 4,
+        out_shape=shapes * 2,
         scratch_shapes=[
-            pltpu.VMEM((order, width), jnp.bfloat16),
-            pltpu.VMEM((tall, width), jnp.float32),
             pltpu.VMEM((2 * count, width, owned), jnp.float32),
             pltpu.SemaphoreType.DMA((2 * count, 2)),
         ],
         cost_estimate=pl.CostEstimate(
-            flops=4 * depth * order * width,
+            flops=2 * depth * order * width,
             bytes_accessed=2 * depth * order + 4 * order * width,
             transcendentals=0,
         ),
         compiler_params=pltpu.CompilerParams(vmem_limit_bytes=VMEM_BYTES),
-        name="front",
-    )(table, row_counts, panel_cols[None, :], row_weights[None, :], scenario_rows)
-
-
-def prior_kernel(cols_ref, prior_ref, gram_ref, local_0, local_1, given_ref, kept_ref, picked):
-    place = lax.axis_index("scen")
-    core = lax.rem(place, 2)
-    owned, order = prior_ref.shape
-    width = cols_ref.shape[1]
-    half = width // 2
-    tall = order // 4
-    picked[...] = jnp.zeros_like(picked)
-
-    @pl.loop(0, order // tall)
-    def _(n):
-        at = pl.ds(pl.multiple_of(n * tall, tall), tall)
-        both = jnp.concatenate(split(prior_ref[:, at]), axis=0)
-        chosen = chosen_rows(n * tall, tall, cols_ref[...])
-        picked[...] += jnp.dot(both, chosen, preferred_element_type=jnp.float32)
-
-    local = (picked[:owned] + picked[owned:]).T
-    local_0[...] = local[:half]
-    local_1[...] = local[half:]
-    chosen = chosen_rows(place * owned, owned, cols_ref[...])
-    block = gram_ref[...] + sum(
-        jnp.dot(part, chosen, preferred_element_type=jnp.float32) for part in split(local)
-    )
-    near, far = pack(0.5 * (block + block.T))
-    kept_ref[...] = jnp.where(core == 0, near, far)
-    given_ref[...] = jnp.where(core == 0, far, near)
-
-
-def prior_parts(panel_cols, prior, gram):
-    owned, order = prior.shape
-    width = panel_cols.shape[0]
-    half = width // 2
-    local = jax.ShapeDtypeStruct((half, owned), jnp.float32)
-    rows = jax.ShapeDtypeStruct((TILE, 5 * TILE), jnp.float32)
-    return pl.pallas_call(
-        prior_kernel,
-        out_shape=[local, local, rows, rows],
-        in_specs=vmem(3),
-        out_specs=vmem(4),
-        scratch_shapes=[pltpu.VMEM((2 * owned, width), jnp.float32)],
-        cost_estimate=pl.CostEstimate(
-            flops=4 * owned * order * width, bytes_accessed=4 * owned * order, transcendentals=0
-        ),
-        compiler_params=pltpu.CompilerParams(vmem_limit_bytes=VMEM_BYTES),
-        name="prior_parts",
-    )(panel_cols[None, :], prior, gram)
+        name="gram_blocks",
+    )(table, scaled, scenario_rows)
 
 
 def update_kernel(count, table_ref, weight_ref, prior_ref, *refs):
     sources, out_ref, scratch = refs[:-7], refs[-7], refs[-6:]
     held, before, total, in_sem, prior_sem, out_sem = scratch
     place = lax.axis_index("scen")
-    half, owned = held.shape[2], held.shape[3]
+    width, owned = held.shape[1], held.shape[2]
     chips = count // 2
     wide = 4
-
-    def entry(n):
-        return table_ref[(count + chips) * place + n]
 
     fetch = pltpu.make_async_copy(prior_ref, before, prior_sem)
     loads = []
@@ -394,15 +405,11 @@
         core, slot = n // chips, n % chips
         pieces = sources[core * (chips + 1) : (core + 1) * (chips + 1)]
         pieces = pieces[slot : slot + 1] if slot < chips - 1 else pieces[slot:]
-        rows = half // len(pieces)
+        rows = width // len(pieces)
         copies = [
-            pltpu.make_async_copy(
-                piece, held.at[n, 0, pl.ds(i * rows, rows)], in_sem.at[n, i]
-            )
+            pltpu.make_async_copy(piece, held.at[n, pl.ds(i * rows, rows)], in_sem.at[n, i])
             for i, piece in enumerate(pieces)
         ]
-        second = sources[2 * (chips + 1) + core].at[entry(count + slot)]
-        copies.append(pltpu.make_async_copy(second, held.at[n, 1], in_sem.at[n, 2]))
         for copy in copies:
             copy.start()
         loads.append(copies)
@@ -413,12 +420,13 @@
         for n in range(first, first + wide):
             for copy in loads[n]:
                 copy.wait()
-        panel = [held[n].reshape(2 * half, owned) for n in range(first, first + wide)]
+        panel = [held[n] for n in range(first, first + wide)]
         outer = dot_split(weights, split(jnp.concatenate(panel, axis=1)))
         if first == 0:
             fetch.wait()
         for i in range(wide):
-            cols = pl.ds(pl.multiple_of(entry(first + i) * owned, owned), owned)
+            at = table_ref[count * place + first + i] * owned
+            cols = pl.ds(pl.multiple_of(at, owned), owned)
             total[:, cols] = before[:, cols] - outer[:, i * owned : (i + 1) * owned]
     store = pltpu.make_async_copy(total, out_ref, out_sem)
     store.start()
@@ -427,7 +435,7 @@
 
 def update_rows(table, count, weights, prior, sources):
     owned, order = prior.shape
-    half = weights.shape[1] // 2
+    width = weights.shape[1]
     return pl.pallas_call(
         lambda *refs: update_kernel(count, *refs),
         out_shape=jax.ShapeDtypeStruct(prior.shape, jnp.float32),
@@ -436,16 +444,16 @@
         + [pl.BlockSpec(memory_space=pl.ANY)] * (1 + len(sources)),
         out_specs=pl.BlockSpec(memory_space=pl.ANY),
         scratch_shapes=[
-            pltpu.VMEM((count, 2, half, owned), jnp.float32),
+            pltpu.VMEM((count, width, owned), jnp.float32),
             pltpu.VMEM(prior.shape, jnp.float32),
             pltpu.VMEM(prior.shape, jnp.float32),
-            pltpu.SemaphoreType.DMA((count, 3)),
+            pltpu.SemaphoreType.DMA((count, 2)),
             pltpu.SemaphoreType.DMA,
             pltpu.SemaphoreType.DMA,
         ],
         cost_estimate=pl.CostEstimate(
-            flops=12 * owned * order * half,
-            bytes_accessed=8 * owned * order + 8 * order * half,
+            flops=6 * owned * order * width,
+            bytes_accessed=8 * owned * order + 4 * order * width,
             transcendentals=0,
         ),
         compiler_params=pltpu.CompilerParams(vmem_limit_bytes=VMEM_BYTES),
@@ -502,7 +510,7 @@
         fronts += [2 * ring[q] + c for c in (1 - core, core) for q in where]
         fronts += list(range(chips)) + where
         where = [(at + offset) % chips for offset in back]
-        updates += [2 * ring[q] + c for c in (core, 1 - core) for q in where] + where
+        updates += [2 * ring[q] + c for c in (core, 1 - core) for q in where]
         factors += [
             (2 * c + w) * lines + (z - by) % lines
             for c in (core, 1 - core) for w in (y, 1 - y) for by in range(lines)
@@ -518,7 +526,8 @@
     parts = lax.axis_size("scen")
     chips = parts // 2
     far = lines = chips // 2
-    half = panel_cols.shape[0] // 2
+    owned = prior_schur.shape[0]
+    cut = panel_cols.shape[0] // 4
     place = lax.axis_index("scen")
     y, z = place // 2 % 2, place // 4
     ring = RINGS[chips]
@@ -543,77 +552,74 @@
     def shift(values, by):
         return lax.ppermute(values, "scen", [(d, (d + 4 * by) % parts) for d in range(parts)])
 
-    gram, given_0, given_1, kept_0, kept_1 = front(
-        front_table, chips, prior_schur.shape[0], row_counts, panel_cols, row_weights, scenario_rows
-    )
-    got_1, got_0 = swap(given_1, 1), swap(given_0, 1)
-    local_0, local_1, block_given, block_kept = prior_parts(panel_cols, prior_schur, gram)
-    got_0, got_1, block_given, block_kept = together((got_0, got_1, block_given, block_kept))
-    block = (block_kept + swap(block_given, 1)).reshape(2, lines, -1, block_kept.shape[1])
+    scaled, local, block_given, block_kept = pick_columns(
+        row_counts, panel_cols, row_weights, prior_schur, scenario_rows
+    )
+    block_given, scaled = together((block_given, scaled))
+    block_got = swap(block_given, 1)
+    given_0, given_1, kept_0, kept_1 = gram_blocks(
+        front_table, chips, cut, owned, scaled, scenario_rows
+    )
+    block_got, given_0, given_1 = together((block_got, given_0, given_1))
+    block = (block_kept + block_got).reshape(2, lines, -1, block_kept.shape[1])
+    beside = slab(block, 1 - y)
+    got_1, got_0, beside = swap(given_1, 1), swap(given_0, 1), swap(beside, 2)
+    got_1, got_0, beside = together((got_1, got_0, beside))
 
     summed = lax.psum_scatter(
         kept_1 + got_1, "scen", scatter_dimension=0, axis_index_groups=groups
     )
-
-    sides = {1: slice(0, half // 2), -1: slice(half // 2, half)}
 
     def partial(offset):
         n = offsets.index(offset)
         return kept_0[n] + got_0[n]
 
-    beside = slab(block, 1 - y)
+    side = cut // 2
+    block = slab(block, y) + beside
+    beside = [slab(block, (z + by) % lines) for by in range(1, lines)]
     arrived = None
     for d in range(far, 0, -1):
         if d == far:
-            ahead = [partial(far)[sides[way]] for way in (1, -1)]
+            ahead = [partial(far)[:side], partial(far)[side:]]
         else:
             ahead = [partial(way * d) + arrived[n] for n, way in enumerate((1, -1))]
         ahead, beside = together((ahead, beside))
         arrived = [step(ahead[0], 1), step(ahead[1], -1)]
         if d == far:
-            beside = swap(beside, 2)
+            beside = [shift(beside[by - 1], by) for by in range(1, lines)]
         elif d == far - 1:
-            beside = [shift(beside[by - 1], by) for by in range(1, lines)]
+            beside = [beside] + [shift(beside, by) for by in range(1, lines)]
         elif d == far - 2:
-            beside = [beside] + [shift(beside, by) for by in range(1, lines)]
+            beside = [beside] + [swap(beside, bit) for bit in (2, 1, 3)]
         else:
-            beside = [beside] + [swap(beside, bit) for bit in (2, 1, 3)]
+            beside = stages[0](None)
         arrived, beside = together((arrived, beside))
         if d == far:
             arrived = [
-                jnp.pad(arrived[0], ((0, half // 2), (0, 0))),
-                jnp.pad(arrived[1], ((half // 2, 0), (0, 0))),
+                jnp.pad(arrived[0], ((0, side), (0, 0))), jnp.pad(arrived[1], ((side, 0), (0, 0)))
             ]
-            block = slab(block, y) + beside
-            beside = [slab(block, (z + by) % lines) for by in range(1, lines)]
+            beside = sum(beside) + slab(block, z)
         elif d == far - 1:
-            beside = sum(beside) + slab(block, z)
+            beside = jnp.stack(beside)
         elif d == far - 2:
-            beside = jnp.stack(beside)
-    arrived, summed = together((arrived, summed))
-    stages = factor_stages(factor_table, beside, regular)
-    panel_0 = partial(0) + arrived[0] + arrived[1] + local_0
-    panel_1 = summed + local_1
-
-    second = lax.all_gather(panel_1, "scen", axis_index_groups=groups)
-    first = [panel_0]
-    ahead = [panel_0, panel_0]
-    work = None
+            stages = factor_stages(factor_table, beside, regular)
+    arrived, summed, work = together((arrived, summed, beside))
+    panel = jnp.concatenate([partial(0) + arrived[0] + arrived[1], summed]) + local
+
+    shards = [panel]
+    ahead = [panel, panel]
     for d in range(1, far + 1):
         if d == far:
-            ahead = [ahead[n][sides[way]] for n, way in enumerate((1, -1))]
-        if d > 1:
-            ahead, work = together((ahead, work))
+            middle = panel.shape[0] // 2
+            ahead = [ahead[0][:middle], ahead[1][middle:]]
+        ahead, work = together((ahead, work))
         ahead = [step(ahead[0], 1), step(ahead[1], -1)]
-        ahead, work = together((ahead, stages[d - 1](work)))
-        first += ahead
-    ahead, second = together((ahead, second))
-    first[-2:] = ahead
-    sources = first + [swap(piece, 1) for piece in first] + [second, swap(second, 1)]
-
-    for stage in stages[far:]:
-        work = stage(work)
-    factor_rows, weights = solve_rows(work, panel_0, panel_1)
+        work = stages[d](work) if d < len(stages) else solve_rows(work, panel)
+        ahead, work = together((ahead, work))
+        shards += ahead
+    sources = shards + [swap(piece, 1) for piece in shards]
+
+    factor_rows, weights = work
     return update_rows(update_table, parts, weights, prior_schur, sources), factor_rows
 
 
@@ -649,7 +655,7 @@
     inverse = None
     for stage in factor_stages(table, [block, block_other], regular):
         inverse = stage(inverse)
-    factor_rows, weights = solve_rows(inverse, panel_rows.T[:half], panel_rows.T[half:])
+    factor_rows, weights = solve_rows(inverse, panel_rows.T)
     even = jnp.where(core == 0, panel_half, panel_rest)
     odd = jnp.where(core == 0, panel_rest, panel_half)
     panel = jnp.stack([even, odd], axis=1).reshape(order, width)

time: 190 us -> 190 us (level)
  local copies, waits for them, and re-layouts: 5.53 us -> 2.75 us
  waiting for transfers between devices: 52.4 us -> 54.8 us
  other arithmetic: 8.92 us -> 11.3 us
    ppermute x16, waiting for transfers between devices: 20.9 us -> 33.7 us  [step(): return lax.ppermute(values, 'scen', pairs)]
    ppermute x17 -> x16, waiting for transfers between devices: 13.1 us -> 6.47 us  [swap(): return lax.ppermute(values, 'scen', [(d, d ^ bit) for d in range(parts)])]
    ppermute x6, waiting for transfers between devices: 18.3 us -> 14.6 us  [shift(): lax.ppermute(values, 'scen', [(d, (d + 4 * by) % parts) for d in range(pa...]
    add x1, other arithmetic: 1.63 us -> 3.96 us  [shards_on_ring(): kept_1 + got_1]
    unnamed x54 -> x38, local copies, waits for them, and re-layouts: 4.84 us -> 2.66 us
    ppermute x17 -> x16, starting transfers between devices: 8.81 us -> 8.51 us  [swap(): return lax.ppermute(values, 'scen', [(d, d ^ bit) for d in range(parts)])]
  transfers between devices with their start and end apart: 41 -> 39, of which waited for: 14 -> 19; matrix products, arithmetic and copies ran while one was open for 3% -> 3% of each run, Pallas kernels for 21% -> 24%
where the time goes in v6:
time: 190 us
  Pallas kernels  70.8 us (37%)
  waiting for transfers between devices  54.8 us (29%)
  starting transfers between devices  35 us (18%)
  between operations  15.1 us (8%)
  other arithmetic  11.3 us (6%)
  local copies, waits for them, and re-layouts  2.75 us (1%)
    ppermute x16, waiting for transfers between devices, step(): return lax.ppermute(values, 'scen', pairs)  33.7 us
    pallas_call x3, Pallas kernels, shards_on_ring(): work = stages[d](work) if d < len(stages) else solve_rows(work, panel)  21.6 us
    ppermute x16, starting transfers between devices, step(): return lax.ppermute(values, 'scen', pairs)  17.1 us
    pallas_call x1, Pallas kernels, pick_columns(): pl.pallas_call(pick_kernel, grid=(depth // tall,), in_specs=[pl.BlockSpec...  14.7 us
    ppermute x6, waiting for transfers between devices, shift(): lax.ppermute(values, 'scen', [(d, (d + 4 * by) % parts) for d in range(pa...  14.6 us
    pallas_call x1, Pallas kernels, update_rows(): pl.pallas_call(lambda *refs: update_kernel(count, *refs), out_shape=jax.S...  11.4 us
    pallas_call x1, Pallas kernels, gram_blocks(): pl.pallas_call(gram_kernel, grid=(depth // tall,), in_specs=[pl.BlockSpec...  11.2 us
    ppermute x6, starting transfers between devices, shift(): lax.ppermute(values, 'scen', [(d, (d + 4 * by) % parts) for d in range(pa...  9.28 us
  transfers between devices with their start and end apart: 39, of which 19 were waited for; matrix products, arithmetic and copies ran while one was open for 3% of the time, Pallas kernels for 24%

profile of v6, /device:TPU:0, one launch (start us, length us, event | category | flops | bytes accessed | tf_op | source)
XLA Modules:
  0.0 189.8 jit_solution(1139070378824262325)
XLA Ops:
  7.9 14.7 %pick_columns.1 = (bf16[512,1024]{1,0:T(8,128)(2,1)}, f32[512,256]{1,0:T(8,128)}, f32[128,640]{1,0:T(8,128)}, f32[128,640]{1,0:T(8,128)}) custom-call(s32[1]{0:T(128)S(6)} %copy.11.counts_ref, s32[1,512]{1,0:T(1,128)} %bitcast.49, f32[1,1024]{1,0:T(1,128)} %bitcast.48, f32[256,4096]{1,0:T(8,128)} %refs_2_.1, bf16[1024,4096]{1,0:T(8,128)(2,1)} %rows_ref.3), custom_call_target="tpu_custom_call" | custom-call | flops 6442450944 | bytes 12582912 | tf_op jit(solution)/shard_map/pick_columns/pallas_call | solution.py:273
  22.6 0.5 collective-permute-start
  23.1 11.2 %gram_blocks.1 = (f32[8,128,256]{2,1,0:T(8,128)}, f32[8,384,256]{2,1,0:T(8,128)}, f32[8,128,256]{2,1,0:T(8,128)}, f32[8,384,256]{2,1,0:T(8,128)}) custom-call(s32[512]{0:T(512)} %constant.82.clone.table_ref, bf16[512,1024]{1,0:T(8,128)(2,1)} %get-tuple-element.82.scaled_ref, bf16[1024,4096]{1,0:T(8,128)(2,1)} %rows_ref.3), custom_call_target="tpu_custom_call" | custom-call | flops 4294967296 | bytes 16777216 | tf_op jit(solution)/shard_map/gram_blocks/pallas_call | solution.py:370
  34.5 0.4 collective-permute-start.2
  34.9 1.1 add.143
  36.1 2.7 %collective-permute-start.3 = (f32[4,16,640]{2,1,0:T(8,128)S(1)}, f32[4,16,640]{2,1,0:T(8,128)S(1)}, u32[]{:S(2)}, u32[]{:S(2)}) collective-permute-start(f32[4,16,640]{2,1,0:T(8,128)S(1)} %dynamic-slice_bitcast_fusion), channel_id=1, source_target_pairs={{0,2},{1,3},{2,0},{3,1},{4,6},{5,7},{6,4},{7,5},{8,10},{9,11},{10,... | collective-permute-start | bytes 491528 | tf_op jit(solution)/shard_map/ppermute | solution.py:545
  38.7 4.8 %collective-permute-done.3 = f32[4,16,640]{2,1,0:T(8,128)S(1)} collective-permute-done((f32[4,16,640]{2,1,0:T(8,128)S(1)}, f32[4,16,640]{2,1,0:T(8,128)S(1)}, u32[]{:S(2)}, u32[]{:S(2)}) %collective-permute-start.3) | collective-permute-done | bytes 163872 | tf_op jit(solution)/shard_map/ppermute | solution.py:545
  43.6 0.7 copy-done.13
  44.2 4.0 %add.182 = f32[8,384,256]{2,1,0:T(8,128)} add(f32[8,384,256]{2,1,0:T(8,128)} %get-tuple-element.125, f32[8,384,256]{2,1,0:T(8,128)S(1)} %collective-permute-done.1) | non-fusion elementwise | flops 786432 | bytes 9437184 | tf_op jit(solution)/shard_map/add | solution.py:570
  48.3 0.8 copy-done.14
  49.1 0.4 copy-done.3
  49.5 0.9 slice_add_fusion
  50.4 1.8 collective-permute-start.4
  52.5 1.8 collective-permute-start.6
  54.3 2.6 %collective-permute-start.7 = (f32[16,640]{1,0:T(8,128)S(1)}, f32[16,640]{1,0:T(8,128)S(1)}, u32[]{:S(2)}, u32[]{:S(2)}) collective-permute-start(f32[16,640]{1,0:T(8,128)S(1)} %get-tuple-element.96), channel_id=1, source_target_pairs={{0,8},{1,9},{2,10},{3,11},{4,12},{5,13},{6,14},{7,15},{8,0},{9,1},... | collective-permute-start | bytes 122888 | tf_op jit(solution)/shard_map/ppermute | solution.py:553
  56.9 1.3 collective-permute-start.8
  58.2 1.6 collective-permute-done.6
  59.8 1.7 collective-permute-done.7
  61.6 0.5 collective-permute-done.8
  62.1 1.0 bitcast_add_fusion.3
  63.1 1.4 collective-permute-start.9
  64.5 0.7 collective-permute-start.10
  65.2 3.0 %collective-permute-start.13 = (f32[16,640]{1,0:T(8,128)S(1)}, f32[16,640]{1,0:T(8,128)S(1)}, u32[]{:S(2)}, u32[]{:S(2)}) collective-permute-start(f32[16,640]{1,0:T(8,128)S(1)} %bitcast_add_fusion.8), channel_id=1, source_target_pairs={{0,12},{1,13},{2,14},{3,15},{4,0},{5,1},{6,2},{7,3},{8,4},{9,5},{1... | collective-permute-start | bytes 122888 | tf_op jit(solution)/shard_map/ppermute | solution.py:553
  68.2 0.6 collective-permute-start.11
  68.8 5.7 %collective-permute-done.13 = f32[16,640]{1,0:T(8,128)S(1)} collective-permute-done((f32[16,640]{1,0:T(8,128)S(1)}, f32[16,640]{1,0:T(8,128)S(1)}, u32[]{:S(2)}, u32[]{:S(2)}) %collective-permute-start.13) | collective-permute-done | bytes 40992 | tf_op jit(solution)/shard_map/ppermute | solution.py:553
  74.5 3.0 %collective-permute-done.12 = f32[16,640]{1,0:T(8,128)S(1)} collective-permute-done((f32[16,640]{1,0:T(8,128)S(1)}, f32[16,640]{1,0:T(8,128)S(1)}, u32[]{:S(2)}, u32[]{:S(2)}) %collective-permute-start.12) | collective-permute-done | bytes 40992 | tf_op jit(solution)/shard_map/ppermute | solution.py:553
  77.4 2.2 %collective-permute-done.11 = f32[16,640]{1,0:T(8,128)S(1)} collective-permute-done((f32[16,640]{1,0:T(8,128)S(1)}, f32[16,640]{1,0:T(8,128)S(1)}, u32[]{:S(2)}, u32[]{:S(2)}) %collective-permute-start.11) | collective-permute-done | bytes 40992 | tf_op jit(solution)/shard_map/ppermute | solution.py:553
  79.6 1.1 bitcast_add_fusion.2
  80.9 2.0 %collective-permute-start.16 = (f32[4,16,640]{2,1,0:T(8,128)S(1)}, f32[4,16,640]{2,1,0:T(8,128)S(1)}, u32[]{:S(2)}, u32[]{:S(2)}) collective-permute-start(f32[4,16,640]{2,1,0:T(8,128)S(1)} %pad_maximum_fusion.refs_0_), channel_id=1, source_target_pairs={{0,2},{1,3},{2,0},{3,1},{4,6},{5,7},{6,4},{7,5},{8,10},{9,11},{10,... | collective-permute-start | bytes 491528 | tf_op jit(solution)/shard_map/ppermute | solution.py:545
  82.9 2.0 %collective-permute-start.15 = (f32[128,256]{1,0:T(8,128)S(1)}, f32[128,256]{1,0:T(8,128)S(1)}, u32[]{:S(2)}, u32[]{:S(2)}) collective-permute-start(f32[128,256]{1,0:T(8,128)S(1)} %get-tuple-element.113), channel_id=1, source_target_pairs={{0,2},{1,3},{4,0},{5,1},{8,4},{9,5},{12,8},{13,9},{14,12},{15,13},... | collective-permute-start | bytes 393224 | tf_op jit(solution)/shard_map/ppermute | solution.py:542
  84.9 15.9 %collective-permute-done.14 = f32[128,256]{1,0:T(8,128)S(1)} collective-permute-done((f32[128,256]{1,0:T(8,128)S(1)}, f32[128,256]{1,0:T(8,128)S(1)}, u32[]{:S(2)}, u32[]{:S(2)}) %collective-permute-start.14) | collective-permute-done | bytes 131104 | tf_op jit(solution)/shard_map/ppermute | solution.py:542
  100.8 0.3 collective-permute-done.15
  101.2 1.2 bitcast_add_fusion.1
  102.4 2.5 %collective-permute-start.20 = (f32[128,256]{1,0:T(8,128)S(1)}, f32[128,256]{1,0:T(8,128)S(1)}, u32[]{:S(2)}, u32[]{:S(2)}) collective-permute-start(f32[128,256]{1,0:T(8,128)S(1)} %get-tuple-element.122), channel_id=1, source_target_pairs={{0,2},{1,3},{4,0},{5,1},{8,4},{9,5},{12,8},{13,9},{14,12},{15,13},... | collective-permute-start | bytes 393224 | tf_op jit(solution)/shard_map/ppermute | solution.py:542
  105.0 7.8 %factor_0.1.work_ref = f32[512,512]{1,0:T(8,128)} custom-call(s32[256]{0:T(256)} %constant.84.clone.table_ref, f32[1,512]{1,0:T(1,128)} %bitcast.50, f32[4,16,640]{2,1,0:T(8,128)} %copy-done.15, f32[4,16,640]{2,1,0:T(8,128)} %copy-done.18, f32[4,16,640]{2,1,0:T(8,128)} %copy-done.17, f32[4,16,640]{2,1,0:T(8,128)} %copy-done.16), custom_call_target="tpu_custom_call" | custom-call | flops 6710886400 | bytes 2097152 | tf_op jit(solution)/shard_map/factor_0/pallas_call | solution.py:143
  112.9 0.9 fusion
  113.8 1.1 maximum_add_fusion.panel_ref.refs_3_
  114.9 1.0 collective-permute-start.29
  115.8 0.3 collective-permute-start.21
  116.2 1.7 collective-permute-start.22
  117.9 7.5 %factor_1.1.work_ref = f32[512,512]{1,0:T(8,128)} custom-call(f32[512,512]{1,0:T(8,128)} %factor_0.1.work_ref), custom_call_target="tpu_custom_call" | custom-call | flops 6710886400 | bytes 2097152 | tf_op jit(solution)/shard_map/factor_1/pallas_call | solution.py:617
  125.4 4.4 %collective-permute-done.21.refs_4_ = f32[512,256]{1,0:T(8,128)S(1)} collective-permute-done((f32[512,256]{1,0:T(8,128)S(1)}, f32[512,256]{1,0:T(8,128)S(1)}, u32[]{:S(2)}, u32[]{:S(2)}) %collective-permute-start.21) | collective-permute-done | bytes 524320 | tf_op jit(solution)/shard_map/ppermute | solution.py:542
  130.0 0.3 collective-permute-start.23
  130.3 1.7 collective-permute-start.24
  132.0 0.5 collective-permute-start.31
  132.5 7.3 %factor_2.1.work_ref = f32[512,512]{1,0:T(8,128)} custom-call(f32[512,512]{1,0:T(8,128)} %factor_1.1.work_ref), custom_call_target="tpu_custom_call" | custom-call | flops 6710886400 | bytes 2097152 | tf_op jit(solution)/shard_map/factor_2/pallas_call | solution.py:617
  139.8 3.3 %collective-permute-done.23.refs_6_ = f32[512,256]{1,0:T(8,128)} collective-permute-done((f32[512,256]{1,0:T(8,128)S(1)}, f32[512,256]{1,0:T(8,128)}, u32[]{:S(2)}, u32[]{:S(2)}) %collective-permute-start.23) | collective-permute-done | bytes 524320 | tf_op jit(solution)/shard_map/ppermute | solution.py:542
  143.2 0.3 collective-permute-done.24.refs_7_
  143.5 0.3 collective-permute-start.25
  143.8 1.7 collective-permute-start.26
  145.5 6.9 %factor_3.1.inverse_ref = f32[512,512]{1,0:T(8,128)} custom-call(f32[512,512]{1,0:T(8,128)} %factor_2.1.work_ref), custom_call_target="tpu_custom_call" | custom-call | flops 6710886400 | bytes 2097152 | tf_op jit(solution)/shard_map/factor_3/pallas_call | solution.py:617
  152.4 3.5 %collective-permute-done.25.refs_8_ = f32[512,256]{1,0:T(8,128)S(1)} collective-permute-done((f32[512,256]{1,0:T(8,128)}, f32[512,256]{1,0:T(8,128)S(1)}, u32[]{:S(2)}, u32[]{:S(2)}) %collective-permute-start.25) | collective-permute-done | bytes 524320 | tf_op jit(solution)/shard_map/ppermute | solution.py:542
  155.8 0.3 collective-permute-done.26.refs_9_
  156.2 1.8 collective-permute-start.27
  157.9 0.5 collective-permute-start.28
  158.5 0.5 collective-permute-start.33
  159.0 3.8 %collective-permute-done.27.refs_10_ = f32[256,256]{1,0:T(8,128)S(1)} collective-permute-done((f32[256,256]{1,0:T(8,128)S(1)}, f32[256,256]{1,0:T(8,128)S(1)}, u32[]{:S(2)}, u32[]{:S(2)}) %collective-permute-start.27) | collective-permute-done | bytes 262176 | tf_op jit(solution)/shard_map/ppermute | solution.py:542
  162.8 1.6 collective-permute-done.28.refs_11_
  164.4 4.0 %solve_rows.1 = (f32[256,512]{1,0:T(8,128)}, f32[256,512]{1,0:T(8,128)}) custom-call(f32[512,512]{1,0:T(8,128)} %factor_3.1.inverse_ref, f32[512,256]{1,0:T(8,128)} %copy-done), custom_call_target="tpu_custom_call" | custom-call | flops 805306368 | bytes 2097152 | tf_op jit(solution)/shard_map/solve_rows/pallas_call | solution.py:171
  168.4 0.5 collective-permute-start.36
  169.0 1.1 collective-permute-done.36.refs_19_
  170.1 0.6 collective-permute-done.37.refs_20_
  170.8 0.7 copy-done.12
  171.5 11.4 %update_rows.1 = f32[256,4096]{1,0:T(8,128)} custom-call(s32[256]{0:T(256)} %constant.83.clone.refs_0_, f32[256,512]{1,0:T(8,128)} %get-tuple-element.150.refs_1_, f32[256,4096]{1,0:T(8,128)} %refs_2_.1, f32[512,256]{1,0:T(8,128)} %copy-done, f32[512,256]{1,0:T(8,128)} %copy-done.6, f32[512,256]{1,0:T(8,128)} %copy-done.7, ...), custom_call_target="tpu_custom_call" | custom-call | flops 3221225472 | bytes 16777216 | tf_op jit(solution)/shard_map/update_rows/pallas_call | solution.py:439
  (77 shorter events, 1.3 us)
Async XLA Ops:
  7.2 105.7 %reduce-scatter.2.cloned.1.call-start = ((), (), s32[]{:S(2)}) async-start(), calls=%async_computation.1 | async-start | bytes 3538944 | tf_op jit(solution)/shard_map/reduce_scatter | solution.py:569
  22.6 11.8 %collective-permute-start = (f32[128,640]{1,0:T(8,128)}, f32[128,640]{1,0:T(8,128)}, u32[]{:S(2)}, u32[]{:S(2)}) collective-permute-start(f32[128,640]{1,0:T(8,128)} %get-tuple-element.84), channel_id=1, source_target_pairs={{0,1},{1,0},{2,3},{3,2},{4,5},{5,4},{6,7},{7,6},{8,9},{9,8},{10,11... | collective-permute-start | bytes 983048 | tf_op jit(solution)/shard_map/ppermute | solution.py:545
  34.4 9.2 %collective-permute-start.1 = (f32[8,384,256]{2,1,0:T(8,128)}, f32[8,384,256]{2,1,0:T(8,128)S(1)}, u32[]{:S(2)}, u32[]{:S(2)}) collective-permute-start(f32[8,384,256]{2,1,0:T(8,128)} %get-tuple-element.87), channel_id=1, source_target_pairs={{0,1},{1,0},{2,3},{3,2},{4,5},{5,4},{6,7},{7,6},{8,9},{9,8},{10,11... | collective-permute-start | bytes 9437192 | tf_op jit(solution)/shard_map/ppermute | solution.py:545
  34.5 9.1 %collective-permute-start.2 = (f32[8,128,256]{2,1,0:T(8,128)}, f32[8,128,256]{2,1,0:T(8,128)}, u32[]{:S(2)}, u32[]{:S(2)}) collective-permute-start(f32[8,128,256]{2,1,0:T(8,128)} %get-tuple-element.88), channel_id=1, source_target_pairs={{0,1},{1,0},{2,3},{3,2},{4,5},{5,4},{6,7},{7,6},{8,9},{9,8},{10,11... | collective-permute-start | bytes 3145736 | tf_op jit(solution)/shard_map/ppermute | solution.py:545
  36.1 7.5 %collective-permute-start.3 = (f32[4,16,640]{2,1,0:T(8,128)S(1)}, f32[4,16,640]{2,1,0:T(8,128)S(1)}, u32[]{:S(2)}, u32[]{:S(2)}) collective-permute-start(f32[4,16,640]{2,1,0:T(8,128)S(1)} %dynamic-slice_bitcast_fusion), channel_id=1, source_target_pairs={{0,2},{1,3},{2,0},{3,1},{4,6},{5,7},{6,4},{7,5},{8,10},{9,11},{10,... | collective-permute-start | bytes 491528 | tf_op jit(solution)/shard_map/ppermute | solution.py:545
  43.5 0.7 copy-start.13
  48.2 0.9 copy-start.14
  48.2 1.3 copy-start.3
  50.4 11.6 %collective-permute-start.4 = (f32[64,256]{1,0:T(8,128)S(1)}, f32[64,256]{1,0:T(8,128)S(1)}, u32[]{:S(2)}, u32[]{:S(2)}) collective-permute-start(f32[64,256]{1,0:T(8,128)S(1)} %get-tuple-element.93), channel_id=1, source_target_pairs={{0,4},{1,5},{4,8},{5,9},{8,12},{9,13},{12,14},{13,15},{14,10},{15,... | collective-permute-start | bytes 196616 | tf_op jit(solution)/shard_map/ppermute | solution.py:542
  52.3 9.8 %collective-permute-start.5 = (f32[64,256]{1,0:T(8,128)S(1)}, f32[64,256]{1,0:T(8,128)S(1)}, u32[]{:S(2)}, u32[]{:S(2)}) collective-permute-start(f32[64,256]{1,0:T(8,128)S(1)} %get-tuple-element.94), channel_id=1, source_target_pairs={{0,2},{1,3},{4,0},{5,1},{8,4},{9,5},{12,8},{13,9},{14,12},{15,13},... | collective-permute-start | bytes 196616 | tf_op jit(solution)/shard_map/ppermute | solution.py:542
  52.5 7.3 %collective-permute-start.6 = (f32[16,640]{1,0:T(8,128)S(1)}, f32[16,640]{1,0:T(8,128)S(1)}, u32[]{:S(2)}, u32[]{:S(2)}) collective-permute-start(f32[16,640]{1,0:T(8,128)S(1)} %get-tuple-element.95), channel_id=1, source_target_pairs={{0,4},{1,5},{2,6},{3,7},{4,8},{5,9},{6,10},{7,11},{8,12},{9,13},{1... | collective-permute-start | bytes 122888 | tf_op jit(solution)/shard_map/ppermute | solution.py:553
  54.3 7.2 %collective-permute-start.7 = (f32[16,640]{1,0:T(8,128)S(1)}, f32[16,640]{1,0:T(8,128)S(1)}, u32[]{:S(2)}, u32[]{:S(2)}) collective-permute-start(f32[16,640]{1,0:T(8,128)S(1)} %get-tuple-element.96), channel_id=1, source_target_pairs={{0,8},{1,9},{2,10},{3,11},{4,12},{5,13},{6,14},{7,15},{8,0},{9,1},... | collective-permute-start | bytes 122888 | tf_op jit(solution)/shard_map/ppermute | solution.py:553
  56.9 5.2 %collective-permute-start.8 = (f32[16,640]{1,0:T(8,128)S(1)}, f32[16,640]{1,0:T(8,128)S(1)}, u32[]{:S(2)}, u32[]{:S(2)}) collective-permute-start(f32[16,640]{1,0:T(8,128)S(1)} %get-tuple-element.97), channel_id=1, source_target_pairs={{0,12},{1,13},{2,14},{3,15},{4,0},{5,1},{6,2},{7,3},{8,4},{9,5},{1... | collective-permute-start | bytes 122888 | tf_op jit(solution)/shard_map/ppermute | solution.py:553
  63.1 16.5 %collective-permute-start.9 = (f32[128,256]{1,0:T(8,128)S(1)}, f32[128,256]{1,0:T(8,128)S(1)}, u32[]{:S(2)}, u32[]{:S(2)}) collective-permute-start(f32[128,256]{1,0:T(8,128)S(1)} %get-tuple-element.103), channel_id=1, source_target_pairs={{0,4},{1,5},{4,8},{5,9},{8,12},{9,13},{12,14},{13,15},{14,10},{15,... | collective-permute-start | bytes 393224 | tf_op jit(solution)/shard_map/ppermute | solution.py:542
  64.5 15.1 %collective-permute-start.10 = (f32[128,256]{1,0:T(8,128)S(1)}, f32[128,256]{1,0:T(8,128)S(1)}, u32[]{:S(2)}, u32[]{:S(2)}) collective-permute-start(f32[128,256]{1,0:T(8,128)S(1)} %get-tuple-element.104), channel_id=1, source_target_pairs={{0,2},{1,3},{4,0},{5,1},{8,4},{9,5},{12,8},{13,9},{14,12},{15,13},... | collective-permute-start | bytes 393224 | tf_op jit(solution)/shard_map/ppermute | solution.py:542
  65.2 9.3 %collective-permute-start.13 = (f32[16,640]{1,0:T(8,128)S(1)}, f32[16,640]{1,0:T(8,128)S(1)}, u32[]{:S(2)}, u32[]{:S(2)}) collective-permute-start(f32[16,640]{1,0:T(8,128)S(1)} %bitcast_add_fusion.8), channel_id=1, source_target_pairs={{0,12},{1,13},{2,14},{3,15},{4,0},{5,1},{6,2},{7,3},{8,4},{9,5},{1... | collective-permute-start | bytes 122888 | tf_op jit(solution)/shard_map/ppermute | solution.py:553
  68.2 9.3 %collective-permute-start.12 = (f32[16,640]{1,0:T(8,128)S(1)}, f32[16,640]{1,0:T(8,128)S(1)}, u32[]{:S(2)}, u32[]{:S(2)}) collective-permute-start(f32[16,640]{1,0:T(8,128)S(1)} %bitcast_add_fusion.8), channel_id=1, source_target_pairs={{0,8},{1,9},{2,10},{3,11},{4,12},{5,13},{6,14},{7,15},{8,0},{9,1},... | collective-permute-start | bytes 122888 | tf_op jit(solution)/shard_map/ppermute | solution.py:553
  68.2 11.4 %collective-permute-start.11 = (f32[16,640]{1,0:T(8,128)S(1)}, f32[16,640]{1,0:T(8,128)S(1)}, u32[]{:S(2)}, u32[]{:S(2)}) collective-permute-start(f32[16,640]{1,0:T(8,128)S(1)} %bitcast_add_fusion.8), channel_id=1, source_target_pairs={{0,4},{1,5},{2,6},{3,7},{4,8},{5,9},{6,10},{7,11},{8,12},{9,13},{1... | collective-permute-start | bytes 122888 | tf_op jit(solution)/shard_map/ppermute | solution.py:553
  79.6 25.4 %copy-start.15 = (f32[4,16,640]{2,1,0:T(8,128)}, f32[4,16,640]{2,1,0:T(8,128)S(1)}, u32[]{:S(2)}) copy-start(f32[4,16,640]{2,1,0:T(8,128)S(1)} %pad_maximum_fusion.refs_0_) | copy-start | bytes 491524
  80.7 20.5 %collective-permute-start.18 = (f32[4,16,640]{2,1,0:T(8,128)S(1)}, f32[4,16,640]{2,1,0:T(8,128)S(1)}, u32[]{:S(2)}, u32[]{:S(2)}) collective-permute-start(f32[4,16,640]{2,1,0:T(8,128)S(1)} %pad_maximum_fusion.refs_0_), channel_id=1, source_target_pairs={{0,3},{1,2},{2,1},{3,0},{4,7},{5,6},{6,5},{7,4},{8,11},{9,10},{10,... | collective-permute-start | bytes 491528 | tf_op jit(solution)/shard_map/ppermute | solution.py:545
  80.8 20.4 %collective-permute-start.17 = (f32[4,16,640]{2,1,0:T(8,128)S(1)}, f32[4,16,640]{2,1,0:T(8,128)S(1)}, u32[]{:S(2)}, u32[]{:S(2)}) collective-permute-start(f32[4,16,640]{2,1,0:T(8,128)S(1)} %pad_maximum_fusion.refs_0_), channel_id=1, source_target_pairs={{0,1},{1,0},{2,3},{3,2},{4,5},{5,4},{6,7},{7,6},{8,9},{9,8},{10,11... | collective-permute-start | bytes 491528 | tf_op jit(solution)/shard_map/ppermute | solution.py:545
  80.9 20.3 %collective-permute-start.16 = (f32[4,16,640]{2,1,0:T(8,128)S(1)}, f32[4,16,640]{2,1,0:T(8,128)S(1)}, u32[]{:S(2)}, u32[]{:S(2)}) collective-permute-start(f32[4,16,640]{2,1,0:T(8,128)S(1)} %pad_maximum_fusion.refs_0_), channel_id=1, source_target_pairs={{0,2},{1,3},{2,0},{3,1},{4,6},{5,7},{6,4},{7,5},{8,10},{9,11},{10,... | collective-permute-start | bytes 491528 | tf_op jit(solution)/shard_map/ppermute | solution.py:545
  82.9 17.9 %collective-permute-start.14 = (f32[128,256]{1,0:T(8,128)S(1)}, f32[128,256]{1,0:T(8,128)S(1)}, u32[]{:S(2)}, u32[]{:S(2)}) collective-permute-start(f32[128,256]{1,0:T(8,128)S(1)} %get-tuple-element.112), channel_id=1, source_target_pairs={{0,4},{1,5},{4,8},{5,9},{8,12},{9,13},{12,14},{13,15},{14,10},{15,... | collective-permute-start | bytes 393224 | tf_op jit(solution)/shard_map/ppermute | solution.py:542
  82.9 18.2 %collective-permute-start.15 = (f32[128,256]{1,0:T(8,128)S(1)}, f32[128,256]{1,0:T(8,128)S(1)}, u32[]{:S(2)}, u32[]{:S(2)}) collective-permute-start(f32[128,256]{1,0:T(8,128)S(1)} %get-tuple-element.113), channel_id=1, source_target_pairs={{0,2},{1,3},{4,0},{5,1},{8,4},{9,5},{12,8},{13,9},{14,12},{15,13},... | collective-permute-start | bytes 393224 | tf_op jit(solution)/shard_map/ppermute | solution.py:542
  101.2 3.8 %copy-start.16 = (f32[4,16,640]{2,1,0:T(8,128)}, f32[4,16,640]{2,1,0:T(8,128)S(1)}, u32[]{:S(2)}) copy-start(f32[4,16,640]{2,1,0:T(8,128)S(1)} %collective-permute-done.18.refs_3_) | copy-start | bytes 491524
  101.2 3.8 %copy-start.17 = (f32[4,16,640]{2,1,0:T(8,128)}, f32[4,16,640]{2,1,0:T(8,128)S(1)}, u32[]{:S(2)}) copy-start(f32[4,16,640]{2,1,0:T(8,128)S(1)} %collective-permute-done.17.refs_2_) | copy-start | bytes 491524
  101.2 3.8 %copy-start.18 = (f32[4,16,640]{2,1,0:T(8,128)}, f32[4,16,640]{2,1,0:T(8,128)S(1)}, u32[]{:S(2)}) copy-start(f32[4,16,640]{2,1,0:T(8,128)S(1)} %collective-permute-done.16.refs_1_) | copy-start | bytes 491524
  102.4 10.4 %collective-permute-start.19 = (f32[128,256]{1,0:T(8,128)S(1)}, f32[128,256]{1,0:T(8,128)S(1)}, u32[]{:S(2)}, u32[]{:S(2)}) collective-permute-start(f32[128,256]{1,0:T(8,128)S(1)} %get-tuple-element.121), channel_id=1, source_target_pairs={{0,4},{1,5},{4,8},{5,9},{8,12},{9,13},{12,14},{13,15},{14,10},{15,... | collective-permute-start | bytes 393224 | tf_op jit(solution)/shard_map/ppermute | solution.py:542
  102.4 10.4 %collective-permute-start.20 = (f32[128,256]{1,0:T(8,128)S(1)}, f32[128,256]{1,0:T(8,128)S(1)}, u32[]{:S(2)}, u32[]{:S(2)}) collective-permute-start(f32[128,256]{1,0:T(8,128)S(1)} %get-tuple-element.122), channel_id=1, source_target_pairs={{0,2},{1,3},{4,0},{5,1},{8,4},{9,5},{12,8},{13,9},{14,12},{15,13},... | collective-permute-start | bytes 393224 | tf_op jit(solution)/shard_map/ppermute | solution.py:542
  105.0 8.8 %copy-start.4 = (f32[512,256]{1,0:T(8,128)S(1)}, f32[512,256]{1,0:T(8,128)}, u32[]{:S(2)}) copy-start(f32[512,256]{1,0:T(8,128)} %get-tuple-element.131) | copy-start | bytes 1572868
  114.9 10.5 %copy-start = (f32[512,256]{1,0:T(8,128)}, f32[512,256]{1,0:T(8,128)S(1)}, u32[]{:S(2)}) copy-start(f32[512,256]{1,0:T(8,128)S(1)} %maximum_add_fusion.panel_ref.refs_3_) | copy-start | bytes 1572868
  114.9 43.6 %collective-permute-start.29 = (f32[512,256]{1,0:T(8,128)S(1)}, f32[512,256]{1,0:T(8,128)S(1)}, u32[]{:S(2)}, u32[]{:S(2)}) collective-permute-start(f32[512,256]{1,0:T(8,128)S(1)} %maximum_add_fusion.panel_ref.refs_3_), channel_id=1, source_target_pairs={{0,1},{1,0},{2,3},{3,2},{4,5},{5,4},{6,7},{7,6},{8,9},{9,8},{10,11... | collective-permute-start | bytes 1572872 | tf_op jit(solution)/shard_map/ppermute | solution.py:545
  115.8 13.9 %collective-permute-start.21 = (f32[512,256]{1,0:T(8,128)S(1)}, f32[512,256]{1,0:T(8,128)S(1)}, u32[]{:S(2)}, u32[]{:S(2)}) collective-permute-start(f32[512,256]{1,0:T(8,128)S(1)} %maximum_add_fusion.panel_ref.refs_3_), channel_id=1, source_target_pairs={{0,4},{1,5},{4,8},{5,9},{8,12},{9,13},{12,14},{13,15},{14,10},{15,... | collective-permute-start | bytes 1572872 | tf_op jit(solution)/shard_map/ppermute | solution.py:542
  116.2 13.8 %collective-permute-start.22 = (f32[512,256]{1,0:T(8,128)S(1)}, f32[512,256]{1,0:T(8,128)S(1)}, u32[]{:S(2)}, u32[]{:S(2)}) collective-permute-start(f32[512,256]{1,0:T(8,128)S(1)} %maximum_add_fusion.panel_ref.refs_3_), channel_id=1, source_target_pairs={{0,2},{1,3},{4,0},{5,1},{8,4},{9,5},{12,8},{13,9},{14,12},{15,13},... | collective-permute-start | bytes 1572872 | tf_op jit(solution)/shard_map/ppermute | solution.py:542
  129.7 10.1 %copy-start.6 = (f32[512,256]{1,0:T(8,128)}, f32[512,256]{1,0:T(8,128)S(1)}, u32[]{:S(2)}) copy-start(f32[512,256]{1,0:T(8,128)S(1)} %collective-permute-done.21.refs_4_) | copy-start | bytes 1572868
  130.0 9.9 %copy-start.7 = (f32[512,256]{1,0:T(8,128)}, f32[512,256]{1,0:T(8,128)S(1)}, u32[]{:S(2)}) copy-start(f32[512,256]{1,0:T(8,128)S(1)} %collective-permute-done.22.refs_5_) | copy-start | bytes 1572868
  130.0 13.2 %collective-permute-start.23 = (f32[512,256]{1,0:T(8,128)S(1)}, f32[512,256]{1,0:T(8,128)}, u32[]{:S(2)}, u32[]{:S(2)}) collective-permute-start(f32[512,256]{1,0:T(8,128)S(1)} %collective-permute-done.21.refs_4_), channel_id=1, source_target_pairs={{0,4},{1,5},{4,8},{5,9},{8,12},{9,13},{12,14},{13,15},{14,10},{15,... | collective-permute-start | bytes 1572872 | tf_op jit(solution)/shard_map/ppermute | solution.py:542
  130.3 13.2 %collective-permute-start.24 = (f32[512,256]{1,0:T(8,128)S(1)}, f32[512,256]{1,0:T(8,128)}, u32[]{:S(2)}, u32[]{:S(2)}) collective-permute-start(f32[512,256]{1,0:T(8,128)S(1)} %collective-permute-done.22.refs_5_), channel_id=1, source_target_pairs={{0,2},{1,3},{4,0},{5,1},{8,4},{9,5},{12,8},{13,9},{14,12},{15,13},... | collective-permute-start | bytes 1572872 | tf_op jit(solution)/shard_map/ppermute | solution.py:542
  132.0 26.5 %collective-permute-start.30 = (f32[512,256]{1,0:T(8,128)S(1)}, f32[512,256]{1,0:T(8,128)}, u32[]{:S(2)}, u32[]{:S(2)}) collective-permute-start(f32[512,256]{1,0:T(8,128)S(1)} %collective-permute-done.21.refs_4_), channel_id=1, source_target_pairs={{0,1},{1,0},{2,3},{3,2},{4,5},{5,4},{6,7},{7,6},{8,9},{9,8},{10,11... | collective-permute-start | bytes 1572872 | tf_op jit(solution)/shard_map/ppermute | solution.py:545
  132.0 36.4 %collective-permute-start.31 = (f32[512,256]{1,0:T(8,128)S(1)}, f32[512,256]{1,0:T(8,128)}, u32[]{:S(2)}, u32[]{:S(2)}) collective-permute-start(f32[512,256]{1,0:T(8,128)S(1)} %collective-permute-done.22.refs_5_), channel_id=1, source_target_pairs={{0,1},{1,0},{2,3},{3,2},{4,5},{5,4},{6,7},{7,6},{8,9},{9,8},{10,11... | collective-permute-start | bytes 1572872 | tf_op jit(solution)/shard_map/ppermute | solution.py:545
  143.5 12.3 %collective-permute-start.25 = (f32[512,256]{1,0:T(8,128)}, f32[512,256]{1,0:T(8,128)S(1)}, u32[]{:S(2)}, u32[]{:S(2)}) collective-permute-start(f32[512,256]{1,0:T(8,128)} %collective-permute-done.23.refs_6_), channel_id=1, source_target_pairs={{0,4},{1,5},{4,8},{5,9},{8,12},{9,13},{12,14},{13,15},{14,10},{15,... | collective-permute-start | bytes 1572872 | tf_op jit(solution)/shard_map/ppermute | solution.py:542
  143.8 12.3 %collective-permute-start.26 = (f32[512,256]{1,0:T(8,128)}, f32[512,256]{1,0:T(8,128)S(1)}, u32[]{:S(2)}, u32[]{:S(2)}) collective-permute-start(f32[512,256]{1,0:T(8,128)} %collective-permute-done.24.refs_7_), channel_id=1, source_target_pairs={{0,2},{1,3},{4,0},{5,1},{8,4},{9,5},{12,8},{13,9},{14,12},{15,13},... | collective-permute-start | bytes 1572872 | tf_op jit(solution)/shard_map/ppermute | solution.py:542
  155.8 14.9 %copy-start.1 = (f32[512,256]{1,0:T(8,128)}, f32[512,256]{1,0:T(8,128)S(1)}, u32[]{:S(2)}) copy-start(f32[512,256]{1,0:T(8,128)S(1)} %collective-permute-done.25.refs_8_) | copy-start | bytes 1572868
  156.1 14.6 %copy-start.2 = (f32[512,256]{1,0:T(8,128)}, f32[512,256]{1,0:T(8,128)S(1)}, u32[]{:S(2)}) copy-start(f32[512,256]{1,0:T(8,128)S(1)} %collective-permute-done.26.refs_9_) | copy-start | bytes 1572868
  156.2 6.6 %collective-permute-start.27 = (f32[256,256]{1,0:T(8,128)S(1)}, f32[256,256]{1,0:T(8,128)S(1)}, u32[]{:S(2)}, u32[]{:S(2)}) collective-permute-start(f32[256,256]{1,0:T(8,128)S(1)} %slice.88), channel_id=1, source_target_pairs={{0,4},{1,5},{4,8},{5,9},{8,12},{9,13},{12,14},{13,15},{14,10},{15,... | collective-permute-start | bytes 786440 | tf_op jit(solution)/shard_map/ppermute | solution.py:542
  157.9 6.5 %collective-permute-start.28 = (f32[256,256]{1,0:T(8,128)S(1)}, f32[256,256]{1,0:T(8,128)}, u32[]{:S(2)}, u32[]{:S(2)}) collective-permute-start(f32[256,256]{1,0:T(8,128)S(1)} %slice.89), channel_id=1, source_target_pairs={{0,2},{1,3},{4,0},{5,1},{8,4},{9,5},{12,8},{13,9},{14,12},{15,13},... | collective-permute-start | bytes 786440 | tf_op jit(solution)/shard_map/ppermute | solution.py:542
  158.5 12.2 %copy-start.5 = (f32[512,256]{1,0:T(8,128)}, f32[512,256]{1,0:T(8,128)S(1)}, u32[]{:S(2)}) copy-start(f32[512,256]{1,0:T(8,128)S(1)} %collective-permute-done.29.refs_12_) | copy-start | bytes 1572868
  158.5 10.5 %collective-permute-start.32 = (f32[512,256]{1,0:T(8,128)}, f32[512,256]{1,0:T(8,128)S(1)}, u32[]{:S(2)}, u32[]{:S(2)}) collective-permute-start(f32[512,256]{1,0:T(8,128)} %collective-permute-done.23.refs_6_), channel_id=1, source_target_pairs={{0,1},{1,0},{2,3},{3,2},{4,5},{5,4},{6,7},{7,6},{8,9},{9,8},{10,11... | collective-permute-start | bytes 1572872 | tf_op jit(solution)/shard_map/ppermute | solution.py:545
  158.5 10.5 %collective-permute-start.33 = (f32[512,256]{1,0:T(8,128)}, f32[512,256]{1,0:T(8,128)S(1)}, u32[]{:S(2)}, u32[]{:S(2)}) collective-permute-start(f32[512,256]{1,0:T(8,128)} %collective-permute-done.24.refs_7_), channel_id=1, source_target_pairs={{0,1},{1,0},{2,3},{3,2},{4,5},{5,4},{6,7},{7,6},{8,9},{9,8},{10,11... | collective-permute-start | bytes 1572872 | tf_op jit(solution)/shard_map/ppermute | solution.py:545
  162.8 7.9 %copy-start.10 = (f32[256,256]{1,0:T(8,128)}, f32[256,256]{1,0:T(8,128)S(1)}, u32[]{:S(2)}) copy-start(f32[256,256]{1,0:T(8,128)S(1)} %collective-permute-done.27.refs_10_) | copy-start | bytes 786436
  162.8 6.2 %collective-permute-start.34 = (f32[512,256]{1,0:T(8,128)S(1)}, f32[512,256]{1,0:T(8,128)}, u32[]{:S(2)}, u32[]{:S(2)}) collective-permute-start(f32[512,256]{1,0:T(8,128)S(1)} %collective-permute-done.25.refs_8_), channel_id=1, source_target_pairs={{0,1},{1,0},{2,3},{3,2},{4,5},{5,4},{6,7},{7,6},{8,9},{9,8},{10,11... | collective-permute-start | bytes 1572872 | tf_op jit(solution)/shard_map/ppermute | solution.py:545
  164.4 4.6 %collective-permute-start.35 = (f32[512,256]{1,0:T(8,128)S(1)}, f32[512,256]{1,0:T(8,128)}, u32[]{:S(2)}, u32[]{:S(2)}) collective-permute-start(f32[512,256]{1,0:T(8,128)S(1)} %collective-permute-done.26.refs_9_), channel_id=1, source_target_pairs={{0,1},{1,0},{2,3},{3,2},{4,5},{5,4},{6,7},{7,6},{8,9},{9,8},{10,11... | collective-permute-start | bytes 1572872 | tf_op jit(solution)/shard_map/ppermute | solution.py:545
  168.4 1.7 collective-permute-start.36
  168.9 1.8 copy-start.8
  168.9 1.7 collective-permute-start.37
  169.0 1.7 copy-start.9
  170.1 0.7 copy-start.11
  170.8 0.7 copy-start.12
Sparse Core Ops, SparseCore 0:
  48.3 56.5 reduce-scatter.1

commit v7 on v6

--- a/solution.py
+++ b/solution.py
@@ -158,26 +158,30 @@
     ]
 
 
-def solve_kernel(inverse_ref, panel_ref, factor_ref, weight_ref):
+def solve_kernel(inverse_ref, first_ref, second_ref, factor_ref, weight_0, weight_1):
+    half = first_ref.shape[0]
     inverse = inverse_ref[...]
-    rows = dot_split(split(inverse), split(panel_ref[...])).T
+    panel = jnp.concatenate([first_ref[...], second_ref[...]], axis=0)
+    rows = dot_split(split(inverse), split(panel)).T
     factor_ref[...] = rows
-    weight_ref[...] = dot_split(split(rows), split(inverse))
-
-
-def solve_rows(inverse, panel):
-    width, owned = panel.shape
-    shape = jax.ShapeDtypeStruct((owned, width), jnp.float32)
+    weights = dot_split(split(rows), split(inverse))
+    weight_0[...] = weights[:, :half]
+    weight_1[...] = weights[:, half:]
+
+
+def solve_rows(inverse, first, second):
+    half, owned = first.shape
+    shapes = [jax.ShapeDtypeStruct((owned, width), jnp.float32) for width in (2 * half, half, half)]
     return pl.pallas_call(
         solve_kernel,
-        out_shape=(shape, shape),
-        in_specs=vmem(2),
-        out_specs=vmem(2),
+        out_shape=shapes,
+        in_specs=vmem(3),
+        out_specs=vmem(3),
         cost_estimate=pl.CostEstimate(
-            flops=12 * owned * width * width, bytes_accessed=8 * width * width, transcendentals=0
+            flops=48 * owned * half * half, bytes_accessed=32 * half * half, transcendentals=0
         ),
         name="solve_rows",
-    )(inverse, panel)
+    )(inverse, first, second)
 
 
 def pack(block):
@@ -203,7 +207,7 @@
 
 def pick_kernel(
     counts_ref, cols_ref, weights_ref, prior_ref, rows_ref,
-    scaled_ref, local_ref, given_ref, kept_ref,
+    scaled_ref, local_0, local_1, given_ref, kept_ref,
     pick, picked, block, held, prior_sem,
 ):
     step, last = pl.program_id(0), pl.num_programs(0) - 1
@@ -252,7 +256,8 @@
             picked[...] += jnp.dot(both, pick[at, :], preferred_element_type=jnp.float32)
 
         local = (picked[:owned] + picked[owned : 2 * owned]).T
-        local_ref[...] = local
+        local_0[...] = local[: width // 2]
+        local_1[...] = local[width // 2 :]
         chosen = chosen_rows(place * owned, owned, cols_ref[...])
         total = block[...] + sum(
             jnp.dot(part, chosen, preferred_element_type=jnp.float32) for part in split(local)
@@ -268,6 +273,7 @@
     width = panel_cols.shape[0]
     owned = prior.shape[0]
     tall = 512
+    local = jax.ShapeDtypeStruct((width // 2, owned), jnp.float32)
     rows = jax.ShapeDtypeStruct((TILE, 5 * TILE), jnp.float32)
     whole = lambda shape: pl.BlockSpec(shape, lambda i: (0, 0))
     return pl.pallas_call(
@@ -280,14 +286,10 @@
             pl.BlockSpec(memory_space=pl.ANY),
             pl.BlockSpec((tall, order), lambda i: (i, 0)),
         ],
-        out_specs=[pl.BlockSpec((width, tall), lambda i: (0, i)), whole((width, owned))]
+        out_specs=[pl.BlockSpec((width, tall), lambda i: (0, i))]
+        + [whole(local.shape)] * 2
         + [whole(rows.shape)] * 2,
-        out_shape=[
-            jax.ShapeDtypeStruct((width, depth), jnp.bfloat16),
-            jax.ShapeDtypeStruct((width, owned), jnp.float32),
-            rows,
-            rows,
-        ],
+        out_shape=[jax.ShapeDtypeStruct((width, depth), jnp.bfloat16)] + [local] * 2 + [rows] * 2,
         scratch_shapes=[
             pltpu.VMEM((order, width), jnp.bfloat16),
             pltpu.VMEM((tall, width), jnp.float32),
@@ -309,16 +311,15 @@
     table_ref, scaled_ref, rows_ref, given_0, given_1, kept_0, kept_1, total, sems
 ):
     step, last = pl.program_id(0), pl.num_programs(0) - 1
-    count, cut = given_0.shape[0], given_0.shape[1]
-    width, owned = total.shape[1], total.shape[2]
+    count, half, owned = given_0.shape
     wide = 4
-    base = 4 * count * lax.axis_index("scen")
+    base = 2 * count * lax.axis_index("scen")
 
     def stores(n, which):
         refs = ((given_0, given_1), (kept_0, kept_1))[which]
-        for h, (ref, rows) in enumerate(zip(refs, (pl.ds(0, cut), pl.ds(cut, width - cut)))):
-            slot = table_ref[base + 2 * count + h * count + lax.rem(n, count)]
-            yield pltpu.make_async_copy(total.at[n, rows], ref.at[slot], sems.at[n, h])
+        for h, ref in enumerate(refs):
+            rows = total.at[n, pl.ds(h * half, half)]
+            yield pltpu.make_async_copy(rows, ref.at[lax.rem(n, count)], sems.at[n, h])
 
     for which in range(2):
 
@@ -360,13 +361,11 @@
                     store.wait()
 
 
-def gram_blocks(table, count, cut, owned, scaled, scenario_rows):
+def gram_blocks(table, count, owned, scaled, scenario_rows):
     depth, order = scenario_rows.shape
     width = scaled.shape[0]
     tall = 512
-    shapes = [
-        jax.ShapeDtypeStruct((count, rows, owned), jnp.float32) for rows in (cut, width - cut)
-    ]
+    pieces = jax.ShapeDtypeStruct((count, width // 2, owned), jnp.float32)
     return pl.pallas_call(
         gram_kernel,
         grid=(depth // tall,),
@@ -376,7 +375,7 @@
             pl.BlockSpec((tall, order), lambda i: (i, 0)),
         ],
         out_specs=[pl.BlockSpec(memory_space=pl.ANY)] * 4,
-        out_shape=shapes * 2,
+        out_shape=[pieces] * 4,
         scratch_shapes=[
             pltpu.VMEM((2 * count, width, owned), jnp.float32),
             pltpu.SemaphoreType.DMA((2 * count, 2)),
@@ -500,26 +499,20 @@
 
 def tables(chips):
     ring, far, lines = RINGS[chips], chips // 2, chips // 2
-    offsets = work_offsets(far)
     back = [0] + [-way * d for d in range(1, far) for way in (1, -1)] + [far]
-    fronts, updates, factors = [], [], []
+    grams, updates, factors = [], [], []
     for place in range(2 * chips):
         chip, core = place // 2, place % 2
         z, y, at = chip // 2, chip % 2, ring.index(chip)
-        where = [(at + offset) % chips for offset in offsets]
-        fronts += [2 * ring[q] + c for c in (1 - core, core) for q in where]
-        fronts += list(range(chips)) + where
-        where = [(at + offset) % chips for offset in back]
-        updates += [2 * ring[q] + c for c in (core, 1 - core) for q in where]
+        grams += [2 * q + c for c in (1 - core, core) for q in ring]
+        updates += [
+            2 * ring[(at + offset) % chips] + c for c in (core, 1 - core) for offset in back
+        ]
         factors += [
             (2 * c + w) * lines + (z - by) % lines
             for c in (core, 1 - core) for w in (y, 1 - y) for by in range(lines)
         ]
-    return [jnp.array(table, jnp.int32) for table in (fronts, updates, factors)]
-
-
-def work_offsets(far):
-    return [far] + [way * d for d in range(far - 1, 0, -1) for way in (1, -1)] + [0]
+    return [jnp.array(table, jnp.int32) for table in (grams, updates, factors)]
 
 
 def shards_on_ring(scenario_rows, row_weights, row_counts, panel_cols, regular, prior_schur):
@@ -527,13 +520,12 @@
     chips = parts // 2
     far = lines = chips // 2
     owned = prior_schur.shape[0]
-    cut = panel_cols.shape[0] // 4
+    half = panel_cols.shape[0] // 2
     place = lax.axis_index("scen")
     y, z = place // 2 % 2, place // 4
     ring = RINGS[chips]
     groups = [[2 * chip + c for chip in ring] for c in range(2)]
-    offsets = work_offsets(far)
-    front_table, update_table, factor_table = tables(chips)
+    gram_table, update_table, factor_table = tables(chips)
 
     def step(values, way):
         pairs = [
@@ -552,75 +544,73 @@
     def shift(values, by):
         return lax.ppermute(values, "scen", [(d, (d + 4 * by) % parts) for d in range(parts)])
 
-    scaled, local, block_given, block_kept = pick_columns(
+    scaled, local_0, local_1, block_given, block_kept = pick_columns(
         row_counts, panel_cols, row_weights, prior_schur, scenario_rows
     )
     block_given, scaled = together((block_given, scaled))
     block_got = swap(block_given, 1)
     given_0, given_1, kept_0, kept_1 = gram_blocks(
-        front_table, chips, cut, owned, scaled, scenario_rows
-    )
-    block_got, given_0, given_1 = together((block_got, given_0, given_1))
+        gram_table, chips, owned, scaled, scenario_rows
+    )
+    block_got, given_0 = together((block_got, given_0))
     block = (block_kept + block_got).reshape(2, lines, -1, block_kept.shape[1])
-    beside = slab(block, 1 - y)
-    got_1, got_0, beside = swap(given_1, 1), swap(given_0, 1), swap(beside, 2)
-    got_1, got_0, beside = together((got_1, got_0, beside))
-
-    summed = lax.psum_scatter(
-        kept_1 + got_1, "scen", scatter_dimension=0, axis_index_groups=groups
-    )
-
-    def partial(offset):
-        n = offsets.index(offset)
-        return kept_0[n] + got_0[n]
-
-    side = cut // 2
+    got_0 = swap(given_0, 1)
+    beside = swap(slab(block, 1 - y), 2)
+
+    def sum_rows(values):
+        return lax.psum_scatter(values, "scen", scatter_dimension=0, axis_index_groups=groups)
+
+    got_0, given_1 = together((got_0, given_1))
+    panel_0 = sum_rows(kept_0 + got_0)
+    got_1 = swap(given_1, 1)
     block = slab(block, y) + beside
     beside = [slab(block, (z + by) % lines) for by in range(1, lines)]
-    arrived = None
-    for d in range(far, 0, -1):
-        if d == far:
-            ahead = [partial(far)[:side], partial(far)[side:]]
-        else:
-            ahead = [partial(way * d) + arrived[n] for n, way in enumerate((1, -1))]
-        ahead, beside = together((ahead, beside))
-        arrived = [step(ahead[0], 1), step(ahead[1], -1)]
-        if d == far:
-            beside = [shift(beside[by - 1], by) for by in range(1, lines)]
-        elif d == far - 1:
-            beside = [beside] + [shift(beside, by) for by in range(1, lines)]
-        elif d == far - 2:
-            beside = [beside] + [swap(beside, bit) for bit in (2, 1, 3)]
-        else:
-            beside = stages[0](None)
-        arrived, beside = together((arrived, beside))
-        if d == far:
-            arrived = [
-                jnp.pad(arrived[0], ((0, side), (0, 0))), jnp.pad(arrived[1], ((side, 0), (0, 0)))
-            ]
-            beside = sum(beside) + slab(block, z)
-        elif d == far - 1:
-            beside = jnp.stack(beside)
-        elif d == far - 2:
-            stages = factor_stages(factor_table, beside, regular)
-    arrived, summed, work = together((arrived, summed, beside))
-    panel = jnp.concatenate([partial(0) + arrived[0] + arrived[1], summed]) + local
-
-    shards = [panel]
-    ahead = [panel, panel]
-    for d in range(1, far + 1):
-        if d == far:
-            middle = panel.shape[0] // 2
-            ahead = [ahead[0][:middle], ahead[1][middle:]]
+    beside, got_1 = together(([shift(beside[by - 1], by) for by in range(1, lines)], got_1))
+    panel_1 = sum_rows(kept_1 + got_1)
+    beside = sum(beside) + slab(block, z)
+    beside = jnp.stack([beside] + [shift(beside, by) for by in range(1, lines)])
+    beside = [beside] + [swap(beside, bit) for bit in (2, 1, 3)]
+    stages = factor_stages(factor_table, beside, regular)
+    work = stages[1](stages[0](None))
+    panel_0, work = together((panel_0, work))
+    panel_0 += local_0
+
+    shards_0 = [panel_0]
+    ahead = [panel_0, panel_0]
+    for d in range(1, far):
         ahead, work = together((ahead, work))
         ahead = [step(ahead[0], 1), step(ahead[1], -1)]
-        work = stages[d](work) if d < len(stages) else solve_rows(work, panel)
+        if 1 + d < len(stages):
+            work = stages[1 + d](work)
         ahead, work = together((ahead, work))
-        shards += ahead
-    sources = shards + [swap(piece, 1) for piece in shards]
-
-    factor_rows, weights = work
-    return update_rows(update_table, parts, weights, prior_schur, sources), factor_rows
+        shards_0 += ahead
+    panel_1, ahead, work = together((panel_1, ahead, work))
+    panel_1 += local_1
+    shards_1 = [panel_1]
+    ahead, (panel_1, work) = together((ahead, (panel_1, work)))
+    ahead = [ahead[0][: half // 2], ahead[1][half // 2 :]]
+    last = [step(ahead[0], 1), step(ahead[1], -1)]
+    ahead = [step(panel_1, 1), step(panel_1, -1)]
+    ahead, last, work = together((ahead, last, solve_rows(work, panel_0, panel_1)))
+    shards_0 += last
+    shards_1 += ahead
+    factor_rows, weights_0, weights_1 = work
+
+    def sources(shards):
+        return shards + [swap(piece, 1) for piece in shards]
+
+    updated = prior_schur
+    sources_0 = sources(shards_0)
+    for d in range(2, far + 1):
+        if d == far:
+            ahead = [ahead[0][: half // 2], ahead[1][half // 2 :]]
+        ahead, updated = together((ahead, updated))
+        ahead = [step(ahead[0], 1), step(ahead[1], -1)]
+        if d == far - 1:
+            updated = update_rows(update_table, parts, weights_0, updated, sources_0)
+        ahead, updated = together((ahead, updated))
+        shards_1 += ahead
+    return update_rows(update_table, parts, weights_1, updated, sources(shards_1)), factor_rows
 
 
 def shards_by_groups(scenario_rows, row_weights, row_counts, panel_cols, regular, prior_schur):
@@ -655,7 +645,8 @@
     inverse = None
     for stage in factor_stages(table, [block, block_other], regular):
         inverse = stage(inverse)
-    factor_rows, weights = solve_rows(inverse, panel_rows.T)
+    factor_rows, *weights = solve_rows(inverse, panel_rows.T[:half], panel_rows.T[half:])
+    weights = jnp.concatenate(weights, axis=1)
     even = jnp.where(core == 0, panel_half, panel_rest)
     odd = jnp.where(core == 0, panel_rest, panel_half)
     panel = jnp.stack([even, odd], axis=1).reshape(order, width)

time: 190 us -> 199 us (1.047)
  Pallas kernels: 70.8 us -> 76.8 us
  waiting for transfers between devices: 54.8 us -> 60.4 us
  other arithmetic: 11.3 us -> 8.66 us
    ppermute x16 -> x25, waiting for transfers between devices: 6.47 us -> 21.1 us  [swap(): return lax.ppermute(values, 'scen', [(d, d ^ bit) for d in range(parts)])]
    pallas_call x1 -> x2, Pallas kernels: 11.4 us -> 17.6 us  [update_rows(): pl.pallas_call(lambda *refs: update_kernel(count, *refs), out_shape=jax.S...]
    ppermute x16, waiting for transfers between devices: 33.7 us -> 27.7 us  [step(): return lax.ppermute(values, 'scen', pairs)]
    ppermute x6, waiting for transfers between devices: 14.6 us -> 11.5 us  [shift(): lax.ppermute(values, 'scen', [(d, (d + 4 * by) % parts) for d in range(pa...]
    add x7 -> x4, other arithmetic: 10.2 us -> 8.58 us  [the longest x1 3.31 us: shards_on_ring(): panel_0 = sum_rows(kept_0 + got_0)]
    ppermute x16 -> x25, starting transfers between devices: 8.51 us -> 8.96 us  [swap(): return lax.ppermute(values, 'scen', [(d, d ^ bit) for d in range(parts)])]
  transfers between devices with their start and end apart: 39 -> 49, of which waited for: 19 -> 21; matrix products, arithmetic and copies ran while one was open for 3% -> 2% of each run, Pallas kernels for 24% -> 27%
where the time goes in v7:
time: 199 us; the launch traced here: 198 us
  Pallas kernels  76.8 us (39%)
  waiting for transfers between devices  60.4 us (30%)
  starting transfers between devices  33.9 us (17%)
  between operations  15.1 us (8%)
  other arithmetic  8.66 us (4%)
  local copies, waits for them, and re-layouts  3.48 us (2%)
    ppermute x16, waiting for transfers between devices, step(): return lax.ppermute(values, 'scen', pairs)  27.7 us
    ppermute x25, waiting for transfers between devices, swap(): return lax.ppermute(values, 'scen', [(d, d ^ bit) for d in range(parts)])  21.1 us
    pallas_call x2, Pallas kernels, update_rows(): pl.pallas_call(lambda *refs: update_kernel(count, *refs), out_shape=jax.S...  17.6 us
    ppermute x16, starting transfers between devices, step(): return lax.ppermute(values, 'scen', pairs)  16.6 us
    pallas_call x1, Pallas kernels, pick_columns(): pl.pallas_call(pick_kernel, grid=(depth // tall,), in_specs=[pl.BlockSpec...  14.8 us
    pallas_call x2, Pallas kernels, shards_on_ring(): work = stages[1 + d](work)  14.1 us
    ppermute x6, waiting for transfers between devices, shift(): lax.ppermute(values, 'scen', [(d, (d + 4 * by) % parts) for d in range(pa...  11.5 us
    pallas_call x1, Pallas kernels, gram_blocks(): pl.pallas_call(gram_kernel, grid=(depth // tall,), in_specs=[pl.BlockSpec...  11.2 us
  transfers between devices with their start and end apart: 49, of which 21 were waited for; matrix products, arithmetic and copies ran while one was open for 2% of the time, Pallas kernels for 27%

profile of v7, /device:TPU:0, one launch (start us, length us, event | category | flops | bytes accessed | tf_op | source)
XLA Modules:
  0.0 198.3 jit_solution(15676688911147998423)
XLA Ops:
  7.9 14.8 %pick_columns.1 = (bf16[512,1024]{1,0:T(8,128)(2,1)}, f32[256,256]{1,0:T(8,128)}, f32[256,256]{1,0:T(8,128)}, f32[128,640]{1,0:T(8,128)}, f32[128,640]{1,0:T(8,128)}) custom-call(s32[1]{0:T(128)S(6)} %copy.11.counts_ref, s32[1,512]{1,0:T(1,128)} %bitcast.31, f32[1,1024]{1,0:T(1,128)} %bitcast.30, f32[256,4096]{1,0:T(8,128)} %refs_2_, bf16[1024,4096]{1,0:T(8,128)(2,1)} %rows_ref.3), custom_call_target="tpu_custom_call" | custom-call | flops 6442450944 | bytes 12582912 | tf_op jit(solution)/shard_map/pick_columns/pallas_call | solution.py:279
  22.6 0.5 collective-permute-start
  23.1 11.2 %gram_blocks.1 = (f32[8,256,256]{2,1,0:T(8,128)}, f32[8,256,256]{2,1,0:T(8,128)}, f32[8,256,256]{2,1,0:T(8,128)}, f32[8,256,256]{2,1,0:T(8,128)}) custom-call(s32[256]{0:T(256)} %constant.79.clone.table_ref, bf16[512,1024]{1,0:T(8,128)(2,1)} %get-tuple-element.76.scaled_ref, bf16[1024,4096]{1,0:T(8,128)(2,1)} %rows_ref.3), custom_call_target="tpu_custom_call" | custom-call | flops 4294967296 | bytes 16777216 | tf_op jit(solution)/shard_map/gram_blocks/pallas_call | solution.py:369
  34.4 4.3 %collective-permute-done.5 = f32[8,256,256]{2,1,0:T(8,128)S(1)} collective-permute-done((f32[8,256,256]{2,1,0:T(8,128)}, f32[8,256,256]{2,1,0:T(8,128)S(1)}, u32[]{:S(2)}, u32[]{:S(2)}) %collective-permute-start.5) | collective-permute-done | bytes 2097184 | tf_op jit(solution)/shard_map/ppermute | solution.py:537
  38.7 3.3 %add.91 = f32[8,256,256]{2,1,0:T(8,128)} add(f32[8,256,256]{2,1,0:T(8,128)} %get-tuple-element.86, f32[8,256,256]{2,1,0:T(8,128)S(1)} %collective-permute-done.5) | non-fusion elementwise | flops 524288 | bytes 6291456 | tf_op jit(solution)/shard_map/add | solution.py:564
  42.1 0.2 collective-permute-start.6
  42.3 0.7 copy-done.7
  43.1 2.7 %collective-permute-start.1 = (f32[4,16,640]{2,1,0:T(8,128)S(1)}, f32[4,16,640]{2,1,0:T(8,128)S(1)}, u32[]{:S(2)}, u32[]{:S(2)}) collective-permute-start(f32[4,16,640]{2,1,0:T(8,128)S(1)} %dynamic-slice_bitcast_fusion), channel_id=1, source_target_pairs={{0,2},{1,3},{2,0},{3,1},{4,6},{5,7},{6,4},{7,5},{8,10},{9,11},{10,... | collective-permute-start | bytes 491528 | tf_op jit(solution)/shard_map/ppermute | solution.py:537
  45.8 4.7 %collective-permute-done.1 = f32[4,16,640]{2,1,0:T(8,128)S(1)} collective-permute-done((f32[4,16,640]{2,1,0:T(8,128)S(1)}, f32[4,16,640]{2,1,0:T(8,128)S(1)}, u32[]{:S(2)}, u32[]{:S(2)}) %collective-permute-start.1) | collective-permute-done | bytes 163872 | tf_op jit(solution)/shard_map/ppermute | solution.py:537
  50.6 3.9 %collective-permute-start.4 = (f32[16,640]{1,0:T(8,128)S(1)}, f32[16,640]{1,0:T(8,128)S(1)}, u32[]{:S(2)}, u32[]{:S(2)}) collective-permute-start(f32[16,640]{1,0:T(8,128)S(1)} %get-tuple-element.146), channel_id=1, source_target_pairs={{0,12},{1,13},{2,14},{3,15},{4,0},{5,1},{6,2},{7,3},{8,4},{9,5},{1... | collective-permute-start | bytes 122888 | tf_op jit(solution)/shard_map/ppermute | solution.py:545
  54.5 1.0 collective-permute-start.2
  55.5 1.4 collective-permute-done.4
  56.9 4.4 %collective-permute-done.3 = f32[16,640]{1,0:T(8,128)S(1)} collective-permute-done((f32[16,640]{1,0:T(8,128)S(1)}, f32[16,640]{1,0:T(8,128)S(1)}, u32[]{:S(2)}, u32[]{:S(2)}) %collective-permute-start.3) | collective-permute-done | bytes 40992 | tf_op jit(solution)/shard_map/ppermute | solution.py:545
  61.3 3.2 %add.90 = f32[8,256,256]{2,1,0:T(8,128)} add(f32[8,256,256]{2,1,0:T(8,128)S(1)} %copy-done, f32[8,256,256]{2,1,0:T(8,128)} %collective-permute-done.6) | non-fusion elementwise | flops 524288 | bytes 6291456 | tf_op jit(solution)/shard_map/add | solution.py:569
  64.6 0.8 collective-permute-start.9
  65.4 1.4 collective-permute-start.8
  66.8 1.2 collective-permute-start.7
  68.0 1.8 collective-permute-done.9
  69.8 2.5 %collective-permute-done.8 = f32[16,640]{1,0:T(8,128)S(1)} collective-permute-done((f32[16,640]{1,0:T(8,128)S(1)}, f32[16,640]{1,0:T(8,128)S(1)}, u32[]{:S(2)}, u32[]{:S(2)}) %collective-permute-start.8) | collective-permute-done | bytes 40992 | tf_op jit(solution)/shard_map/ppermute | solution.py:545
  72.3 1.4 collective-permute-done.7
  73.7 1.8 collective-permute-start.11
  75.5 0.4 collective-permute-start.10
  75.9 7.0 %collective-permute-done.12.refs_3_ = f32[4,16,640]{2,1,0:T(8,128)S(1)} collective-permute-done((f32[4,16,640]{2,1,0:T(8,128)S(1)}, f32[4,16,640]{2,1,0:T(8,128)S(1)}, u32[]{:S(2)}, u32[]{:S(2)}) %collective-permute-start.12) | collective-permute-done | bytes 163872 | tf_op jit(solution)/shard_map/ppermute | solution.py:537
  82.9 3.8 %collective-permute-done.10.refs_1_ = f32[4,16,640]{2,1,0:T(8,128)S(1)} collective-permute-done((f32[4,16,640]{2,1,0:T(8,128)S(1)}, f32[4,16,640]{2,1,0:T(8,128)S(1)}, u32[]{:S(2)}, u32[]{:S(2)}) %collective-permute-start.10) | collective-permute-done | bytes 163872 | tf_op jit(solution)/shard_map/ppermute | solution.py:537
  86.7 0.7 copy-done.41
  87.4 7.7 %factor_0.1.work_ref = f32[512,512]{1,0:T(8,128)} custom-call(s32[256]{0:T(256)} %constant.81.clone.table_ref, f32[1,512]{1,0:T(1,128)} %bitcast.32, f32[4,16,640]{2,1,0:T(8,128)} %copy-done.31, f32[4,16,640]{2,1,0:T(8,128)} %copy-done.41, f32[4,16,640]{2,1,0:T(8,128)} %copy-done.40, f32[4,16,640]{2,1,0:T(8,128)} %copy-done.39), custom_call_target="tpu_custom_call" | custom-call | flops 6710886400 | bytes 2097152 | tf_op jit(solution)/shard_map/factor_0/pallas_call | solution.py:143
  95.0 7.6 %factor_1.1.work_ref = f32[512,512]{1,0:T(8,128)} custom-call(f32[512,512]{1,0:T(8,128)} %factor_0.1.work_ref), custom_call_target="tpu_custom_call" | custom-call | flops 6710886400 | bytes 2097152 | tf_op jit(solution)/shard_map/factor_1/pallas_call | solution.py:574
  102.6 1.0 add.96.first_ref.refs_3_
  103.7 2.0 %collective-permute-start.14 = (f32[256,256]{1,0:T(8,128)S(1)}, f32[256,256]{1,0:T(8,128)S(1)}, u32[]{:S(2)}, u32[]{:S(2)}) collective-permute-start(f32[256,256]{1,0:T(8,128)S(1)} %add.96.first_ref.refs_3_), channel_id=1, source_target_pairs={{0,2},{1,3},{4,0},{5,1},{8,4},{9,5},{12,8},{13,9},{14,12},{15,13},... | collective-permute-start | bytes 786440 | tf_op jit(solution)/shard_map/ppermute | solution.py:534
  105.7 7.3 %factor_2.1.work_ref = f32[512,512]{1,0:T(8,128)} custom-call(f32[512,512]{1,0:T(8,128)} %factor_1.1.work_ref), custom_call_target="tpu_custom_call" | custom-call | flops 6710886400 | bytes 2097152 | tf_op jit(solution)/shard_map/factor_2/pallas_call | solution.py:584
  113.0 3.7 %collective-permute-done.13.refs_4_ = f32[256,256]{1,0:T(8,128)S(1)} collective-permute-done((f32[256,256]{1,0:T(8,128)S(1)}, f32[256,256]{1,0:T(8,128)S(1)}, u32[]{:S(2)}, u32[]{:S(2)}) %collective-permute-start.13) | collective-permute-done | bytes 262176 | tf_op jit(solution)/shard_map/ppermute | solution.py:534
  116.7 1.7 collective-permute-done.14.refs_5_
  118.6 1.8 collective-permute-start.16
  120.4 6.9 %factor_3.1.inverse_ref = f32[512,512]{1,0:T(8,128)} custom-call(f32[512,512]{1,0:T(8,128)} %factor_2.1.work_ref), custom_call_target="tpu_custom_call" | custom-call | flops 6710886400 | bytes 2097152 | tf_op jit(solution)/shard_map/factor_3/pallas_call | solution.py:584
  127.3 1.1 collective-permute-done.15.refs_6_
  128.3 0.5 collective-permute-start.17
  128.8 1.6 collective-permute-start.18
  130.4 5.7 %collective-permute-done.17.refs_8_ = f32[256,256]{1,0:T(8,128)S(1)} collective-permute-done((f32[256,256]{1,0:T(8,128)S(1)}, f32[256,256]{1,0:T(8,128)S(1)}, u32[]{:S(2)}, u32[]{:S(2)}) %collective-permute-start.17) | collective-permute-done | bytes 262176 | tf_op jit(solution)/shard_map/ppermute | solution.py:534
  136.2 1.1 add.97.second_ref.refs_3_
  137.3 1.7 collective-permute-start.20
  139.0 0.7 collective-permute-start.22
  139.7 1.4 collective-permute-start.21
  141.2 0.4 collective-permute-start.19
  141.5 5.4 %collective-permute-done.22.refs_11_ = f32[128,256]{1,0:T(8,128)S(1)} collective-permute-done((f32[128,256]{1,0:T(8,128)S(1)}, f32[128,256]{1,0:T(8,128)S(1)}, u32[]{:S(2)}, u32[]{:S(2)}) %collective-permute-start.22) | collective-permute-done | bytes 131104 | tf_op jit(solution)/shard_map/ppermute | solution.py:534
  147.0 0.5 collective-permute-start.29
  147.6 3.9 %solve_rows.1 = (f32[256,512]{1,0:T(8,128)}, f32[256,256]{1,0:T(8,128)}, f32[256,256]{1,0:T(8,128)}) custom-call(f32[512,512]{1,0:T(8,128)} %factor_3.1.inverse_ref, f32[256,256]{1,0:T(8,128)} %copy-done.2, f32[256,256]{1,0:T(8,128)} %copy-done.1), custom_call_target="tpu_custom_call" | custom-call | flops 805306368 | bytes 2097152 | tf_op jit(solution)/shard_map/solve_rows/pallas_call | solution.py:175
  151.7 1.9 collective-permute-start.24
  153.7 0.5 collective-permute-start.32
  154.3 5.9 %collective-permute-done.23.refs_6_ = f32[256,256]{1,0:T(8,128)S(1)} collective-permute-done((f32[256,256]{1,0:T(8,128)S(1)}, f32[256,256]{1,0:T(8,128)S(1)}, u32[]{:S(2)}, u32[]{:S(2)}) %collective-permute-start.23) | collective-permute-done | bytes 262176 | tf_op jit(solution)/shard_map/ppermute | solution.py:534
  160.3 0.5 collective-permute-start.35
  160.7 0.6 collective-permute-start.25
  161.4 1.4 collective-permute-start.26
  162.8 0.5 collective-permute-start.39
  163.5 0.4 copy-done.36
  163.9 8.8 %update_rows.2.refs_2_ = f32[256,4096]{1,0:T(8,128)} custom-call(s32[256]{0:T(256)} %constant.80.clone.refs_0_, f32[256,256]{1,0:T(8,128)} %get-tuple-element.126.refs_1_, f32[256,4096]{1,0:T(8,128)} %refs_2_, f32[256,256]{1,0:T(8,128)} %copy-done.2, f32[256,256]{1,0:T(8,128)} %copy-done.12, f32[256,256]{1,0:T(8,128)} %copy-done.13, f32[256,256]{1,0:T(8,128)} %copy-done.15, ...), custom_call_target="tpu_custom_call" | custom-call | flops 1610612736 | bytes 12582912 | tf_op jit(solution)/shard_map/update_rows/pallas_call | solution.py:438
  173.0 0.7 collective-permute-start.36
  173.7 1.4 collective-permute-start.37
  175.2 3.7 %collective-permute-done.36.refs_10_ = f32[128,256]{1,0:T(8,128)S(1)} collective-permute-done((f32[128,256]{1,0:T(8,128)S(1)}, f32[128,256]{1,0:T(8,128)S(1)}, u32[]{:S(2)}, u32[]{:S(2)}) %collective-permute-start.36) | collective-permute-done | bytes 131104 | tf_op jit(solution)/shard_map/ppermute | solution.py:534
  178.9 0.4 collective-permute-done.37.refs_11_
  179.4 0.4 collective-permute-start.45
  179.9 1.1 collective-permute-done.45.refs_19_
  181.3 0.4 copy-done.37
  182.0 0.7 copy-done.30
  182.7 8.8 %update_rows.3 = f32[256,4096]{1,0:T(8,128)} custom-call(s32[256]{0:T(256)} %constant.80.clone.refs_0_, f32[256,256]{1,0:T(8,128)} %get-tuple-element.118.refs_1_, f32[256,4096]{1,0:T(8,128)} %update_rows.2.refs_2_, f32[256,256]{1,0:T(8,128)} %copy-done.1, f32[256,256]{1,0:T(8,128)} %copy-done.11, f32[256,256]{1,0:T(8,128)} %copy-done.10, ...), custom_call_target="tpu_custom_call" | custom-call | flops 1610612736 | bytes 12582912 | tf_op jit(solution)/shard_map/update_rows/pallas_call | solution.py:438
  (143 shorter events, 2.7 us)
Async XLA Ops:
  7.2 95.4 %reduce-scatter.5.cloned.1.call-start = ((), (), s32[]{:S(2)}) async-start(), calls=%async_computation.3 | async-start | bytes 2359296 | tf_op jit(solution)/shard_map/reduce_scatter | solution.py:561
  22.6 11.7 %collective-permute-start = (f32[128,640]{1,0:T(8,128)}, f32[128,640]{1,0:T(8,128)S(1)}, u32[]{:S(2)}, u32[]{:S(2)}) collective-permute-start(f32[128,640]{1,0:T(8,128)} %get-tuple-element.79), channel_id=1, source_target_pairs={{0,1},{1,0},{2,3},{3,2},{4,5},{5,4},{6,7},{7,6},{8,9},{9,8},{10,11... | collective-permute-start | bytes 983048 | tf_op jit(solution)/shard_map/ppermute | solution.py:537
  34.3 4.4 %collective-permute-start.5 = (f32[8,256,256]{2,1,0:T(8,128)}, f32[8,256,256]{2,1,0:T(8,128)S(1)}, u32[]{:S(2)}, u32[]{:S(2)}) collective-permute-start(f32[8,256,256]{2,1,0:T(8,128)} %get-tuple-element.82), channel_id=1, source_target_pairs={{0,1},{1,0},{2,3},{3,2},{4,5},{5,4},{6,7},{7,6},{8,9},{9,8},{10,11... | collective-permute-start | bytes 6291464 | tf_op jit(solution)/shard_map/ppermute | solution.py:537
  42.1 19.3 %copy-start = (f32[8,256,256]{2,1,0:T(8,128)S(1)}, f32[8,256,256]{2,1,0:T(8,128)}, u32[]{:S(2)}) copy-start(f32[8,256,256]{2,1,0:T(8,128)} %get-tuple-element.77) | copy-start | bytes 6291460
  42.1 94.1 %reduce-scatter.3.cloned.1.call-start = ((), (), s32[]{:S(2)}) async-start(), calls=%async_computation.2 | async-start | bytes 2359296 | tf_op jit(solution)/shard_map/reduce_scatter | solution.py:561
  42.1 19.2 %collective-permute-start.6 = (f32[8,256,256]{2,1,0:T(8,128)}, f32[8,256,256]{2,1,0:T(8,128)}, u32[]{:S(2)}, u32[]{:S(2)}) collective-permute-start(f32[8,256,256]{2,1,0:T(8,128)} %get-tuple-element.84), channel_id=1, source_target_pairs={{0,1},{1,0},{2,3},{3,2},{4,5},{5,4},{6,7},{7,6},{8,9},{9,8},{10,11... | collective-permute-start | bytes 6291464 | tf_op jit(solution)/shard_map/ppermute | solution.py:537
  43.1 7.5 %collective-permute-start.1 = (f32[4,16,640]{2,1,0:T(8,128)S(1)}, f32[4,16,640]{2,1,0:T(8,128)S(1)}, u32[]{:S(2)}, u32[]{:S(2)}) collective-permute-start(f32[4,16,640]{2,1,0:T(8,128)S(1)} %dynamic-slice_bitcast_fusion), channel_id=1, source_target_pairs={{0,2},{1,3},{2,0},{3,1},{4,6},{5,7},{6,4},{7,5},{8,10},{9,11},{10,... | collective-permute-start | bytes 491528 | tf_op jit(solution)/shard_map/ppermute | solution.py:537
  50.6 6.3 %collective-permute-start.4 = (f32[16,640]{1,0:T(8,128)S(1)}, f32[16,640]{1,0:T(8,128)S(1)}, u32[]{:S(2)}, u32[]{:S(2)}) collective-permute-start(f32[16,640]{1,0:T(8,128)S(1)} %get-tuple-element.146), channel_id=1, source_target_pairs={{0,12},{1,13},{2,14},{3,15},{4,0},{5,1},{6,2},{7,3},{8,4},{9,5},{1... | collective-permute-start | bytes 122888 | tf_op jit(solution)/shard_map/ppermute | solution.py:545
  54.5 6.8 %collective-permute-start.3 = (f32[16,640]{1,0:T(8,128)S(1)}, f32[16,640]{1,0:T(8,128)S(1)}, u32[]{:S(2)}, u32[]{:S(2)}) collective-permute-start(f32[16,640]{1,0:T(8,128)S(1)} %get-tuple-element.147), channel_id=1, source_target_pairs={{0,8},{1,9},{2,10},{3,11},{4,12},{5,13},{6,14},{7,15},{8,0},{9,1},... | collective-permute-start | bytes 122888 | tf_op jit(solution)/shard_map/ppermute | solution.py:545
  54.5 6.8 %collective-permute-start.2 = (f32[16,640]{1,0:T(8,128)S(1)}, f32[16,640]{1,0:T(8,128)S(1)}, u32[]{:S(2)}, u32[]{:S(2)}) collective-permute-start(f32[16,640]{1,0:T(8,128)S(1)} %get-tuple-element.148), channel_id=1, source_target_pairs={{0,4},{1,5},{2,6},{3,7},{4,8},{5,9},{6,10},{7,11},{8,12},{9,13},{1... | collective-permute-start | bytes 122888 | tf_op jit(solution)/shard_map/ppermute | solution.py:545
  64.6 5.3 %collective-permute-start.9 = (f32[16,640]{1,0:T(8,128)S(1)}, f32[16,640]{1,0:T(8,128)S(1)}, u32[]{:S(2)}, u32[]{:S(2)}) collective-permute-start(f32[16,640]{1,0:T(8,128)S(1)} %bitcast_add_fusion.1), channel_id=1, source_target_pairs={{0,12},{1,13},{2,14},{3,15},{4,0},{5,1},{6,2},{7,3},{8,4},{9,5},{1... | collective-permute-start | bytes 122888 | tf_op jit(solution)/shard_map/ppermute | solution.py:545
  65.4 6.9 %collective-permute-start.8 = (f32[16,640]{1,0:T(8,128)S(1)}, f32[16,640]{1,0:T(8,128)S(1)}, u32[]{:S(2)}, u32[]{:S(2)}) collective-permute-start(f32[16,640]{1,0:T(8,128)S(1)} %bitcast_add_fusion.1), channel_id=1, source_target_pairs={{0,8},{1,9},{2,10},{3,11},{4,12},{5,13},{6,14},{7,15},{8,0},{9,1},... | collective-permute-start | bytes 122888 | tf_op jit(solution)/shard_map/ppermute | solution.py:545
  66.8 6.8 %collective-permute-start.7 = (f32[16,640]{1,0:T(8,128)S(1)}, f32[16,640]{1,0:T(8,128)S(1)}, u32[]{:S(2)}, u32[]{:S(2)}) collective-permute-start(f32[16,640]{1,0:T(8,128)S(1)} %bitcast_add_fusion.1), channel_id=1, source_target_pairs={{0,4},{1,5},{2,6},{3,7},{4,8},{5,9},{6,10},{7,11},{8,12},{9,13},{1... | collective-permute-start | bytes 122888 | tf_op jit(solution)/shard_map/ppermute | solution.py:545
  73.7 13.0 %copy-start.31 = (f32[4,16,640]{2,1,0:T(8,128)}, f32[4,16,640]{2,1,0:T(8,128)S(1)}, u32[]{:S(2)}) copy-start(f32[4,16,640]{2,1,0:T(8,128)S(1)} %pad_maximum_fusion.refs_0_) | copy-start | bytes 491524
  73.7 9.3 %collective-permute-start.12 = (f32[4,16,640]{2,1,0:T(8,128)S(1)}, f32[4,16,640]{2,1,0:T(8,128)S(1)}, u32[]{:S(2)}, u32[]{:S(2)}) collective-permute-start(f32[4,16,640]{2,1,0:T(8,128)S(1)} %pad_maximum_fusion.refs_0_), channel_id=1, source_target_pairs={{0,3},{1,2},{2,1},{3,0},{4,7},{5,6},{6,5},{7,4},{8,11},{9,10},{10,... | collective-permute-start | bytes 491528 | tf_op jit(solution)/shard_map/ppermute | solution.py:537
  73.7 9.2 %collective-permute-start.11 = (f32[4,16,640]{2,1,0:T(8,128)S(1)}, f32[4,16,640]{2,1,0:T(8,128)S(1)}, u32[]{:S(2)}, u32[]{:S(2)}) collective-permute-start(f32[4,16,640]{2,1,0:T(8,128)S(1)} %pad_maximum_fusion.refs_0_), channel_id=1, source_target_pairs={{0,1},{1,0},{2,3},{3,2},{4,5},{5,4},{6,7},{7,6},{8,9},{9,8},{10,11... | collective-permute-start | bytes 491528 | tf_op jit(solution)/shard_map/ppermute | solution.py:537
  75.5 11.2 %collective-permute-start.10 = (f32[4,16,640]{2,1,0:T(8,128)S(1)}, f32[4,16,640]{2,1,0:T(8,128)S(1)}, u32[]{:S(2)}, u32[]{:S(2)}) collective-permute-start(f32[4,16,640]{2,1,0:T(8,128)S(1)} %pad_maximum_fusion.refs_0_), channel_id=1, source_target_pairs={{0,2},{1,3},{2,0},{3,1},{4,6},{5,7},{6,4},{7,5},{8,10},{9,11},{10,... | collective-permute-start | bytes 491528 | tf_op jit(solution)/shard_map/ppermute | solution.py:537
  103.6 37.9 %copy-start.2 = (f32[256,256]{1,0:T(8,128)}, f32[256,256]{1,0:T(8,128)S(1)}, u32[]{:S(2)}) copy-start(f32[256,256]{1,0:T(8,128)S(1)} %add.96.first_ref.refs_3_) | copy-start | bytes 786436
  103.6 13.1 %collective-permute-start.13 = (f32[256,256]{1,0:T(8,128)S(1)}, f32[256,256]{1,0:T(8,128)S(1)}, u32[]{:S(2)}, u32[]{:S(2)}) collective-permute-start(f32[256,256]{1,0:T(8,128)S(1)} %add.96.first_ref.refs_3_), channel_id=1, source_target_pairs={{0,4},{1,5},{4,8},{5,9},{8,12},{9,13},{12,14},{13,15},{14,10},{15,... | collective-permute-start | bytes 786440 | tf_op jit(solution)/shard_map/ppermute | solution.py:534
  103.7 14.7 %collective-permute-start.14 = (f32[256,256]{1,0:T(8,128)S(1)}, f32[256,256]{1,0:T(8,128)S(1)}, u32[]{:S(2)}, u32[]{:S(2)}) collective-permute-start(f32[256,256]{1,0:T(8,128)S(1)} %add.96.first_ref.refs_3_), channel_id=1, source_target_pairs={{0,2},{1,3},{4,0},{5,1},{8,4},{9,5},{12,8},{13,9},{14,12},{15,13},... | collective-permute-start | bytes 786440 | tf_op jit(solution)/shard_map/ppermute | solution.py:534
  112.9 23.2 %copy-start.8 = (f32[256,256]{1,0:T(8,128)S(1)}, f32[256,256]{1,0:T(8,128)}, u32[]{:S(2)}) copy-start(f32[256,256]{1,0:T(8,128)} %get-tuple-element.109) | copy-start | bytes 786436
  116.7 30.3 %copy-start.12 = (f32[256,256]{1,0:T(8,128)}, f32[256,256]{1,0:T(8,128)S(1)}, u32[]{:S(2)}) copy-start(f32[256,256]{1,0:T(8,128)S(1)} %collective-permute-done.13.refs_4_) | copy-start | bytes 786436
  118.4 28.6 %copy-start.13 = (f32[256,256]{1,0:T(8,128)}, f32[256,256]{1,0:T(8,128)S(1)}, u32[]{:S(2)}) copy-start(f32[256,256]{1,0:T(8,128)S(1)} %collective-permute-done.14.refs_5_) | copy-start | bytes 786436
  118.4 10.0 %collective-permute-start.15 = (f32[256,256]{1,0:T(8,128)S(1)}, f32[256,256]{1,0:T(8,128)S(1)}, u32[]{:S(2)}, u32[]{:S(2)}) collective-permute-start(f32[256,256]{1,0:T(8,128)S(1)} %collective-permute-done.13.refs_4_), channel_id=1, source_target_pairs={{0,4},{1,5},{4,8},{5,9},{8,12},{9,13},{12,14},{13,15},{14,10},{15,... | collective-permute-start | bytes 786440 | tf_op jit(solution)/shard_map/ppermute | solution.py:534
  118.6 9.8 %collective-permute-start.16 = (f32[256,256]{1,0:T(8,128)S(1)}, f32[256,256]{1,0:T(8,128)S(1)}, u32[]{:S(2)}, u32[]{:S(2)}) collective-permute-start(f32[256,256]{1,0:T(8,128)S(1)} %collective-permute-done.14.refs_5_), channel_id=1, source_target_pairs={{0,2},{1,3},{4,0},{5,1},{8,4},{9,5},{12,8},{13,9},{14,12},{15,13},... | collective-permute-start | bytes 786440 | tf_op jit(solution)/shard_map/ppermute | solution.py:534
  128.3 23.2 %copy-start.15 = (f32[256,256]{1,0:T(8,128)}, f32[256,256]{1,0:T(8,128)S(1)}, u32[]{:S(2)}) copy-start(f32[256,256]{1,0:T(8,128)S(1)} %collective-permute-done.15.refs_6_) | copy-start | bytes 786436
  128.3 25.3 %copy-start.17 = (f32[256,256]{1,0:T(8,128)}, f32[256,256]{1,0:T(8,128)S(1)}, u32[]{:S(2)}) copy-start(f32[256,256]{1,0:T(8,128)S(1)} %collective-permute-done.16.refs_7_) | copy-start | bytes 786436
  128.3 7.8 %collective-permute-start.17 = (f32[256,256]{1,0:T(8,128)S(1)}, f32[256,256]{1,0:T(8,128)S(1)}, u32[]{:S(2)}, u32[]{:S(2)}) collective-permute-start(f32[256,256]{1,0:T(8,128)S(1)} %collective-permute-done.15.refs_6_), channel_id=1, source_target_pairs={{0,4},{1,5},{4,8},{5,9},{8,12},{9,13},{12,14},{13,15},{14,10},{15,... | collective-permute-start | bytes 786440 | tf_op jit(solution)/shard_map/ppermute | solution.py:534
  128.8 7.3 %collective-permute-start.18 = (f32[256,256]{1,0:T(8,128)S(1)}, f32[256,256]{1,0:T(8,128)S(1)}, u32[]{:S(2)}, u32[]{:S(2)}) collective-permute-start(f32[256,256]{1,0:T(8,128)S(1)} %collective-permute-done.16.refs_7_), channel_id=1, source_target_pairs={{0,2},{1,3},{4,0},{5,1},{8,4},{9,5},{12,8},{13,9},{14,12},{15,13},... | collective-permute-start | bytes 786440 | tf_op jit(solution)/shard_map/ppermute | solution.py:534
  136.1 17.6 %copy-start.3 = (f32[256,256]{1,0:T(8,128)}, f32[256,256]{1,0:T(8,128)S(1)}, u32[]{:S(2)}) copy-start(f32[256,256]{1,0:T(8,128)S(1)} %collective-permute-done.17.refs_8_) | copy-start | bytes 786436
  136.2 18.1 %copy-start.4 = (f32[256,256]{1,0:T(8,128)}, f32[256,256]{1,0:T(8,128)S(1)}, u32[]{:S(2)}) copy-start(f32[256,256]{1,0:T(8,128)S(1)} %collective-permute-done.18.refs_9_) | copy-start | bytes 786436
  137.3 10.2 %collective-permute-start.20 = (f32[256,256]{1,0:T(8,128)S(1)}, f32[256,256]{1,0:T(8,128)S(1)}, u32[]{:S(2)}, u32[]{:S(2)}) collective-permute-start(f32[256,256]{1,0:T(8,128)S(1)} %add.97.second_ref.refs_3_), channel_id=1, source_target_pairs={{0,2},{1,3},{4,0},{5,1},{8,4},{9,5},{12,8},{13,9},{14,12},{15,13},... | collective-permute-start | bytes 786440 | tf_op jit(solution)/shard_map/ppermute | solution.py:534
  139.0 8.0 %collective-permute-start.22 = (f32[128,256]{1,0:T(8,128)S(1)}, f32[128,256]{1,0:T(8,128)S(1)}, u32[]{:S(2)}, u32[]{:S(2)}) collective-permute-start(f32[128,256]{1,0:T(8,128)S(1)} %slice.13), channel_id=1, source_target_pairs={{0,2},{1,3},{4,0},{5,1},{8,4},{9,5},{12,8},{13,9},{14,12},{15,13},... | collective-permute-start | bytes 393224 | tf_op jit(solution)/shard_map/ppermute | solution.py:534
  139.7 7.3 %collective-permute-start.21 = (f32[128,256]{1,0:T(8,128)S(1)}, f32[128,256]{1,0:T(8,128)}, u32[]{:S(2)}, u32[]{:S(2)}) collective-permute-start(f32[128,256]{1,0:T(8,128)S(1)} %slice.12), channel_id=1, source_target_pairs={{0,4},{1,5},{4,8},{5,9},{8,12},{9,13},{12,14},{13,15},{14,10},{15,... | collective-permute-start | bytes 393224 | tf_op jit(solution)/shard_map/ppermute | solution.py:534
  141.2 10.4 %collective-permute-start.19 = (f32[256,256]{1,0:T(8,128)S(1)}, f32[256,256]{1,0:T(8,128)S(1)}, u32[]{:S(2)}, u32[]{:S(2)}) collective-permute-start(f32[256,256]{1,0:T(8,128)S(1)} %add.97.second_ref.refs_3_), channel_id=1, source_target_pairs={{0,4},{1,5},{4,8},{5,9},{8,12},{9,13},{12,14},{13,15},{14,10},{15,... | collective-permute-start | bytes 786440 | tf_op jit(solution)/shard_map/ppermute | solution.py:534
  141.5 10.2 %collective-permute-start.27 = (f32[256,256]{1,0:T(8,128)S(1)}, f32[256,256]{1,0:T(8,128)S(1)}, u32[]{:S(2)}, u32[]{:S(2)}) collective-permute-start(f32[256,256]{1,0:T(8,128)S(1)} %add.96.first_ref.refs_3_), channel_id=1, source_target_pairs={{0,1},{1,0},{2,3},{3,2},{4,5},{5,4},{6,7},{7,6},{8,9},{9,8},{10,11... | collective-permute-start | bytes 786440 | tf_op jit(solution)/shard_map/ppermute | solution.py:537
  147.0 16.4 %copy-start.32 = (f32[128,256]{1,0:T(8,128)}, f32[128,256]{1,0:T(8,128)S(1)}, u32[]{:S(2)}) copy-start(f32[128,256]{1,0:T(8,128)S(1)} %collective-permute-done.22.refs_11_) | copy-start | bytes 393220
  147.0 6.6 %collective-permute-start.28 = (f32[256,256]{1,0:T(8,128)S(1)}, f32[256,256]{1,0:T(8,128)S(1)}, u32[]{:S(2)}, u32[]{:S(2)}) collective-permute-start(f32[256,256]{1,0:T(8,128)S(1)} %collective-permute-done.13.refs_4_), channel_id=1, source_target_pairs={{0,1},{1,0},{2,3},{3,2},{4,5},{5,4},{6,7},{7,6},{8,9},{9,8},{10,11... | collective-permute-start | bytes 786440 | tf_op jit(solution)/shard_map/ppermute | solution.py:537
  147.0 6.7 %collective-permute-start.29 = (f32[256,256]{1,0:T(8,128)S(1)}, f32[256,256]{1,0:T(8,128)S(1)}, u32[]{:S(2)}, u32[]{:S(2)}) collective-permute-start(f32[256,256]{1,0:T(8,128)S(1)} %collective-permute-done.14.refs_5_), channel_id=1, source_target_pairs={{0,1},{1,0},{2,3},{3,2},{4,5},{5,4},{6,7},{7,6},{8,9},{9,8},{10,11... | collective-permute-start | bytes 786440 | tf_op jit(solution)/shard_map/ppermute | solution.py:537
  147.5 25.3 %copy-start.10 = (f32[256,256]{1,0:T(8,128)}, f32[256,256]{1,0:T(8,128)S(1)}, u32[]{:S(2)}) copy-start(f32[256,256]{1,0:T(8,128)S(1)} %collective-permute-done.20.refs_5_) | copy-start | bytes 786436
  147.5 6.8 %collective-permute-start.30 = (f32[256,256]{1,0:T(8,128)S(1)}, f32[256,256]{1,0:T(8,128)}, u32[]{:S(2)}, u32[]{:S(2)}) collective-permute-start(f32[256,256]{1,0:T(8,128)S(1)} %collective-permute-done.15.refs_6_), channel_id=1, source_target_pairs={{0,1},{1,0},{2,3},{3,2},{4,5},{5,4},{6,7},{7,6},{8,9},{9,8},{10,11... | collective-permute-start | bytes 786440 | tf_op jit(solution)/shard_map/ppermute | solution.py:537
  151.5 21.2 %copy-start.11 = (f32[256,256]{1,0:T(8,128)}, f32[256,256]{1,0:T(8,128)S(1)}, u32[]{:S(2)}) copy-start(f32[256,256]{1,0:T(8,128)S(1)} %collective-permute-done.19.refs_4_) | copy-start | bytes 786436
  151.5 8.7 %collective-permute-start.23 = (f32[256,256]{1,0:T(8,128)S(1)}, f32[256,256]{1,0:T(8,128)S(1)}, u32[]{:S(2)}, u32[]{:S(2)}) collective-permute-start(f32[256,256]{1,0:T(8,128)S(1)} %collective-permute-done.19.refs_4_), channel_id=1, source_target_pairs={{0,4},{1,5},{4,8},{5,9},{8,12},{9,13},{12,14},{13,15},{14,10},{15,... | collective-permute-start | bytes 786440 | tf_op jit(solution)/shard_map/ppermute | solution.py:534
  151.7 8.6 %collective-permute-start.24 = (f32[256,256]{1,0:T(8,128)S(1)}, f32[256,256]{1,0:T(8,128)S(1)}, u32[]{:S(2)}, u32[]{:S(2)}) collective-permute-start(f32[256,256]{1,0:T(8,128)S(1)} %collective-permute-done.20.refs_5_), channel_id=1, source_target_pairs={{0,2},{1,3},{4,0},{5,1},{8,4},{9,5},{12,8},{13,9},{14,12},{15,13},... | collective-permute-start | bytes 786440 | tf_op jit(solution)/shard_map/ppermute | solution.py:534
  153.6 7.1 %collective-permute-start.31 = (f32[256,256]{1,0:T(8,128)S(1)}, f32[256,256]{1,0:T(8,128)S(1)}, u32[]{:S(2)}, u32[]{:S(2)}) collective-permute-start(f32[256,256]{1,0:T(8,128)S(1)} %collective-permute-done.16.refs_7_), channel_id=1, source_target_pairs={{0,1},{1,0},{2,3},{3,2},{4,5},{5,4},{6,7},{7,6},{8,9},{9,8},{10,11... | collective-permute-start | bytes 786440 | tf_op jit(solution)/shard_map/ppermute | solution.py:537
  153.7 7.7 %collective-permute-start.32 = (f32[256,256]{1,0:T(8,128)S(1)}, f32[256,256]{1,0:T(8,128)S(1)}, u32[]{:S(2)}, u32[]{:S(2)}) collective-permute-start(f32[256,256]{1,0:T(8,128)S(1)} %collective-permute-done.17.refs_8_), channel_id=1, source_target_pairs={{0,1},{1,0},{2,3},{3,2},{4,5},{5,4},{6,7},{7,6},{8,9},{9,8},{10,11... | collective-permute-start | bytes 786440 | tf_op jit(solution)/shard_map/ppermute | solution.py:537
  154.3 8.5 %collective-permute-start.33 = (f32[256,256]{1,0:T(8,128)S(1)}, f32[256,256]{1,0:T(8,128)S(1)}, u32[]{:S(2)}, u32[]{:S(2)}) collective-permute-start(f32[256,256]{1,0:T(8,128)S(1)} %collective-permute-done.18.refs_9_), channel_id=1, source_target_pairs={{0,1},{1,0},{2,3},{3,2},{4,5},{5,4},{6,7},{7,6},{8,9},{9,8},{10,11... | collective-permute-start | bytes 786440 | tf_op jit(solution)/shard_map/ppermute | solution.py:537
  160.2 12.6 %copy-start.14 = (f32[256,256]{1,0:T(8,128)}, f32[256,256]{1,0:T(8,128)S(1)}, u32[]{:S(2)}) copy-start(f32[256,256]{1,0:T(8,128)S(1)} %collective-permute-done.23.refs_6_) | copy-start | bytes 786436
  160.2 2.6 %collective-permute-start.34 = (f32[128,256]{1,0:T(8,128)}, f32[128,256]{1,0:T(8,128)S(1)}, u32[]{:S(2)}, u32[]{:S(2)}) collective-permute-start(f32[128,256]{1,0:T(8,128)} %collective-permute-done.21.refs_10_), channel_id=1, source_target_pairs={{0,1},{1,0},{2,3},{3,2},{4,5},{5,4},{6,7},{7,6},{8,9},{9,8},{10,11... | collective-permute-start | bytes 393224 | tf_op jit(solution)/shard_map/ppermute | solution.py:537
  160.3 14.8 %copy-start.16 = (f32[256,256]{1,0:T(8,128)}, f32[256,256]{1,0:T(8,128)S(1)}, u32[]{:S(2)}) copy-start(f32[256,256]{1,0:T(8,128)S(1)} %collective-permute-done.24.refs_7_) | copy-start | bytes 786436
  160.3 3.0 %collective-permute-start.35 = (f32[128,256]{1,0:T(8,128)S(1)}, f32[128,256]{1,0:T(8,128)S(1)}, u32[]{:S(2)}, u32[]{:S(2)}) collective-permute-start(f32[128,256]{1,0:T(8,128)S(1)} %collective-permute-done.22.refs_11_), channel_id=1, source_target_pairs={{0,1},{1,0},{2,3},{3,2},{4,5},{5,4},{6,7},{7,6},{8,9},{9,8},{10,11... | collective-permute-start | bytes 393224 | tf_op jit(solution)/shard_map/ppermute | solution.py:537
  160.7 12.0 %collective-permute-start.25 = (f32[256,256]{1,0:T(8,128)S(1)}, f32[256,256]{1,0:T(8,128)S(1)}, u32[]{:S(2)}, u32[]{:S(2)}) collective-permute-start(f32[256,256]{1,0:T(8,128)S(1)} %collective-permute-done.23.refs_6_), channel_id=1, source_target_pairs={{0,4},{1,5},{4,8},{5,9},{8,12},{9,13},{12,14},{13,15},{14,10},{15,... | collective-permute-start | bytes 786440 | tf_op jit(solution)/shard_map/ppermute | solution.py:534
  161.4 11.6 %collective-permute-start.26 = (f32[256,256]{1,0:T(8,128)S(1)}, f32[256,256]{1,0:T(8,128)S(1)}, u32[]{:S(2)}, u32[]{:S(2)}) collective-permute-start(f32[256,256]{1,0:T(8,128)S(1)} %collective-permute-done.24.refs_7_), channel_id=1, source_target_pairs={{0,2},{1,3},{4,0},{5,1},{8,4},{9,5},{12,8},{13,9},{14,12},{15,13},... | collective-permute-start | bytes 786440 | tf_op jit(solution)/shard_map/ppermute | solution.py:534
  162.8 10.9 %collective-permute-start.38 = (f32[256,256]{1,0:T(8,128)}, f32[256,256]{1,0:T(8,128)S(1)}, u32[]{:S(2)}, u32[]{:S(2)}) collective-permute-start(f32[256,256]{1,0:T(8,128)} %copy-done.1), channel_id=1, source_target_pairs={{0,1},{1,0},{2,3},{3,2},{4,5},{5,4},{6,7},{7,6},{8,9},{9,8},{10,11... | collective-permute-start | bytes 786440 | tf_op jit(solution)/shard_map/ppermute | solution.py:537
  162.8 12.3 %collective-permute-start.39 = (f32[256,256]{1,0:T(8,128)S(1)}, f32[256,256]{1,0:T(8,128)S(1)}, u32[]{:S(2)}, u32[]{:S(2)}) collective-permute-start(f32[256,256]{1,0:T(8,128)S(1)} %collective-permute-done.19.refs_4_), channel_id=1, source_target_pairs={{0,1},{1,0},{2,3},{3,2},{4,5},{5,4},{6,7},{7,6},{8,9},{9,8},{10,11... | collective-permute-start | bytes 786440 | tf_op jit(solution)/shard_map/ppermute | solution.py:537
  163.3 16.1 %collective-permute-start.40 = (f32[256,256]{1,0:T(8,128)S(1)}, f32[256,256]{1,0:T(8,128)S(1)}, u32[]{:S(2)}, u32[]{:S(2)}) collective-permute-start(f32[256,256]{1,0:T(8,128)S(1)} %collective-permute-done.20.refs_5_), channel_id=1, source_target_pairs={{0,1},{1,0},{2,3},{3,2},{4,5},{5,4},{6,7},{7,6},{8,9},{9,8},{10,11... | collective-permute-start | bytes 786440 | tf_op jit(solution)/shard_map/ppermute | solution.py:537
  172.8 7.0 %collective-permute-start.41 = (f32[256,256]{1,0:T(8,128)S(1)}, f32[256,256]{1,0:T(8,128)S(1)}, u32[]{:S(2)}, u32[]{:S(2)}) collective-permute-start(f32[256,256]{1,0:T(8,128)S(1)} %collective-permute-done.23.refs_6_), channel_id=1, source_target_pairs={{0,1},{1,0},{2,3},{3,2},{4,5},{5,4},{6,7},{7,6},{8,9},{9,8},{10,11... | collective-permute-start | bytes 786440 | tf_op jit(solution)/shard_map/ppermute | solution.py:537
  173.0 5.9 %collective-permute-start.36 = (f32[128,256]{1,0:T(8,128)S(1)}, f32[128,256]{1,0:T(8,128)S(1)}, u32[]{:S(2)}, u32[]{:S(2)}) collective-permute-start(f32[128,256]{1,0:T(8,128)S(1)} %slice.14), channel_id=1, source_target_pairs={{0,4},{1,5},{4,8},{5,9},{8,12},{9,13},{12,14},{13,15},{14,10},{15,... | collective-permute-start | bytes 393224 | tf_op jit(solution)/shard_map/ppermute | solution.py:534
  173.7 5.6 %collective-permute-start.37 = (f32[128,256]{1,0:T(8,128)S(1)}, f32[128,256]{1,0:T(8,128)S(1)}, u32[]{:S(2)}, u32[]{:S(2)}) collective-permute-start(f32[128,256]{1,0:T(8,128)S(1)} %slice.15), channel_id=1, source_target_pairs={{0,2},{1,3},{4,0},{5,1},{8,4},{9,5},{12,8},{13,9},{14,12},{15,13},... | collective-permute-start | bytes 393224 | tf_op jit(solution)/shard_map/ppermute | solution.py:534
  175.1 4.8 %collective-permute-start.42 = (f32[256,256]{1,0:T(8,128)S(1)}, f32[256,256]{1,0:T(8,128)S(1)}, u32[]{:S(2)}, u32[]{:S(2)}) collective-permute-start(f32[256,256]{1,0:T(8,128)S(1)} %collective-permute-done.24.refs_7_), channel_id=1, source_target_pairs={{0,1},{1,0},{2,3},{3,2},{4,5},{5,4},{6,7},{7,6},{8,9},{9,8},{10,11... | collective-permute-start | bytes 786440 | tf_op jit(solution)/shard_map/ppermute | solution.py:537
  178.9 2.3 %collective-permute-start.43 = (f32[256,256]{1,0:T(8,128)S(1)}, f32[256,256]{1,0:T(8,128)S(1)}, u32[]{:S(2)}, u32[]{:S(2)}) collective-permute-start(f32[256,256]{1,0:T(8,128)S(1)} %collective-permute-done.25.refs_8_), channel_id=1, source_target_pairs={{0,1},{1,0},{2,3},{3,2},{4,5},{5,4},{6,7},{7,6},{8,9},{9,8},{10,11... | collective-permute-start | bytes 786440 | tf_op jit(solution)/shard_map/ppermute | solution.py:537
  179.3 1.9 collective-permute-start.44
  179.4 1.6 collective-permute-start.45
  179.8 1.4 collective-permute-start.46
  (27 other events, 107.1 us)
Sparse Core Ops, SparseCore 0:
  42.2 42.3 reduce-scatter.4
  86.9 39.5 reduce-scatter.2

commit v8 on v7

--- a/solution.py
+++ b/solution.py
@@ -109,7 +109,7 @@
         work[at, to] = jnp.zeros((TILE, TILE), jnp.float32)
 
 
-def factor_first(table_ref, regular_ref, *refs):
+def factor_kernel(table_ref, regular_ref, *refs):
     parts, out_ref, packed = refs[:-2], refs[-2], refs[-1]
     count, rows = parts[0].shape[0], parts[0].shape[1]
     place = lax.axis_index("scen")
@@ -123,62 +123,43 @@
     for i in range(size // TILE):
         at = pl.ds(i * TILE, TILE)
         out_ref[at, at] += jnp.where(row_id == col_id, regular_ref[:, at], 0.0)
-    factor_step(0, out_ref)
-
-
-def factor_next(k, work_ref, out_ref):
-    out_ref[...] = work_ref[...]
-    factor_step(k, out_ref)
-
-
-def factor_stages(table, parts, regular):
+    for k in range(size // TILE):
+        factor_step(k, out_ref)
+
+
+def inverse_factor(table, parts, regular):
     size = regular.shape[0]
-    settings = dict(
+    return pl.pallas_call(
+        factor_kernel,
         out_shape=jax.ShapeDtypeStruct((size, size), jnp.float32),
+        in_specs=[pl.BlockSpec(memory_space=pltpu.SMEM)] + vmem(1 + len(parts)),
         out_specs=vmem(1)[0],
+        scratch_shapes=[pltpu.VMEM((2 * TILE, 5 * TILE), jnp.float32)],
         cost_estimate=pl.CostEstimate(
-            flops=50 * size**3, bytes_accessed=8 * size * size, transcendentals=size
+            flops=150 * size**3, bytes_accessed=8 * size * size, transcendentals=size
         ),
-    )
-    first = lambda work: pl.pallas_call(
-        factor_first,
-        in_specs=[pl.BlockSpec(memory_space=pltpu.SMEM)] + vmem(1 + len(parts)),
-        scratch_shapes=[pltpu.VMEM((2 * TILE, 5 * TILE), jnp.float32)],
-        name="factor_0",
-        **settings,
+        name="inverse_factor",
     )(table, regular[None, :], *parts)
-    return [first] + [
-        pl.pallas_call(
-            lambda work_ref, out_ref, k=k: factor_next(k, work_ref, out_ref),
-            in_specs=vmem(1),
-            name=f"factor_{k}",
-            **settings,
-        )
-        for k in range(1, size // TILE)
-    ]
-
-
-def solve_kernel(inverse_ref, first_ref, second_ref, factor_ref, weight_0, weight_1):
-    half = first_ref.shape[0]
+
+
+def solve_kernel(inverse_ref, first_ref, second_ref, factor_ref, weight_ref):
     inverse = inverse_ref[...]
     panel = jnp.concatenate([first_ref[...], second_ref[...]], axis=0)
     rows = dot_split(split(inverse), split(panel)).T
     factor_ref[...] = rows
-    weights = dot_split(split(rows), split(inverse))
-    weight_0[...] = weights[:, :half]
-    weight_1[...] = weights[:, half:]
+    weight_ref[...] = dot_split(split(rows), split(inverse))
 
 
 def solve_rows(inverse, first, second):
-    half, owned = first.shape
-    shapes = [jax.ShapeDtypeStruct((owned, width), jnp.float32) for width in (2 * half, half, half)]
+    width, owned = inverse.shape[0], first.shape[1]
+    shape = jax.ShapeDtypeStruct((owned, width), jnp.float32)
     return pl.pallas_call(
         solve_kernel,
-        out_shape=shapes,
+        out_shape=(shape, shape),
         in_specs=vmem(3),
-        out_specs=vmem(3),
+        out_specs=vmem(2),
         cost_estimate=pl.CostEstimate(
-            flops=48 * owned * half * half, bytes_accessed=32 * half * half, transcendentals=0
+            flops=12 * owned * width * width, bytes_accessed=8 * width * width, transcendentals=0
         ),
         name="solve_rows",
     )(inverse, first, second)
@@ -256,8 +237,9 @@
             picked[...] += jnp.dot(both, pick[at, :], preferred_element_type=jnp.float32)
 
         local = (picked[:owned] + picked[owned : 2 * owned]).T
-        local_0[...] = local[: width // 2]
-        local_1[...] = local[width // 2 :]
+        cut = local_0.shape[0]
+        local_0[...] = local[:cut]
+        local_1[...] = local[cut:]
         chosen = chosen_rows(place * owned, owned, cols_ref[...])
         total = block[...] + sum(
             jnp.dot(part, chosen, preferred_element_type=jnp.float32) for part in split(local)
@@ -268,12 +250,12 @@
         given_ref[...] = jnp.where(core == 0, far, near)
 
 
-def pick_columns(row_counts, panel_cols, row_weights, prior, scenario_rows):
+def pick_columns(cut, row_counts, panel_cols, row_weights, prior, scenario_rows):
     depth, order = scenario_rows.shape
     width = panel_cols.shape[0]
     owned = prior.shape[0]
     tall = 512
-    local = jax.ShapeDtypeStruct((width // 2, owned), jnp.float32)
+    local = [jax.ShapeDtypeStruct((n, owned), jnp.float32) for n in (cut, width - cut)]
     rows = jax.ShapeDtypeStruct((TILE, 5 * TILE), jnp.float32)
     whole = lambda shape: pl.BlockSpec(shape, lambda i: (0, 0))
     return pl.pallas_call(
@@ -287,9 +269,9 @@
             pl.BlockSpec((tall, order), lambda i: (i, 0)),
         ],
         out_specs=[pl.BlockSpec((width, tall), lambda i: (0, i))]
-        + [whole(local.shape)] * 2
+        + [whole(part.shape) for part in local]
         + [whole(rows.shape)] * 2,
-        out_shape=[jax.ShapeDtypeStruct((width, depth), jnp.bfloat16)] + [local] * 2 + [rows] * 2,
+        out_shape=[jax.ShapeDtypeStruct((width, depth), jnp.bfloat16)] + local + [rows] * 2,
         scratch_shapes=[
             pltpu.VMEM((order, width), jnp.bfloat16),
             pltpu.VMEM((tall, width), jnp.float32),
@@ -311,14 +293,14 @@
     table_ref, scaled_ref, rows_ref, given_0, given_1, kept_0, kept_1, total, sems
 ):
     step, last = pl.program_id(0), pl.num_programs(0) - 1
-    count, half, owned = given_0.shape
+    count, cut, owned = given_0.shape
     wide = 4
     base = 2 * count * lax.axis_index("scen")
 
     def stores(n, which):
         refs = ((given_0, given_1), (kept_0, kept_1))[which]
         for h, ref in enumerate(refs):
-            rows = total.at[n, pl.ds(h * half, half)]
+            rows = total.at[n, pl.ds(h * cut, ref.shape[1])]
             yield pltpu.make_async_copy(rows, ref.at[lax.rem(n, count)], sems.at[n, h])
 
     for which in range(2):
@@ -361,11 +343,13 @@
                     store.wait()
 
 
-def gram_blocks(table, count, owned, scaled, scenario_rows):
+def gram_blocks(table, count, cut, owned, scaled, scenario_rows):
     depth, order = scenario_rows.shape
     width = scaled.shape[0]
     tall = 512
-    pieces = jax.ShapeDtypeStruct((count, width // 2, owned), jnp.float32)
+    pieces = [
+        jax.ShapeDtypeStruct((count, rows, owned), jnp.float32) for rows in (cut, width - cut)
+    ]
     return pl.pallas_call(
         gram_kernel,
         grid=(depth // tall,),
@@ -375,7 +359,7 @@
             pl.BlockSpec((tall, order), lambda i: (i, 0)),
         ],
         out_specs=[pl.BlockSpec(memory_space=pl.ANY)] * 4,
-        out_shape=[pieces] * 4,
+        out_shape=pieces * 2,
         scratch_shapes=[
             pltpu.VMEM((2 * count, width, owned), jnp.float32),
             pltpu.SemaphoreType.DMA((2 * count, 2)),
@@ -393,43 +377,43 @@
 def update_kernel(count, table_ref, weight_ref, prior_ref, *refs):
     sources, out_ref, scratch = refs[:-7], refs[-7], refs[-6:]
     held, before, total, in_sem, prior_sem, out_sem = scratch
-    place = lax.axis_index("scen")
-    width, owned = held.shape[1], held.shape[2]
+    base = count * lax.axis_index("scen")
+    owned = held.shape[2]
     chips = count // 2
     wide = 4
-
-    fetch = pltpu.make_async_copy(prior_ref, before, prior_sem)
+    chunks = [pl.ds(n * owned, wide * owned) for n in range(0, count, wide)]
+
     loads = []
     for n in range(count):
         core, slot = n // chips, n % chips
-        pieces = sources[core * (chips + 1) : (core + 1) * (chips + 1)]
-        pieces = pieces[slot : slot + 1] if slot < chips - 1 else pieces[slot:]
-        rows = width // len(pieces)
-        copies = [
-            pltpu.make_async_copy(piece, held.at[n, pl.ds(i * rows, rows)], in_sem.at[n, i])
-            for i, piece in enumerate(pieces)
-        ]
-        for copy in copies:
-            copy.start()
-        loads.append(copies)
-        if n == wide - 1:
-            fetch.start()
+        row = 0
+        for part in range(2):
+            first = (2 * part + core) * (chips + 1)
+            pieces = sources[first : first + chips + 1]
+            pieces = pieces[slot : slot + 1] if slot < chips - 1 else pieces[slot:]
+            for i, piece in enumerate(pieces):
+                to = held.at[n, pl.ds(row, piece.shape[0])]
+                loads.append(pltpu.make_async_copy(piece, to, in_sem.at[n, 2 * part + i]))
+                row += piece.shape[0]
+    fetches = [
+        pltpu.make_async_copy(prior_ref.at[:, cols], before.at[:, cols], prior_sem.at[m])
+        for m, cols in enumerate(chunks)
+    ]
+    for copy in loads + fetches:
+        copy.start()
     weights = split(weight_ref[...])
-    for first in range(0, count, wide):
-        for n in range(first, first + wide):
-            for copy in loads[n]:
-                copy.wait()
-        panel = [held[n] for n in range(first, first + wide)]
+    for load in loads:
+        load.wait()
+    stores = []
+    for m, cols in enumerate(chunks):
+        panel = [held[table_ref[base + wide * m + i]] for i in range(wide)]
         outer = dot_split(weights, split(jnp.concatenate(panel, axis=1)))
-        if first == 0:
-            fetch.wait()
-        for i in range(wide):
-            at = table_ref[count * place + first + i] * owned
-            cols = pl.ds(pl.multiple_of(at, owned), owned)
-            total[:, cols] = before[:, cols] - outer[:, i * owned : (i + 1) * owned]
-    store = pltpu.make_async_copy(total, out_ref, out_sem)
-    store.start()
-    store.wait()
+        fetches[m].wait()
+        total[:, cols] = before[:, cols] - outer
+        stores.append(pltpu.make_async_copy(total.at[:, cols], out_ref.at[:, cols], out_sem.at[m]))
+        stores[m].start()
+    for store in stores:
+        store.wait()
 
 
 def update_rows(table, count, weights, prior, sources):
@@ -446,9 +430,9 @@
             pltpu.VMEM((count, width, owned), jnp.float32),
             pltpu.VMEM(prior.shape, jnp.float32),
             pltpu.VMEM(prior.shape, jnp.float32),
-            pltpu.SemaphoreType.DMA((count, 2)),
-            pltpu.SemaphoreType.DMA,
-            pltpu.SemaphoreType.DMA,
+            pltpu.SemaphoreType.DMA((count, 4)),
+            pltpu.SemaphoreType.DMA((count // 4,)),
+            pltpu.SemaphoreType.DMA((count // 4,)),
         ],
         cost_estimate=pl.CostEstimate(
             flops=6 * owned * order * width,
@@ -505,9 +489,8 @@
         chip, core = place // 2, place % 2
         z, y, at = chip // 2, chip % 2, ring.index(chip)
         grams += [2 * q + c for c in (1 - core, core) for q in ring]
-        updates += [
-            2 * ring[(at + offset) % chips] + c for c in (core, 1 - core) for offset in back
-        ]
+        blocks = [2 * ring[(at + offset) % chips] + c for c in (core, 1 - core) for offset in back]
+        updates += [blocks.index(block) for block in range(2 * chips)]
         factors += [
             (2 * c + w) * lines + (z - by) % lines
             for c in (core, 1 - core) for w in (y, 1 - y) for by in range(lines)
@@ -520,7 +503,7 @@
     chips = parts // 2
     far = lines = chips // 2
     owned = prior_schur.shape[0]
-    half = panel_cols.shape[0] // 2
+    cut = panel_cols.shape[0] * 5 // 8
     place = lax.axis_index("scen")
     y, z = place // 2 % 2, place // 4
     ring = RINGS[chips]
@@ -544,73 +527,65 @@
     def shift(values, by):
         return lax.ppermute(values, "scen", [(d, (d + 4 * by) % parts) for d in range(parts)])
 
+    def sum_rows(values):
+        return lax.psum_scatter(values, "scen", scatter_dimension=0, axis_index_groups=groups)
+
+    def across(panel, ahead):
+        middle = panel.shape[0] // 2
+        return [step(ahead[0][:middle], 1), step(ahead[1][middle:], -1)]
+
     scaled, local_0, local_1, block_given, block_kept = pick_columns(
-        row_counts, panel_cols, row_weights, prior_schur, scenario_rows
+        cut, row_counts, panel_cols, row_weights, prior_schur, scenario_rows
     )
     block_given, scaled = together((block_given, scaled))
     block_got = swap(block_given, 1)
     given_0, given_1, kept_0, kept_1 = gram_blocks(
-        gram_table, chips, owned, scaled, scenario_rows
-    )
-    block_got, given_0 = together((block_got, given_0))
+        gram_table, chips, cut, owned, scaled, scenario_rows
+    )
+    block_got, given_0, given_1 = together((block_got, given_0, given_1))
     block = (block_kept + block_got).reshape(2, lines, -1, block_kept.shape[1])
-    got_0 = swap(given_0, 1)
-    beside = swap(slab(block, 1 - y), 2)
-
-    def sum_rows(values):
-        return lax.psum_scatter(values, "scen", scatter_dimension=0, axis_index_groups=groups)
-
-    got_0, given_1 = together((got_0, given_1))
+    beside, given_0 = together((slab(block, 1 - y), given_0))
+    got_0, beside = together((swap(given_0, 1), swap(beside, 2)))
+
     panel_0 = sum_rows(kept_0 + got_0)
     got_1 = swap(given_1, 1)
     block = slab(block, y) + beside
     beside = [slab(block, (z + by) % lines) for by in range(1, lines)]
-    beside, got_1 = together(([shift(beside[by - 1], by) for by in range(1, lines)], got_1))
-    panel_1 = sum_rows(kept_1 + got_1)
+    beside = [shift(beside[by - 1], by) for by in range(1, lines)]
+    beside, got_1 = together((beside, got_1))
     beside = sum(beside) + slab(block, z)
-    beside = jnp.stack([beside] + [shift(beside, by) for by in range(1, lines)])
-    beside = [beside] + [swap(beside, bit) for bit in (2, 1, 3)]
-    stages = factor_stages(factor_table, beside, regular)
-    work = stages[1](stages[0](None))
-    panel_0, work = together((panel_0, work))
+    beside = [beside] + [shift(beside, by) for by in range(1, lines)]
+    beside, sums_1 = together((beside, kept_1 + got_1))
+    panel_1 = sum_rows(sums_1)
+    beside = jnp.stack(beside)
+    beside = jnp.concatenate([beside, swap(beside, 2)])
+    inverse = inverse_factor(factor_table, [beside, swap(beside, 1)], regular)
+    panel_0, inverse = together((panel_0, inverse))
     panel_0 += local_0
 
     shards_0 = [panel_0]
     ahead = [panel_0, panel_0]
     for d in range(1, far):
-        ahead, work = together((ahead, work))
-        ahead = [step(ahead[0], 1), step(ahead[1], -1)]
-        if 1 + d < len(stages):
-            work = stages[1 + d](work)
-        ahead, work = together((ahead, work))
+        ahead = together([step(ahead[0], 1), step(ahead[1], -1)])
         shards_0 += ahead
-    panel_1, ahead, work = together((panel_1, ahead, work))
+    panel_1, ahead = together((panel_1, ahead))
     panel_1 += local_1
+    ahead, panel_1 = together((ahead, panel_1))
     shards_1 = [panel_1]
-    ahead, (panel_1, work) = together((ahead, (panel_1, work)))
-    ahead = [ahead[0][: half // 2], ahead[1][half // 2 :]]
-    last = [step(ahead[0], 1), step(ahead[1], -1)]
-    ahead = [step(panel_1, 1), step(panel_1, -1)]
-    ahead, last, work = together((ahead, last, solve_rows(work, panel_0, panel_1)))
+    last, ahead = across(panel_0, ahead), [step(panel_1, 1), step(panel_1, -1)]
+    last, ahead, solved = together((last, ahead, solve_rows(inverse, panel_0, panel_1)))
     shards_0 += last
     shards_1 += ahead
-    factor_rows, weights_0, weights_1 = work
-
-    def sources(shards):
-        return shards + [swap(piece, 1) for piece in shards]
-
-    updated = prior_schur
-    sources_0 = sources(shards_0)
-    for d in range(2, far + 1):
-        if d == far:
-            ahead = [ahead[0][: half // 2], ahead[1][half // 2 :]]
-        ahead, updated = together((ahead, updated))
-        ahead = [step(ahead[0], 1), step(ahead[1], -1)]
-        if d == far - 1:
-            updated = update_rows(update_table, parts, weights_0, updated, sources_0)
-        ahead, updated = together((ahead, updated))
+    for d in range(2, far):
+        ahead = together([step(ahead[0], 1), step(ahead[1], -1)])
         shards_1 += ahead
-    return update_rows(update_table, parts, weights_1, updated, sources(shards_1)), factor_rows
+    shards_1 += across(panel_1, ahead)
+
+    factor_rows, weights = solved
+    sources = []
+    for shards in (shards_0, shards_1):
+        sources += shards + [swap(piece, 1) for piece in shards]
+    return update_rows(update_table, parts, weights, prior_schur, sources), factor_rows
 
 
 def shards_by_groups(scenario_rows, row_weights, row_counts, panel_cols, regular, prior_schur):
@@ -642,11 +617,8 @@
     panel_half = lax.all_gather(panel_rows, "scen", axis_index_groups=same_core)
     panel_rest = swap_cores(panel_half)
     table = jnp.array([c ^ (d % 2) for d in range(parts) for c in range(2)], jnp.int32)
-    inverse = None
-    for stage in factor_stages(table, [block, block_other], regular):
-        inverse = stage(inverse)
-    factor_rows, *weights = solve_rows(inverse, panel_rows.T[:half], panel_rows.T[half:])
-    weights = jnp.concatenate(weights, axis=1)
+    inverse = inverse_factor(table, [block, block_other], regular)
+    factor_rows, weights = solve_rows(inverse, panel_rows.T[:half], panel_rows.T[half:])
     even = jnp.where(core == 0, panel_half, panel_rest)
     odd = jnp.where(core == 0, panel_rest, panel_half)
     panel = jnp.stack([even, odd], axis=1).reshape(order, width)

time: 199 us -> 199 us (level)
  waiting for transfers between devices: 60.4 us -> 74.2 us
  Pallas kernels: 76.8 us -> 63.7 us
    ppermute x16, waiting for transfers between devices: 27.7 us -> 47.8 us  [step(): return lax.ppermute(values, 'scen', pairs)]
    pallas_call x5 -> x2, Pallas kernels: 33.3 us -> 26.3 us  [the longest x1 22.3 us: inverse_factor(): pl.pallas_call(factor_kernel, out_shape=jax.ShapeDtypeStruct((size, size)...]
    pallas_call x2 -> x1, Pallas kernels: 17.6 us -> 11.5 us  [update_rows(): pl.pallas_call(lambda *refs: update_kernel(count, *refs), out_shape=jax.S...]
    ppermute x25 -> x24, waiting for transfers between devices: 21.1 us -> 16.5 us  [swap(): return lax.ppermute(values, 'scen', [(d, d ^ bit) for d in range(parts)])]
    ppermute x25 -> x24, starting transfers between devices: 8.96 us -> 7.68 us  [swap(): return lax.ppermute(values, 'scen', [(d, d ^ bit) for d in range(parts)])]
  transfers between devices with their start and end apart: 49 -> 48, of which waited for: 21 -> 25; matrix products, arithmetic and copies ran while one was open for 2% -> 2% of each run, Pallas kernels for 27% -> 19%
where the time goes in v8:
time: 199 us; the launch traced here: 198 us
  waiting for transfers between devices  74.2 us (37%)
  Pallas kernels  63.7 us (32%)
  starting transfers between devices  32.8 us (16%)
  between operations  15.3 us (8%)
  other arithmetic  8.96 us (5%)
  local copies, waits for them, and re-layouts  3.43 us (2%)
    ppermute x16, waiting for transfers between devices, step(): return lax.ppermute(values, 'scen', pairs)  47.8 us
    pallas_call x1, Pallas kernels, inverse_factor(): pl.pallas_call(factor_kernel, out_shape=jax.ShapeDtypeStruct((size, size)...  22.3 us
    ppermute x16, starting transfers between devices, step(): return lax.ppermute(values, 'scen', pairs)  16.6 us
    ppermute x24, waiting for transfers between devices, swap(): return lax.ppermute(values, 'scen', [(d, d ^ bit) for d in range(parts)])  16.5 us
    pallas_call x1, Pallas kernels, pick_columns(): pl.pallas_call(pick_kernel, grid=(depth // tall,), in_specs=[pl.BlockSpec...  14.8 us
    pallas_call x1, Pallas kernels, update_rows(): pl.pallas_call(lambda *refs: update_kernel(count, *refs), out_shape=jax.S...  11.5 us
    pallas_call x1, Pallas kernels, gram_blocks(): pl.pallas_call(gram_kernel, grid=(depth // tall,), in_specs=[pl.BlockSpec...  11.2 us
    ppermute x6, waiting for transfers between devices, shift(): lax.ppermute(values, 'scen', [(d, (d + 4 * by) % parts) for d in range(pa...  9.93 us
  transfers between devices with their start and end apart: 48, of which 25 were waited for; matrix products, arithmetic and copies ran while one was open for 2% of the time, Pallas kernels for 19%

profile of v8, /device:TPU:0, one launch (start us, length us, event | category | flops | bytes accessed | tf_op | source)
XLA Modules:
  0.0 198.4 jit_solution(876640798570426172)
XLA Ops:
  7.9 14.8 %pick_columns.1 = (bf16[512,1024]{1,0:T(8,128)(2,1)}, f32[320,256]{1,0:T(8,128)}, f32[192,256]{1,0:T(8,128)}, f32[128,640]{1,0:T(8,128)}, f32[128,640]{1,0:T(8,128)}) custom-call(s32[1]{0:T(128)S(6)} %copy.15.counts_ref, s32[1,512]{1,0:T(1,128)} %bitcast.35, f32[1,1024]{1,0:T(1,128)} %bitcast.34, f32[256,4096]{1,0:T(8,128)} %refs_2_.1, ...), custom_call_target="tpu_custom_call" | custom-call | flops 6442450944 | bytes 12582912 | tf_op jit(solution)/shard_map/pick_columns/pallas_call | solution.py:261
  22.6 0.5 collective-permute-start
  23.1 11.2 %gram_blocks.1 = (f32[8,320,256]{2,1,0:T(8,128)}, f32[8,192,256]{2,1,0:T(8,128)}, f32[8,320,256]{2,1,0:T(8,128)}, f32[8,192,256]{2,1,0:T(8,128)}) custom-call(s32[256]{0:T(256)} %constant.79.clone.table_ref, bf16[512,1024]{1,0:T(8,128)(2,1)} %get-tuple-element.59.scaled_ref, bf16[1024,4096]{1,0:T(8,128)(2,1)} %rows_ref.3), custom_call_target="tpu_custom_call" | custom-call | flops 4294967296 | bytes 16777216 | tf_op jit(solution)/shard_map/gram_blocks/pallas_call | solution.py:353
  34.6 3.0 %collective-permute-start.2 = (f32[4,16,640]{2,1,0:T(8,128)S(1)}, f32[4,16,640]{2,1,0:T(8,128)S(1)}, u32[]{:S(2)}, u32[]{:S(2)}) collective-permute-start(f32[4,16,640]{2,1,0:T(8,128)S(1)} %dynamic-slice_bitcast_fusion), channel_id=1, source_target_pairs={{0,2},{1,3},{2,0},{3,1},{4,6},{5,7},{6,4},{7,5},{8,10},{9,11},{10,... | collective-permute-start | bytes 491528 | tf_op jit(solution)/shard_map/ppermute | solution.py:520
  37.5 4.4 %collective-permute-done.2 = f32[4,16,640]{2,1,0:T(8,128)S(1)} collective-permute-done((f32[4,16,640]{2,1,0:T(8,128)S(1)}, f32[4,16,640]{2,1,0:T(8,128)S(1)}, u32[]{:S(2)}, u32[]{:S(2)}) %collective-permute-start.2) | collective-permute-done | bytes 163872 | tf_op jit(solution)/shard_map/ppermute | solution.py:520
  42.0 0.7 copy-done.34
  42.6 3.6 %add.95 = f32[8,320,256]{2,1,0:T(8,128)} add(f32[8,320,256]{2,1,0:T(8,128)} %get-tuple-element.74, f32[8,320,256]{2,1,0:T(8,128)S(1)} %collective-permute-done.1) | non-fusion elementwise | flops 655360 | bytes 7864320 | tf_op jit(solution)/shard_map/add | solution.py:550
  46.5 1.1 bitcast_add_fusion
  47.5 0.7 copy-done.5
  48.2 3.9 %collective-permute-start.5 = (f32[16,640]{1,0:T(8,128)S(1)}, f32[16,640]{1,0:T(8,128)S(1)}, u32[]{:S(2)}, u32[]{:S(2)}) collective-permute-start(f32[16,640]{1,0:T(8,128)S(1)} %get-tuple-element.108), channel_id=1, source_target_pairs={{0,12},{1,13},{2,14},{3,15},{4,0},{5,1},{6,2},{7,3},{8,4},{9,5},{1... | collective-permute-start | bytes 122888 | tf_op jit(solution)/shard_map/ppermute | solution.py:528
  52.1 1.0 collective-permute-start.3
  53.1 1.2 collective-permute-done.5
  54.3 4.3 %collective-permute-done.4 = f32[16,640]{1,0:T(8,128)S(1)} collective-permute-done((f32[16,640]{1,0:T(8,128)S(1)}, f32[16,640]{1,0:T(8,128)S(1)}, u32[]{:S(2)}, u32[]{:S(2)}) %collective-permute-start.4) | collective-permute-done | bytes 40992 | tf_op jit(solution)/shard_map/ppermute | solution.py:528
  58.6 0.8 bitcast_add_fusion.1
  59.4 1.2 collective-permute-start.9
  60.6 1.3 collective-permute-start.8
  62.0 1.0 collective-permute-start.7
  62.9 1.4 add.94
  64.3 0.6 collective-permute-done.9
  64.9 3.1 %collective-permute-done.8 = f32[16,640]{1,0:T(8,128)S(1)} collective-permute-done((f32[16,640]{1,0:T(8,128)S(1)}, f32[16,640]{1,0:T(8,128)S(1)}, u32[]{:S(2)}, u32[]{:S(2)}) %collective-permute-start.8) | collective-permute-done | bytes 40992 | tf_op jit(solution)/shard_map/ppermute | solution.py:528
  68.0 0.7 collective-permute-done.7
  68.7 1.9 collective-permute-start.10
  70.7 7.7 %collective-permute-done.10 = f32[4,16,640]{2,1,0:T(8,128)S(1)} collective-permute-done((f32[4,16,640]{2,1,0:T(8,128)S(1)}, f32[4,16,640]{2,1,0:T(8,128)S(1)}, u32[]{:S(2)}, u32[]{:S(2)}) %collective-permute-start.10) | collective-permute-done | bytes 163872 | tf_op jit(solution)/shard_map/ppermute | solution.py:520
  78.5 1.6 collective-permute-done.11.refs_1_
  80.1 0.7 copy-done.40
  80.9 22.3 %inverse_factor.1.inverse_ref = f32[512,512]{1,0:T(8,128)} custom-call(s32[256]{0:T(256)} %constant.81.clone.table_ref, f32[1,512]{1,0:T(1,128)} %bitcast.36, f32[8,16,640]{2,1,0:T(8,128)} %copy-done.39, f32[8,16,640]{2,1,0:T(8,128)} %copy-done.40), custom_call_target="tpu_custom_call" | custom-call | flops 20132659200 | bytes 2097152 | tf_op jit(solution)/shard_map/inverse_factor/pallas_call | solution.py:132
  103.2 1.0 add.96.first_ref.refs_3_
  104.2 1.8 collective-permute-start.13
  106.3 15.0 %collective-permute-done.13.refs_5_ = f32[320,256]{1,0:T(8,128)S(1)} collective-permute-done((f32[320,256]{1,0:T(8,128)S(1)}, f32[320,256]{1,0:T(8,128)S(1)}, u32[]{:S(2)}, u32[]{:S(2)}) %collective-permute-start.13) | collective-permute-done | bytes 327712 | tf_op jit(solution)/shard_map/ppermute | solution.py:517
  121.2 0.8 collective-permute-done.12.refs_4_
  122.0 2.0 %collective-permute-start.15 = (f32[320,256]{1,0:T(8,128)S(1)}, f32[320,256]{1,0:T(8,128)S(1)}, u32[]{:S(2)}, u32[]{:S(2)}) collective-permute-start(f32[320,256]{1,0:T(8,128)S(1)} %collective-permute-done.13.refs_5_), channel_id=1, source_target_pairs={{0,2},{1,3},{4,0},{5,1},{8,4},{9,5},{12,8},{13,9},{14,12},{15,13},... | collective-permute-start | bytes 983048 | tf_op jit(solution)/shard_map/ppermute | solution.py:517
  124.1 7.0 %collective-permute-done.14.refs_6_ = f32[320,256]{1,0:T(8,128)S(1)} collective-permute-done((f32[320,256]{1,0:T(8,128)S(1)}, f32[320,256]{1,0:T(8,128)S(1)}, u32[]{:S(2)}, u32[]{:S(2)}) %collective-permute-start.14) | collective-permute-done | bytes 327712 | tf_op jit(solution)/shard_map/ppermute | solution.py:517
  131.0 1.1 collective-permute-start.16
  132.1 1.0 collective-permute-start.17
  133.1 6.0 %collective-permute-done.16.refs_8_ = f32[320,256]{1,0:T(8,128)S(1)} collective-permute-done((f32[320,256]{1,0:T(8,128)S(1)}, f32[320,256]{1,0:T(8,128)S(1)}, u32[]{:S(2)}, u32[]{:S(2)}) %collective-permute-start.16) | collective-permute-done | bytes 327712 | tf_op jit(solution)/shard_map/ppermute | solution.py:517
  139.2 0.7 collective-permute-done.17.refs_9_
  139.9 1.1 add.97.second_ref.refs_21_
  141.0 1.1 collective-permute-start.19
  142.1 1.0 collective-permute-start.18
  143.3 1.1 collective-permute-start.21
  144.4 2.0 collective-permute-done.19.refs_11_
  146.4 1.1 collective-permute-start.20
  147.5 1.8 collective-permute-done.18.refs_10_
  149.3 4.0 %solve_rows.1 = (f32[256,512]{1,0:T(8,128)}, f32[256,512]{1,0:T(8,128)}) custom-call(f32[512,512]{1,0:T(8,128)} %inverse_factor.1.inverse_ref, f32[320,256]{1,0:T(8,128)} %copy-done.1, f32[192,256]{1,0:T(8,128)} %copy-done.2), custom_call_target="tpu_custom_call" | custom-call | flops 805306368 | bytes 2097152 | tf_op jit(solution)/shard_map/solve_rows/pallas_call | solution.py:156
  153.3 1.0 collective-permute-start.31
  154.8 1.1 collective-permute-start.32
  155.9 5.0 %collective-permute-done.31.refs_24_ = f32[192,256]{1,0:T(8,128)S(1)} collective-permute-done((f32[192,256]{1,0:T(8,128)}, f32[192,256]{1,0:T(8,128)S(1)}, u32[]{:S(2)}, u32[]{:S(2)}) %collective-permute-start.31) | collective-permute-done | bytes 196640 | tf_op jit(solution)/shard_map/ppermute | solution.py:517
  160.8 1.2 collective-permute-done.32.refs_25_
  162.0 1.1 collective-permute-start.33
  163.2 1.0 collective-permute-start.34
  164.2 0.5 collective-permute-start.39
  164.7 4.6 %collective-permute-done.33.refs_26_ = f32[192,256]{1,0:T(8,128)S(1)} collective-permute-done((f32[192,256]{1,0:T(8,128)S(1)}, f32[192,256]{1,0:T(8,128)S(1)}, u32[]{:S(2)}, u32[]{:S(2)}) %collective-permute-start.33) | collective-permute-done | bytes 196640 | tf_op jit(solution)/shard_map/ppermute | solution.py:517
  169.4 0.8 collective-permute-done.34.refs_27_
  170.2 0.8 collective-permute-done.29.refs_19_
  171.1 0.7 collective-permute-done.30.refs_20_
  171.8 1.0 collective-permute-start.36
  172.7 1.1 collective-permute-start.35
  173.8 0.5 collective-permute-start.43
  174.3 2.3 %collective-permute-done.36.refs_29_ = f32[96,256]{1,0:T(8,128)S(1)} collective-permute-done((f32[96,256]{1,0:T(8,128)S(1)}, f32[96,256]{1,0:T(8,128)S(1)}, u32[]{:S(2)}, u32[]{:S(2)}) %collective-permute-start.36) | collective-permute-done | bytes 98336 | tf_op jit(solution)/shard_map/ppermute | solution.py:517
  176.6 0.7 collective-permute-done.35.refs_28_
  177.4 0.6 collective-permute-done.45.refs_38_
  177.9 0.7 collective-permute-done.44.refs_37_
  179.4 0.7 copy-done.29
  180.0 11.5 %update_rows.1 = f32[256,4096]{1,0:T(8,128)} custom-call(s32[256]{0:T(256)} %constant.80.clone.refs_0_, f32[256,512]{1,0:T(8,128)} %get-tuple-element.98.refs_1_, f32[256,4096]{1,0:T(8,128)} %refs_2_.1, f32[320,256]{1,0:T(8,128)} %copy-done.1, f32[320,256]{1,0:T(8,128)} %copy-done.11, f32[320,256]{1,0:T(8,128)} %copy-done.10, f32[320,256]{1,0:T(8,128)} %copy-done.12, ...), custom_call_target="tpu_custom_call" | custom-call | flops 3221225472 | bytes 16777216 | tf_op jit(solution)/shard_map/update_rows/pallas_call | solution.py:422
  (140 shorter events, 2.5 us)
Async XLA Ops:
  7.2 96.0 %reduce-scatter.5.cloned.1.call-start = ((), (), s32[]{:S(2)}) async-start(), calls=%async_computation.3 | async-start | bytes 2949120 | tf_op jit(solution)/shard_map/reduce_scatter | solution.py:531
  22.6 11.7 %collective-permute-start = (f32[128,640]{1,0:T(8,128)}, f32[128,640]{1,0:T(8,128)S(1)}, u32[]{:S(2)}, u32[]{:S(2)}) collective-permute-start(f32[128,640]{1,0:T(8,128)} %get-tuple-element.58), channel_id=1, source_target_pairs={{0,1},{1,0},{2,3},{3,2},{4,5},{5,4},{6,7},{7,6},{8,9},{9,8},{10,11... | collective-permute-start | bytes 983048 | tf_op jit(solution)/shard_map/ppermute | solution.py:520
  34.4 7.6 %collective-permute-start.1 = (f32[8,320,256]{2,1,0:T(8,128)}, f32[8,320,256]{2,1,0:T(8,128)S(1)}, u32[]{:S(2)}, u32[]{:S(2)}) collective-permute-start(f32[8,320,256]{2,1,0:T(8,128)} %get-tuple-element.64), channel_id=1, source_target_pairs={{0,1},{1,0},{2,3},{3,2},{4,5},{5,4},{6,7},{7,6},{8,9},{9,8},{10,11... | collective-permute-start | bytes 7864328 | tf_op jit(solution)/shard_map/ppermute | solution.py:520
  34.6 7.4 %collective-permute-start.2 = (f32[4,16,640]{2,1,0:T(8,128)S(1)}, f32[4,16,640]{2,1,0:T(8,128)S(1)}, u32[]{:S(2)}, u32[]{:S(2)}) collective-permute-start(f32[4,16,640]{2,1,0:T(8,128)S(1)} %dynamic-slice_bitcast_fusion), channel_id=1, source_target_pairs={{0,2},{1,3},{2,0},{3,1},{4,6},{5,7},{6,4},{7,5},{8,10},{9,11},{10,... | collective-permute-start | bytes 491528 | tf_op jit(solution)/shard_map/ppermute | solution.py:520
  46.2 16.7 %copy-start = (f32[8,192,256]{2,1,0:T(8,128)S(1)}, f32[8,192,256]{2,1,0:T(8,128)}, u32[]{:S(2)}) copy-start(f32[8,192,256]{2,1,0:T(8,128)} %get-tuple-element.71) | copy-start | bytes 4718596
  46.2 93.6 %reduce-scatter.3.cloned.1.call-start = ((), (), s32[]{:S(2)}) async-start(), calls=%async_computation.2 | async-start | bytes 1769472 | tf_op jit(solution)/shard_map/reduce_scatter | solution.py:531
  46.3 6.8 %collective-permute-start.6 = (f32[8,192,256]{2,1,0:T(8,128)}, f32[8,192,256]{2,1,0:T(8,128)S(1)}, u32[]{:S(2)}, u32[]{:S(2)}) collective-permute-start(f32[8,192,256]{2,1,0:T(8,128)} %get-tuple-element.67), channel_id=1, source_target_pairs={{0,1},{1,0},{2,3},{3,2},{4,5},{5,4},{6,7},{7,6},{8,9},{9,8},{10,11... | collective-permute-start | bytes 4718600 | tf_op jit(solution)/shard_map/ppermute | solution.py:520
  48.2 6.1 %collective-permute-start.5 = (f32[16,640]{1,0:T(8,128)S(1)}, f32[16,640]{1,0:T(8,128)S(1)}, u32[]{:S(2)}, u32[]{:S(2)}) collective-permute-start(f32[16,640]{1,0:T(8,128)S(1)} %get-tuple-element.108), channel_id=1, source_target_pairs={{0,12},{1,13},{2,14},{3,15},{4,0},{5,1},{6,2},{7,3},{8,4},{9,5},{1... | collective-permute-start | bytes 122888 | tf_op jit(solution)/shard_map/ppermute | solution.py:528
  52.1 6.6 %collective-permute-start.4 = (f32[16,640]{1,0:T(8,128)S(1)}, f32[16,640]{1,0:T(8,128)S(1)}, u32[]{:S(2)}, u32[]{:S(2)}) collective-permute-start(f32[16,640]{1,0:T(8,128)S(1)} %get-tuple-element.109), channel_id=1, source_target_pairs={{0,8},{1,9},{2,10},{3,11},{4,12},{5,13},{6,14},{7,15},{8,0},{9,1},... | collective-permute-start | bytes 122888 | tf_op jit(solution)/shard_map/ppermute | solution.py:528
  52.1 6.6 %collective-permute-start.3 = (f32[16,640]{1,0:T(8,128)S(1)}, f32[16,640]{1,0:T(8,128)S(1)}, u32[]{:S(2)}, u32[]{:S(2)}) collective-permute-start(f32[16,640]{1,0:T(8,128)S(1)} %get-tuple-element.110), channel_id=1, source_target_pairs={{0,4},{1,5},{2,6},{3,7},{4,8},{5,9},{6,10},{7,11},{8,12},{9,13},{1... | collective-permute-start | bytes 122888 | tf_op jit(solution)/shard_map/ppermute | solution.py:528
  59.4 5.5 %collective-permute-start.9 = (f32[16,640]{1,0:T(8,128)S(1)}, f32[16,640]{1,0:T(8,128)S(1)}, u32[]{:S(2)}, u32[]{:S(2)}) collective-permute-start(f32[16,640]{1,0:T(8,128)S(1)} %bitcast_add_fusion.1), channel_id=1, source_target_pairs={{0,12},{1,13},{2,14},{3,15},{4,0},{5,1},{6,2},{7,3},{8,4},{9,5},{1... | collective-permute-start | bytes 122888 | tf_op jit(solution)/shard_map/ppermute | solution.py:528
  60.6 7.4 %collective-permute-start.8 = (f32[16,640]{1,0:T(8,128)S(1)}, f32[16,640]{1,0:T(8,128)S(1)}, u32[]{:S(2)}, u32[]{:S(2)}) collective-permute-start(f32[16,640]{1,0:T(8,128)S(1)} %bitcast_add_fusion.1), channel_id=1, source_target_pairs={{0,8},{1,9},{2,10},{3,11},{4,12},{5,13},{6,14},{7,15},{8,0},{9,1},... | collective-permute-start | bytes 122888 | tf_op jit(solution)/shard_map/ppermute | solution.py:528
  62.0 6.8 %collective-permute-start.7 = (f32[16,640]{1,0:T(8,128)S(1)}, f32[16,640]{1,0:T(8,128)S(1)}, u32[]{:S(2)}, u32[]{:S(2)}) collective-permute-start(f32[16,640]{1,0:T(8,128)S(1)} %bitcast_add_fusion.1), channel_id=1, source_target_pairs={{0,4},{1,5},{2,6},{3,7},{4,8},{5,9},{6,10},{7,11},{8,12},{9,13},{1... | collective-permute-start | bytes 122888 | tf_op jit(solution)/shard_map/ppermute | solution.py:528
  68.7 9.7 %collective-permute-start.10 = (f32[4,16,640]{2,1,0:T(8,128)S(1)}, f32[4,16,640]{2,1,0:T(8,128)S(1)}, u32[]{:S(2)}, u32[]{:S(2)}) collective-permute-start(f32[4,16,640]{2,1,0:T(8,128)S(1)} %pad_maximum_fusion), channel_id=1, source_target_pairs={{0,2},{1,3},{2,0},{3,1},{4,6},{5,7},{6,4},{7,5},{8,10},{9,11},{10,... | collective-permute-start | bytes 491528 | tf_op jit(solution)/shard_map/ppermute | solution.py:520
  78.4 1.7 collective-permute-start.11
  80.8 22.3 %copy-start.8 = (f32[320,256]{1,0:T(8,128)S(1)}, f32[320,256]{1,0:T(8,128)}, u32[]{:S(2)}) copy-start(f32[320,256]{1,0:T(8,128)} %get-tuple-element.81) | copy-start | bytes 983044
  80.9 59.0 %copy-start.30 = (f32[192,256]{1,0:T(8,128)S(1)}, f32[192,256]{1,0:T(8,128)}, u32[]{:S(2)}) copy-start(f32[192,256]{1,0:T(8,128)} %get-tuple-element.91) | copy-start | bytes 589828
  104.2 45.1 %copy-start.1 = (f32[320,256]{1,0:T(8,128)}, f32[320,256]{1,0:T(8,128)S(1)}, u32[]{:S(2)}) copy-start(f32[320,256]{1,0:T(8,128)S(1)} %add.96.first_ref.refs_3_) | copy-start | bytes 983044
  104.2 17.0 %collective-permute-start.13 = (f32[320,256]{1,0:T(8,128)S(1)}, f32[320,256]{1,0:T(8,128)S(1)}, u32[]{:S(2)}, u32[]{:S(2)}) collective-permute-start(f32[320,256]{1,0:T(8,128)S(1)} %add.96.first_ref.refs_3_), channel_id=1, source_target_pairs={{0,2},{1,3},{4,0},{5,1},{8,4},{9,5},{12,8},{13,9},{14,12},{15,13},... | collective-permute-start | bytes 983048 | tf_op jit(solution)/shard_map/ppermute | solution.py:517
  106.0 16.1 %collective-permute-start.12 = (f32[320,256]{1,0:T(8,128)S(1)}, f32[320,256]{1,0:T(8,128)S(1)}, u32[]{:S(2)}, u32[]{:S(2)}) collective-permute-start(f32[320,256]{1,0:T(8,128)S(1)} %add.96.first_ref.refs_3_), channel_id=1, source_target_pairs={{0,4},{1,5},{4,8},{5,9},{8,12},{9,13},{12,14},{13,15},{14,10},{15,... | collective-permute-start | bytes 983048 | tf_op jit(solution)/shard_map/ppermute | solution.py:517
  121.2 57.4 %copy-start.10 = (f32[320,256]{1,0:T(8,128)}, f32[320,256]{1,0:T(8,128)S(1)}, u32[]{:S(2)}) copy-start(f32[320,256]{1,0:T(8,128)S(1)} %collective-permute-done.13.refs_5_) | copy-start | bytes 983044
  122.0 56.6 %copy-start.11 = (f32[320,256]{1,0:T(8,128)}, f32[320,256]{1,0:T(8,128)S(1)}, u32[]{:S(2)}) copy-start(f32[320,256]{1,0:T(8,128)S(1)} %collective-permute-done.12.refs_4_) | copy-start | bytes 983044
  122.0 9.0 %collective-permute-start.14 = (f32[320,256]{1,0:T(8,128)S(1)}, f32[320,256]{1,0:T(8,128)S(1)}, u32[]{:S(2)}, u32[]{:S(2)}) collective-permute-start(f32[320,256]{1,0:T(8,128)S(1)} %collective-permute-done.12.refs_4_), channel_id=1, source_target_pairs={{0,4},{1,5},{4,8},{5,9},{8,12},{9,13},{12,14},{13,15},{14,10},{15,... | collective-permute-start | bytes 983048 | tf_op jit(solution)/shard_map/ppermute | solution.py:517
  122.0 9.0 %collective-permute-start.15 = (f32[320,256]{1,0:T(8,128)S(1)}, f32[320,256]{1,0:T(8,128)S(1)}, u32[]{:S(2)}, u32[]{:S(2)}) collective-permute-start(f32[320,256]{1,0:T(8,128)S(1)} %collective-permute-done.13.refs_5_), channel_id=1, source_target_pairs={{0,2},{1,3},{4,0},{5,1},{8,4},{9,5},{12,8},{13,9},{14,12},{15,13},... | collective-permute-start | bytes 983048 | tf_op jit(solution)/shard_map/ppermute | solution.py:517
  131.0 47.6 %copy-start.12 = (f32[320,256]{1,0:T(8,128)}, f32[320,256]{1,0:T(8,128)S(1)}, u32[]{:S(2)}) copy-start(f32[320,256]{1,0:T(8,128)S(1)} %collective-permute-done.14.refs_6_) | copy-start | bytes 983044
  131.0 47.6 %copy-start.13 = (f32[320,256]{1,0:T(8,128)}, f32[320,256]{1,0:T(8,128)S(1)}, u32[]{:S(2)}) copy-start(f32[320,256]{1,0:T(8,128)S(1)} %collective-permute-done.15.refs_7_) | copy-start | bytes 983044
  131.0 8.1 %collective-permute-start.16 = (f32[320,256]{1,0:T(8,128)S(1)}, f32[320,256]{1,0:T(8,128)S(1)}, u32[]{:S(2)}, u32[]{:S(2)}) collective-permute-start(f32[320,256]{1,0:T(8,128)S(1)} %collective-permute-done.14.refs_6_), channel_id=1, source_target_pairs={{0,4},{1,5},{4,8},{5,9},{8,12},{9,13},{12,14},{13,15},{14,10},{15,... | collective-permute-start | bytes 983048 | tf_op jit(solution)/shard_map/ppermute | solution.py:517
  132.1 7.7 %collective-permute-start.17 = (f32[320,256]{1,0:T(8,128)S(1)}, f32[320,256]{1,0:T(8,128)S(1)}, u32[]{:S(2)}, u32[]{:S(2)}) collective-permute-start(f32[320,256]{1,0:T(8,128)S(1)} %collective-permute-done.15.refs_7_), channel_id=1, source_target_pairs={{0,2},{1,3},{4,0},{5,1},{8,4},{9,5},{12,8},{13,9},{14,12},{15,13},... | collective-permute-start | bytes 983048 | tf_op jit(solution)/shard_map/ppermute | solution.py:517
  139.2 39.5 %copy-start.3 = (f32[320,256]{1,0:T(8,128)}, f32[320,256]{1,0:T(8,128)S(1)}, u32[]{:S(2)}) copy-start(f32[320,256]{1,0:T(8,128)S(1)} %collective-permute-done.16.refs_8_) | copy-start | bytes 983044
  139.8 38.9 %copy-start.4 = (f32[320,256]{1,0:T(8,128)}, f32[320,256]{1,0:T(8,128)S(1)}, u32[]{:S(2)}) copy-start(f32[320,256]{1,0:T(8,128)S(1)} %collective-permute-done.17.refs_9_) | copy-start | bytes 983044
  141.0 5.4 %collective-permute-start.19 = (f32[160,256]{1,0:T(8,128)S(1)}, f32[160,256]{1,0:T(8,128)S(1)}, u32[]{:S(2)}, u32[]{:S(2)}) collective-permute-start(f32[160,256]{1,0:T(8,128)S(1)} %slice.13), channel_id=1, source_target_pairs={{0,2},{1,3},{4,0},{5,1},{8,4},{9,5},{12,8},{13,9},{14,12},{15,13},... | collective-permute-start | bytes 491528 | tf_op jit(solution)/shard_map/ppermute | solution.py:517
  142.1 12.4 %collective-permute-start.22 = (f32[320,256]{1,0:T(8,128)S(1)}, f32[320,256]{1,0:T(8,128)S(1)}, u32[]{:S(2)}, u32[]{:S(2)}) collective-permute-start(f32[320,256]{1,0:T(8,128)S(1)} %add.96.first_ref.refs_3_), channel_id=1, source_target_pairs={{0,1},{1,0},{2,3},{3,2},{4,5},{5,4},{6,7},{7,6},{8,9},{9,8},{10,11... | collective-permute-start | bytes 983048 | tf_op jit(solution)/shard_map/ppermute | solution.py:520
  142.1 7.2 %collective-permute-start.18 = (f32[160,256]{1,0:T(8,128)S(1)}, f32[160,256]{1,0:T(8,128)}, u32[]{:S(2)}, u32[]{:S(2)}) collective-permute-start(f32[160,256]{1,0:T(8,128)S(1)} %slice.12), channel_id=1, source_target_pairs={{0,4},{1,5},{4,8},{5,9},{8,12},{9,13},{12,14},{13,15},{14,10},{15,... | collective-permute-start | bytes 491528 | tf_op jit(solution)/shard_map/ppermute | solution.py:517
  143.1 11.7 %collective-permute-start.23 = (f32[320,256]{1,0:T(8,128)S(1)}, f32[320,256]{1,0:T(8,128)S(1)}, u32[]{:S(2)}, u32[]{:S(2)}) collective-permute-start(f32[320,256]{1,0:T(8,128)S(1)} %collective-permute-done.12.refs_4_), channel_id=1, source_target_pairs={{0,1},{1,0},{2,3},{3,2},{4,5},{5,4},{6,7},{7,6},{8,9},{9,8},{10,11... | collective-permute-start | bytes 983048 | tf_op jit(solution)/shard_map/ppermute | solution.py:520
  143.3 9.9 %collective-permute-start.21 = (f32[192,256]{1,0:T(8,128)S(1)}, f32[192,256]{1,0:T(8,128)}, u32[]{:S(2)}, u32[]{:S(2)}) collective-permute-start(f32[192,256]{1,0:T(8,128)S(1)} %add.97.second_ref.refs_21_), channel_id=1, source_target_pairs={{0,2},{1,3},{4,0},{5,1},{8,4},{9,5},{12,8},{13,9},{14,12},{15,13},... | collective-permute-start | bytes 589832 | tf_op jit(solution)/shard_map/ppermute | solution.py:517
  146.4 6.9 %collective-permute-start.20 = (f32[192,256]{1,0:T(8,128)S(1)}, f32[192,256]{1,0:T(8,128)}, u32[]{:S(2)}, u32[]{:S(2)}) collective-permute-start(f32[192,256]{1,0:T(8,128)S(1)} %add.97.second_ref.refs_21_), channel_id=1, source_target_pairs={{0,4},{1,5},{4,8},{5,9},{8,12},{9,13},{12,14},{13,15},{14,10},{15,... | collective-permute-start | bytes 589832 | tf_op jit(solution)/shard_map/ppermute | solution.py:517
  149.2 6.6 %collective-permute-start.24 = (f32[320,256]{1,0:T(8,128)S(1)}, f32[320,256]{1,0:T(8,128)S(1)}, u32[]{:S(2)}, u32[]{:S(2)}) collective-permute-start(f32[320,256]{1,0:T(8,128)S(1)} %collective-permute-done.13.refs_5_), channel_id=1, source_target_pairs={{0,1},{1,0},{2,3},{3,2},{4,5},{5,4},{6,7},{7,6},{8,9},{9,8},{10,11... | collective-permute-start | bytes 983048 | tf_op jit(solution)/shard_map/ppermute | solution.py:520
  153.3 7.6 %collective-permute-start.31 = (f32[192,256]{1,0:T(8,128)}, f32[192,256]{1,0:T(8,128)S(1)}, u32[]{:S(2)}, u32[]{:S(2)}) collective-permute-start(f32[192,256]{1,0:T(8,128)} %collective-permute-done.20.refs_22_), channel_id=1, source_target_pairs={{0,4},{1,5},{4,8},{5,9},{8,12},{9,13},{12,14},{13,15},{14,10},{15,... | collective-permute-start | bytes 589832 | tf_op jit(solution)/shard_map/ppermute | solution.py:517
  154.3 7.8 %collective-permute-start.25 = (f32[320,256]{1,0:T(8,128)S(1)}, f32[320,256]{1,0:T(8,128)S(1)}, u32[]{:S(2)}, u32[]{:S(2)}) collective-permute-start(f32[320,256]{1,0:T(8,128)S(1)} %collective-permute-done.14.refs_6_), channel_id=1, source_target_pairs={{0,1},{1,0},{2,3},{3,2},{4,5},{5,4},{6,7},{7,6},{8,9},{9,8},{10,11... | collective-permute-start | bytes 983048 | tf_op jit(solution)/shard_map/ppermute | solution.py:520
  154.5 24.2 %copy-start.14 = (f32[320,256]{1,0:T(8,128)}, f32[320,256]{1,0:T(8,128)S(1)}, u32[]{:S(2)}) copy-start(f32[320,256]{1,0:T(8,128)S(1)} %collective-permute-done.22.refs_12_) | copy-start | bytes 983044
  154.5 8.7 %collective-permute-start.26 = (f32[320,256]{1,0:T(8,128)S(1)}, f32[320,256]{1,0:T(8,128)S(1)}, u32[]{:S(2)}, u32[]{:S(2)}) collective-permute-start(f32[320,256]{1,0:T(8,128)S(1)} %collective-permute-done.15.refs_7_), channel_id=1, source_target_pairs={{0,1},{1,0},{2,3},{3,2},{4,5},{5,4},{6,7},{7,6},{8,9},{9,8},{10,11... | collective-permute-start | bytes 983048 | tf_op jit(solution)/shard_map/ppermute | solution.py:520
  154.8 23.9 %copy-start.15 = (f32[320,256]{1,0:T(8,128)}, f32[320,256]{1,0:T(8,128)S(1)}, u32[]{:S(2)}) copy-start(f32[320,256]{1,0:T(8,128)S(1)} %collective-permute-done.23.refs_13_) | copy-start | bytes 983044
  154.8 7.2 %collective-permute-start.32 = (f32[192,256]{1,0:T(8,128)}, f32[192,256]{1,0:T(8,128)S(1)}, u32[]{:S(2)}, u32[]{:S(2)}) collective-permute-start(f32[192,256]{1,0:T(8,128)} %collective-permute-done.21.refs_23_), channel_id=1, source_target_pairs={{0,2},{1,3},{4,0},{5,1},{8,4},{9,5},{12,8},{13,9},{14,12},{15,13},... | collective-permute-start | bytes 589832 | tf_op jit(solution)/shard_map/ppermute | solution.py:517
  155.9 22.9 %copy-start.16 = (f32[320,256]{1,0:T(8,128)}, f32[320,256]{1,0:T(8,128)S(1)}, u32[]{:S(2)}) copy-start(f32[320,256]{1,0:T(8,128)S(1)} %collective-permute-done.24.refs_14_) | copy-start | bytes 983044
  155.9 8.3 %collective-permute-start.27 = (f32[320,256]{1,0:T(8,128)S(1)}, f32[320,256]{1,0:T(8,128)S(1)}, u32[]{:S(2)}, u32[]{:S(2)}) collective-permute-start(f32[320,256]{1,0:T(8,128)S(1)} %collective-permute-done.16.refs_8_), channel_id=1, source_target_pairs={{0,1},{1,0},{2,3},{3,2},{4,5},{5,4},{6,7},{7,6},{8,9},{9,8},{10,11... | collective-permute-start | bytes 983048 | tf_op jit(solution)/shard_map/ppermute | solution.py:520
  160.8 17.9 %copy-start.21 = (f32[192,256]{1,0:T(8,128)}, f32[192,256]{1,0:T(8,128)S(1)}, u32[]{:S(2)}) copy-start(f32[192,256]{1,0:T(8,128)S(1)} %collective-permute-done.31.refs_24_) | copy-start | bytes 589828
  160.8 3.8 %collective-permute-start.28 = (f32[320,256]{1,0:T(8,128)S(1)}, f32[320,256]{1,0:T(8,128)S(1)}, u32[]{:S(2)}, u32[]{:S(2)}) collective-permute-start(f32[320,256]{1,0:T(8,128)S(1)} %collective-permute-done.17.refs_9_), channel_id=1, source_target_pairs={{0,1},{1,0},{2,3},{3,2},{4,5},{5,4},{6,7},{7,6},{8,9},{9,8},{10,11... | collective-permute-start | bytes 983048 | tf_op jit(solution)/shard_map/ppermute | solution.py:520
  162.0 16.7 %copy-start.22 = (f32[192,256]{1,0:T(8,128)}, f32[192,256]{1,0:T(8,128)S(1)}, u32[]{:S(2)}) copy-start(f32[192,256]{1,0:T(8,128)S(1)} %collective-permute-done.32.refs_25_) | copy-start | bytes 589828
  162.0 2.1 %collective-permute-start.37 = (f32[192,256]{1,0:T(8,128)}, f32[192,256]{1,0:T(8,128)S(1)}, u32[]{:S(2)}, u32[]{:S(2)}) collective-permute-start(f32[192,256]{1,0:T(8,128)} %copy-done.2), channel_id=1, source_target_pairs={{0,1},{1,0},{2,3},{3,2},{4,5},{5,4},{6,7},{7,6},{8,9},{9,8},{10,11... | collective-permute-start | bytes 589832 | tf_op jit(solution)/shard_map/ppermute | solution.py:520
  162.0 16.7 %copy-start.17 = (f32[320,256]{1,0:T(8,128)}, f32[320,256]{1,0:T(8,128)S(1)}, u32[]{:S(2)}) copy-start(f32[320,256]{1,0:T(8,128)S(1)} %collective-permute-done.25.refs_15_) | copy-start | bytes 983044
  162.0 7.3 %collective-permute-start.33 = (f32[192,256]{1,0:T(8,128)S(1)}, f32[192,256]{1,0:T(8,128)S(1)}, u32[]{:S(2)}, u32[]{:S(2)}) collective-permute-start(f32[192,256]{1,0:T(8,128)S(1)} %collective-permute-done.31.refs_24_), channel_id=1, source_target_pairs={{0,4},{1,5},{4,8},{5,9},{8,12},{9,13},{12,14},{13,15},{14,10},{15,... | collective-permute-start | bytes 589832 | tf_op jit(solution)/shard_map/ppermute | solution.py:517
  163.2 7.0 %collective-permute-start.34 = (f32[192,256]{1,0:T(8,128)S(1)}, f32[192,256]{1,0:T(8,128)S(1)}, u32[]{:S(2)}, u32[]{:S(2)}) collective-permute-start(f32[192,256]{1,0:T(8,128)S(1)} %collective-permute-done.32.refs_25_), channel_id=1, source_target_pairs={{0,2},{1,3},{4,0},{5,1},{8,4},{9,5},{12,8},{13,9},{14,12},{15,13},... | collective-permute-start | bytes 589832 | tf_op jit(solution)/shard_map/ppermute | solution.py:517
  164.1 8.6 %collective-permute-start.38 = (f32[192,256]{1,0:T(8,128)}, f32[192,256]{1,0:T(8,128)S(1)}, u32[]{:S(2)}, u32[]{:S(2)}) collective-permute-start(f32[192,256]{1,0:T(8,128)} %collective-permute-done.20.refs_22_), channel_id=1, source_target_pairs={{0,1},{1,0},{2,3},{3,2},{4,5},{5,4},{6,7},{7,6},{8,9},{9,8},{10,11... | collective-permute-start | bytes 589832 | tf_op jit(solution)/shard_map/ppermute | solution.py:520
  164.2 9.6 %collective-permute-start.39 = (f32[192,256]{1,0:T(8,128)}, f32[192,256]{1,0:T(8,128)S(1)}, u32[]{:S(2)}, u32[]{:S(2)}) collective-permute-start(f32[192,256]{1,0:T(8,128)} %collective-permute-done.21.refs_23_), channel_id=1, source_target_pairs={{0,1},{1,0},{2,3},{3,2},{4,5},{5,4},{6,7},{7,6},{8,9},{9,8},{10,11... | collective-permute-start | bytes 589832 | tf_op jit(solution)/shard_map/ppermute | solution.py:520
  164.7 9.2 %collective-permute-start.40 = (f32[192,256]{1,0:T(8,128)S(1)}, f32[192,256]{1,0:T(8,128)S(1)}, u32[]{:S(2)}, u32[]{:S(2)}) collective-permute-start(f32[192,256]{1,0:T(8,128)S(1)} %collective-permute-done.31.refs_24_), channel_id=1, source_target_pairs={{0,1},{1,0},{2,3},{3,2},{4,5},{5,4},{6,7},{7,6},{8,9},{9,8},{10,11... | collective-permute-start | bytes 589832 | tf_op jit(solution)/shard_map/ppermute | solution.py:520
  169.4 1.6 collective-permute-start.29
  170.2 1.6 collective-permute-start.30
  171.0 6.4 %collective-permute-start.41 = (f32[192,256]{1,0:T(8,128)S(1)}, f32[192,256]{1,0:T(8,128)S(1)}, u32[]{:S(2)}, u32[]{:S(2)}) collective-permute-start(f32[192,256]{1,0:T(8,128)S(1)} %collective-permute-done.32.refs_25_), channel_id=1, source_target_pairs={{0,1},{1,0},{2,3},{3,2},{4,5},{5,4},{6,7},{7,6},{8,9},{9,8},{10,11... | collective-permute-start | bytes 589832 | tf_op jit(solution)/shard_map/ppermute | solution.py:520
  171.8 4.8 %collective-permute-start.36 = (f32[96,256]{1,0:T(8,128)S(1)}, f32[96,256]{1,0:T(8,128)S(1)}, u32[]{:S(2)}, u32[]{:S(2)}) collective-permute-start(f32[96,256]{1,0:T(8,128)S(1)} %slice.15), channel_id=1, source_target_pairs={{0,2},{1,3},{4,0},{5,1},{8,4},{9,5},{12,8},{13,9},{14,12},{15,13},... | collective-permute-start | bytes 294920 | tf_op jit(solution)/shard_map/ppermute | solution.py:517
  172.7 4.6 %collective-permute-start.35 = (f32[96,256]{1,0:T(8,128)S(1)}, f32[96,256]{1,0:T(8,128)S(1)}, u32[]{:S(2)}, u32[]{:S(2)}) collective-permute-start(f32[96,256]{1,0:T(8,128)S(1)} %slice.14), channel_id=1, source_target_pairs={{0,4},{1,5},{4,8},{5,9},{8,12},{9,13},{12,14},{13,15},{14,10},{15,... | collective-permute-start | bytes 294920 | tf_op jit(solution)/shard_map/ppermute | solution.py:517
  173.8 4.8 %collective-permute-start.42 = (f32[192,256]{1,0:T(8,128)S(1)}, f32[192,256]{1,0:T(8,128)S(1)}, u32[]{:S(2)}, u32[]{:S(2)}) collective-permute-start(f32[192,256]{1,0:T(8,128)S(1)} %collective-permute-done.33.refs_26_), channel_id=1, source_target_pairs={{0,1},{1,0},{2,3},{3,2},{4,5},{5,4},{6,7},{7,6},{8,9},{9,8},{10,11... | collective-permute-start | bytes 589832 | tf_op jit(solution)/shard_map/ppermute | solution.py:520
  173.8 4.8 %collective-permute-start.43 = (f32[192,256]{1,0:T(8,128)S(1)}, f32[192,256]{1,0:T(8,128)S(1)}, u32[]{:S(2)}, u32[]{:S(2)}) collective-permute-start(f32[192,256]{1,0:T(8,128)S(1)} %collective-permute-done.34.refs_27_), channel_id=1, source_target_pairs={{0,1},{1,0},{2,3},{3,2},{4,5},{5,4},{6,7},{7,6},{8,9},{9,8},{10,11... | collective-permute-start | bytes 589832 | tf_op jit(solution)/shard_map/ppermute | solution.py:520
  176.6 1.3 collective-permute-start.45
  177.3 1.3 collective-permute-start.44
  (25 other events, 141.3 us)
Sparse Core Ops, SparseCore 0:
  46.4 42.1 reduce-scatter.4
  90.9 34.9 reduce-scatter.2

commit v9 on v8

--- a/solution.py
+++ b/solution.py
@@ -109,7 +109,7 @@
         work[at, to] = jnp.zeros((TILE, TILE), jnp.float32)
 
 
-def factor_kernel(table_ref, regular_ref, *refs):
+def factor_first(table_ref, regular_ref, *refs):
     parts, out_ref, packed = refs[:-2], refs[-2], refs[-1]
     count, rows = parts[0].shape[0], parts[0].shape[1]
     place = lax.axis_index("scen")
@@ -123,23 +123,35 @@
     for i in range(size // TILE):
         at = pl.ds(i * TILE, TILE)
         out_ref[at, at] += jnp.where(row_id == col_id, regular_ref[:, at], 0.0)
-    for k in range(size // TILE):
+    for k in range(size // TILE // 2):
         factor_step(k, out_ref)
 
 
-def inverse_factor(table, parts, regular):
+def factor_last(work_ref, out_ref):
+    out_ref[...] = work_ref[...]
+    tiles = out_ref.shape[0] // TILE
+    for k in range(tiles // 2, tiles):
+        factor_step(k, out_ref)
+
+
+def factor_stages(table, parts, regular):
     size = regular.shape[0]
-    return pl.pallas_call(
-        factor_kernel,
+    settings = dict(
         out_shape=jax.ShapeDtypeStruct((size, size), jnp.float32),
+        out_specs=vmem(1)[0],
+        cost_estimate=pl.CostEstimate(
+            flops=75 * size**3, bytes_accessed=8 * size * size, transcendentals=size
+        ),
+    )
+    first = lambda: pl.pallas_call(
+        factor_first,
         in_specs=[pl.BlockSpec(memory_space=pltpu.SMEM)] + vmem(1 + len(parts)),
-        out_specs=vmem(1)[0],
         scratch_shapes=[pltpu.VMEM((2 * TILE, 5 * TILE), jnp.float32)],
-        cost_estimate=pl.CostEstimate(
-            flops=150 * size**3, bytes_accessed=8 * size * size, transcendentals=size
-        ),
-        name="inverse_factor",
+        name="factor_first",
+        **settings,
     )(table, regular[None, :], *parts)
+    last = pl.pallas_call(factor_last, in_specs=vmem(1), name="factor_last", **settings)
+    return first, last
 
 
 def solve_kernel(inverse_ref, first_ref, second_ref, factor_ref, weight_ref):
@@ -377,24 +389,26 @@
 def update_kernel(count, table_ref, weight_ref, prior_ref, *refs):
     sources, out_ref, scratch = refs[:-7], refs[-7], refs[-6:]
     held, before, total, in_sem, prior_sem, out_sem = scratch
-    base = count * lax.axis_index("scen")
+    chips = count // 2
+    base = (count + chips) * lax.axis_index("scen")
     owned = held.shape[2]
-    chips = count // 2
     wide = 4
     chunks = [pl.ds(n * owned, wide * owned) for n in range(0, count, wide)]
 
     loads = []
     for n in range(count):
         core, slot = n // chips, n % chips
-        row = 0
+        copies = []
         for part in range(2):
             first = (2 * part + core) * (chips + 1)
             pieces = sources[first : first + chips + 1]
-            pieces = pieces[slot : slot + 1] if slot < chips - 1 else pieces[slot:]
-            for i, piece in enumerate(pieces):
-                to = held.at[n, pl.ds(row, piece.shape[0])]
-                loads.append(pltpu.make_async_copy(piece, to, in_sem.at[n, 2 * part + i]))
-                row += piece.shape[0]
+            copies += pieces[slot : slot + 1] if slot < chips - 1 else pieces[slot:]
+        copies.append(sources[4 * (chips + 1) + core].at[table_ref[base + count + slot]])
+        row = 0
+        for i, piece in enumerate(copies):
+            to = held.at[n, pl.ds(row, piece.shape[0])]
+            loads.append(pltpu.make_async_copy(piece, to, in_sem.at[n, i]))
+            row += piece.shape[0]
     fetches = [
         pltpu.make_async_copy(prior_ref.at[:, cols], before.at[:, cols], prior_sem.at[m])
         for m, cols in enumerate(chunks)
@@ -430,7 +444,7 @@
             pltpu.VMEM((count, width, owned), jnp.float32),
             pltpu.VMEM(prior.shape, jnp.float32),
             pltpu.VMEM(prior.shape, jnp.float32),
-            pltpu.SemaphoreType.DMA((count, 4)),
+            pltpu.SemaphoreType.DMA((count, 5)),
             pltpu.SemaphoreType.DMA((count // 4,)),
             pltpu.SemaphoreType.DMA((count // 4,)),
         ],
@@ -439,7 +453,7 @@
             bytes_accessed=8 * owned * order + 4 * order * width,
             transcendentals=0,
         ),
-        compiler_params=pltpu.CompilerParams(vmem_limit_bytes=VMEM_BYTES),
+        compiler_params=pltpu.CompilerParams(vmem_limit_bytes=26 * 2**20),
         name="update_rows",
     )(table, weights, prior, *sources)
 
@@ -491,6 +505,7 @@
         grams += [2 * q + c for c in (1 - core, core) for q in ring]
         blocks = [2 * ring[(at + offset) % chips] + c for c in (core, 1 - core) for offset in back]
         updates += [blocks.index(block) for block in range(2 * chips)]
+        updates += [(at + offset) % chips for offset in back]
         factors += [
             (2 * c + w) * lines + (z - by) % lines
             for c in (core, 1 - core) for w in (y, 1 - y) for by in range(lines)
@@ -544,8 +559,8 @@
     )
     block_got, given_0, given_1 = together((block_got, given_0, given_1))
     block = (block_kept + block_got).reshape(2, lines, -1, block_kept.shape[1])
-    beside, given_0 = together((slab(block, 1 - y), given_0))
-    got_0, beside = together((swap(given_0, 1), swap(beside, 2)))
+    got_0, beside = together((swap(given_0, 1), slab(block, 1 - y)))
+    beside = swap(beside, 2)
 
     panel_0 = sum_rows(kept_0 + got_0)
     got_1 = swap(given_1, 1)
@@ -559,32 +574,37 @@
     panel_1 = sum_rows(sums_1)
     beside = jnp.stack(beside)
     beside = jnp.concatenate([beside, swap(beside, 2)])
-    inverse = inverse_factor(factor_table, [beside, swap(beside, 1)], regular)
-    panel_0, inverse = together((panel_0, inverse))
+    factor_start, factor_end = factor_stages(factor_table, [beside, swap(beside, 1)], regular)
+    panel_0, work = together((panel_0, factor_start()))
     panel_0 += local_0
 
     shards_0 = [panel_0]
-    ahead = [panel_0, panel_0]
-    for d in range(1, far):
+    ahead, inverse = together(([step(panel_0, 1), step(panel_0, -1)], factor_end(work)))
+    shards_0 += ahead
+    for d in range(2, far):
         ahead = together([step(ahead[0], 1), step(ahead[1], -1)])
         shards_0 += ahead
     panel_1, ahead = together((panel_1, ahead))
     panel_1 += local_1
-    ahead, panel_1 = together((ahead, panel_1))
-    shards_1 = [panel_1]
-    last, ahead = across(panel_0, ahead), [step(panel_1, 1), step(panel_1, -1)]
+    middle = panel_1.shape[0] // 2
+    gathered = lax.all_gather(panel_1[middle:], "scen", axis_index_groups=groups)
+    ahead, part = together((ahead, panel_1[:middle]))
+    shards_1 = [part]
+    last, ahead = across(panel_0, ahead), [step(part, 1), step(part, -1)]
     last, ahead, solved = together((last, ahead, solve_rows(inverse, panel_0, panel_1)))
     shards_0 += last
     shards_1 += ahead
     for d in range(2, far):
         ahead = together([step(ahead[0], 1), step(ahead[1], -1)])
         shards_1 += ahead
-    shards_1 += across(panel_1, ahead)
+    ahead, gathered = together((across(part, ahead), gathered))
+    shards_1 += ahead
 
     factor_rows, weights = solved
     sources = []
     for shards in (shards_0, shards_1):
         sources += shards + [swap(piece, 1) for piece in shards]
+    sources += [gathered, swap(gathered, 1)]
     return update_rows(update_table, parts, weights, prior_schur, sources), factor_rows
 
 
@@ -617,7 +637,8 @@
     panel_half = lax.all_gather(panel_rows, "scen", axis_index_groups=same_core)
     panel_rest = swap_cores(panel_half)
     table = jnp.array([c ^ (d % 2) for d in range(parts) for c in range(2)], jnp.int32)
-    inverse = inverse_factor(table, [block, block_other], regular)
+    factor_start, factor_end = factor_stages(table, [block, block_other], regular)
+    inverse = factor_end(factor_start())
     factor_rows, weights = solve_rows(inverse, panel_rows.T[:half], panel_rows.T[half:])
     even = jnp.where(core == 0, panel_half, panel_rest)
     odd = jnp.where(core == 0, panel_rest, panel_half)

time: 199 us -> 219 us (1.10)
  blocking collectives: 0 us -> 22.2 us
  waiting for transfers between devices: 74.2 us -> 61.6 us
  Pallas kernels: 63.7 us -> 68.8 us
  local copies, waits for them, and re-layouts: 3.43 us -> 6.15 us
    all_gather x0 -> x1, blocking collectives: none -> 22.2 us  [shards_on_ring(): lax.all_gather(panel_1[middle:], 'scen', axis_index_groups=groups)]
    ppermute x16, waiting for transfers between devices: 47.8 us -> 28.6 us  [step(): return lax.ppermute(values, 'scen', pairs)]
    ppermute x24 -> x25, waiting for transfers between devices: 16.5 us -> 22.3 us  [swap(): return lax.ppermute(values, 'scen', [(d, d ^ bit) for d in range(parts)])]
    pallas_call x1, Pallas kernels: 11.5 us -> 14.3 us  [update_rows(): pl.pallas_call(lambda *refs: update_kernel(count, *refs), out_shape=jax.S...]
    pallas_call x1 -> x2, Pallas kernels: 22.3 us -> 24.6 us  [the longest x1 12.6 us: factor_stages(): pl.pallas_call(factor_first, in_specs=[pl.BlockSpec(memory_space=pltpu.SM...]
    unnamed x86 -> x28, local copies, waits for them, and re-layouts: 3.35 us -> 5.38 us
    ppermute x24 -> x25, starting transfers between devices: 7.68 us -> 9.44 us  [swap(): return lax.ppermute(values, 'scen', [(d, d ^ bit) for d in range(parts)])]
  transfers between devices with their start and end apart: 48 -> 49, of which waited for: 25 -> 29; matrix products, arithmetic and copies ran while one was open for 2% -> 3% of each run, Pallas kernels for 19% -> 18%
where the time goes in v9:
time: 219 us; the launch traced here: 218 us
  Pallas kernels  68.8 us (31%)
  waiting for transfers between devices  61.6 us (28%)
  starting transfers between devices  34.4 us (16%)
  blocking collectives  22.2 us (10%)
  between operations  14.9 us (7%)
  other arithmetic  10.5 us (5%)
  local copies, waits for them, and re-layouts  6.15 us (3%)
    ppermute x16, waiting for transfers between devices, step(): return lax.ppermute(values, 'scen', pairs)  28.6 us
    ppermute x25, waiting for transfers between devices, swap(): return lax.ppermute(values, 'scen', [(d, d ^ bit) for d in range(parts)])  22.3 us
    all_gather x1, blocking collectives, shards_on_ring(): lax.all_gather(panel_1[middle:], 'scen', axis_index_groups=groups)  22.2 us
    ppermute x16, starting transfers between devices, step(): return lax.ppermute(values, 'scen', pairs)  16.4 us
    pallas_call x1, Pallas kernels, pick_columns(): pl.pallas_call(pick_kernel, grid=(depth // tall,), in_specs=[pl.BlockSpec...  14.7 us
    pallas_call x1, Pallas kernels, update_rows(): pl.pallas_call(lambda *refs: update_kernel(count, *refs), out_shape=jax.S...  14.3 us
    pallas_call x1, Pallas kernels, factor_stages(): pl.pallas_call(factor_first, in_specs=[pl.BlockSpec(memory_space=pltpu.SM...  12.6 us
    pallas_call x1, Pallas kernels, shards_on_ring(): factor_end(work)  11.9 us
  transfers between devices with their start and end apart: 49, of which 29 were waited for; matrix products, arithmetic and copies ran while one was open for 3% of the time, Pallas kernels for 18%

profile of v9, /device:TPU:0, one launch (start us, length us, event | category | flops | bytes accessed | tf_op | source)
XLA Modules:
  0.0 218.4 jit_solution(13687306233445818726)
XLA Ops:
  7.9 14.7 %pick_columns.1 = (bf16[512,1024]{1,0:T(8,128)(2,1)}, f32[320,256]{1,0:T(8,128)}, f32[192,256]{1,0:T(8,128)}, f32[128,640]{1,0:T(8,128)}, f32[128,640]{1,0:T(8,128)}) custom-call(s32[1]{0:T(128)S(6)} %copy.15.counts_ref, s32[1,512]{1,0:T(1,128)} %bitcast.38, f32[1,1024]{1,0:T(1,128)} %bitcast.37, f32[256,4096]{1,0:T(8,128)} %refs_2_.1, ...), custom_call_target="tpu_custom_call" | custom-call | flops 6442450944 | bytes 12582912 | tf_op jit(solution)/shard_map/pick_columns/pallas_call | solution.py:273
  22.6 0.5 collective-permute-start
  23.1 11.2 %gram_blocks.1 = (f32[8,320,256]{2,1,0:T(8,128)}, f32[8,192,256]{2,1,0:T(8,128)}, f32[8,320,256]{2,1,0:T(8,128)}, f32[8,192,256]{2,1,0:T(8,128)}) custom-call(s32[256]{0:T(256)} %constant.79.clone.table_ref, bf16[512,1024]{1,0:T(8,128)(2,1)} %get-tuple-element.61.scaled_ref, bf16[1024,4096]{1,0:T(8,128)(2,1)} %rows_ref.3), custom_call_target="tpu_custom_call" | custom-call | flops 4294967296 | bytes 16777216 | tf_op jit(solution)/shard_map/gram_blocks/pallas_call | solution.py:365
  34.3 0.7 copy-done.8
  35.1 1.0 add.76
  36.1 0.7 dynamic-slice_bitcast_fusion
  36.8 3.3 %collective-permute-done.1 = f32[8,320,256]{2,1,0:T(8,128)S(1)} collective-permute-done((f32[8,320,256]{2,1,0:T(8,128)}, f32[8,320,256]{2,1,0:T(8,128)S(1)}, u32[]{:S(2)}, u32[]{:S(2)}) %collective-permute-start.1) | collective-permute-done | bytes 2621472 | tf_op jit(solution)/shard_map/ppermute | solution.py:535
  40.2 3.6 %add.95 = f32[8,320,256]{2,1,0:T(8,128)} add(f32[8,320,256]{2,1,0:T(8,128)} %get-tuple-element.74, f32[8,320,256]{2,1,0:T(8,128)S(1)} %collective-permute-done.1) | non-fusion elementwise | flops 655360 | bytes 7864320 | tf_op jit(solution)/shard_map/add | solution.py:565
  44.0 2.9 %collective-permute-start.2 = (f32[4,16,640]{2,1,0:T(8,128)}, f32[4,16,640]{2,1,0:T(8,128)}, u32[]{:S(2)}, u32[]{:S(2)}) collective-permute-start(f32[4,16,640]{2,1,0:T(8,128)} %dynamic-slice_bitcast_fusion), channel_id=1, source_target_pairs={{0,2},{1,3},{2,0},{3,1},{4,6},{5,7},{6,4},{7,5},{8,10},{9,11},{10,... | collective-permute-start | bytes 491528 | tf_op jit(solution)/shard_map/ppermute | solution.py:535
  46.9 4.8 %collective-permute-done.2 = f32[4,16,640]{2,1,0:T(8,128)} collective-permute-done((f32[4,16,640]{2,1,0:T(8,128)}, f32[4,16,640]{2,1,0:T(8,128)}, u32[]{:S(2)}, u32[]{:S(2)}) %collective-permute-start.2) | collective-permute-done | bytes 163872 | tf_op jit(solution)/shard_map/ppermute | solution.py:535
  51.7 1.0 bitcast_add_fusion
  52.7 0.7 copy-done.5
  53.4 3.9 %collective-permute-start.5 = (f32[16,640]{1,0:T(8,128)S(1)}, f32[16,640]{1,0:T(8,128)S(1)}, u32[]{:S(2)}, u32[]{:S(2)}) collective-permute-start(f32[16,640]{1,0:T(8,128)S(1)} %get-tuple-element.114), channel_id=1, source_target_pairs={{0,12},{1,13},{2,14},{3,15},{4,0},{5,1},{6,2},{7,3},{8,4},{9,5},{1... | collective-permute-start | bytes 122888 | tf_op jit(solution)/shard_map/ppermute | solution.py:543
  57.3 1.0 collective-permute-start.3
  58.3 2.0 collective-permute-done.5
  60.3 3.7 %collective-permute-done.4 = f32[16,640]{1,0:T(8,128)S(1)} collective-permute-done((f32[16,640]{1,0:T(8,128)S(1)}, f32[16,640]{1,0:T(8,128)S(1)}, u32[]{:S(2)}, u32[]{:S(2)}) %collective-permute-start.4) | collective-permute-done | bytes 40992 | tf_op jit(solution)/shard_map/ppermute | solution.py:543
  64.1 0.8 bitcast_add_fusion.1
  64.9 1.2 collective-permute-start.9
  66.1 1.7 collective-permute-start.8
  67.9 0.6 collective-permute-start.7
  68.5 1.5 add.94
  70.0 3.3 %collective-permute-done.8 = f32[16,640]{1,0:T(8,128)S(1)} collective-permute-done((f32[16,640]{1,0:T(8,128)S(1)}, f32[16,640]{1,0:T(8,128)S(1)}, u32[]{:S(2)}, u32[]{:S(2)}) %collective-permute-start.8) | collective-permute-done | bytes 40992 | tf_op jit(solution)/shard_map/ppermute | solution.py:543
  73.3 1.4 collective-permute-done.7
  74.7 1.3 collective-permute-start.10
  76.1 7.2 %collective-permute-done.10 = f32[4,16,640]{2,1,0:T(8,128)S(1)} collective-permute-done((f32[4,16,640]{2,1,0:T(8,128)S(1)}, f32[4,16,640]{2,1,0:T(8,128)S(1)}, u32[]{:S(2)}, u32[]{:S(2)}) %collective-permute-start.10) | collective-permute-done | bytes 163872 | tf_op jit(solution)/shard_map/ppermute | solution.py:535
  83.4 1.6 collective-permute-done.11.refs_1_
  85.0 0.7 copy-done.11
  85.8 12.6 %factor_first.1.work_ref = f32[512,512]{1,0:T(8,128)} custom-call(s32[256]{0:T(256)} %constant.81.clone.table_ref, f32[1,512]{1,0:T(1,128)} %bitcast.39, f32[8,16,640]{2,1,0:T(8,128)} %copy-done.10, f32[8,16,640]{2,1,0:T(8,128)} %copy-done.11), custom_call_target="tpu_custom_call" | custom-call | flops 10066329600 | bytes 2097152 | tf_op jit(solution)/shard_map/factor_first/pallas_call | solution.py:146
  98.4 1.7 add.96.first_ref.refs_3_
  100.1 1.7 collective-permute-start.13
  102.2 11.9 %factor_last.1.inverse_ref = f32[512,512]{1,0:T(8,128)} custom-call(f32[512,512]{1,0:T(8,128)} %factor_first.1.work_ref), custom_call_target="tpu_custom_call" | custom-call | flops 10066329600 | bytes 2097152 | tf_op jit(solution)/shard_map/factor_last/pallas_call | solution.py:582
  114.1 2.9 %collective-permute-done.13.refs_5_ = f32[320,256]{1,0:T(8,128)S(1)} collective-permute-done((f32[320,256]{1,0:T(8,128)}, f32[320,256]{1,0:T(8,128)S(1)}, u32[]{:S(2)}, u32[]{:S(2)}) %collective-permute-start.13) | collective-permute-done | bytes 327712 | tf_op jit(solution)/shard_map/ppermute | solution.py:532
  117.4 2.0 collective-permute-start.15
  119.4 9.8 %collective-permute-done.14.refs_6_ = f32[320,256]{1,0:T(8,128)S(1)} collective-permute-done((f32[320,256]{1,0:T(8,128)S(1)}, f32[320,256]{1,0:T(8,128)S(1)}, u32[]{:S(2)}, u32[]{:S(2)}) %collective-permute-start.14) | collective-permute-done | bytes 327712 | tf_op jit(solution)/shard_map/ppermute | solution.py:532
  129.2 1.5 collective-permute-start.16
  130.7 0.5 collective-permute-start.17
  131.2 6.7 %collective-permute-done.16.refs_8_ = f32[320,256]{1,0:T(8,128)S(1)} collective-permute-done((f32[320,256]{1,0:T(8,128)S(1)}, f32[320,256]{1,0:T(8,128)S(1)}, u32[]{:S(2)}, u32[]{:S(2)}) %collective-permute-start.16) | collective-permute-done | bytes 327712 | tf_op jit(solution)/shard_map/ppermute | solution.py:532
  137.9 1.4 collective-permute-done.17.refs_9_
  139.4 1.0 add.97.second_ref
  140.4 0.4 collective-permute-start.19
  140.8 1.7 collective-permute-start.18
  142.8 1.7 collective-permute-start.20
  144.5 4.0 %solve_rows.1 = (f32[256,512]{1,0:T(8,128)}, f32[256,512]{1,0:T(8,128)}) custom-call(f32[512,512]{1,0:T(8,128)} %factor_last.1.inverse_ref, f32[320,256]{1,0:T(8,128)} %add.96.first_ref.refs_3_, f32[192,256]{1,0:T(8,128)} %copy-done.4), custom_call_target="tpu_custom_call" | custom-call | flops 805306368 | bytes 2097152 | tf_op jit(solution)/shard_map/solve_rows/pallas_call | solution.py:168
  148.5 1.0 collective-permute-start.31
  149.5 1.1 collective-permute-start.32
  150.6 3.4 %collective-permute-done.31.refs_24_ = f32[96,256]{1,0:T(8,128)S(1)} collective-permute-done((f32[96,256]{1,0:T(8,128)S(1)}, f32[96,256]{1,0:T(8,128)S(1)}, u32[]{:S(2)}, u32[]{:S(2)}) %collective-permute-start.31) | collective-permute-done | bytes 98336 | tf_op jit(solution)/shard_map/ppermute | solution.py:532
  154.1 0.9 collective-permute-done.32.refs_25_
  154.9 0.8 collective-permute-start.33
  155.7 1.2 collective-permute-start.34
  156.9 0.5 collective-permute-start.23
  157.5 2.1 collective-permute-done.33.refs_26_
  159.5 1.0 collective-permute-done.34.refs_27_
  160.6 1.6 collective-permute-start.36
  162.2 0.5 collective-permute-start.35
  162.6 22.2 %all-gather = f32[768,256]{1,0:T(8,128)S(1)} all-gather(f32[96,256]{1,0:T(8,128)S(1)} %get-tuple-element.112), channel_id=2, replica_groups={{0,4,8,12,14,10,6,2},{1,5,9,13,15,11,7,3},{16,20,24,28,30,26,22,18},{17..., dimensions={0}, use_global_device_ids=true | all-gather | bytes 884736 | tf_op jit(solution)/shard_map/all_gather | solution.py:590
  184.9 0.5 collective-permute-start.24
  185.5 0.4 collective-permute-start.26
  186.0 1.6 collective-permute-done.24.refs_14_
  189.1 0.8 collective-permute-done.38.refs_31_
  190.4 0.9 collective-permute-done.29.refs_19_
  193.3 0.5 collective-permute-done.44.refs_37_
  194.0 2.2 %copy-done = f32[256,4096]{1,0:T(8,128)S(1)} copy-done((f32[256,4096]{1,0:T(8,128)S(1)}, f32[256,4096]{1,0:T(8,128)}, u32[]{:S(2)}) %copy-start) | copy-done | bytes 4194328
  196.2 1.0 copy-done.1
  197.3 14.3 %update_rows.1 = f32[256,4096]{1,0:T(8,128)} custom-call(s32[384]{0:T(512)S(1)} %copy-done.2, f32[256,512]{1,0:T(8,128)S(1)} %copy-done.1, f32[256,4096]{1,0:T(8,128)S(1)} %copy-done, f32[320,256]{1,0:T(8,128)} %add.96.first_ref.refs_3_, f32[320,256]{1,0:T(8,128)S(1)} %collective-permute-done.12.refs_4_, f32[320,256]{1,0:T(8,128)S(1)} %collective-permute-done.13.refs_5_, ...), custom_call_target="tpu_custom_call" | custom-call | flops 3221225472 | bytes 16777216 | tf_op jit(solution)/shard_map/update_rows/pallas_call | solution.py:436
  (87 shorter events, 6.3 us)
Async XLA Ops:
  7.2 91.2 %reduce-scatter.5.cloned.1.call-start = ((), (), s32[]{:S(2)}) async-start(), calls=%async_computation.3 | async-start | bytes 2949120 | tf_op jit(solution)/shard_map/reduce_scatter | solution.py:546
  22.6 12.5 %copy-start.7 = (f32[128,640]{1,0:T(8,128)S(1)}, f32[128,640]{1,0:T(8,128)}, u32[]{:S(2)}) copy-start(f32[128,640]{1,0:T(8,128)} %get-tuple-element.57) | copy-start | bytes 983044
  22.6 11.7 %collective-permute-start = (f32[128,640]{1,0:T(8,128)}, f32[128,640]{1,0:T(8,128)S(1)}, u32[]{:S(2)}, u32[]{:S(2)}) collective-permute-start(f32[128,640]{1,0:T(8,128)} %get-tuple-element.60), channel_id=1, source_target_pairs={{0,1},{1,0},{2,3},{3,2},{4,5},{5,4},{6,7},{7,6},{8,9},{9,8},{10,11... | collective-permute-start | bytes 983048 | tf_op jit(solution)/shard_map/ppermute | solution.py:535
  34.3 0.7 copy-start.8
  35.0 5.1 %collective-permute-start.1 = (f32[8,320,256]{2,1,0:T(8,128)}, f32[8,320,256]{2,1,0:T(8,128)S(1)}, u32[]{:S(2)}, u32[]{:S(2)}) collective-permute-start(f32[8,320,256]{2,1,0:T(8,128)} %get-tuple-element.65), channel_id=1, source_target_pairs={{0,1},{1,0},{2,3},{3,2},{4,5},{5,4},{6,7},{7,6},{8,9},{9,8},{10,11... | collective-permute-start | bytes 7864328 | tf_op jit(solution)/shard_map/ppermute | solution.py:535
  43.7 24.8 %copy-start.3 = (f32[8,192,256]{2,1,0:T(8,128)S(1)}, f32[8,192,256]{2,1,0:T(8,128)}, u32[]{:S(2)}) copy-start(f32[8,192,256]{2,1,0:T(8,128)} %get-tuple-element.71) | copy-start | bytes 4718596
  43.8 95.6 %reduce-scatter.3.cloned.1.call-start = ((), (), s32[]{:S(2)}) async-start(), calls=%async_computation.2 | async-start | bytes 1769472 | tf_op jit(solution)/shard_map/reduce_scatter | solution.py:546
  43.8 14.5 %collective-permute-start.6 = (f32[8,192,256]{2,1,0:T(8,128)}, f32[8,192,256]{2,1,0:T(8,128)S(1)}, u32[]{:S(2)}, u32[]{:S(2)}) collective-permute-start(f32[8,192,256]{2,1,0:T(8,128)} %get-tuple-element.67), channel_id=1, source_target_pairs={{0,1},{1,0},{2,3},{3,2},{4,5},{5,4},{6,7},{7,6},{8,9},{9,8},{10,11... | collective-permute-start | bytes 4718600 | tf_op jit(solution)/shard_map/ppermute | solution.py:535
  44.0 7.7 %collective-permute-start.2 = (f32[4,16,640]{2,1,0:T(8,128)}, f32[4,16,640]{2,1,0:T(8,128)}, u32[]{:S(2)}, u32[]{:S(2)}) collective-permute-start(f32[4,16,640]{2,1,0:T(8,128)} %dynamic-slice_bitcast_fusion), channel_id=1, source_target_pairs={{0,2},{1,3},{2,0},{3,1},{4,6},{5,7},{6,4},{7,5},{8,10},{9,11},{10,... | collective-permute-start | bytes 491528 | tf_op jit(solution)/shard_map/ppermute | solution.py:535
  52.7 0.7 copy-start.5
  53.4 6.9 %collective-permute-start.5 = (f32[16,640]{1,0:T(8,128)S(1)}, f32[16,640]{1,0:T(8,128)S(1)}, u32[]{:S(2)}, u32[]{:S(2)}) collective-permute-start(f32[16,640]{1,0:T(8,128)S(1)} %get-tuple-element.114), channel_id=1, source_target_pairs={{0,12},{1,13},{2,14},{3,15},{4,0},{5,1},{6,2},{7,3},{8,4},{9,5},{1... | collective-permute-start | bytes 122888 | tf_op jit(solution)/shard_map/ppermute | solution.py:543
  57.3 6.7 %collective-permute-start.4 = (f32[16,640]{1,0:T(8,128)S(1)}, f32[16,640]{1,0:T(8,128)S(1)}, u32[]{:S(2)}, u32[]{:S(2)}) collective-permute-start(f32[16,640]{1,0:T(8,128)S(1)} %get-tuple-element.115), channel_id=1, source_target_pairs={{0,8},{1,9},{2,10},{3,11},{4,12},{5,13},{6,14},{7,15},{8,0},{9,1},... | collective-permute-start | bytes 122888 | tf_op jit(solution)/shard_map/ppermute | solution.py:543
  57.3 6.8 %collective-permute-start.3 = (f32[16,640]{1,0:T(8,128)S(1)}, f32[16,640]{1,0:T(8,128)S(1)}, u32[]{:S(2)}, u32[]{:S(2)}) collective-permute-start(f32[16,640]{1,0:T(8,128)S(1)} %get-tuple-element.116), channel_id=1, source_target_pairs={{0,4},{1,5},{2,6},{3,7},{4,8},{5,9},{6,10},{7,11},{8,12},{9,13},{1... | collective-permute-start | bytes 122888 | tf_op jit(solution)/shard_map/ppermute | solution.py:543
  64.9 5.1 %collective-permute-start.9 = (f32[16,640]{1,0:T(8,128)S(1)}, f32[16,640]{1,0:T(8,128)S(1)}, u32[]{:S(2)}, u32[]{:S(2)}) collective-permute-start(f32[16,640]{1,0:T(8,128)S(1)} %bitcast_add_fusion.1), channel_id=1, source_target_pairs={{0,12},{1,13},{2,14},{3,15},{4,0},{5,1},{6,2},{7,3},{8,4},{9,5},{1... | collective-permute-start | bytes 122888 | tf_op jit(solution)/shard_map/ppermute | solution.py:543
  66.1 7.1 %collective-permute-start.8 = (f32[16,640]{1,0:T(8,128)S(1)}, f32[16,640]{1,0:T(8,128)S(1)}, u32[]{:S(2)}, u32[]{:S(2)}) collective-permute-start(f32[16,640]{1,0:T(8,128)S(1)} %bitcast_add_fusion.1), channel_id=1, source_target_pairs={{0,8},{1,9},{2,10},{3,11},{4,12},{5,13},{6,14},{7,15},{8,0},{9,1},... | collective-permute-start | bytes 122888 | tf_op jit(solution)/shard_map/ppermute | solution.py:543
  67.9 6.8 %collective-permute-start.7 = (f32[16,640]{1,0:T(8,128)S(1)}, f32[16,640]{1,0:T(8,128)S(1)}, u32[]{:S(2)}, u32[]{:S(2)}) collective-permute-start(f32[16,640]{1,0:T(8,128)S(1)} %bitcast_add_fusion.1), channel_id=1, source_target_pairs={{0,4},{1,5},{2,6},{3,7},{4,8},{5,9},{6,10},{7,11},{8,12},{9,13},{1... | collective-permute-start | bytes 122888 | tf_op jit(solution)/shard_map/ppermute | solution.py:543
  74.7 8.6 %collective-permute-start.10 = (f32[4,16,640]{2,1,0:T(8,128)S(1)}, f32[4,16,640]{2,1,0:T(8,128)S(1)}, u32[]{:S(2)}, u32[]{:S(2)}) collective-permute-start(f32[4,16,640]{2,1,0:T(8,128)S(1)} %pad_maximum_fusion), channel_id=1, source_target_pairs={{0,2},{1,3},{2,0},{3,1},{4,6},{5,7},{6,4},{7,5},{8,10},{9,11},{10,... | collective-permute-start | bytes 491528 | tf_op jit(solution)/shard_map/ppermute | solution.py:535
  83.3 1.7 copy-start.10
  83.3 1.7 collective-permute-start.11
  85.0 0.7 copy-start.11
  85.8 12.6 %copy-start.6 = (f32[320,256]{1,0:T(8,128)S(1)}, f32[320,256]{1,0:T(8,128)}, u32[]{:S(2)}) copy-start(f32[320,256]{1,0:T(8,128)} %get-tuple-element.81) | copy-start | bytes 983044
  100.1 39.2 %copy-start.9 = (f32[192,256]{1,0:T(8,128)S(1)}, f32[192,256]{1,0:T(8,128)}, u32[]{:S(2)}) copy-start(f32[192,256]{1,0:T(8,128)} %get-tuple-element.92) | copy-start | bytes 589828
  100.1 16.8 %collective-permute-start.13 = (f32[320,256]{1,0:T(8,128)}, f32[320,256]{1,0:T(8,128)S(1)}, u32[]{:S(2)}, u32[]{:S(2)}) collective-permute-start(f32[320,256]{1,0:T(8,128)} %add.96.first_ref.refs_3_), channel_id=1, source_target_pairs={{0,2},{1,3},{4,0},{5,1},{8,4},{9,5},{12,8},{13,9},{14,12},{15,13},... | collective-permute-start | bytes 983048 | tf_op jit(solution)/shard_map/ppermute | solution.py:532
  101.8 15.6 %collective-permute-start.12 = (f32[320,256]{1,0:T(8,128)}, f32[320,256]{1,0:T(8,128)S(1)}, u32[]{:S(2)}, u32[]{:S(2)}) collective-permute-start(f32[320,256]{1,0:T(8,128)} %add.96.first_ref.refs_3_), channel_id=1, source_target_pairs={{0,4},{1,5},{4,8},{5,9},{8,12},{9,13},{12,14},{13,15},{14,10},{15,... | collective-permute-start | bytes 983048 | tf_op jit(solution)/shard_map/ppermute | solution.py:532
  117.4 11.8 %collective-permute-start.14 = (f32[320,256]{1,0:T(8,128)S(1)}, f32[320,256]{1,0:T(8,128)S(1)}, u32[]{:S(2)}, u32[]{:S(2)}) collective-permute-start(f32[320,256]{1,0:T(8,128)S(1)} %collective-permute-done.12.refs_4_), channel_id=1, source_target_pairs={{0,4},{1,5},{4,8},{5,9},{8,12},{9,13},{12,14},{13,15},{14,10},{15,... | collective-permute-start | bytes 983048 | tf_op jit(solution)/shard_map/ppermute | solution.py:532
  117.4 11.8 %collective-permute-start.15 = (f32[320,256]{1,0:T(8,128)S(1)}, f32[320,256]{1,0:T(8,128)S(1)}, u32[]{:S(2)}, u32[]{:S(2)}) collective-permute-start(f32[320,256]{1,0:T(8,128)S(1)} %collective-permute-done.13.refs_5_), channel_id=1, source_target_pairs={{0,2},{1,3},{4,0},{5,1},{8,4},{9,5},{12,8},{13,9},{14,12},{15,13},... | collective-permute-start | bytes 983048 | tf_op jit(solution)/shard_map/ppermute | solution.py:532
  129.2 8.8 %collective-permute-start.16 = (f32[320,256]{1,0:T(8,128)S(1)}, f32[320,256]{1,0:T(8,128)S(1)}, u32[]{:S(2)}, u32[]{:S(2)}) collective-permute-start(f32[320,256]{1,0:T(8,128)S(1)} %collective-permute-done.14.refs_6_), channel_id=1, source_target_pairs={{0,4},{1,5},{4,8},{5,9},{8,12},{9,13},{12,14},{13,15},{14,10},{15,... | collective-permute-start | bytes 983048 | tf_op jit(solution)/shard_map/ppermute | solution.py:532
  130.7 8.7 %collective-permute-start.17 = (f32[320,256]{1,0:T(8,128)S(1)}, f32[320,256]{1,0:T(8,128)S(1)}, u32[]{:S(2)}, u32[]{:S(2)}) collective-permute-start(f32[320,256]{1,0:T(8,128)S(1)} %collective-permute-done.15.refs_7_), channel_id=1, source_target_pairs={{0,2},{1,3},{4,0},{5,1},{8,4},{9,5},{12,8},{13,9},{14,12},{15,13},... | collective-permute-start | bytes 983048 | tf_op jit(solution)/shard_map/ppermute | solution.py:532
  140.3 4.2 %copy-start.4 = (f32[192,256]{1,0:T(8,128)}, f32[192,256]{1,0:T(8,128)S(1)}, u32[]{:S(2)}) copy-start(f32[192,256]{1,0:T(8,128)S(1)} %add.97.second_ref) | copy-start | bytes 589828
  140.3 53.7 %copy-start.2 = (s32[384]{0:T(512)S(1)}, s32[384]{0:T(512)}, u32[]{:S(2)}) copy-start(s32[384]{0:T(512)} %constant.80.clone.refs_0_) | copy-start | bytes 4612
  140.4 8.1 %collective-permute-start.19 = (f32[160,256]{1,0:T(8,128)S(1)}, f32[160,256]{1,0:T(8,128)S(1)}, u32[]{:S(2)}, u32[]{:S(2)}) collective-permute-start(f32[160,256]{1,0:T(8,128)S(1)} %slice.20), channel_id=1, source_target_pairs={{0,2},{1,3},{4,0},{5,1},{8,4},{9,5},{12,8},{13,9},{14,12},{15,13},... | collective-permute-start | bytes 491528 | tf_op jit(solution)/shard_map/ppermute | solution.py:532
  140.8 7.8 %collective-permute-start.18 = (f32[160,256]{1,0:T(8,128)S(1)}, f32[160,256]{1,0:T(8,128)S(1)}, u32[]{:S(2)}, u32[]{:S(2)}) collective-permute-start(f32[160,256]{1,0:T(8,128)S(1)} %slice.19), channel_id=1, source_target_pairs={{0,4},{1,5},{4,8},{5,9},{8,12},{9,13},{12,14},{13,15},{14,10},{15,... | collective-permute-start | bytes 491528 | tf_op jit(solution)/shard_map/ppermute | solution.py:532
  142.5 6.0 %collective-permute-start.21 = (f32[96,256]{1,0:T(8,128)S(1)}, f32[96,256]{1,0:T(8,128)S(1)}, u32[]{:S(2)}, u32[]{:S(2)}) collective-permute-start(f32[96,256]{1,0:T(8,128)S(1)} %get-tuple-element.95.refs_21_), channel_id=1, source_target_pairs={{0,2},{1,3},{4,0},{5,1},{8,4},{9,5},{12,8},{13,9},{14,12},{15,13},... | collective-permute-start | bytes 294920 | tf_op jit(solution)/shard_map/ppermute | solution.py:532
  142.8 5.7 %collective-permute-start.20 = (f32[96,256]{1,0:T(8,128)S(1)}, f32[96,256]{1,0:T(8,128)S(1)}, u32[]{:S(2)}, u32[]{:S(2)}) collective-permute-start(f32[96,256]{1,0:T(8,128)S(1)} %get-tuple-element.95.refs_21_), channel_id=1, source_target_pairs={{0,4},{1,5},{4,8},{5,9},{8,12},{9,13},{12,14},{13,15},{14,10},{15,... | collective-permute-start | bytes 294920 | tf_op jit(solution)/shard_map/ppermute | solution.py:532
  148.5 5.5 %collective-permute-start.31 = (f32[96,256]{1,0:T(8,128)S(1)}, f32[96,256]{1,0:T(8,128)S(1)}, u32[]{:S(2)}, u32[]{:S(2)}) collective-permute-start(f32[96,256]{1,0:T(8,128)S(1)} %collective-permute-done.20.refs_22_), channel_id=1, source_target_pairs={{0,4},{1,5},{4,8},{5,9},{8,12},{9,13},{12,14},{13,15},{14,10},{15,... | collective-permute-start | bytes 294920 | tf_op jit(solution)/shard_map/ppermute | solution.py:532
  149.5 5.4 %collective-permute-start.32 = (f32[96,256]{1,0:T(8,128)S(1)}, f32[96,256]{1,0:T(8,128)S(1)}, u32[]{:S(2)}, u32[]{:S(2)}) collective-permute-start(f32[96,256]{1,0:T(8,128)S(1)} %collective-permute-done.21.refs_23_), channel_id=1, source_target_pairs={{0,2},{1,3},{4,0},{5,1},{8,4},{9,5},{12,8},{13,9},{14,12},{15,13},... | collective-permute-start | bytes 294920 | tf_op jit(solution)/shard_map/ppermute | solution.py:532
  154.9 4.6 %collective-permute-start.33 = (f32[96,256]{1,0:T(8,128)S(1)}, f32[96,256]{1,0:T(8,128)S(1)}, u32[]{:S(2)}, u32[]{:S(2)}) collective-permute-start(f32[96,256]{1,0:T(8,128)S(1)} %collective-permute-done.31.refs_24_), channel_id=1, source_target_pairs={{0,4},{1,5},{4,8},{5,9},{8,12},{9,13},{12,14},{13,15},{14,10},{15,... | collective-permute-start | bytes 294920 | tf_op jit(solution)/shard_map/ppermute | solution.py:532
  155.7 4.8 %collective-permute-start.34 = (f32[96,256]{1,0:T(8,128)S(1)}, f32[96,256]{1,0:T(8,128)S(1)}, u32[]{:S(2)}, u32[]{:S(2)}) collective-permute-start(f32[96,256]{1,0:T(8,128)S(1)} %collective-permute-done.32.refs_25_), channel_id=1, source_target_pairs={{0,2},{1,3},{4,0},{5,1},{8,4},{9,5},{12,8},{13,9},{14,12},{15,13},... | collective-permute-start | bytes 294920 | tf_op jit(solution)/shard_map/ppermute | solution.py:532
  156.9 28.5 %collective-permute-start.22 = (f32[320,256]{1,0:T(8,128)}, f32[320,256]{1,0:T(8,128)S(1)}, u32[]{:S(2)}, u32[]{:S(2)}) collective-permute-start(f32[320,256]{1,0:T(8,128)} %add.96.first_ref.refs_3_), channel_id=1, source_target_pairs={{0,1},{1,0},{2,3},{3,2},{4,5},{5,4},{6,7},{7,6},{8,9},{9,8},{10,11... | collective-permute-start | bytes 983048 | tf_op jit(solution)/shard_map/ppermute | solution.py:535
  156.9 29.0 %collective-permute-start.23 = (f32[320,256]{1,0:T(8,128)S(1)}, f32[320,256]{1,0:T(8,128)S(1)}, u32[]{:S(2)}, u32[]{:S(2)}) collective-permute-start(f32[320,256]{1,0:T(8,128)S(1)} %collective-permute-done.12.refs_4_), channel_id=1, source_target_pairs={{0,1},{1,0},{2,3},{3,2},{4,5},{5,4},{6,7},{7,6},{8,9},{9,8},{10,11... | collective-permute-start | bytes 983048 | tf_op jit(solution)/shard_map/ppermute | solution.py:535
  160.6 24.2 %collective-permute-start.36 = (f32[48,256]{1,0:T(8,128)S(1)}, f32[48,256]{1,0:T(8,128)S(1)}, u32[]{:S(2)}, u32[]{:S(2)}) collective-permute-start(f32[48,256]{1,0:T(8,128)S(1)} %slice.22), channel_id=1, source_target_pairs={{0,2},{1,3},{4,0},{5,1},{8,4},{9,5},{12,8},{13,9},{14,12},{15,13},... | collective-permute-start | bytes 147464 | tf_op jit(solution)/shard_map/ppermute | solution.py:532
  162.2 22.7 %collective-permute-start.35 = (f32[48,256]{1,0:T(8,128)S(1)}, f32[48,256]{1,0:T(8,128)S(1)}, u32[]{:S(2)}, u32[]{:S(2)}) collective-permute-start(f32[48,256]{1,0:T(8,128)S(1)} %slice.21), channel_id=1, source_target_pairs={{0,4},{1,5},{4,8},{5,9},{8,12},{9,13},{12,14},{13,15},{14,10},{15,... | collective-permute-start | bytes 147464 | tf_op jit(solution)/shard_map/ppermute | solution.py:532
  184.8 9.2 %collective-permute-start.46 = (f32[8,96,256]{2,1,0:T(8,128)S(1)}, f32[8,96,256]{2,1,0:T(8,128)S(1)}, u32[]{:S(2)}, u32[]{:S(2)}) collective-permute-start(f32[8,96,256]{2,1,0:T(8,128)S(1)} %bitcast.27), channel_id=1, source_target_pairs={{0,1},{1,0},{2,3},{3,2},{4,5},{5,4},{6,7},{7,6},{8,9},{9,8},{10,11... | collective-permute-start | bytes 2359304 | tf_op jit(solution)/shard_map/ppermute | solution.py:535
  184.9 2.7 %collective-permute-start.24 = (f32[320,256]{1,0:T(8,128)S(1)}, f32[320,256]{1,0:T(8,128)S(1)}, u32[]{:S(2)}, u32[]{:S(2)}) collective-permute-start(f32[320,256]{1,0:T(8,128)S(1)} %collective-permute-done.13.refs_5_), channel_id=1, source_target_pairs={{0,1},{1,0},{2,3},{3,2},{4,5},{5,4},{6,7},{7,6},{8,9},{9,8},{10,11... | collective-permute-start | bytes 983048 | tf_op jit(solution)/shard_map/ppermute | solution.py:535
  185.4 2.7 %collective-permute-start.25 = (f32[320,256]{1,0:T(8,128)S(1)}, f32[320,256]{1,0:T(8,128)S(1)}, u32[]{:S(2)}, u32[]{:S(2)}) collective-permute-start(f32[320,256]{1,0:T(8,128)S(1)} %collective-permute-done.14.refs_6_), channel_id=1, source_target_pairs={{0,1},{1,0},{2,3},{3,2},{4,5},{5,4},{6,7},{7,6},{8,9},{9,8},{10,11... | collective-permute-start | bytes 983048 | tf_op jit(solution)/shard_map/ppermute | solution.py:535
  185.5 3.1 %collective-permute-start.26 = (f32[320,256]{1,0:T(8,128)S(1)}, f32[320,256]{1,0:T(8,128)S(1)}, u32[]{:S(2)}, u32[]{:S(2)}) collective-permute-start(f32[320,256]{1,0:T(8,128)S(1)} %collective-permute-done.15.refs_7_), channel_id=1, source_target_pairs={{0,1},{1,0},{2,3},{3,2},{4,5},{5,4},{6,7},{7,6},{8,9},{9,8},{10,11... | collective-permute-start | bytes 983048 | tf_op jit(solution)/shard_map/ppermute | solution.py:535
  185.9 2.8 %collective-permute-start.37 = (f32[96,256]{1,0:T(8,128)S(1)}, f32[96,256]{1,0:T(8,128)S(1)}, u32[]{:S(2)}, u32[]{:S(2)}) collective-permute-start(f32[96,256]{1,0:T(8,128)S(1)} %get-tuple-element.95.refs_21_), channel_id=1, source_target_pairs={{0,1},{1,0},{2,3},{3,2},{4,5},{5,4},{6,7},{7,6},{8,9},{9,8},{10,11... | collective-permute-start | bytes 294920 | tf_op jit(solution)/shard_map/ppermute | solution.py:535
  187.6 4.2 %collective-permute-start.27 = (f32[320,256]{1,0:T(8,128)S(1)}, f32[320,256]{1,0:T(8,128)S(1)}, u32[]{:S(2)}, u32[]{:S(2)}) collective-permute-start(f32[320,256]{1,0:T(8,128)S(1)} %collective-permute-done.16.refs_8_), channel_id=1, source_target_pairs={{0,1},{1,0},{2,3},{3,2},{4,5},{5,4},{6,7},{7,6},{8,9},{9,8},{10,11... | collective-permute-start | bytes 983048 | tf_op jit(solution)/shard_map/ppermute | solution.py:535
  188.1 3.9 %collective-permute-start.28 = (f32[320,256]{1,0:T(8,128)S(1)}, f32[320,256]{1,0:T(8,128)S(1)}, u32[]{:S(2)}, u32[]{:S(2)}) collective-permute-start(f32[320,256]{1,0:T(8,128)S(1)} %collective-permute-done.17.refs_9_), channel_id=1, source_target_pairs={{0,1},{1,0},{2,3},{3,2},{4,5},{5,4},{6,7},{7,6},{8,9},{9,8},{10,11... | collective-permute-start | bytes 983048 | tf_op jit(solution)/shard_map/ppermute | solution.py:535
  188.6 1.3 collective-permute-start.38
  188.7 1.3 collective-permute-start.39
  189.9 1.4 collective-permute-start.29
  190.0 1.5 collective-permute-start.30
  191.3 1.3 collective-permute-start.40
  191.5 1.3 collective-permute-start.41
  191.8 1.3 collective-permute-start.42
  192.0 1.3 collective-permute-start.43
  192.6 1.2 collective-permute-start.44
  192.8 1.2 collective-permute-start.45
  194.0 2.2 %copy-start = (f32[256,4096]{1,0:T(8,128)S(1)}, f32[256,4096]{1,0:T(8,128)}, u32[]{:S(2)}) copy-start(f32[256,4096]{1,0:T(8,128)} %refs_2_.1) | copy-start | bytes 12582916
  196.2 1.0 copy-start.1
Sparse Core Ops, SparseCore 0:
  43.9 44.6 reduce-scatter.4
  90.9 36.2 reduce-scatter.2

commit v10 on v9

--- a/solution.py
+++ b/solution.py
@@ -123,35 +123,44 @@
     for i in range(size // TILE):
         at = pl.ds(i * TILE, TILE)
         out_ref[at, at] += jnp.where(row_id == col_id, regular_ref[:, at], 0.0)
-    for k in range(size // TILE // 2):
-        factor_step(k, out_ref)
-
-
-def factor_last(work_ref, out_ref):
+    factor_step(0, out_ref)
+
+
+def factor_next(steps, work_ref, out_ref):
     out_ref[...] = work_ref[...]
-    tiles = out_ref.shape[0] // TILE
-    for k in range(tiles // 2, tiles):
+    for k in steps:
         factor_step(k, out_ref)
 
 
 def factor_stages(table, parts, regular):
     size = regular.shape[0]
     settings = dict(
-        out_shape=jax.ShapeDtypeStruct((size, size), jnp.float32),
-        out_specs=vmem(1)[0],
-        cost_estimate=pl.CostEstimate(
-            flops=75 * size**3, bytes_accessed=8 * size * size, transcendentals=size
-        ),
-    )
+        out_shape=jax.ShapeDtypeStruct((size, size), jnp.float32), out_specs=vmem(1)[0]
+    )
+
+    def cost(steps):
+        return pl.CostEstimate(
+            flops=50 * steps * size**3, bytes_accessed=8 * size * size, transcendentals=size
+        )
+
     first = lambda: pl.pallas_call(
         factor_first,
         in_specs=[pl.BlockSpec(memory_space=pltpu.SMEM)] + vmem(1 + len(parts)),
         scratch_shapes=[pltpu.VMEM((2 * TILE, 5 * TILE), jnp.float32)],
+        cost_estimate=cost(1),
         name="factor_first",
         **settings,
     )(table, regular[None, :], *parts)
-    last = pl.pallas_call(factor_last, in_specs=vmem(1), name="factor_last", **settings)
-    return first, last
+    return [first] + [
+        pl.pallas_call(
+            lambda *refs, steps=steps: factor_next(steps, *refs),
+            in_specs=vmem(1),
+            cost_estimate=cost(len(steps)),
+            name=f"factor_{steps[0]}",
+            **settings,
+        )
+        for steps in ((1, 2), (3,))
+    ]
 
 
 def solve_kernel(inverse_ref, first_ref, second_ref, factor_ref, weight_ref):
@@ -398,12 +407,9 @@
     loads = []
     for n in range(count):
         core, slot = n // chips, n % chips
-        copies = []
-        for part in range(2):
-            first = (2 * part + core) * (chips + 1)
-            pieces = sources[first : first + chips + 1]
-            copies += pieces[slot : slot + 1] if slot < chips - 1 else pieces[slot:]
-        copies.append(sources[4 * (chips + 1) + core].at[table_ref[base + count + slot]])
+        pieces = sources[core * (chips + 1) : (core + 1) * (chips + 1)]
+        copies = list(pieces[slot : slot + 1] if slot < chips - 1 else pieces[slot:])
+        copies.append(sources[2 * (chips + 1) + core].at[table_ref[base + count + slot]])
         row = 0
         for i, piece in enumerate(copies):
             to = held.at[n, pl.ds(row, piece.shape[0])]
@@ -444,7 +450,7 @@
             pltpu.VMEM((count, width, owned), jnp.float32),
             pltpu.VMEM(prior.shape, jnp.float32),
             pltpu.VMEM(prior.shape, jnp.float32),
-            pltpu.SemaphoreType.DMA((count, 5)),
+            pltpu.SemaphoreType.DMA((count, 3)),
             pltpu.SemaphoreType.DMA((count // 4,)),
             pltpu.SemaphoreType.DMA((count // 4,)),
         ],
@@ -453,7 +459,7 @@
             bytes_accessed=8 * owned * order + 4 * order * width,
             transcendentals=0,
         ),
-        compiler_params=pltpu.CompilerParams(vmem_limit_bytes=26 * 2**20),
+        compiler_params=pltpu.CompilerParams(vmem_limit_bytes=VMEM_BYTES),
         name="update_rows",
     )(table, weights, prior, *sources)
 
@@ -518,7 +524,7 @@
     chips = parts // 2
     far = lines = chips // 2
     owned = prior_schur.shape[0]
-    cut = panel_cols.shape[0] * 5 // 8
+    cut = panel_cols.shape[0] * 23 // 32
     place = lax.axis_index("scen")
     y, z = place // 2 % 2, place // 4
     ring = RINGS[chips]
@@ -574,37 +580,29 @@
     panel_1 = sum_rows(sums_1)
     beside = jnp.stack(beside)
     beside = jnp.concatenate([beside, swap(beside, 2)])
-    factor_start, factor_end = factor_stages(factor_table, [beside, swap(beside, 1)], regular)
-    panel_0, work = together((panel_0, factor_start()))
+    stages = factor_stages(factor_table, [beside, swap(beside, 1)], regular)
+    panel_0, work = together((panel_0, stages[0]()))
     panel_0 += local_0
 
-    shards_0 = [panel_0]
-    ahead, inverse = together(([step(panel_0, 1), step(panel_0, -1)], factor_end(work)))
-    shards_0 += ahead
-    for d in range(2, far):
-        ahead = together([step(ahead[0], 1), step(ahead[1], -1)])
-        shards_0 += ahead
+    shards = [panel_0]
+    ahead = [panel_0, panel_0]
+    for d in range(1, far):
+        ahead, work = together((ahead, work))
+        ahead = [step(ahead[0], 1), step(ahead[1], -1)]
+        if d < len(stages):
+            work = stages[d](work)
+        ahead, work = together((ahead, work))
+        shards += ahead
     panel_1, ahead = together((panel_1, ahead))
     panel_1 += local_1
-    middle = panel_1.shape[0] // 2
-    gathered = lax.all_gather(panel_1[middle:], "scen", axis_index_groups=groups)
-    ahead, part = together((ahead, panel_1[:middle]))
-    shards_1 = [part]
-    last, ahead = across(panel_0, ahead), [step(part, 1), step(part, -1)]
-    last, ahead, solved = together((last, ahead, solve_rows(inverse, panel_0, panel_1)))
-    shards_0 += last
-    shards_1 += ahead
-    for d in range(2, far):
-        ahead = together([step(ahead[0], 1), step(ahead[1], -1)])
-        shards_1 += ahead
-    ahead, gathered = together((across(part, ahead), gathered))
-    shards_1 += ahead
+    gathered = lax.all_gather(panel_1, "scen", axis_index_groups=groups)
+    ahead, panel_1 = together((ahead, panel_1))
+    solved = solve_rows(work, panel_0, panel_1)
+    ahead, solved, gathered = together((across(panel_0, ahead), solved, gathered))
+    shards += ahead
 
     factor_rows, weights = solved
-    sources = []
-    for shards in (shards_0, shards_1):
-        sources += shards + [swap(piece, 1) for piece in shards]
-    sources += [gathered, swap(gathered, 1)]
+    sources = shards + [swap(piece, 1) for piece in shards] + [gathered, swap(gathered, 1)]
     return update_rows(update_table, parts, weights, prior_schur, sources), factor_rows
 
 
@@ -637,8 +635,8 @@
     panel_half = lax.all_gather(panel_rows, "scen", axis_index_groups=same_core)
     panel_rest = swap_cores(panel_half)
     table = jnp.array([c ^ (d % 2) for d in range(parts) for c in range(2)], jnp.int32)
-    factor_start, factor_end = factor_stages(table, [block, block_other], regular)
-    inverse = factor_end(factor_start())
+    stages = factor_stages(table, [block, block_other], regular)
+    inverse = stages[2](stages[1](stages[0]()))
     factor_rows, weights = solve_rows(inverse, panel_rows.T[:half], panel_rows.T[half:])
     even = jnp.where(core == 0, panel_half, panel_rest)
     odd = jnp.where(core == 0, panel_rest, panel_half)

time: 219 us -> 193 us (0.88)
  blocking collectives: 22.2 us -> 0 us
  waiting for transfers between devices: 61.6 us -> 73.3 us
  starting transfers between devices: 34.4 us -> 24.8 us
  local copies, waits for them, and re-layouts: 6.15 us -> 2.47 us
    all_gather x0 -> x1, waiting for transfers between devices: none -> 22.9 us  [shards_on_ring(): gathered = lax.all_gather(panel_1, 'scen', axis_index_groups=groups)]
    all_gather x1 -> x0, blocking collectives: 22.2 us -> none  [shards_on_ring(): lax.all_gather(panel_1[middle:], 'scen', axis_index_groups=groups)]
    ppermute x16 -> x8, waiting for transfers between devices: 28.6 us -> 17.1 us  [step(): return lax.ppermute(values, 'scen', pairs)]
    ppermute x16 -> x8, starting transfers between devices: 16.4 us -> 8.26 us  [step(): return lax.ppermute(values, 'scen', pairs)]
    pallas_call x1 -> x2, Pallas kernels: 11.9 us -> 19.2 us  [shards_on_ring(): work = stages[d](work)]
    pallas_call x1, Pallas kernels: 12.6 us -> 7.72 us  [factor_stages(): pl.pallas_call(factor_first, in_specs=[pl.BlockSpec(memory_space=pltpu.SM...]
    unnamed x28 -> x54, local copies, waits for them, and re-layouts: 5.38 us -> 2.39 us
    pallas_call x1, Pallas kernels: 14.3 us -> 11.3 us  [update_rows(): pl.pallas_call(lambda *refs: update_kernel(count, *refs), out_shape=jax.S...]
  transfers between devices with their start and end apart: 49 -> 33, of which waited for: 29 -> 25; matrix products, arithmetic and copies ran while one was open for 3% -> 2% of each run, Pallas kernels for 18% -> 22%
where the time goes in v10:
time: 193 us; the launch traced here: 192 us
  waiting for transfers between devices  73.3 us (38%)
  Pallas kernels  68.1 us (35%)
  starting transfers between devices  24.8 us (13%)
  between operations  14.7 us (8%)
  other arithmetic  9.01 us (5%)
  local copies, waits for them, and re-layouts  2.47 us (1%)
    all_gather x1, waiting for transfers between devices, shards_on_ring(): gathered = lax.all_gather(panel_1, 'scen', axis_index_groups=groups)  22.9 us
    ppermute x16, waiting for transfers between devices, swap(): return lax.ppermute(values, 'scen', [(d, d ^ bit) for d in range(parts)])  22.8 us
    pallas_call x2, Pallas kernels, shards_on_ring(): work = stages[d](work)  19.2 us
    ppermute x8, waiting for transfers between devices, step(): return lax.ppermute(values, 'scen', pairs)  17.1 us
    pallas_call x1, Pallas kernels, pick_columns(): pl.pallas_call(pick_kernel, grid=(depth // tall,), in_specs=[pl.BlockSpec...  14.7 us
    pallas_call x1, Pallas kernels, update_rows(): pl.pallas_call(lambda *refs: update_kernel(count, *refs), out_shape=jax.S...  11.3 us
    pallas_call x1, Pallas kernels, gram_blocks(): pl.pallas_call(gram_kernel, grid=(depth // tall,), in_specs=[pl.BlockSpec...  11.1 us
    ppermute x6, waiting for transfers between devices, shift(): lax.ppermute(values, 'scen', [(d, (d + 4 * by) % parts) for d in range(pa...  10.5 us
  transfers between devices with their start and end apart: 33, of which 25 were waited for; matrix products, arithmetic and copies ran while one was open for 2% of the time, Pallas kernels for 22%

profile of v10, /device:TPU:0, one launch (start us, length us, event | category | flops | bytes accessed | tf_op | source)
XLA Modules:
  0.0 192.4 jit_solution(11359405122143038690)
XLA Ops:
  7.9 14.7 %pick_columns.1 = (bf16[512,1024]{1,0:T(8,128)(2,1)}, f32[368,256]{1,0:T(8,128)}, f32[144,256]{1,0:T(8,128)}, f32[128,640]{1,0:T(8,128)}, f32[128,640]{1,0:T(8,128)}) custom-call(s32[1]{0:T(128)S(6)} %copy.15.counts_ref, s32[1,512]{1,0:T(1,128)} %bitcast.38, f32[1,1024]{1,0:T(1,128)} %bitcast.37, f32[256,4096]{1,0:T(8,128)} %refs_2_.1, ...), custom_call_target="tpu_custom_call" | custom-call | flops 6442450944 | bytes 12582912 | tf_op jit(solution)/shard_map/pick_columns/pallas_call | solution.py:282
  22.6 0.5 collective-permute-start
  23.1 11.1 %gram_blocks.1 = (f32[8,368,256]{2,1,0:T(8,128)}, f32[8,144,256]{2,1,0:T(8,128)}, f32[8,368,256]{2,1,0:T(8,128)}, f32[8,144,256]{2,1,0:T(8,128)}) custom-call(s32[256]{0:T(256)} %constant.79.clone.table_ref, bf16[512,1024]{1,0:T(8,128)(2,1)} %get-tuple-element.62.scaled_ref, bf16[1024,4096]{1,0:T(8,128)(2,1)} %rows_ref.3), custom_call_target="tpu_custom_call" | custom-call | flops 4294967296 | bytes 16777216 | tf_op jit(solution)/shard_map/gram_blocks/pallas_call | solution.py:374
  34.2 0.1 collective-permute-start.1
  34.4 1.1 add.76
  35.5 4.5 %collective-permute-done.1 = f32[8,368,256]{2,1,0:T(8,128)S(1)} collective-permute-done((f32[8,368,256]{2,1,0:T(8,128)}, f32[8,368,256]{2,1,0:T(8,128)S(1)}, u32[]{:S(2)}, u32[]{:S(2)}) %collective-permute-start.1) | collective-permute-done | bytes 3014688 | tf_op jit(solution)/shard_map/ppermute | solution.py:541
  40.0 3.9 %add.95 = f32[8,368,256]{2,1,0:T(8,128)} add(f32[8,368,256]{2,1,0:T(8,128)} %get-tuple-element.75, f32[8,368,256]{2,1,0:T(8,128)S(1)} %collective-permute-done.1) | non-fusion elementwise | flops 753664 | bytes 9043968 | tf_op jit(solution)/shard_map/add | solution.py:571
  43.9 0.2 collective-permute-start.6
  44.1 2.9 %collective-permute-start.2 = (f32[4,16,640]{2,1,0:T(8,128)S(1)}, f32[4,16,640]{2,1,0:T(8,128)S(1)}, u32[]{:S(2)}, u32[]{:S(2)}) collective-permute-start(f32[4,16,640]{2,1,0:T(8,128)S(1)} %dynamic-slice_bitcast_fusion), channel_id=1, source_target_pairs={{0,2},{1,3},{2,0},{3,1},{4,6},{5,7},{6,4},{7,5},{8,10},{9,11},{10,... | collective-permute-start | bytes 491528 | tf_op jit(solution)/shard_map/ppermute | solution.py:541
  47.0 4.5 %collective-permute-done.2 = f32[4,16,640]{2,1,0:T(8,128)S(1)} collective-permute-done((f32[4,16,640]{2,1,0:T(8,128)S(1)}, f32[4,16,640]{2,1,0:T(8,128)S(1)}, u32[]{:S(2)}, u32[]{:S(2)}) %collective-permute-start.2) | collective-permute-done | bytes 163872 | tf_op jit(solution)/shard_map/ppermute | solution.py:541
  51.6 3.9 %collective-permute-start.5 = (f32[16,640]{1,0:T(8,128)S(1)}, f32[16,640]{1,0:T(8,128)S(1)}, u32[]{:S(2)}, u32[]{:S(2)}) collective-permute-start(f32[16,640]{1,0:T(8,128)S(1)} %get-tuple-element.114), channel_id=1, source_target_pairs={{0,12},{1,13},{2,14},{3,15},{4,0},{5,1},{6,2},{7,3},{8,4},{9,5},{1... | collective-permute-start | bytes 122888 | tf_op jit(solution)/shard_map/ppermute | solution.py:549
  55.5 1.0 collective-permute-start.3
  56.5 1.7 collective-permute-done.5
  58.2 3.5 %collective-permute-done.4 = f32[16,640]{1,0:T(8,128)S(1)} collective-permute-done((f32[16,640]{1,0:T(8,128)S(1)}, f32[16,640]{1,0:T(8,128)S(1)}, u32[]{:S(2)}, u32[]{:S(2)}) %collective-permute-start.4) | collective-permute-done | bytes 40992 | tf_op jit(solution)/shard_map/ppermute | solution.py:549
  61.8 0.4 collective-permute-done.3
  62.1 1.2 collective-permute-start.9
  63.3 1.9 collective-permute-start.8
  65.2 0.8 collective-permute-start.7
  66.0 1.2 add.94
  67.2 0.1 collective-permute-done.9
  67.3 3.6 %collective-permute-done.8 = f32[16,640]{1,0:T(8,128)S(1)} collective-permute-done((f32[16,640]{1,0:T(8,128)S(1)}, f32[16,640]{1,0:T(8,128)S(1)}, u32[]{:S(2)}, u32[]{:S(2)}) %collective-permute-start.8) | collective-permute-done | bytes 40992 | tf_op jit(solution)/shard_map/ppermute | solution.py:549
  70.9 1.1 collective-permute-done.7
  72.0 1.6 collective-permute-start.10
  73.7 7.4 %collective-permute-done.10 = f32[4,16,640]{2,1,0:T(8,128)S(1)} collective-permute-done((f32[4,16,640]{2,1,0:T(8,128)S(1)}, f32[4,16,640]{2,1,0:T(8,128)S(1)}, u32[]{:S(2)}, u32[]{:S(2)}) %collective-permute-start.10) | collective-permute-done | bytes 163872 | tf_op jit(solution)/shard_map/ppermute | solution.py:541
  81.3 1.5 collective-permute-done.11.refs_1_
  82.9 0.7 copy-done.24
  83.6 7.7 %factor_first.1.refs_0_ = f32[512,512]{1,0:T(8,128)} custom-call(s32[256]{0:T(256)} %constant.81.clone.table_ref, f32[1,512]{1,0:T(1,128)} %bitcast.39, f32[8,16,640]{2,1,0:T(8,128)} %copy-done.23, f32[8,16,640]{2,1,0:T(8,128)} %copy-done.24), custom_call_target="tpu_custom_call" | custom-call | flops 6710886400 | bytes 2097152 | tf_op jit(solution)/shard_map/factor_first/pallas_call | solution.py:146
  91.3 1.0 add.96.first_ref.refs_3_
  92.4 0.8 collective-permute-start.12
  93.2 1.2 collective-permute-start.13
  94.5 12.3 %factor_1.1.refs_0_ = f32[512,512]{1,0:T(8,128)} custom-call(f32[512,512]{1,0:T(8,128)} %factor_first.1.refs_0_), custom_call_target="tpu_custom_call" | custom-call | flops 13421772800 | bytes 2097152 | tf_op jit(solution)/shard_map/factor_1/pallas_call | solution.py:593
  106.8 0.8 collective-permute-start.14
  107.7 1.2 collective-permute-start.15
  108.9 6.9 %factor_3.1.inverse_ref = f32[512,512]{1,0:T(8,128)} custom-call(f32[512,512]{1,0:T(8,128)} %factor_1.1.refs_0_), custom_call_target="tpu_custom_call" | custom-call | flops 6710886400 | bytes 2097152 | tf_op jit(solution)/shard_map/factor_3/pallas_call | solution.py:593
  115.8 7.6 %collective-permute-done.14.refs_6_ = f32[368,256]{1,0:T(8,128)S(1)} collective-permute-done((f32[368,256]{1,0:T(8,128)S(1)}, f32[368,256]{1,0:T(8,128)S(1)}, u32[]{:S(2)}, u32[]{:S(2)}) %collective-permute-start.14) | collective-permute-done | bytes 376864 | tf_op jit(solution)/shard_map/ppermute | solution.py:538
  123.4 0.2 collective-permute-done.15.refs_7_
  123.6 1.2 collective-permute-start.16
  124.8 0.8 collective-permute-start.17
  125.6 8.0 %collective-permute-done.16.refs_8_ = f32[368,256]{1,0:T(8,128)S(1)} collective-permute-done((f32[368,256]{1,0:T(8,128)S(1)}, f32[368,256]{1,0:T(8,128)S(1)}, u32[]{:S(2)}, u32[]{:S(2)}) %collective-permute-start.16) | collective-permute-done | bytes 376864 | tf_op jit(solution)/shard_map/ppermute | solution.py:538
  133.6 0.3 collective-permute-done.17.refs_9_
  133.9 1.7 add.97.second_ref
  135.7 1.5 collective-permute-start.19
  137.2 0.5 collective-permute-start.18
  137.7 4.0 %solve_rows.1 = (f32[256,512]{1,0:T(8,128)}, f32[256,512]{1,0:T(8,128)}) custom-call(f32[512,512]{1,0:T(8,128)} %factor_3.1.inverse_ref, f32[368,256]{1,0:T(8,128)} %copy-done, f32[144,256]{1,0:T(8,128)} %add.97.second_ref), custom_call_target="tpu_custom_call" | custom-call | flops 805306368 | bytes 2097152 | tf_op jit(solution)/shard_map/solve_rows/pallas_call | solution.py:177
  141.8 1.0 collective-permute-done.18.refs_10_
  142.8 22.9 %all-gather.3.cloned.1.call-done = f32[1152,256]{1,0:T(8,128)} async-done(((f32[144,256]{1,0:T(8,128)}), f32[1152,256]{1,0:T(8,128)}) %all-gather.3.cloned.1.call-update) | async-done | bytes 1179664 | tf_op jit(solution)/shard_map/all_gather | solution.py:598
  165.7 0.5 collective-permute-start.20
  166.3 0.4 collective-permute-start.22
  166.8 1.9 collective-permute-done.20.refs_12_
  168.7 0.4 collective-permute-start.24
  169.1 0.2 collective-permute-done.21.refs_13_
  169.3 0.4 collective-permute-start.25
  169.6 0.5 collective-permute-done.22.refs_14_
  170.3 0.4 collective-permute-done.23.refs_15_
  170.9 0.4 collective-permute-done.24.refs_16_
  171.3 0.1 collective-permute-start.28
  171.4 0.4 collective-permute-done.25.refs_17_
  171.8 0.5 collective-permute-done.26.refs_18_
  172.3 0.3 collective-permute-done.27.refs_19_
  172.6 0.3 collective-permute-done.28.refs_20_
  173.1 0.2 copy-done.20
  173.3 0.3 copy-done.21
  173.5 1.0 copy-done.2
  174.6 11.3 %update_rows.1 = f32[256,4096]{1,0:T(8,128)} custom-call(s32[384]{0:T(512)} %constant.80.clone.refs_0_, f32[256,512]{1,0:T(8,128)} %get-tuple-element.105.refs_1_, f32[256,4096]{1,0:T(8,128)} %refs_2_.1, f32[368,256]{1,0:T(8,128)} %copy-done, f32[368,256]{1,0:T(8,128)} %copy-done.7, f32[368,256]{1,0:T(8,128)} %copy-done.8, f32[368,256]{1,0:T(8,128)} %copy-done.9, ...), custom_call_target="tpu_custom_call" | custom-call | flops 3221225472 | bytes 16777216 | tf_op jit(solution)/shard_map/update_rows/pallas_call | solution.py:442
  (79 shorter events, 1.0 us)
Async XLA Ops:
  7.2 84.2 %reduce-scatter.5.cloned.1.call-start = ((), (), s32[]{:S(2)}) async-start(), calls=%async_computation.3 | async-start | bytes 3391488 | tf_op jit(solution)/shard_map/reduce_scatter | solution.py:552
  22.6 11.7 %collective-permute-start = (f32[128,640]{1,0:T(8,128)}, f32[128,640]{1,0:T(8,128)}, u32[]{:S(2)}, u32[]{:S(2)}) collective-permute-start(f32[128,640]{1,0:T(8,128)} %get-tuple-element.61), channel_id=1, source_target_pairs={{0,1},{1,0},{2,3},{3,2},{4,5},{5,4},{6,7},{7,6},{8,9},{9,8},{10,11... | collective-permute-start | bytes 983048 | tf_op jit(solution)/shard_map/ppermute | solution.py:541
  34.2 5.7 %collective-permute-start.1 = (f32[8,368,256]{2,1,0:T(8,128)}, f32[8,368,256]{2,1,0:T(8,128)S(1)}, u32[]{:S(2)}, u32[]{:S(2)}) collective-permute-start(f32[8,368,256]{2,1,0:T(8,128)} %get-tuple-element.66), channel_id=1, source_target_pairs={{0,1},{1,0},{2,3},{3,2},{4,5},{5,4},{6,7},{7,6},{8,9},{9,8},{10,11... | collective-permute-start | bytes 9043976 | tf_op jit(solution)/shard_map/ppermute | solution.py:541
  43.9 22.1 %copy-start.3 = (f32[8,144,256]{2,1,0:T(8,128)S(1)}, f32[8,144,256]{2,1,0:T(8,128)}, u32[]{:S(2)}) copy-start(f32[8,144,256]{2,1,0:T(8,128)} %get-tuple-element.72) | copy-start | bytes 3538948
  43.9 90.0 %reduce-scatter.3.cloned.1.call-start = ((), (), s32[]{:S(2)}) async-start(), calls=%async_computation.2 | async-start | bytes 1327104 | tf_op jit(solution)/shard_map/reduce_scatter | solution.py:552
  43.9 12.5 %collective-permute-start.6 = (f32[8,144,256]{2,1,0:T(8,128)}, f32[8,144,256]{2,1,0:T(8,128)S(1)}, u32[]{:S(2)}, u32[]{:S(2)}) collective-permute-start(f32[8,144,256]{2,1,0:T(8,128)} %get-tuple-element.68), channel_id=1, source_target_pairs={{0,1},{1,0},{2,3},{3,2},{4,5},{5,4},{6,7},{7,6},{8,9},{9,8},{10,11... | collective-permute-start | bytes 3538952 | tf_op jit(solution)/shard_map/ppermute | solution.py:541
  44.1 7.4 %collective-permute-start.2 = (f32[4,16,640]{2,1,0:T(8,128)S(1)}, f32[4,16,640]{2,1,0:T(8,128)S(1)}, u32[]{:S(2)}, u32[]{:S(2)}) collective-permute-start(f32[4,16,640]{2,1,0:T(8,128)S(1)} %dynamic-slice_bitcast_fusion), channel_id=1, source_target_pairs={{0,2},{1,3},{2,0},{3,1},{4,6},{5,7},{6,4},{7,5},{8,10},{9,11},{10,... | collective-permute-start | bytes 491528 | tf_op jit(solution)/shard_map/ppermute | solution.py:541
  51.6 6.6 %collective-permute-start.5 = (f32[16,640]{1,0:T(8,128)S(1)}, f32[16,640]{1,0:T(8,128)S(1)}, u32[]{:S(2)}, u32[]{:S(2)}) collective-permute-start(f32[16,640]{1,0:T(8,128)S(1)} %get-tuple-element.114), channel_id=1, source_target_pairs={{0,12},{1,13},{2,14},{3,15},{4,0},{5,1},{6,2},{7,3},{8,4},{9,5},{1... | collective-permute-start | bytes 122888 | tf_op jit(solution)/shard_map/ppermute | solution.py:549
  55.5 6.3 %collective-permute-start.4 = (f32[16,640]{1,0:T(8,128)S(1)}, f32[16,640]{1,0:T(8,128)S(1)}, u32[]{:S(2)}, u32[]{:S(2)}) collective-permute-start(f32[16,640]{1,0:T(8,128)S(1)} %get-tuple-element.115), channel_id=1, source_target_pairs={{0,8},{1,9},{2,10},{3,11},{4,12},{5,13},{6,14},{7,15},{8,0},{9,1},... | collective-permute-start | bytes 122888 | tf_op jit(solution)/shard_map/ppermute | solution.py:549
  55.5 6.7 %collective-permute-start.3 = (f32[16,640]{1,0:T(8,128)S(1)}, f32[16,640]{1,0:T(8,128)S(1)}, u32[]{:S(2)}, u32[]{:S(2)}) collective-permute-start(f32[16,640]{1,0:T(8,128)S(1)} %get-tuple-element.116), channel_id=1, source_target_pairs={{0,4},{1,5},{2,6},{3,7},{4,8},{5,9},{6,10},{7,11},{8,12},{9,13},{1... | collective-permute-start | bytes 122888 | tf_op jit(solution)/shard_map/ppermute | solution.py:549
  62.1 5.2 %collective-permute-start.9 = (f32[16,640]{1,0:T(8,128)S(1)}, f32[16,640]{1,0:T(8,128)S(1)}, u32[]{:S(2)}, u32[]{:S(2)}) collective-permute-start(f32[16,640]{1,0:T(8,128)S(1)} %bitcast_add_fusion.1), channel_id=1, source_target_pairs={{0,12},{1,13},{2,14},{3,15},{4,0},{5,1},{6,2},{7,3},{8,4},{9,5},{1... | collective-permute-start | bytes 122888 | tf_op jit(solution)/shard_map/ppermute | solution.py:549
  63.3 7.6 %collective-permute-start.8 = (f32[16,640]{1,0:T(8,128)S(1)}, f32[16,640]{1,0:T(8,128)S(1)}, u32[]{:S(2)}, u32[]{:S(2)}) collective-permute-start(f32[16,640]{1,0:T(8,128)S(1)} %bitcast_add_fusion.1), channel_id=1, source_target_pairs={{0,8},{1,9},{2,10},{3,11},{4,12},{5,13},{6,14},{7,15},{8,0},{9,1},... | collective-permute-start | bytes 122888 | tf_op jit(solution)/shard_map/ppermute | solution.py:549
  65.2 6.8 %collective-permute-start.7 = (f32[16,640]{1,0:T(8,128)S(1)}, f32[16,640]{1,0:T(8,128)S(1)}, u32[]{:S(2)}, u32[]{:S(2)}) collective-permute-start(f32[16,640]{1,0:T(8,128)S(1)} %bitcast_add_fusion.1), channel_id=1, source_target_pairs={{0,4},{1,5},{2,6},{3,7},{4,8},{5,9},{6,10},{7,11},{8,12},{9,13},{1... | collective-permute-start | bytes 122888 | tf_op jit(solution)/shard_map/ppermute | solution.py:549
  72.0 9.1 %collective-permute-start.10 = (f32[4,16,640]{2,1,0:T(8,128)S(1)}, f32[4,16,640]{2,1,0:T(8,128)S(1)}, u32[]{:S(2)}, u32[]{:S(2)}) collective-permute-start(f32[4,16,640]{2,1,0:T(8,128)S(1)} %pad_maximum_fusion), channel_id=1, source_target_pairs={{0,2},{1,3},{2,0},{3,1},{4,6},{5,7},{6,4},{7,5},{8,10},{9,11},{10,... | collective-permute-start | bytes 491528 | tf_op jit(solution)/shard_map/ppermute | solution.py:541
  81.2 1.7 copy-start.23
  81.2 1.7 collective-permute-start.11
  81.3 84.4 %all-gather.3.cloned.1.call-start = ((), (), s32[]{:S(2)}) async-start(), calls=%async_computation.4 | async-start | bytes 1327104 | tf_op jit(solution)/shard_map/all_gather | solution.py:598
  82.9 0.7 copy-start.24
  83.6 7.7 %copy-start.6 = (f32[368,256]{1,0:T(8,128)S(1)}, f32[368,256]{1,0:T(8,128)}, u32[]{:S(2)}) copy-start(f32[368,256]{1,0:T(8,128)} %get-tuple-element.82) | copy-start | bytes 1130500
  92.4 14.4 %copy-start = (f32[368,256]{1,0:T(8,128)}, f32[368,256]{1,0:T(8,128)S(1)}, u32[]{:S(2)}) copy-start(f32[368,256]{1,0:T(8,128)S(1)} %add.96.first_ref.refs_3_) | copy-start | bytes 1130500
  92.4 14.4 %collective-permute-start.12 = (f32[368,256]{1,0:T(8,128)S(1)}, f32[368,256]{1,0:T(8,128)S(1)}, u32[]{:S(2)}, u32[]{:S(2)}) collective-permute-start(f32[368,256]{1,0:T(8,128)S(1)} %add.96.first_ref.refs_3_), channel_id=1, source_target_pairs={{0,4},{1,5},{4,8},{5,9},{8,12},{9,13},{12,14},{13,15},{14,10},{15,... | collective-permute-start | bytes 1130504 | tf_op jit(solution)/shard_map/ppermute | solution.py:538
  93.2 13.6 %collective-permute-start.13 = (f32[368,256]{1,0:T(8,128)S(1)}, f32[368,256]{1,0:T(8,128)S(1)}, u32[]{:S(2)}, u32[]{:S(2)}) collective-permute-start(f32[368,256]{1,0:T(8,128)S(1)} %add.96.first_ref.refs_3_), channel_id=1, source_target_pairs={{0,2},{1,3},{4,0},{5,1},{8,4},{9,5},{12,8},{13,9},{14,12},{15,13},... | collective-permute-start | bytes 1130504 | tf_op jit(solution)/shard_map/ppermute | solution.py:538
  106.8 27.1 %copy-start.22 = (f32[144,256]{1,0:T(8,128)S(1)}, f32[144,256]{1,0:T(8,128)}, u32[]{:S(2)}) copy-start(f32[144,256]{1,0:T(8,128)} %get-tuple-element.98) | copy-start | bytes 442372
  106.8 59.4 %copy-start.7 = (f32[368,256]{1,0:T(8,128)}, f32[368,256]{1,0:T(8,128)S(1)}, u32[]{:S(2)}) copy-start(f32[368,256]{1,0:T(8,128)S(1)} %collective-permute-done.12.refs_4_) | copy-start | bytes 1130500
  106.8 59.5 %copy-start.8 = (f32[368,256]{1,0:T(8,128)}, f32[368,256]{1,0:T(8,128)S(1)}, u32[]{:S(2)}) copy-start(f32[368,256]{1,0:T(8,128)S(1)} %collective-permute-done.13.refs_5_) | copy-start | bytes 1130500
  106.8 16.6 %collective-permute-start.14 = (f32[368,256]{1,0:T(8,128)S(1)}, f32[368,256]{1,0:T(8,128)S(1)}, u32[]{:S(2)}, u32[]{:S(2)}) collective-permute-start(f32[368,256]{1,0:T(8,128)S(1)} %collective-permute-done.12.refs_4_), channel_id=1, source_target_pairs={{0,4},{1,5},{4,8},{5,9},{8,12},{9,13},{12,14},{13,15},{14,10},{15,... | collective-permute-start | bytes 1130504 | tf_op jit(solution)/shard_map/ppermute | solution.py:538
  107.7 15.9 %collective-permute-start.15 = (f32[368,256]{1,0:T(8,128)S(1)}, f32[368,256]{1,0:T(8,128)S(1)}, u32[]{:S(2)}, u32[]{:S(2)}) collective-permute-start(f32[368,256]{1,0:T(8,128)S(1)} %collective-permute-done.13.refs_5_), channel_id=1, source_target_pairs={{0,2},{1,3},{4,0},{5,1},{8,4},{9,5},{12,8},{13,9},{14,12},{15,13},... | collective-permute-start | bytes 1130504 | tf_op jit(solution)/shard_map/ppermute | solution.py:538
  115.8 49.9 %copy-start.1 = (f32[368,256]{1,0:T(8,128)S(1)}, f32[368,256]{1,0:T(8,128)}, u32[]{:S(2)}) copy-start(f32[368,256]{1,0:T(8,128)} %copy-done) | copy-start | bytes 1130500
  123.4 49.5 %copy-start.9 = (f32[368,256]{1,0:T(8,128)}, f32[368,256]{1,0:T(8,128)S(1)}, u32[]{:S(2)}) copy-start(f32[368,256]{1,0:T(8,128)S(1)} %collective-permute-done.14.refs_6_) | copy-start | bytes 1130500
  123.6 49.3 %copy-start.10 = (f32[368,256]{1,0:T(8,128)}, f32[368,256]{1,0:T(8,128)S(1)}, u32[]{:S(2)}) copy-start(f32[368,256]{1,0:T(8,128)S(1)} %collective-permute-done.15.refs_7_) | copy-start | bytes 1130500
  123.6 10.0 %collective-permute-start.16 = (f32[368,256]{1,0:T(8,128)S(1)}, f32[368,256]{1,0:T(8,128)S(1)}, u32[]{:S(2)}, u32[]{:S(2)}) collective-permute-start(f32[368,256]{1,0:T(8,128)S(1)} %collective-permute-done.14.refs_6_), channel_id=1, source_target_pairs={{0,4},{1,5},{4,8},{5,9},{8,12},{9,13},{12,14},{13,15},{14,10},{15,... | collective-permute-start | bytes 1130504 | tf_op jit(solution)/shard_map/ppermute | solution.py:538
  124.8 9.1 %collective-permute-start.17 = (f32[368,256]{1,0:T(8,128)S(1)}, f32[368,256]{1,0:T(8,128)S(1)}, u32[]{:S(2)}, u32[]{:S(2)}) collective-permute-start(f32[368,256]{1,0:T(8,128)S(1)} %collective-permute-done.15.refs_7_), channel_id=1, source_target_pairs={{0,2},{1,3},{4,0},{5,1},{8,4},{9,5},{12,8},{13,9},{14,12},{15,13},... | collective-permute-start | bytes 1130504 | tf_op jit(solution)/shard_map/ppermute | solution.py:538
  133.6 39.3 %copy-start.4 = (f32[368,256]{1,0:T(8,128)}, f32[368,256]{1,0:T(8,128)S(1)}, u32[]{:S(2)}) copy-start(f32[368,256]{1,0:T(8,128)S(1)} %collective-permute-done.16.refs_8_) | copy-start | bytes 1130500
  133.9 39.0 %copy-start.5 = (f32[368,256]{1,0:T(8,128)}, f32[368,256]{1,0:T(8,128)S(1)}, u32[]{:S(2)}) copy-start(f32[368,256]{1,0:T(8,128)S(1)} %collective-permute-done.17.refs_9_) | copy-start | bytes 1130500
  135.7 6.1 %collective-permute-start.19 = (f32[184,256]{1,0:T(8,128)S(1)}, f32[184,256]{1,0:T(8,128)S(1)}, u32[]{:S(2)}, u32[]{:S(2)}) collective-permute-start(f32[184,256]{1,0:T(8,128)S(1)} %slice.7), channel_id=1, source_target_pairs={{0,2},{1,3},{4,0},{5,1},{8,4},{9,5},{12,8},{13,9},{14,12},{15,13},... | collective-permute-start | bytes 565256 | tf_op jit(solution)/shard_map/ppermute | solution.py:538
  137.2 5.6 %collective-permute-start.18 = (f32[184,256]{1,0:T(8,128)S(1)}, f32[184,256]{1,0:T(8,128)S(1)}, u32[]{:S(2)}, u32[]{:S(2)}) collective-permute-start(f32[184,256]{1,0:T(8,128)S(1)} %slice.6), channel_id=1, source_target_pairs={{0,4},{1,5},{4,8},{5,9},{8,12},{9,13},{12,14},{13,15},{14,10},{15,... | collective-permute-start | bytes 565256 | tf_op jit(solution)/shard_map/ppermute | solution.py:538
  141.8 31.1 %copy-start.18 = (f32[184,256]{1,0:T(8,128)}, f32[184,256]{1,0:T(8,128)S(1)}, u32[]{:S(2)}) copy-start(f32[184,256]{1,0:T(8,128)S(1)} %collective-permute-done.19.refs_11_) | copy-start | bytes 565252
  142.8 30.1 %copy-start.19 = (f32[184,256]{1,0:T(8,128)}, f32[184,256]{1,0:T(8,128)S(1)}, u32[]{:S(2)}) copy-start(f32[184,256]{1,0:T(8,128)S(1)} %collective-permute-done.18.refs_10_) | copy-start | bytes 565252
  165.7 7.2 %collective-permute-start.29 = (f32[8,144,256]{2,1,0:T(8,128)}, f32[8,144,256]{2,1,0:T(8,128)S(1)}, u32[]{:S(2)}, u32[]{:S(2)}) collective-permute-start(f32[8,144,256]{2,1,0:T(8,128)} %bitcast.29), channel_id=1, source_target_pairs={{0,1},{1,0},{2,3},{3,2},{4,5},{5,4},{6,7},{7,6},{8,9},{9,8},{10,11... | collective-permute-start | bytes 3538952 | tf_op jit(solution)/shard_map/ppermute | solution.py:541
  165.7 3.0 %collective-permute-start.20 = (f32[368,256]{1,0:T(8,128)S(1)}, f32[368,256]{1,0:T(8,128)S(1)}, u32[]{:S(2)}, u32[]{:S(2)}) collective-permute-start(f32[368,256]{1,0:T(8,128)S(1)} %copy-done.1), channel_id=1, source_target_pairs={{0,1},{1,0},{2,3},{3,2},{4,5},{5,4},{6,7},{7,6},{8,9},{9,8},{10,11... | collective-permute-start | bytes 1130504 | tf_op jit(solution)/shard_map/ppermute | solution.py:541
  166.2 3.0 %collective-permute-start.21 = (f32[368,256]{1,0:T(8,128)S(1)}, f32[368,256]{1,0:T(8,128)S(1)}, u32[]{:S(2)}, u32[]{:S(2)}) collective-permute-start(f32[368,256]{1,0:T(8,128)S(1)} %collective-permute-done.12.refs_4_), channel_id=1, source_target_pairs={{0,1},{1,0},{2,3},{3,2},{4,5},{5,4},{6,7},{7,6},{8,9},{9,8},{10,11... | collective-permute-start | bytes 1130504 | tf_op jit(solution)/shard_map/ppermute | solution.py:541
  166.3 3.9 %collective-permute-start.22 = (f32[368,256]{1,0:T(8,128)S(1)}, f32[368,256]{1,0:T(8,128)S(1)}, u32[]{:S(2)}, u32[]{:S(2)}) collective-permute-start(f32[368,256]{1,0:T(8,128)S(1)} %collective-permute-done.13.refs_5_), channel_id=1, source_target_pairs={{0,1},{1,0},{2,3},{3,2},{4,5},{5,4},{6,7},{7,6},{8,9},{9,8},{10,11... | collective-permute-start | bytes 1130504 | tf_op jit(solution)/shard_map/ppermute | solution.py:541
  166.7 4.0 %collective-permute-start.23 = (f32[368,256]{1,0:T(8,128)S(1)}, f32[368,256]{1,0:T(8,128)S(1)}, u32[]{:S(2)}, u32[]{:S(2)}) collective-permute-start(f32[368,256]{1,0:T(8,128)S(1)} %collective-permute-done.14.refs_6_), channel_id=1, source_target_pairs={{0,1},{1,0},{2,3},{3,2},{4,5},{5,4},{6,7},{7,6},{8,9},{9,8},{10,11... | collective-permute-start | bytes 1130504 | tf_op jit(solution)/shard_map/ppermute | solution.py:541
  168.7 4.2 %copy-start.11 = (f32[368,256]{1,0:T(8,128)}, f32[368,256]{1,0:T(8,128)S(1)}, u32[]{:S(2)}) copy-start(f32[368,256]{1,0:T(8,128)S(1)} %collective-permute-done.20.refs_12_) | copy-start | bytes 1130500
  168.7 2.5 %collective-permute-start.24 = (f32[368,256]{1,0:T(8,128)S(1)}, f32[368,256]{1,0:T(8,128)S(1)}, u32[]{:S(2)}, u32[]{:S(2)}) collective-permute-start(f32[368,256]{1,0:T(8,128)S(1)} %collective-permute-done.15.refs_7_), channel_id=1, source_target_pairs={{0,1},{1,0},{2,3},{3,2},{4,5},{5,4},{6,7},{7,6},{8,9},{9,8},{10,11... | collective-permute-start | bytes 1130504 | tf_op jit(solution)/shard_map/ppermute | solution.py:541
  169.3 3.7 %copy-start.12 = (f32[368,256]{1,0:T(8,128)}, f32[368,256]{1,0:T(8,128)S(1)}, u32[]{:S(2)}) copy-start(f32[368,256]{1,0:T(8,128)S(1)} %collective-permute-done.21.refs_13_) | copy-start | bytes 1130500
  169.3 2.5 %collective-permute-start.25 = (f32[368,256]{1,0:T(8,128)S(1)}, f32[368,256]{1,0:T(8,128)S(1)}, u32[]{:S(2)}, u32[]{:S(2)}) collective-permute-start(f32[368,256]{1,0:T(8,128)S(1)} %collective-permute-done.16.refs_8_), channel_id=1, source_target_pairs={{0,1},{1,0},{2,3},{3,2},{4,5},{5,4},{6,7},{7,6},{8,9},{9,8},{10,11... | collective-permute-start | bytes 1130504 | tf_op jit(solution)/shard_map/ppermute | solution.py:541
  170.2 2.8 %copy-start.13 = (f32[368,256]{1,0:T(8,128)}, f32[368,256]{1,0:T(8,128)S(1)}, u32[]{:S(2)}) copy-start(f32[368,256]{1,0:T(8,128)S(1)} %collective-permute-done.22.refs_14_) | copy-start | bytes 1130500
  170.2 2.2 %collective-permute-start.26 = (f32[368,256]{1,0:T(8,128)S(1)}, f32[368,256]{1,0:T(8,128)S(1)}, u32[]{:S(2)}, u32[]{:S(2)}) collective-permute-start(f32[368,256]{1,0:T(8,128)S(1)} %collective-permute-done.17.refs_9_), channel_id=1, source_target_pairs={{0,1},{1,0},{2,3},{3,2},{4,5},{5,4},{6,7},{7,6},{8,9},{9,8},{10,11... | collective-permute-start | bytes 1130504 | tf_op jit(solution)/shard_map/ppermute | solution.py:541
  170.7 2.2 %copy-start.14 = (f32[368,256]{1,0:T(8,128)}, f32[368,256]{1,0:T(8,128)S(1)}, u32[]{:S(2)}) copy-start(f32[368,256]{1,0:T(8,128)S(1)} %collective-permute-done.23.refs_15_) | copy-start | bytes 1130500
  170.7 1.9 collective-permute-start.27
  171.3 1.7 copy-start.15
  171.3 1.6 collective-permute-start.28
  171.8 1.2 copy-start.16
  172.3 0.8 copy-start.17
  172.6 0.7 copy-start.20
  172.9 0.7 copy-start.21
  173.5 1.0 copy-start.2
Sparse Core Ops, SparseCore 0:
  44.0 47.0 reduce-scatter.4
  93.5 32.4 reduce-scatter.2
  135.7 29.9 all-gather.2

commit v11 on v10

--- a/solution.py
+++ b/solution.py
@@ -407,9 +407,11 @@
     loads = []
     for n in range(count):
         core, slot = n // chips, n % chips
-        pieces = sources[core * (chips + 1) : (core + 1) * (chips + 1)]
-        copies = list(pieces[slot : slot + 1] if slot < chips - 1 else pieces[slot:])
-        copies.append(sources[2 * (chips + 1) + core].at[table_ref[base + count + slot]])
+        if len(sources) == 2:
+            copies = [sources[core].at[table_ref[base + count + slot]]]
+        else:
+            pieces = sources[core * (chips + 1) : (core + 1) * (chips + 1)]
+            copies = pieces[slot : slot + 1] if slot < chips - 1 else pieces[slot:]
         row = 0
         for i, piece in enumerate(copies):
             to = held.at[n, pl.ds(row, piece.shape[0])]
@@ -450,7 +452,7 @@
             pltpu.VMEM((count, width, owned), jnp.float32),
             pltpu.VMEM(prior.shape, jnp.float32),
             pltpu.VMEM(prior.shape, jnp.float32),
-            pltpu.SemaphoreType.DMA((count, 3)),
+            pltpu.SemaphoreType.DMA((count, 2)),
             pltpu.SemaphoreType.DMA((count // 4,)),
             pltpu.SemaphoreType.DMA((count // 4,)),
         ],
@@ -524,7 +526,7 @@
     chips = parts // 2
     far = lines = chips // 2
     owned = prior_schur.shape[0]
-    cut = panel_cols.shape[0] * 23 // 32
+    cut = panel_cols.shape[0] * 3 // 4
     place = lax.axis_index("scen")
     y, z = place // 2 % 2, place // 4
     ring = RINGS[chips]
@@ -586,24 +588,27 @@
 
     shards = [panel_0]
     ahead = [panel_0, panel_0]
+    gathered = None
     for d in range(1, far):
         ahead, work = together((ahead, work))
+        if d == far - 1:
+            panel_1, ahead = together((panel_1, ahead))
+            panel_1 += local_1
+            gathered = lax.all_gather(panel_1, "scen", axis_index_groups=groups)
+            ahead, panel_1 = together((ahead, panel_1))
         ahead = [step(ahead[0], 1), step(ahead[1], -1)]
         if d < len(stages):
             work = stages[d](work)
         ahead, work = together((ahead, work))
         shards += ahead
-    panel_1, ahead = together((panel_1, ahead))
-    panel_1 += local_1
-    gathered = lax.all_gather(panel_1, "scen", axis_index_groups=groups)
-    ahead, panel_1 = together((ahead, panel_1))
-    solved = solve_rows(work, panel_0, panel_1)
-    ahead, solved, gathered = together((across(panel_0, ahead), solved, gathered))
+    ahead, solved = together((across(panel_0, ahead), solve_rows(work, panel_0, panel_1)))
     shards += ahead
-
     factor_rows, weights = solved
-    sources = shards + [swap(piece, 1) for piece in shards] + [gathered, swap(gathered, 1)]
-    return update_rows(update_table, parts, weights, prior_schur, sources), factor_rows
+    shards = shards + [swap(piece, 1) for piece in shards]
+    updated = update_rows(update_table, parts, weights[:, :cut], prior_schur, shards)
+    updated, gathered, weights = together((updated, gathered, weights))
+    sources = [gathered, swap(gathered, 1)]
+    return update_rows(update_table, parts, weights[:, cut:], updated, sources), factor_rows
 
 
 def shards_by_groups(scenario_rows, row_weights, row_counts, panel_cols, regular, prior_schur):

time: 193 us -> 186 us (0.964)
  waiting for transfers between devices: 73.3 us -> 54.8 us
  Pallas kernels: 68.1 us -> 75 us
  local copies, waits for them, and re-layouts: 2.47 us -> 6.76 us
    all_gather x1, waiting for transfers between devices: 22.9 us -> 0.02 us  [shards_on_ring(): gathered = lax.all_gather(panel_1, 'scen', axis_index_groups=groups)]
    ppermute x8, waiting for transfers between devices: 17.1 us -> 24 us  [step(): return lax.ppermute(values, 'scen', pairs)]
    pallas_call x1 -> x2, Pallas kernels: 11.3 us -> 18.2 us  [update_rows(): pl.pallas_call(lambda *refs: update_kernel(count, *refs), out_shape=jax.S...]
    reduce_scatter x2, waiting for transfers between devices: 0.01 us -> 5.18 us  [sum_rows(): lax.psum_scatter(values, 'scen', scatter_dimension=0, axis_index_groups=g...]
    ppermute x16, waiting for transfers between devices: 22.8 us -> 18.3 us  [swap(): return lax.ppermute(values, 'scen', [(d, d ^ bit) for d in range(parts)])]
    slice x0 -> x2, local copies, waits for them, and re-layouts: none -> 3.35 us  [the longest x1 1.78 us: shards_on_ring(): weights[:, :cut]]
    ppermute x6, waiting for transfers between devices: 10.5 us -> 7.23 us  [shift(): lax.ppermute(values, 'scen', [(d, (d + 4 * by) % parts) for d in range(pa...]
  transfers between devices with their start and end apart: 33 -> 33, of which waited for: 25 -> 19; matrix products, arithmetic and copies ran while one was open for 2% -> 4% of each run, Pallas kernels for 22% -> 28%
where the time goes in v11:
time: 186 us
  Pallas kernels  75 us (40%)
  waiting for transfers between devices  54.8 us (29%)
  starting transfers between devices  25.7 us (14%)
  between operations  14.7 us (8%)
  other arithmetic  8.88 us (5%)
  local copies, waits for them, and re-layouts  6.76 us (4%)
    ppermute x8, waiting for transfers between devices, step(): return lax.ppermute(values, 'scen', pairs)  24 us
    pallas_call x2, Pallas kernels, shards_on_ring(): work = stages[d](work)  19.2 us
    ppermute x16, waiting for transfers between devices, swap(): return lax.ppermute(values, 'scen', [(d, d ^ bit) for d in range(parts)])  18.3 us
    pallas_call x2, Pallas kernels, update_rows(): pl.pallas_call(lambda *refs: update_kernel(count, *refs), out_shape=jax.S...  18.2 us
    pallas_call x1, Pallas kernels, pick_columns(): pl.pallas_call(pick_kernel, grid=(depth // tall,), in_specs=[pl.BlockSpec...  14.7 us
    pallas_call x1, Pallas kernels, gram_blocks(): pl.pallas_call(gram_kernel, grid=(depth // tall,), in_specs=[pl.BlockSpec...  11.2 us
    ppermute x6, starting transfers between devices, shift(): lax.ppermute(values, 'scen', [(d, (d + 4 * by) % parts) for d in range(pa...  10.1 us
    ppermute x8, starting transfers between devices, step(): return lax.ppermute(values, 'scen', pairs)  8.36 us
  transfers between devices with their start and end apart: 33, of which 19 were waited for; matrix products, arithmetic and copies ran while one was open for 4% of the time, Pallas kernels for 28%

profile of v11, /device:TPU:0, one launch (start us, length us, event | category | flops | bytes accessed | tf_op | source)
XLA Modules:
  0.0 185.8 jit_solution(9520225925670007400)
XLA Ops:
  7.9 14.7 %pick_columns.1 = (bf16[512,1024]{1,0:T(8,128)(2,1)}, f32[384,256]{1,0:T(8,128)}, f32[128,256]{1,0:T(8,128)}, f32[128,640]{1,0:T(8,128)}, f32[128,640]{1,0:T(8,128)}) custom-call(s32[1]{0:T(128)S(6)} %copy.15.counts_ref, s32[1,512]{1,0:T(1,128)} %bitcast.38, f32[1,1024]{1,0:T(1,128)} %bitcast.37, f32[256,4096]{1,0:T(8,128)} %refs_2_.1, ...), custom_call_target="tpu_custom_call" | custom-call | flops 6442450944 | bytes 12582912 | tf_op jit(solution)/shard_map/pick_columns/pallas_call | solution.py:282
  22.6 0.5 collective-permute-start
  23.1 11.2 %gram_blocks.1 = (f32[8,384,256]{2,1,0:T(8,128)}, f32[8,128,256]{2,1,0:T(8,128)}, f32[8,384,256]{2,1,0:T(8,128)}, f32[8,128,256]{2,1,0:T(8,128)}) custom-call(s32[256]{0:T(256)} %constant.79.clone.table_ref, bf16[512,1024]{1,0:T(8,128)(2,1)} %get-tuple-element.64.scaled_ref, bf16[1024,4096]{1,0:T(8,128)(2,1)} %rows_ref.3), custom_call_target="tpu_custom_call" | custom-call | flops 4294967296 | bytes 16777216 | tf_op jit(solution)/shard_map/gram_blocks/pallas_call | solution.py:374
  34.3 0.1 collective-permute-start.1
  34.4 1.1 add.76
  35.5 0.7 dynamic-slice_bitcast_fusion
  36.2 4.0 %collective-permute-done.1 = f32[8,384,256]{2,1,0:T(8,128)S(1)} collective-permute-done((f32[8,384,256]{2,1,0:T(8,128)}, f32[8,384,256]{2,1,0:T(8,128)S(1)}, u32[]{:S(2)}, u32[]{:S(2)}) %collective-permute-start.1) | collective-permute-done | bytes 3145760 | tf_op jit(solution)/shard_map/ppermute | solution.py:543
  40.2 4.0 %add.95 = f32[8,384,256]{2,1,0:T(8,128)} add(f32[8,384,256]{2,1,0:T(8,128)} %get-tuple-element.77, f32[8,384,256]{2,1,0:T(8,128)S(1)} %collective-permute-done.1) | non-fusion elementwise | flops 786432 | bytes 9437184 | tf_op jit(solution)/shard_map/add | solution.py:573
  44.2 0.2 collective-permute-start.6
  44.4 2.9 %collective-permute-start.2 = (f32[4,16,640]{2,1,0:T(8,128)}, f32[4,16,640]{2,1,0:T(8,128)S(1)}, u32[]{:S(2)}, u32[]{:S(2)}) collective-permute-start(f32[4,16,640]{2,1,0:T(8,128)} %dynamic-slice_bitcast_fusion), channel_id=1, source_target_pairs={{0,2},{1,3},{2,0},{3,1},{4,6},{5,7},{6,4},{7,5},{8,10},{9,11},{10,... | collective-permute-start | bytes 491528 | tf_op jit(solution)/shard_map/ppermute | solution.py:543
  47.3 4.7 %collective-permute-done.2 = f32[4,16,640]{2,1,0:T(8,128)S(1)} collective-permute-done((f32[4,16,640]{2,1,0:T(8,128)}, f32[4,16,640]{2,1,0:T(8,128)S(1)}, u32[]{:S(2)}, u32[]{:S(2)}) %collective-permute-start.2) | collective-permute-done | bytes 163872 | tf_op jit(solution)/shard_map/ppermute | solution.py:543
  52.1 1.9 %collective-permute-start.3 = (f32[16,640]{1,0:T(8,128)S(1)}, f32[16,640]{1,0:T(8,128)S(1)}, u32[]{:S(2)}, u32[]{:S(2)}) collective-permute-start(f32[16,640]{1,0:T(8,128)S(1)} %get-tuple-element.120), channel_id=1, source_target_pairs={{0,4},{1,5},{2,6},{3,7},{4,8},{5,9},{6,10},{7,11},{8,12},{9,13},{1... | collective-permute-start | bytes 122888 | tf_op jit(solution)/shard_map/ppermute | solution.py:551
  54.0 2.6 %collective-permute-start.4 = (f32[16,640]{1,0:T(8,128)S(1)}, f32[16,640]{1,0:T(8,128)S(1)}, u32[]{:S(2)}, u32[]{:S(2)}) collective-permute-start(f32[16,640]{1,0:T(8,128)S(1)} %get-tuple-element.119), channel_id=1, source_target_pairs={{0,8},{1,9},{2,10},{3,11},{4,12},{5,13},{6,14},{7,15},{8,0},{9,1},... | collective-permute-start | bytes 122888 | tf_op jit(solution)/shard_map/ppermute | solution.py:551
  56.5 1.4 collective-permute-start.5
  57.9 1.0 collective-permute-done.3
  58.9 1.8 collective-permute-done.4
  60.7 0.8 collective-permute-done.5
  61.5 1.2 collective-permute-start.7
  62.7 2.7 %collective-permute-start.8 = (f32[16,640]{1,0:T(8,128)S(1)}, f32[16,640]{1,0:T(8,128)S(1)}, u32[]{:S(2)}, u32[]{:S(2)}) collective-permute-start(f32[16,640]{1,0:T(8,128)S(1)} %bitcast_add_fusion.1), channel_id=1, source_target_pairs={{0,8},{1,9},{2,10},{3,11},{4,12},{5,13},{6,14},{7,15},{8,0},{9,1},... | collective-permute-start | bytes 122888 | tf_op jit(solution)/shard_map/ppermute | solution.py:551
  65.4 0.4 collective-permute-start.9
  65.8 1.2 add.94
  67.0 1.9 collective-permute-done.7
  68.8 0.9 collective-permute-done.8
  69.7 0.9 collective-permute-done.9
  70.6 1.6 collective-permute-start.10
  72.3 7.1 %collective-permute-done.10 = f32[4,16,640]{2,1,0:T(8,128)S(1)} collective-permute-done((f32[4,16,640]{2,1,0:T(8,128)S(1)}, f32[4,16,640]{2,1,0:T(8,128)S(1)}, u32[]{:S(2)}, u32[]{:S(2)}) %collective-permute-start.10) | collective-permute-done | bytes 163872 | tf_op jit(solution)/shard_map/ppermute | solution.py:543
  79.4 0.1 collective-permute-start.11
  79.5 1.5 collective-permute-done.11.refs_1_
  81.1 0.7 copy-done.18
  81.8 7.7 %factor_first.1.refs_0_ = f32[512,512]{1,0:T(8,128)} custom-call(s32[256]{0:T(256)} %constant.81.clone.table_ref, f32[1,512]{1,0:T(1,128)} %bitcast.39, f32[8,16,640]{2,1,0:T(8,128)} %copy-done.17, f32[8,16,640]{2,1,0:T(8,128)} %copy-done.18), custom_call_target="tpu_custom_call" | custom-call | flops 6710886400 | bytes 2097152 | tf_op jit(solution)/shard_map/factor_first/pallas_call | solution.py:146
  89.5 3.3 %reduce-scatter.5.cloned.1.call-done = f32[1,384,256]{2,1,0:T(8,128)} async-done(((f32[8,384,256]{2,1,0:T(8,128)}), f32[1,384,256]{2,1,0:T(8,128)}) %reduce-scatter.5.cloned.1.call-update) | async-done | bytes 393232 | tf_op jit(solution)/shard_map/reduce_scatter | solution.py:554
  92.8 1.0 add.96.first_ref.refs_3_
  93.9 1.0 collective-permute-start.12
  94.9 1.1 collective-permute-start.13
  95.9 12.3 %factor_1.1.refs_0_ = f32[512,512]{1,0:T(8,128)} custom-call(f32[512,512]{1,0:T(8,128)} %factor_first.1.refs_0_), custom_call_target="tpu_custom_call" | custom-call | flops 13421772800 | bytes 2097152 | tf_op jit(solution)/shard_map/factor_1/pallas_call | solution.py:601
  108.3 1.0 collective-permute-start.14
  109.3 1.1 collective-permute-start.15
  110.4 6.9 %factor_3.1.inverse_ref = f32[512,512]{1,0:T(8,128)} custom-call(f32[512,512]{1,0:T(8,128)} %factor_1.1.refs_0_), custom_call_target="tpu_custom_call" | custom-call | flops 6710886400 | bytes 2097152 | tf_op jit(solution)/shard_map/factor_3/pallas_call | solution.py:601
  117.2 7.1 %collective-permute-done.14.refs_6_ = f32[384,256]{1,0:T(8,128)S(1)} collective-permute-done((f32[384,256]{1,0:T(8,128)S(1)}, f32[384,256]{1,0:T(8,128)S(1)}, u32[]{:S(2)}, u32[]{:S(2)}) %collective-permute-start.14) | collective-permute-done | bytes 393248 | tf_op jit(solution)/shard_map/ppermute | solution.py:540
  124.3 0.5 collective-permute-done.15.refs_7_
  124.8 1.9 %reduce-scatter.3.cloned.1.call-done = f32[1,128,256]{2,1,0:T(8,128)} async-done(((f32[8,128,256]{2,1,0:T(8,128)}), f32[1,128,256]{2,1,0:T(8,128)}) %reduce-scatter.3.cloned.1.call-update) | async-done | bytes 131088 | tf_op jit(solution)/shard_map/reduce_scatter | solution.py:554
  126.7 1.6 add.97.second_ref
  128.3 0.9 collective-permute-start.16
  129.2 1.2 collective-permute-start.17
  130.4 0.5 collective-permute-start.21
  130.9 0.1 collective-permute-start.22
  131.0 7.0 %collective-permute-done.16.refs_8_ = f32[384,256]{1,0:T(8,128)S(1)} collective-permute-done((f32[384,256]{1,0:T(8,128)S(1)}, f32[384,256]{1,0:T(8,128)S(1)}, u32[]{:S(2)}, u32[]{:S(2)}) %collective-permute-start.16) | collective-permute-done | bytes 393248 | tf_op jit(solution)/shard_map/ppermute | solution.py:540
  138.0 1.2 collective-permute-done.17.refs_9_
  139.2 0.5 collective-permute-start.18
  139.7 1.7 collective-permute-start.19
  141.4 7.0 %collective-permute-done.18.refs_10_ = f32[192,256]{1,0:T(8,128)} collective-permute-done((f32[192,256]{1,0:T(8,128)S(1)}, f32[192,256]{1,0:T(8,128)}, u32[]{:S(2)}, u32[]{:S(2)}) %collective-permute-start.18) | collective-permute-done | bytes 196640 | tf_op jit(solution)/shard_map/ppermute | solution.py:540
  148.4 1.3 collective-permute-done.19.refs_11_
  149.6 4.0 %solve_rows.1 = (f32[256,512]{1,0:T(8,128)}, f32[256,512]{1,0:T(8,128)}) custom-call(f32[512,512]{1,0:T(8,128)} %factor_3.1.inverse_ref, f32[384,256]{1,0:T(8,128)} %copy-done, f32[128,256]{1,0:T(8,128)} %add.97.second_ref), custom_call_target="tpu_custom_call" | custom-call | flops 805306368 | bytes 2097152 | tf_op jit(solution)/shard_map/solve_rows/pallas_call | solution.py:177
  153.6 0.5 collective-permute-start.27
  154.2 0.1 collective-permute-start.28
  154.2 1.8 slice.14.refs_1_
  156.1 0.6 copy-done.12
  156.9 0.2 copy-done.13
  157.0 10.6 %update_rows.2.refs_2_ = f32[256,4096]{1,0:T(8,128)} custom-call(s32[384]{0:T(512)} %constant.80.clone.refs_0_, f32[256,384]{1,0:T(8,128)} %slice.14.refs_1_, f32[256,4096]{1,0:T(8,128)} %refs_2_.1, f32[384,256]{1,0:T(8,128)} %copy-done, f32[384,256]{1,0:T(8,128)} %copy-done.6, f32[384,256]{1,0:T(8,128)} %copy-done.7, f32[384,256]{1,0:T(8,128)} %copy-done.8, ...), custom_call_target="tpu_custom_call" | custom-call | flops 2415919104 | bytes 14680064 | tf_op jit(solution)/shard_map/update_rows/pallas_call | solution.py:444
  167.7 0.5 collective-permute-start.29
  168.2 1.6 slice.15.refs_1_
  169.8 0.9 collective-permute-done.29.refs_4_
  170.7 1.0 copy-done.2
  171.7 7.5 %update_rows.3 = f32[256,4096]{1,0:T(8,128)} custom-call(s32[384]{0:T(512)} %constant.80.clone.refs_0_, f32[256,128]{1,0:T(8,128)} %slice.15.refs_1_, f32[256,4096]{1,0:T(8,128)} %update_rows.2.refs_2_, f32[8,128,256]{2,1,0:T(8,128)} %bitcast.30, f32[8,128,256]{2,1,0:T(8,128)} %copy-done.2), custom_call_target="tpu_custom_call" | custom-call | flops 805306368 | bytes 10485760 | tf_op jit(solution)/shard_map/update_rows/pallas_call | solution.py:444
  (70 shorter events, 0.5 us)
Async XLA Ops:
  7.2 85.6 %reduce-scatter.5.cloned.1.call-start = ((), (), s32[]{:S(2)}) async-start(), calls=%async_computation.3 | async-start | bytes 3538944 | tf_op jit(solution)/shard_map/reduce_scatter | solution.py:554
  22.6 11.7 %collective-permute-start = (f32[128,640]{1,0:T(8,128)}, f32[128,640]{1,0:T(8,128)}, u32[]{:S(2)}, u32[]{:S(2)}) collective-permute-start(f32[128,640]{1,0:T(8,128)} %get-tuple-element.63), channel_id=1, source_target_pairs={{0,1},{1,0},{2,3},{3,2},{4,5},{5,4},{6,7},{7,6},{8,9},{9,8},{10,11... | collective-permute-start | bytes 983048 | tf_op jit(solution)/shard_map/ppermute | solution.py:543
  34.3 5.9 %collective-permute-start.1 = (f32[8,384,256]{2,1,0:T(8,128)}, f32[8,384,256]{2,1,0:T(8,128)S(1)}, u32[]{:S(2)}, u32[]{:S(2)}) collective-permute-start(f32[8,384,256]{2,1,0:T(8,128)} %get-tuple-element.68), channel_id=1, source_target_pairs={{0,1},{1,0},{2,3},{3,2},{4,5},{5,4},{6,7},{7,6},{8,9},{9,8},{10,11... | collective-permute-start | bytes 9437192 | tf_op jit(solution)/shard_map/ppermute | solution.py:543
  44.2 21.7 %copy-start.1 = (f32[8,128,256]{2,1,0:T(8,128)S(1)}, f32[8,128,256]{2,1,0:T(8,128)}, u32[]{:S(2)}) copy-start(f32[8,128,256]{2,1,0:T(8,128)} %get-tuple-element.74) | copy-start | bytes 3145732
  44.2 82.5 %reduce-scatter.3.cloned.1.call-start = ((), (), s32[]{:S(2)}) async-start(), calls=%async_computation.2 | async-start | bytes 1179648 | tf_op jit(solution)/shard_map/reduce_scatter | solution.py:554
  44.2 13.6 %collective-permute-start.6 = (f32[8,128,256]{2,1,0:T(8,128)}, f32[8,128,256]{2,1,0:T(8,128)S(1)}, u32[]{:S(2)}, u32[]{:S(2)}) collective-permute-start(f32[8,128,256]{2,1,0:T(8,128)} %get-tuple-element.70), channel_id=1, source_target_pairs={{0,1},{1,0},{2,3},{3,2},{4,5},{5,4},{6,7},{7,6},{8,9},{9,8},{10,11... | collective-permute-start | bytes 3145736 | tf_op jit(solution)/shard_map/ppermute | solution.py:543
  44.4 7.6 %collective-permute-start.2 = (f32[4,16,640]{2,1,0:T(8,128)}, f32[4,16,640]{2,1,0:T(8,128)S(1)}, u32[]{:S(2)}, u32[]{:S(2)}) collective-permute-start(f32[4,16,640]{2,1,0:T(8,128)} %dynamic-slice_bitcast_fusion), channel_id=1, source_target_pairs={{0,2},{1,3},{2,0},{3,1},{4,6},{5,7},{6,4},{7,5},{8,10},{9,11},{10,... | collective-permute-start | bytes 491528 | tf_op jit(solution)/shard_map/ppermute | solution.py:543
  52.1 6.8 %collective-permute-start.3 = (f32[16,640]{1,0:T(8,128)S(1)}, f32[16,640]{1,0:T(8,128)S(1)}, u32[]{:S(2)}, u32[]{:S(2)}) collective-permute-start(f32[16,640]{1,0:T(8,128)S(1)} %get-tuple-element.120), channel_id=1, source_target_pairs={{0,4},{1,5},{2,6},{3,7},{4,8},{5,9},{6,10},{7,11},{8,12},{9,13},{1... | collective-permute-start | bytes 122888 | tf_op jit(solution)/shard_map/ppermute | solution.py:551
  54.0 6.7 %collective-permute-start.4 = (f32[16,640]{1,0:T(8,128)S(1)}, f32[16,640]{1,0:T(8,128)S(1)}, u32[]{:S(2)}, u32[]{:S(2)}) collective-permute-start(f32[16,640]{1,0:T(8,128)S(1)} %get-tuple-element.119), channel_id=1, source_target_pairs={{0,8},{1,9},{2,10},{3,11},{4,12},{5,13},{6,14},{7,15},{8,0},{9,1},... | collective-permute-start | bytes 122888 | tf_op jit(solution)/shard_map/ppermute | solution.py:551
  56.5 5.0 %collective-permute-start.5 = (f32[16,640]{1,0:T(8,128)S(1)}, f32[16,640]{1,0:T(8,128)S(1)}, u32[]{:S(2)}, u32[]{:S(2)}) collective-permute-start(f32[16,640]{1,0:T(8,128)S(1)} %get-tuple-element.118), channel_id=1, source_target_pairs={{0,12},{1,13},{2,14},{3,15},{4,0},{5,1},{6,2},{7,3},{8,4},{9,5},{1... | collective-permute-start | bytes 122888 | tf_op jit(solution)/shard_map/ppermute | solution.py:551
  61.5 7.3 %collective-permute-start.7 = (f32[16,640]{1,0:T(8,128)S(1)}, f32[16,640]{1,0:T(8,128)S(1)}, u32[]{:S(2)}, u32[]{:S(2)}) collective-permute-start(f32[16,640]{1,0:T(8,128)S(1)} %bitcast_add_fusion.1), channel_id=1, source_target_pairs={{0,4},{1,5},{2,6},{3,7},{4,8},{5,9},{6,10},{7,11},{8,12},{9,13},{1... | collective-permute-start | bytes 122888 | tf_op jit(solution)/shard_map/ppermute | solution.py:551
  62.7 7.0 %collective-permute-start.8 = (f32[16,640]{1,0:T(8,128)S(1)}, f32[16,640]{1,0:T(8,128)S(1)}, u32[]{:S(2)}, u32[]{:S(2)}) collective-permute-start(f32[16,640]{1,0:T(8,128)S(1)} %bitcast_add_fusion.1), channel_id=1, source_target_pairs={{0,8},{1,9},{2,10},{3,11},{4,12},{5,13},{6,14},{7,15},{8,0},{9,1},... | collective-permute-start | bytes 122888 | tf_op jit(solution)/shard_map/ppermute | solution.py:551
  65.4 5.2 %collective-permute-start.9 = (f32[16,640]{1,0:T(8,128)S(1)}, f32[16,640]{1,0:T(8,128)S(1)}, u32[]{:S(2)}, u32[]{:S(2)}) collective-permute-start(f32[16,640]{1,0:T(8,128)S(1)} %bitcast_add_fusion.1), channel_id=1, source_target_pairs={{0,12},{1,13},{2,14},{3,15},{4,0},{5,1},{6,2},{7,3},{8,4},{9,5},{1... | collective-permute-start | bytes 122888 | tf_op jit(solution)/shard_map/ppermute | solution.py:551
  70.6 8.7 %collective-permute-start.10 = (f32[4,16,640]{2,1,0:T(8,128)S(1)}, f32[4,16,640]{2,1,0:T(8,128)S(1)}, u32[]{:S(2)}, u32[]{:S(2)}) collective-permute-start(f32[4,16,640]{2,1,0:T(8,128)S(1)} %pad_maximum_fusion), channel_id=1, source_target_pairs={{0,2},{1,3},{2,0},{3,1},{4,6},{5,7},{6,4},{7,5},{8,10},{9,11},{10,... | collective-permute-start | bytes 491528 | tf_op jit(solution)/shard_map/ppermute | solution.py:543
  79.4 1.7 copy-start.17
  79.4 1.7 collective-permute-start.11
  79.5 88.2 %all-gather.3.cloned.1.call-start = ((), (), s32[]{:S(2)}) async-start(), calls=%async_computation.4 | async-start | bytes 1179648 | tf_op jit(solution)/shard_map/all_gather | solution.py:597
  81.1 0.7 copy-start.18
  81.8 11.0 %copy-start.5 = (f32[384,256]{1,0:T(8,128)S(1)}, f32[384,256]{1,0:T(8,128)}, u32[]{:S(2)}) copy-start(f32[384,256]{1,0:T(8,128)} %get-tuple-element.84) | copy-start | bytes 1179652
  93.8 36.6 %copy-start = (f32[384,256]{1,0:T(8,128)}, f32[384,256]{1,0:T(8,128)S(1)}, u32[]{:S(2)}) copy-start(f32[384,256]{1,0:T(8,128)S(1)} %add.96.first_ref.refs_3_) | copy-start | bytes 1179652
  93.9 14.4 %collective-permute-start.12 = (f32[384,256]{1,0:T(8,128)S(1)}, f32[384,256]{1,0:T(8,128)S(1)}, u32[]{:S(2)}, u32[]{:S(2)}) collective-permute-start(f32[384,256]{1,0:T(8,128)S(1)} %add.96.first_ref.refs_3_), channel_id=1, source_target_pairs={{0,4},{1,5},{4,8},{5,9},{8,12},{9,13},{12,14},{13,15},{14,10},{15,... | collective-permute-start | bytes 1179656 | tf_op jit(solution)/shard_map/ppermute | solution.py:540
  94.9 13.4 %collective-permute-start.13 = (f32[384,256]{1,0:T(8,128)S(1)}, f32[384,256]{1,0:T(8,128)S(1)}, u32[]{:S(2)}, u32[]{:S(2)}) collective-permute-start(f32[384,256]{1,0:T(8,128)S(1)} %add.96.first_ref.refs_3_), channel_id=1, source_target_pairs={{0,2},{1,3},{4,0},{5,1},{8,4},{9,5},{12,8},{13,9},{14,12},{15,13},... | collective-permute-start | bytes 1179656 | tf_op jit(solution)/shard_map/ppermute | solution.py:540
  108.3 18.5 %copy-start.16 = (f32[128,256]{1,0:T(8,128)S(1)}, f32[128,256]{1,0:T(8,128)}, u32[]{:S(2)}) copy-start(f32[128,256]{1,0:T(8,128)} %get-tuple-element.97) | copy-start | bytes 393220
  108.3 22.1 %copy-start.6 = (f32[384,256]{1,0:T(8,128)}, f32[384,256]{1,0:T(8,128)S(1)}, u32[]{:S(2)}) copy-start(f32[384,256]{1,0:T(8,128)S(1)} %collective-permute-done.12.refs_4_) | copy-start | bytes 1179652
  108.3 22.7 %copy-start.7 = (f32[384,256]{1,0:T(8,128)}, f32[384,256]{1,0:T(8,128)S(1)}, u32[]{:S(2)}) copy-start(f32[384,256]{1,0:T(8,128)S(1)} %collective-permute-done.13.refs_5_) | copy-start | bytes 1179652
  108.3 16.1 %collective-permute-start.14 = (f32[384,256]{1,0:T(8,128)S(1)}, f32[384,256]{1,0:T(8,128)S(1)}, u32[]{:S(2)}, u32[]{:S(2)}) collective-permute-start(f32[384,256]{1,0:T(8,128)S(1)} %collective-permute-done.12.refs_4_), channel_id=1, source_target_pairs={{0,4},{1,5},{4,8},{5,9},{8,12},{9,13},{12,14},{13,15},{14,10},{15,... | collective-permute-start | bytes 1179656 | tf_op jit(solution)/shard_map/ppermute | solution.py:540
  109.3 15.5 %collective-permute-start.15 = (f32[384,256]{1,0:T(8,128)S(1)}, f32[384,256]{1,0:T(8,128)S(1)}, u32[]{:S(2)}, u32[]{:S(2)}) collective-permute-start(f32[384,256]{1,0:T(8,128)S(1)} %collective-permute-done.13.refs_5_), channel_id=1, source_target_pairs={{0,2},{1,3},{4,0},{5,1},{8,4},{9,5},{12,8},{13,9},{14,12},{15,13},... | collective-permute-start | bytes 1179656 | tf_op jit(solution)/shard_map/ppermute | solution.py:540
  124.3 31.7 %copy-start.8 = (f32[384,256]{1,0:T(8,128)}, f32[384,256]{1,0:T(8,128)S(1)}, u32[]{:S(2)}) copy-start(f32[384,256]{1,0:T(8,128)S(1)} %collective-permute-done.14.refs_6_) | copy-start | bytes 1179652
  124.8 31.3 %copy-start.9 = (f32[384,256]{1,0:T(8,128)}, f32[384,256]{1,0:T(8,128)S(1)}, u32[]{:S(2)}) copy-start(f32[384,256]{1,0:T(8,128)S(1)} %collective-permute-done.15.refs_7_) | copy-start | bytes 1179652
  128.3 9.7 %collective-permute-start.16 = (f32[384,256]{1,0:T(8,128)S(1)}, f32[384,256]{1,0:T(8,128)S(1)}, u32[]{:S(2)}, u32[]{:S(2)}) collective-permute-start(f32[384,256]{1,0:T(8,128)S(1)} %collective-permute-done.14.refs_6_), channel_id=1, source_target_pairs={{0,4},{1,5},{4,8},{5,9},{8,12},{9,13},{12,14},{13,15},{14,10},{15,... | collective-permute-start | bytes 1179656 | tf_op jit(solution)/shard_map/ppermute | solution.py:540
  129.2 10.0 %collective-permute-start.17 = (f32[384,256]{1,0:T(8,128)S(1)}, f32[384,256]{1,0:T(8,128)S(1)}, u32[]{:S(2)}, u32[]{:S(2)}) collective-permute-start(f32[384,256]{1,0:T(8,128)S(1)} %collective-permute-done.15.refs_7_), channel_id=1, source_target_pairs={{0,2},{1,3},{4,0},{5,1},{8,4},{9,5},{12,8},{13,9},{14,12},{15,13},... | collective-permute-start | bytes 1179656 | tf_op jit(solution)/shard_map/ppermute | solution.py:540
  130.4 9.3 %collective-permute-start.20 = (f32[384,256]{1,0:T(8,128)S(1)}, f32[384,256]{1,0:T(8,128)S(1)}, u32[]{:S(2)}, u32[]{:S(2)}) collective-permute-start(f32[384,256]{1,0:T(8,128)S(1)} %add.96.first_ref.refs_3_), channel_id=1, source_target_pairs={{0,1},{1,0},{2,3},{3,2},{4,5},{5,4},{6,7},{7,6},{8,9},{9,8},{10,11... | collective-permute-start | bytes 1179656 | tf_op jit(solution)/shard_map/ppermute | solution.py:543
  130.4 11.0 %collective-permute-start.21 = (f32[384,256]{1,0:T(8,128)S(1)}, f32[384,256]{1,0:T(8,128)S(1)}, u32[]{:S(2)}, u32[]{:S(2)}) collective-permute-start(f32[384,256]{1,0:T(8,128)S(1)} %collective-permute-done.12.refs_4_), channel_id=1, source_target_pairs={{0,1},{1,0},{2,3},{3,2},{4,5},{5,4},{6,7},{7,6},{8,9},{9,8},{10,11... | collective-permute-start | bytes 1179656 | tf_op jit(solution)/shard_map/ppermute | solution.py:543
  130.9 22.7 %collective-permute-start.22 = (f32[384,256]{1,0:T(8,128)S(1)}, f32[384,256]{1,0:T(8,128)}, u32[]{:S(2)}, u32[]{:S(2)}) collective-permute-start(f32[384,256]{1,0:T(8,128)S(1)} %collective-permute-done.13.refs_5_), channel_id=1, source_target_pairs={{0,1},{1,0},{2,3},{3,2},{4,5},{5,4},{6,7},{7,6},{8,9},{9,8},{10,11... | collective-permute-start | bytes 1179656 | tf_op jit(solution)/shard_map/ppermute | solution.py:543
  138.0 18.1 %copy-start.3 = (f32[384,256]{1,0:T(8,128)}, f32[384,256]{1,0:T(8,128)S(1)}, u32[]{:S(2)}) copy-start(f32[384,256]{1,0:T(8,128)S(1)} %collective-permute-done.16.refs_8_) | copy-start | bytes 1179652
  138.0 16.1 %collective-permute-start.23 = (f32[384,256]{1,0:T(8,128)S(1)}, f32[384,256]{1,0:T(8,128)}, u32[]{:S(2)}, u32[]{:S(2)}) collective-permute-start(f32[384,256]{1,0:T(8,128)S(1)} %collective-permute-done.14.refs_6_), channel_id=1, source_target_pairs={{0,1},{1,0},{2,3},{3,2},{4,5},{5,4},{6,7},{7,6},{8,9},{9,8},{10,11... | collective-permute-start | bytes 1179656 | tf_op jit(solution)/shard_map/ppermute | solution.py:543
  139.2 16.9 %copy-start.4 = (f32[384,256]{1,0:T(8,128)}, f32[384,256]{1,0:T(8,128)S(1)}, u32[]{:S(2)}) copy-start(f32[384,256]{1,0:T(8,128)S(1)} %collective-permute-done.17.refs_9_) | copy-start | bytes 1179652
  139.2 9.1 %collective-permute-start.18 = (f32[192,256]{1,0:T(8,128)S(1)}, f32[192,256]{1,0:T(8,128)}, u32[]{:S(2)}, u32[]{:S(2)}) collective-permute-start(f32[192,256]{1,0:T(8,128)S(1)} %slice.12), channel_id=1, source_target_pairs={{0,4},{1,5},{4,8},{5,9},{8,12},{9,13},{12,14},{13,15},{14,10},{15,... | collective-permute-start | bytes 589832 | tf_op jit(solution)/shard_map/ppermute | solution.py:540
  139.7 16.4 %copy-start.10 = (f32[384,256]{1,0:T(8,128)}, f32[384,256]{1,0:T(8,128)S(1)}, u32[]{:S(2)}) copy-start(f32[384,256]{1,0:T(8,128)S(1)} %collective-permute-done.20.refs_12_) | copy-start | bytes 1179652
  139.7 9.9 %collective-permute-start.19 = (f32[192,256]{1,0:T(8,128)S(1)}, f32[192,256]{1,0:T(8,128)}, u32[]{:S(2)}, u32[]{:S(2)}) collective-permute-start(f32[192,256]{1,0:T(8,128)S(1)} %slice.13), channel_id=1, source_target_pairs={{0,2},{1,3},{4,0},{5,1},{8,4},{9,5},{12,8},{13,9},{14,12},{15,13},... | collective-permute-start | bytes 589832 | tf_op jit(solution)/shard_map/ppermute | solution.py:540
  141.4 14.7 %copy-start.11 = (f32[384,256]{1,0:T(8,128)}, f32[384,256]{1,0:T(8,128)S(1)}, u32[]{:S(2)}) copy-start(f32[384,256]{1,0:T(8,128)S(1)} %collective-permute-done.21.refs_13_) | copy-start | bytes 1179652
  141.4 14.6 %collective-permute-start.24 = (f32[384,256]{1,0:T(8,128)S(1)}, f32[384,256]{1,0:T(8,128)S(1)}, u32[]{:S(2)}, u32[]{:S(2)}) collective-permute-start(f32[384,256]{1,0:T(8,128)S(1)} %collective-permute-done.15.refs_7_), channel_id=1, source_target_pairs={{0,1},{1,0},{2,3},{3,2},{4,5},{5,4},{6,7},{7,6},{8,9},{9,8},{10,11... | collective-permute-start | bytes 1179656 | tf_op jit(solution)/shard_map/ppermute | solution.py:543
  148.4 7.7 %collective-permute-start.25 = (f32[384,256]{1,0:T(8,128)S(1)}, f32[384,256]{1,0:T(8,128)S(1)}, u32[]{:S(2)}, u32[]{:S(2)}) collective-permute-start(f32[384,256]{1,0:T(8,128)S(1)} %collective-permute-done.16.refs_8_), channel_id=1, source_target_pairs={{0,1},{1,0},{2,3},{3,2},{4,5},{5,4},{6,7},{7,6},{8,9},{9,8},{10,11... | collective-permute-start | bytes 1179656 | tf_op jit(solution)/shard_map/ppermute | solution.py:543
  149.6 6.4 %collective-permute-start.26 = (f32[384,256]{1,0:T(8,128)S(1)}, f32[384,256]{1,0:T(8,128)}, u32[]{:S(2)}, u32[]{:S(2)}) collective-permute-start(f32[384,256]{1,0:T(8,128)S(1)} %collective-permute-done.17.refs_9_), channel_id=1, source_target_pairs={{0,1},{1,0},{2,3},{3,2},{4,5},{5,4},{6,7},{7,6},{8,9},{9,8},{10,11... | collective-permute-start | bytes 1179656 | tf_op jit(solution)/shard_map/ppermute | solution.py:543
  153.6 2.4 %collective-permute-start.27 = (f32[192,256]{1,0:T(8,128)}, f32[192,256]{1,0:T(8,128)S(1)}, u32[]{:S(2)}, u32[]{:S(2)}) collective-permute-start(f32[192,256]{1,0:T(8,128)} %collective-permute-done.18.refs_10_), channel_id=1, source_target_pairs={{0,1},{1,0},{2,3},{3,2},{4,5},{5,4},{6,7},{7,6},{8,9},{9,8},{10,11... | collective-permute-start | bytes 589832 | tf_op jit(solution)/shard_map/ppermute | solution.py:543
  154.2 1.9 %collective-permute-start.28 = (f32[192,256]{1,0:T(8,128)}, f32[192,256]{1,0:T(8,128)S(1)}, u32[]{:S(2)}, u32[]{:S(2)}) collective-permute-start(f32[192,256]{1,0:T(8,128)} %collective-permute-done.19.refs_11_), channel_id=1, source_target_pairs={{0,1},{1,0},{2,3},{3,2},{4,5},{5,4},{6,7},{7,6},{8,9},{9,8},{10,11... | collective-permute-start | bytes 589832 | tf_op jit(solution)/shard_map/ppermute | solution.py:543
  156.0 0.8 copy-start.12
  156.0 0.8 copy-start.14
  156.0 0.8 copy-start.15
  156.1 1.0 copy-start.13
  167.7 3.0 %collective-permute-start.29 = (f32[8,128,256]{2,1,0:T(8,128)}, f32[8,128,256]{2,1,0:T(8,128)S(1)}, u32[]{:S(2)}, u32[]{:S(2)}) collective-permute-start(f32[8,128,256]{2,1,0:T(8,128)} %bitcast.29), channel_id=1, source_target_pairs={{0,1},{1,0},{2,3},{3,2},{4,5},{5,4},{6,7},{7,6},{8,9},{9,8},{10,11... | collective-permute-start | bytes 3145736 | tf_op jit(solution)/shard_map/ppermute | solution.py:543
  170.7 1.0 copy-start.2
Sparse Core Ops, SparseCore 0:
  44.3 48.4 reduce-scatter.4
  95.1 31.5 reduce-scatter.2
  128.4 30.3 all-gather.2

commit v12 on v11

--- a/solution.py
+++ b/solution.py
@@ -163,24 +163,30 @@
     ]
 
 
-def solve_kernel(inverse_ref, first_ref, second_ref, factor_ref, weight_ref):
+def solve_kernel(inverse_ref, first_ref, second_ref, factor_ref, weight_0, weight_1):
+    cut = first_ref.shape[0]
     inverse = inverse_ref[...]
     panel = jnp.concatenate([first_ref[...], second_ref[...]], axis=0)
     rows = dot_split(split(inverse), split(panel)).T
     factor_ref[...] = rows
-    weight_ref[...] = dot_split(split(rows), split(inverse))
+    weights = dot_split(split(rows), split(inverse))
+    weight_0[...] = weights[:, :cut]
+    weight_1[...] = weights[:, cut:]
 
 
 def solve_rows(inverse, first, second):
     width, owned = inverse.shape[0], first.shape[1]
-    shape = jax.ShapeDtypeStruct((owned, width), jnp.float32)
+    shapes = [
+        jax.ShapeDtypeStruct((owned, part), jnp.float32)
+        for part in (width, first.shape[0], second.shape[0])
+    ]
     return pl.pallas_call(
         solve_kernel,
-        out_shape=(shape, shape),
+        out_shape=shapes,
         in_specs=vmem(3),
-        out_specs=vmem(2),
+        out_specs=vmem(3),
         cost_estimate=pl.CostEstimate(
-            flops=12 * owned * width * width, bytes_accessed=8 * width * width, transcendentals=0
+            flops=75 * owned * width * width, bytes_accessed=8 * width * width, transcendentals=0
         ),
         name="solve_rows",
     )(inverse, first, second)
@@ -597,18 +603,16 @@
             gathered = lax.all_gather(panel_1, "scen", axis_index_groups=groups)
             ahead, panel_1 = together((ahead, panel_1))
         ahead = [step(ahead[0], 1), step(ahead[1], -1)]
-        if d < len(stages):
-            work = stages[d](work)
+        work = stages[d](work) if d < len(stages) else solve_rows(work, panel_0, panel_1)
         ahead, work = together((ahead, work))
         shards += ahead
-    ahead, solved = together((across(panel_0, ahead), solve_rows(work, panel_0, panel_1)))
-    shards += ahead
-    factor_rows, weights = solved
+    factor_rows, weight_0, weight_1 = work
+    shards += across(panel_0, ahead)
     shards = shards + [swap(piece, 1) for piece in shards]
-    updated = update_rows(update_table, parts, weights[:, :cut], prior_schur, shards)
-    updated, gathered, weights = together((updated, gathered, weights))
+    updated = update_rows(update_table, parts, weight_0, prior_schur, shards)
+    updated, gathered = together((updated, gathered))
     sources = [gathered, swap(gathered, 1)]
-    return update_rows(update_table, parts, weights[:, cut:], updated, sources), factor_rows
+    return update_rows(update_table, parts, weight_1, updated, sources), factor_rows
 
 
 def shards_by_groups(scenario_rows, row_weights, row_counts, panel_cols, regular, prior_schur):
@@ -642,7 +646,8 @@
     table = jnp.array([c ^ (d % 2) for d in range(parts) for c in range(2)], jnp.int32)
     stages = factor_stages(table, [block, block_other], regular)
     inverse = stages[2](stages[1](stages[0]()))
-    factor_rows, weights = solve_rows(inverse, panel_rows.T[:half], panel_rows.T[half:])
+    factor_rows, *weights = solve_rows(inverse, panel_rows.T[:half], panel_rows.T[half:])
+    weights = jnp.concatenate(weights, axis=1)
     even = jnp.where(core == 0, panel_half, panel_rest)
     odd = jnp.where(core == 0, panel_rest, panel_half)
     panel = jnp.stack([even, odd], axis=1).reshape(order, width)

time: 186 us -> 189 us (1.016)
  waiting for transfers between devices: 54.8 us -> 60.4 us
  local copies, waits for them, and re-layouts: 6.76 us -> 4 us
    slice x2 -> x0, local copies, waits for them, and re-layouts: 3.35 us -> none  [the longest x1 1.78 us: shards_on_ring(): weights[:, :cut]]
    ppermute x16, waiting for transfers between devices: 18.3 us -> 21.5 us  [swap(): return lax.ppermute(values, 'scen', [(d, d ^ bit) for d in range(parts)])]
    ppermute x8, waiting for transfers between devices: 24 us -> 26.5 us  [step(): return lax.ppermute(values, 'scen', pairs)]
  transfers between devices with their start and end apart: 33 -> 33, of which waited for: 19 -> 21; matrix products, arithmetic and copies ran while one was open for 4% -> 2% of each run, Pallas kernels for 28% -> 28%
where the time goes in v12:
time: 189 us; the launch traced here: 188 us
  Pallas kernels  75 us (40%)
  waiting for transfers between devices  60.4 us (32%)
  starting transfers between devices  25.2 us (13%)
  between operations  14.7 us (8%)
  other arithmetic  8.9 us (5%)
  local copies, waits for them, and re-layouts  4 us (2%)
    ppermute x8, waiting for transfers between devices, step(): return lax.ppermute(values, 'scen', pairs)  26.5 us
    ppermute x16, waiting for transfers between devices, swap(): return lax.ppermute(values, 'scen', [(d, d ^ bit) for d in range(parts)])  21.5 us
    pallas_call x2, Pallas kernels, shards_on_ring(): stages[d](work)  19.2 us
    pallas_call x2, Pallas kernels, update_rows(): pl.pallas_call(lambda *refs: update_kernel(count, *refs), out_shape=jax.S...  18.2 us
    pallas_call x1, Pallas kernels, pick_columns(): pl.pallas_call(pick_kernel, grid=(depth // tall,), in_specs=[pl.BlockSpec...  14.7 us
    pallas_call x1, Pallas kernels, gram_blocks(): pl.pallas_call(gram_kernel, grid=(depth // tall,), in_specs=[pl.BlockSpec...  11.2 us
    ppermute x6, starting transfers between devices, shift(): lax.ppermute(values, 'scen', [(d, (d + 4 * by) % parts) for d in range(pa...  10.1 us
    ppermute x8, starting transfers between devices, step(): return lax.ppermute(values, 'scen', pairs)  8.31 us
  transfers between devices with their start and end apart: 33, of which 21 were waited for; matrix products, arithmetic and copies ran while one was open for 2% of the time, Pallas kernels for 28%

profile of v12, /device:TPU:0, one launch (start us, length us, event | category | flops | bytes accessed | tf_op | source)
XLA Modules:
  0.0 188.3 jit_solution(4678818766058929826)
XLA Ops:
  7.9 14.7 %pick_columns.1 = (bf16[512,1024]{1,0:T(8,128)(2,1)}, f32[384,256]{1,0:T(8,128)}, f32[128,256]{1,0:T(8,128)}, f32[128,640]{1,0:T(8,128)}, f32[128,640]{1,0:T(8,128)}) custom-call(s32[1]{0:T(128)S(6)} %copy.15.counts_ref, s32[1,512]{1,0:T(1,128)} %bitcast.38, f32[1,1024]{1,0:T(1,128)} %bitcast.37, f32[256,4096]{1,0:T(8,128)} %refs_2_.1, ...), custom_call_target="tpu_custom_call" | custom-call | flops 6442450944 | bytes 12582912 | tf_op jit(solution)/shard_map/pick_columns/pallas_call | solution.py:288
  22.6 0.5 collective-permute-start
  23.1 11.2 %gram_blocks.1 = (f32[8,384,256]{2,1,0:T(8,128)}, f32[8,128,256]{2,1,0:T(8,128)}, f32[8,384,256]{2,1,0:T(8,128)}, f32[8,128,256]{2,1,0:T(8,128)}) custom-call(s32[256]{0:T(256)} %constant.79.clone.table_ref, bf16[512,1024]{1,0:T(8,128)(2,1)} %get-tuple-element.62.scaled_ref, bf16[1024,4096]{1,0:T(8,128)(2,1)} %rows_ref.3), custom_call_target="tpu_custom_call" | custom-call | flops 4294967296 | bytes 16777216 | tf_op jit(solution)/shard_map/gram_blocks/pallas_call | solution.py:380
  34.3 0.1 collective-permute-start.1
  34.4 1.1 add.76
  35.5 0.7 dynamic-slice_bitcast_fusion
  36.2 4.0 %collective-permute-done.1 = f32[8,384,256]{2,1,0:T(8,128)S(1)} collective-permute-done((f32[8,384,256]{2,1,0:T(8,128)}, f32[8,384,256]{2,1,0:T(8,128)S(1)}, u32[]{:S(2)}, u32[]{:S(2)}) %collective-permute-start.1) | collective-permute-done | bytes 3145760 | tf_op jit(solution)/shard_map/ppermute | solution.py:549
  40.2 4.0 %add.95 = f32[8,384,256]{2,1,0:T(8,128)} add(f32[8,384,256]{2,1,0:T(8,128)} %get-tuple-element.75, f32[8,384,256]{2,1,0:T(8,128)S(1)} %collective-permute-done.1) | non-fusion elementwise | flops 786432 | bytes 9437184 | tf_op jit(solution)/shard_map/add | solution.py:579
  44.2 0.2 collective-permute-start.6
  44.4 2.9 %collective-permute-start.2 = (f32[4,16,640]{2,1,0:T(8,128)}, f32[4,16,640]{2,1,0:T(8,128)S(1)}, u32[]{:S(2)}, u32[]{:S(2)}) collective-permute-start(f32[4,16,640]{2,1,0:T(8,128)} %dynamic-slice_bitcast_fusion), channel_id=1, source_target_pairs={{0,2},{1,3},{2,0},{3,1},{4,6},{5,7},{6,4},{7,5},{8,10},{9,11},{10,... | collective-permute-start | bytes 491528 | tf_op jit(solution)/shard_map/ppermute | solution.py:549
  47.3 4.7 %collective-permute-done.2 = f32[4,16,640]{2,1,0:T(8,128)S(1)} collective-permute-done((f32[4,16,640]{2,1,0:T(8,128)}, f32[4,16,640]{2,1,0:T(8,128)S(1)}, u32[]{:S(2)}, u32[]{:S(2)}) %collective-permute-start.2) | collective-permute-done | bytes 163872 | tf_op jit(solution)/shard_map/ppermute | solution.py:549
  52.1 1.9 collective-permute-start.3
  54.0 2.6 %collective-permute-start.4 = (f32[16,640]{1,0:T(8,128)S(1)}, f32[16,640]{1,0:T(8,128)S(1)}, u32[]{:S(2)}, u32[]{:S(2)}) collective-permute-start(f32[16,640]{1,0:T(8,128)S(1)} %get-tuple-element.115), channel_id=1, source_target_pairs={{0,8},{1,9},{2,10},{3,11},{4,12},{5,13},{6,14},{7,15},{8,0},{9,1},... | collective-permute-start | bytes 122888 | tf_op jit(solution)/shard_map/ppermute | solution.py:557
  56.5 1.3 collective-permute-start.5
  57.9 1.0 collective-permute-done.3
  58.9 1.8 collective-permute-done.4
  60.7 0.8 collective-permute-done.5
  61.5 1.2 collective-permute-start.7
  62.7 2.7 %collective-permute-start.8 = (f32[16,640]{1,0:T(8,128)S(1)}, f32[16,640]{1,0:T(8,128)S(1)}, u32[]{:S(2)}, u32[]{:S(2)}) collective-permute-start(f32[16,640]{1,0:T(8,128)S(1)} %bitcast_add_fusion.1), channel_id=1, source_target_pairs={{0,8},{1,9},{2,10},{3,11},{4,12},{5,13},{6,14},{7,15},{8,0},{9,1},... | collective-permute-start | bytes 122888 | tf_op jit(solution)/shard_map/ppermute | solution.py:557
  65.4 0.4 collective-permute-start.9
  65.8 1.2 add.94
  67.0 1.8 collective-permute-done.7
  68.9 0.8 collective-permute-done.8
  69.7 0.9 collective-permute-done.9
  70.6 1.6 collective-permute-start.10
  72.3 7.1 %collective-permute-done.10 = f32[4,16,640]{2,1,0:T(8,128)S(1)} collective-permute-done((f32[4,16,640]{2,1,0:T(8,128)S(1)}, f32[4,16,640]{2,1,0:T(8,128)S(1)}, u32[]{:S(2)}, u32[]{:S(2)}) %collective-permute-start.10) | collective-permute-done | bytes 163872 | tf_op jit(solution)/shard_map/ppermute | solution.py:549
  79.4 0.1 collective-permute-start.11
  79.5 1.5 collective-permute-done.11.refs_1_
  81.1 0.7 copy-done.21
  81.8 7.7 %factor_first.1.refs_0_ = f32[512,512]{1,0:T(8,128)} custom-call(s32[256]{0:T(256)} %constant.81.clone.table_ref, f32[1,512]{1,0:T(1,128)} %bitcast.39, f32[8,16,640]{2,1,0:T(8,128)} %copy-done.20, f32[8,16,640]{2,1,0:T(8,128)} %copy-done.21), custom_call_target="tpu_custom_call" | custom-call | flops 6710886400 | bytes 2097152 | tf_op jit(solution)/shard_map/factor_first/pallas_call | solution.py:146
  89.5 3.3 %reduce-scatter.5.cloned.1.call-done = f32[1,384,256]{2,1,0:T(8,128)} async-done(((f32[8,384,256]{2,1,0:T(8,128)}), f32[1,384,256]{2,1,0:T(8,128)}) %reduce-scatter.5.cloned.1.call-update) | async-done | bytes 393232 | tf_op jit(solution)/shard_map/reduce_scatter | solution.py:560
  92.8 1.0 add.96.first_ref.refs_3_
  93.9 1.0 collective-permute-start.12
  94.9 1.1 collective-permute-start.13
  95.9 12.3 %factor_1.1.refs_0_ = f32[512,512]{1,0:T(8,128)} custom-call(f32[512,512]{1,0:T(8,128)} %factor_first.1.refs_0_), custom_call_target="tpu_custom_call" | custom-call | flops 13421772800 | bytes 2097152 | tf_op jit(solution)/shard_map/factor_1/pallas_call | solution.py:606
  108.3 1.0 collective-permute-start.14
  109.3 1.1 collective-permute-start.15
  110.4 6.9 %factor_3.1.inverse_ref = f32[512,512]{1,0:T(8,128)} custom-call(f32[512,512]{1,0:T(8,128)} %factor_1.1.refs_0_), custom_call_target="tpu_custom_call" | custom-call | flops 6710886400 | bytes 2097152 | tf_op jit(solution)/shard_map/factor_3/pallas_call | solution.py:606
  117.2 7.0 %collective-permute-done.14.refs_6_ = f32[384,256]{1,0:T(8,128)S(1)} collective-permute-done((f32[384,256]{1,0:T(8,128)S(1)}, f32[384,256]{1,0:T(8,128)S(1)}, u32[]{:S(2)}, u32[]{:S(2)}) %collective-permute-start.14) | collective-permute-done | bytes 393248 | tf_op jit(solution)/shard_map/ppermute | solution.py:546
  124.3 0.5 collective-permute-done.15.refs_7_
  124.8 1.9 reduce-scatter.3.cloned.1.call-done
  126.7 1.6 add.97.second_ref
  128.2 1.0 collective-permute-start.16
  129.2 0.5 collective-permute-start.21
  129.7 0.1 collective-permute-start.22
  129.8 1.1 collective-permute-start.17
  130.9 6.9 %collective-permute-done.16.refs_8_ = f32[384,256]{1,0:T(8,128)S(1)} collective-permute-done((f32[384,256]{1,0:T(8,128)S(1)}, f32[384,256]{1,0:T(8,128)S(1)}, u32[]{:S(2)}, u32[]{:S(2)}) %collective-permute-start.16) | collective-permute-done | bytes 393248 | tf_op jit(solution)/shard_map/ppermute | solution.py:546
  137.8 4.1 %solve_rows.1 = (f32[256,512]{1,0:T(8,128)}, f32[256,384]{1,0:T(8,128)}, f32[256,128]{1,0:T(8,128)}) custom-call(f32[512,512]{1,0:T(8,128)} %factor_3.1.inverse_ref, f32[384,256]{1,0:T(8,128)} %copy-done, f32[128,256]{1,0:T(8,128)} %add.97.second_ref), custom_call_target="tpu_custom_call" | custom-call | flops 5033164800 | bytes 2097152 | tf_op jit(solution)/shard_map/solve_rows/pallas_call | solution.py:183
  141.9 3.2 %collective-permute-done.17.refs_9_ = f32[384,256]{1,0:T(8,128)S(1)} collective-permute-done((f32[384,256]{1,0:T(8,128)S(1)}, f32[384,256]{1,0:T(8,128)S(1)}, u32[]{:S(2)}, u32[]{:S(2)}) %collective-permute-start.17) | collective-permute-done | bytes 393248 | tf_op jit(solution)/shard_map/ppermute | solution.py:546
  145.2 1.0 collective-permute-start.18
  146.2 1.1 collective-permute-start.19
  147.3 0.5 collective-permute-start.26
  147.8 8.1 %collective-permute-done.18.refs_10_ = f32[192,256]{1,0:T(8,128)S(1)} collective-permute-done((f32[192,256]{1,0:T(8,128)S(1)}, f32[192,256]{1,0:T(8,128)S(1)}, u32[]{:S(2)}, u32[]{:S(2)}) %collective-permute-start.18) | collective-permute-done | bytes 196640 | tf_op jit(solution)/shard_map/ppermute | solution.py:546
  155.9 0.8 collective-permute-done.19.refs_11_
  156.7 0.7 collective-permute-done.27.refs_19_
  157.3 0.8 collective-permute-done.28.refs_20_
  158.2 0.6 copy-done.18
  158.8 0.1 copy-done.13
  158.9 0.7 copy-done.14
  159.6 10.6 %update_rows.2.refs_2_ = f32[256,4096]{1,0:T(8,128)} custom-call(s32[384]{0:T(512)} %constant.80.clone.refs_0_, f32[256,384]{1,0:T(8,128)} %get-tuple-element.104.refs_1_, f32[256,4096]{1,0:T(8,128)} %refs_2_.1, f32[384,256]{1,0:T(8,128)} %copy-done, f32[384,256]{1,0:T(8,128)} %copy-done.6, f32[384,256]{1,0:T(8,128)} %copy-done.7, f32[384,256]{1,0:T(8,128)} %copy-done.8, ...), custom_call_target="tpu_custom_call" | custom-call | flops 2415919104 | bytes 14680064 | tf_op jit(solution)/shard_map/update_rows/pallas_call | solution.py:450
  170.3 0.2 collective-permute-start.29
  170.5 2.7 %collective-permute-done.29.refs_4_ = f32[8,128,256]{2,1,0:T(8,128)S(1)} collective-permute-done((f32[8,128,256]{2,1,0:T(8,128)}, f32[8,128,256]{2,1,0:T(8,128)S(1)}, u32[]{:S(2)}, u32[]{:S(2)}) %collective-permute-start.29) | collective-permute-done | bytes 1048608 | tf_op jit(solution)/shard_map/ppermute | solution.py:549
  173.2 1.0 copy-done.2
  174.2 7.5 %update_rows.3 = f32[256,4096]{1,0:T(8,128)} custom-call(s32[384]{0:T(512)} %constant.80.clone.refs_0_, f32[256,128]{1,0:T(8,128)} %get-tuple-element.103.refs_1_, f32[256,4096]{1,0:T(8,128)} %update_rows.2.refs_2_, f32[8,128,256]{2,1,0:T(8,128)} %bitcast.30, f32[8,128,256]{2,1,0:T(8,128)} %copy-done.2), custom_call_target="tpu_custom_call" | custom-call | flops 805306368 | bytes 10485760 | tf_op jit(solution)/shard_map/update_rows/pallas_call | solution.py:450
  (74 shorter events, 0.4 us)
Async XLA Ops:
  7.2 85.6 %reduce-scatter.5.cloned.1.call-start = ((), (), s32[]{:S(2)}) async-start(), calls=%async_computation.3 | async-start | bytes 3538944 | tf_op jit(solution)/shard_map/reduce_scatter | solution.py:560
  22.6 11.7 %collective-permute-start = (f32[128,640]{1,0:T(8,128)}, f32[128,640]{1,0:T(8,128)}, u32[]{:S(2)}, u32[]{:S(2)}) collective-permute-start(f32[128,640]{1,0:T(8,128)} %get-tuple-element.61), channel_id=1, source_target_pairs={{0,1},{1,0},{2,3},{3,2},{4,5},{5,4},{6,7},{7,6},{8,9},{9,8},{10,11... | collective-permute-start | bytes 983048 | tf_op jit(solution)/shard_map/ppermute | solution.py:549
  34.3 5.9 %collective-permute-start.1 = (f32[8,384,256]{2,1,0:T(8,128)}, f32[8,384,256]{2,1,0:T(8,128)S(1)}, u32[]{:S(2)}, u32[]{:S(2)}) collective-permute-start(f32[8,384,256]{2,1,0:T(8,128)} %get-tuple-element.66), channel_id=1, source_target_pairs={{0,1},{1,0},{2,3},{3,2},{4,5},{5,4},{6,7},{7,6},{8,9},{9,8},{10,11... | collective-permute-start | bytes 9437192 | tf_op jit(solution)/shard_map/ppermute | solution.py:549
  44.2 21.7 %copy-start.1 = (f32[8,128,256]{2,1,0:T(8,128)S(1)}, f32[8,128,256]{2,1,0:T(8,128)}, u32[]{:S(2)}) copy-start(f32[8,128,256]{2,1,0:T(8,128)} %get-tuple-element.72) | copy-start | bytes 3145732
  44.2 82.5 %reduce-scatter.3.cloned.1.call-start = ((), (), s32[]{:S(2)}) async-start(), calls=%async_computation.2 | async-start | bytes 1179648 | tf_op jit(solution)/shard_map/reduce_scatter | solution.py:560
  44.2 13.6 %collective-permute-start.6 = (f32[8,128,256]{2,1,0:T(8,128)}, f32[8,128,256]{2,1,0:T(8,128)S(1)}, u32[]{:S(2)}, u32[]{:S(2)}) collective-permute-start(f32[8,128,256]{2,1,0:T(8,128)} %get-tuple-element.68), channel_id=1, source_target_pairs={{0,1},{1,0},{2,3},{3,2},{4,5},{5,4},{6,7},{7,6},{8,9},{9,8},{10,11... | collective-permute-start | bytes 3145736 | tf_op jit(solution)/shard_map/ppermute | solution.py:549
  44.4 7.6 %collective-permute-start.2 = (f32[4,16,640]{2,1,0:T(8,128)}, f32[4,16,640]{2,1,0:T(8,128)S(1)}, u32[]{:S(2)}, u32[]{:S(2)}) collective-permute-start(f32[4,16,640]{2,1,0:T(8,128)} %dynamic-slice_bitcast_fusion), channel_id=1, source_target_pairs={{0,2},{1,3},{2,0},{3,1},{4,6},{5,7},{6,4},{7,5},{8,10},{9,11},{10,... | collective-permute-start | bytes 491528 | tf_op jit(solution)/shard_map/ppermute | solution.py:549
  52.1 6.8 %collective-permute-start.3 = (f32[16,640]{1,0:T(8,128)S(1)}, f32[16,640]{1,0:T(8,128)S(1)}, u32[]{:S(2)}, u32[]{:S(2)}) collective-permute-start(f32[16,640]{1,0:T(8,128)S(1)} %get-tuple-element.116), channel_id=1, source_target_pairs={{0,4},{1,5},{2,6},{3,7},{4,8},{5,9},{6,10},{7,11},{8,12},{9,13},{1... | collective-permute-start | bytes 122888 | tf_op jit(solution)/shard_map/ppermute | solution.py:557
  54.0 6.7 %collective-permute-start.4 = (f32[16,640]{1,0:T(8,128)S(1)}, f32[16,640]{1,0:T(8,128)S(1)}, u32[]{:S(2)}, u32[]{:S(2)}) collective-permute-start(f32[16,640]{1,0:T(8,128)S(1)} %get-tuple-element.115), channel_id=1, source_target_pairs={{0,8},{1,9},{2,10},{3,11},{4,12},{5,13},{6,14},{7,15},{8,0},{9,1},... | collective-permute-start | bytes 122888 | tf_op jit(solution)/shard_map/ppermute | solution.py:557
  56.5 5.0 %collective-permute-start.5 = (f32[16,640]{1,0:T(8,128)S(1)}, f32[16,640]{1,0:T(8,128)S(1)}, u32[]{:S(2)}, u32[]{:S(2)}) collective-permute-start(f32[16,640]{1,0:T(8,128)S(1)} %get-tuple-element.114), channel_id=1, source_target_pairs={{0,12},{1,13},{2,14},{3,15},{4,0},{5,1},{6,2},{7,3},{8,4},{9,5},{1... | collective-permute-start | bytes 122888 | tf_op jit(solution)/shard_map/ppermute | solution.py:557
  61.5 7.4 %collective-permute-start.7 = (f32[16,640]{1,0:T(8,128)S(1)}, f32[16,640]{1,0:T(8,128)S(1)}, u32[]{:S(2)}, u32[]{:S(2)}) collective-permute-start(f32[16,640]{1,0:T(8,128)S(1)} %bitcast_add_fusion.1), channel_id=1, source_target_pairs={{0,4},{1,5},{2,6},{3,7},{4,8},{5,9},{6,10},{7,11},{8,12},{9,13},{1... | collective-permute-start | bytes 122888 | tf_op jit(solution)/shard_map/ppermute | solution.py:557
  62.7 6.9 %collective-permute-start.8 = (f32[16,640]{1,0:T(8,128)S(1)}, f32[16,640]{1,0:T(8,128)S(1)}, u32[]{:S(2)}, u32[]{:S(2)}) collective-permute-start(f32[16,640]{1,0:T(8,128)S(1)} %bitcast_add_fusion.1), channel_id=1, source_target_pairs={{0,8},{1,9},{2,10},{3,11},{4,12},{5,13},{6,14},{7,15},{8,0},{9,1},... | collective-permute-start | bytes 122888 | tf_op jit(solution)/shard_map/ppermute | solution.py:557
  65.4 5.2 %collective-permute-start.9 = (f32[16,640]{1,0:T(8,128)S(1)}, f32[16,640]{1,0:T(8,128)S(1)}, u32[]{:S(2)}, u32[]{:S(2)}) collective-permute-start(f32[16,640]{1,0:T(8,128)S(1)} %bitcast_add_fusion.1), channel_id=1, source_target_pairs={{0,12},{1,13},{2,14},{3,15},{4,0},{5,1},{6,2},{7,3},{8,4},{9,5},{1... | collective-permute-start | bytes 122888 | tf_op jit(solution)/shard_map/ppermute | solution.py:557
  70.6 8.7 %collective-permute-start.10 = (f32[4,16,640]{2,1,0:T(8,128)S(1)}, f32[4,16,640]{2,1,0:T(8,128)S(1)}, u32[]{:S(2)}, u32[]{:S(2)}) collective-permute-start(f32[4,16,640]{2,1,0:T(8,128)S(1)} %pad_maximum_fusion), channel_id=1, source_target_pairs={{0,2},{1,3},{2,0},{3,1},{4,6},{5,7},{6,4},{7,5},{8,10},{9,11},{10,... | collective-permute-start | bytes 491528 | tf_op jit(solution)/shard_map/ppermute | solution.py:549
  79.4 1.7 copy-start.20
  79.4 1.7 collective-permute-start.11
  79.5 90.8 %all-gather.3.cloned.1.call-start = ((), (), s32[]{:S(2)}) async-start(), calls=%async_computation.4 | async-start | bytes 1179648 | tf_op jit(solution)/shard_map/all_gather | solution.py:603
  81.1 0.7 copy-start.21
  81.8 11.0 %copy-start.5 = (f32[384,256]{1,0:T(8,128)S(1)}, f32[384,256]{1,0:T(8,128)}, u32[]{:S(2)}) copy-start(f32[384,256]{1,0:T(8,128)} %get-tuple-element.82) | copy-start | bytes 1179652
  93.8 35.4 %copy-start = (f32[384,256]{1,0:T(8,128)}, f32[384,256]{1,0:T(8,128)S(1)}, u32[]{:S(2)}) copy-start(f32[384,256]{1,0:T(8,128)S(1)} %add.96.first_ref.refs_3_) | copy-start | bytes 1179652
  93.9 14.4 %collective-permute-start.12 = (f32[384,256]{1,0:T(8,128)S(1)}, f32[384,256]{1,0:T(8,128)S(1)}, u32[]{:S(2)}, u32[]{:S(2)}) collective-permute-start(f32[384,256]{1,0:T(8,128)S(1)} %add.96.first_ref.refs_3_), channel_id=1, source_target_pairs={{0,4},{1,5},{4,8},{5,9},{8,12},{9,13},{12,14},{13,15},{14,10},{15,... | collective-permute-start | bytes 1179656 | tf_op jit(solution)/shard_map/ppermute | solution.py:546
  94.9 13.4 %collective-permute-start.13 = (f32[384,256]{1,0:T(8,128)S(1)}, f32[384,256]{1,0:T(8,128)S(1)}, u32[]{:S(2)}, u32[]{:S(2)}) collective-permute-start(f32[384,256]{1,0:T(8,128)S(1)} %add.96.first_ref.refs_3_), channel_id=1, source_target_pairs={{0,2},{1,3},{4,0},{5,1},{8,4},{9,5},{12,8},{13,9},{14,12},{15,13},... | collective-permute-start | bytes 1179656 | tf_op jit(solution)/shard_map/ppermute | solution.py:546
  108.3 18.4 %copy-start.19 = (f32[128,256]{1,0:T(8,128)S(1)}, f32[128,256]{1,0:T(8,128)}, u32[]{:S(2)}) copy-start(f32[128,256]{1,0:T(8,128)} %get-tuple-element.95) | copy-start | bytes 393220
  108.3 21.0 %copy-start.6 = (f32[384,256]{1,0:T(8,128)}, f32[384,256]{1,0:T(8,128)S(1)}, u32[]{:S(2)}) copy-start(f32[384,256]{1,0:T(8,128)S(1)} %collective-permute-done.12.refs_4_) | copy-start | bytes 1179652
  108.3 21.5 %copy-start.7 = (f32[384,256]{1,0:T(8,128)}, f32[384,256]{1,0:T(8,128)S(1)}, u32[]{:S(2)}) copy-start(f32[384,256]{1,0:T(8,128)S(1)} %collective-permute-done.13.refs_5_) | copy-start | bytes 1179652
  108.3 16.0 %collective-permute-start.14 = (f32[384,256]{1,0:T(8,128)S(1)}, f32[384,256]{1,0:T(8,128)S(1)}, u32[]{:S(2)}, u32[]{:S(2)}) collective-permute-start(f32[384,256]{1,0:T(8,128)S(1)} %collective-permute-done.12.refs_4_), channel_id=1, source_target_pairs={{0,4},{1,5},{4,8},{5,9},{8,12},{9,13},{12,14},{13,15},{14,10},{15,... | collective-permute-start | bytes 1179656 | tf_op jit(solution)/shard_map/ppermute | solution.py:546
  109.3 15.5 %collective-permute-start.15 = (f32[384,256]{1,0:T(8,128)S(1)}, f32[384,256]{1,0:T(8,128)S(1)}, u32[]{:S(2)}, u32[]{:S(2)}) collective-permute-start(f32[384,256]{1,0:T(8,128)S(1)} %collective-permute-done.13.refs_5_), channel_id=1, source_target_pairs={{0,2},{1,3},{4,0},{5,1},{8,4},{9,5},{12,8},{13,9},{14,12},{15,13},... | collective-permute-start | bytes 1179656 | tf_op jit(solution)/shard_map/ppermute | solution.py:546
  124.2 17.7 %copy-start.8 = (f32[384,256]{1,0:T(8,128)}, f32[384,256]{1,0:T(8,128)S(1)}, u32[]{:S(2)}) copy-start(f32[384,256]{1,0:T(8,128)S(1)} %collective-permute-done.14.refs_6_) | copy-start | bytes 1179652
  124.8 20.3 %copy-start.9 = (f32[384,256]{1,0:T(8,128)}, f32[384,256]{1,0:T(8,128)S(1)}, u32[]{:S(2)}) copy-start(f32[384,256]{1,0:T(8,128)S(1)} %collective-permute-done.15.refs_7_) | copy-start | bytes 1179652
  128.2 9.5 %collective-permute-start.16 = (f32[384,256]{1,0:T(8,128)S(1)}, f32[384,256]{1,0:T(8,128)S(1)}, u32[]{:S(2)}, u32[]{:S(2)}) collective-permute-start(f32[384,256]{1,0:T(8,128)S(1)} %collective-permute-done.14.refs_6_), channel_id=1, source_target_pairs={{0,4},{1,5},{4,8},{5,9},{8,12},{9,13},{12,14},{13,15},{14,10},{15,... | collective-permute-start | bytes 1179656 | tf_op jit(solution)/shard_map/ppermute | solution.py:546
  129.2 16.0 %collective-permute-start.20 = (f32[384,256]{1,0:T(8,128)S(1)}, f32[384,256]{1,0:T(8,128)S(1)}, u32[]{:S(2)}, u32[]{:S(2)}) collective-permute-start(f32[384,256]{1,0:T(8,128)S(1)} %add.96.first_ref.refs_3_), channel_id=1, source_target_pairs={{0,1},{1,0},{2,3},{3,2},{4,5},{5,4},{6,7},{7,6},{8,9},{9,8},{10,11... | collective-permute-start | bytes 1179656 | tf_op jit(solution)/shard_map/ppermute | solution.py:549
  129.2 17.0 %collective-permute-start.21 = (f32[384,256]{1,0:T(8,128)S(1)}, f32[384,256]{1,0:T(8,128)S(1)}, u32[]{:S(2)}, u32[]{:S(2)}) collective-permute-start(f32[384,256]{1,0:T(8,128)S(1)} %collective-permute-done.12.refs_4_), channel_id=1, source_target_pairs={{0,1},{1,0},{2,3},{3,2},{4,5},{5,4},{6,7},{7,6},{8,9},{9,8},{10,11... | collective-permute-start | bytes 1179656 | tf_op jit(solution)/shard_map/ppermute | solution.py:549
  129.7 17.6 %collective-permute-start.22 = (f32[384,256]{1,0:T(8,128)S(1)}, f32[384,256]{1,0:T(8,128)}, u32[]{:S(2)}, u32[]{:S(2)}) collective-permute-start(f32[384,256]{1,0:T(8,128)S(1)} %collective-permute-done.13.refs_5_), channel_id=1, source_target_pairs={{0,1},{1,0},{2,3},{3,2},{4,5},{5,4},{6,7},{7,6},{8,9},{9,8},{10,11... | collective-permute-start | bytes 1179656 | tf_op jit(solution)/shard_map/ppermute | solution.py:549
  129.8 15.3 %collective-permute-start.17 = (f32[384,256]{1,0:T(8,128)S(1)}, f32[384,256]{1,0:T(8,128)S(1)}, u32[]{:S(2)}, u32[]{:S(2)}) collective-permute-start(f32[384,256]{1,0:T(8,128)S(1)} %collective-permute-done.15.refs_7_), channel_id=1, source_target_pairs={{0,2},{1,3},{4,0},{5,1},{8,4},{9,5},{12,8},{13,9},{14,12},{15,13},... | collective-permute-start | bytes 1179656 | tf_op jit(solution)/shard_map/ppermute | solution.py:546
  137.8 9.5 %copy-start.3 = (f32[384,256]{1,0:T(8,128)}, f32[384,256]{1,0:T(8,128)S(1)}, u32[]{:S(2)}) copy-start(f32[384,256]{1,0:T(8,128)S(1)} %collective-permute-done.16.refs_8_) | copy-start | bytes 1179652
  137.8 9.5 %collective-permute-start.23 = (f32[384,256]{1,0:T(8,128)S(1)}, f32[384,256]{1,0:T(8,128)}, u32[]{:S(2)}, u32[]{:S(2)}) collective-permute-start(f32[384,256]{1,0:T(8,128)S(1)} %collective-permute-done.14.refs_6_), channel_id=1, source_target_pairs={{0,1},{1,0},{2,3},{3,2},{4,5},{5,4},{6,7},{7,6},{8,9},{9,8},{10,11... | collective-permute-start | bytes 1179656 | tf_op jit(solution)/shard_map/ppermute | solution.py:549
  145.1 13.0 %copy-start.4 = (f32[384,256]{1,0:T(8,128)}, f32[384,256]{1,0:T(8,128)S(1)}, u32[]{:S(2)}) copy-start(f32[384,256]{1,0:T(8,128)S(1)} %collective-permute-done.17.refs_9_) | copy-start | bytes 1179652
  145.1 11.5 %collective-permute-start.24 = (f32[384,256]{1,0:T(8,128)S(1)}, f32[384,256]{1,0:T(8,128)S(1)}, u32[]{:S(2)}, u32[]{:S(2)}) collective-permute-start(f32[384,256]{1,0:T(8,128)S(1)} %collective-permute-done.15.refs_7_), channel_id=1, source_target_pairs={{0,1},{1,0},{2,3},{3,2},{4,5},{5,4},{6,7},{7,6},{8,9},{9,8},{10,11... | collective-permute-start | bytes 1179656 | tf_op jit(solution)/shard_map/ppermute | solution.py:549
  145.2 12.9 %copy-start.10 = (f32[384,256]{1,0:T(8,128)}, f32[384,256]{1,0:T(8,128)S(1)}, u32[]{:S(2)}) copy-start(f32[384,256]{1,0:T(8,128)S(1)} %collective-permute-done.20.refs_12_) | copy-start | bytes 1179652
  145.2 10.7 %collective-permute-start.18 = (f32[192,256]{1,0:T(8,128)S(1)}, f32[192,256]{1,0:T(8,128)S(1)}, u32[]{:S(2)}, u32[]{:S(2)}) collective-permute-start(f32[192,256]{1,0:T(8,128)S(1)} %slice.6), channel_id=1, source_target_pairs={{0,4},{1,5},{4,8},{5,9},{8,12},{9,13},{12,14},{13,15},{14,10},{15,... | collective-permute-start | bytes 589832 | tf_op jit(solution)/shard_map/ppermute | solution.py:546
  146.2 11.9 %copy-start.11 = (f32[384,256]{1,0:T(8,128)}, f32[384,256]{1,0:T(8,128)S(1)}, u32[]{:S(2)}) copy-start(f32[384,256]{1,0:T(8,128)S(1)} %collective-permute-done.21.refs_13_) | copy-start | bytes 1179652
  146.2 10.4 %collective-permute-start.19 = (f32[192,256]{1,0:T(8,128)S(1)}, f32[192,256]{1,0:T(8,128)S(1)}, u32[]{:S(2)}, u32[]{:S(2)}) collective-permute-start(f32[192,256]{1,0:T(8,128)S(1)} %slice.7), channel_id=1, source_target_pairs={{0,2},{1,3},{4,0},{5,1},{8,4},{9,5},{12,8},{13,9},{14,12},{15,13},... | collective-permute-start | bytes 589832 | tf_op jit(solution)/shard_map/ppermute | solution.py:546
  147.3 10.8 %collective-permute-start.25 = (f32[384,256]{1,0:T(8,128)S(1)}, f32[384,256]{1,0:T(8,128)S(1)}, u32[]{:S(2)}, u32[]{:S(2)}) collective-permute-start(f32[384,256]{1,0:T(8,128)S(1)} %collective-permute-done.16.refs_8_), channel_id=1, source_target_pairs={{0,1},{1,0},{2,3},{3,2},{4,5},{5,4},{6,7},{7,6},{8,9},{9,8},{10,11... | collective-permute-start | bytes 1179656 | tf_op jit(solution)/shard_map/ppermute | solution.py:549
  147.3 10.8 %collective-permute-start.26 = (f32[384,256]{1,0:T(8,128)S(1)}, f32[384,256]{1,0:T(8,128)S(1)}, u32[]{:S(2)}, u32[]{:S(2)}) collective-permute-start(f32[384,256]{1,0:T(8,128)S(1)} %collective-permute-done.17.refs_9_), channel_id=1, source_target_pairs={{0,1},{1,0},{2,3},{3,2},{4,5},{5,4},{6,7},{7,6},{8,9},{9,8},{10,11... | collective-permute-start | bytes 1179656 | tf_op jit(solution)/shard_map/ppermute | solution.py:549
  155.9 2.2 %copy-start.15 = (f32[192,256]{1,0:T(8,128)}, f32[192,256]{1,0:T(8,128)S(1)}, u32[]{:S(2)}) copy-start(f32[192,256]{1,0:T(8,128)S(1)} %collective-permute-done.18.refs_10_) | copy-start | bytes 589828
  155.9 1.4 collective-permute-start.27
  156.6 1.5 copy-start.16
  156.6 1.4 collective-permute-start.28
  156.7 1.5 copy-start.12
  157.3 0.8 copy-start.17
  158.1 0.7 copy-start.18
  158.1 0.8 copy-start.13
  158.9 0.7 copy-start.14
  170.3 2.9 %collective-permute-start.29 = (f32[8,128,256]{2,1,0:T(8,128)}, f32[8,128,256]{2,1,0:T(8,128)S(1)}, u32[]{:S(2)}, u32[]{:S(2)}) collective-permute-start(f32[8,128,256]{2,1,0:T(8,128)} %bitcast.29), channel_id=1, source_target_pairs={{0,1},{1,0},{2,3},{3,2},{4,5},{5,4},{6,7},{7,6},{8,9},{9,8},{10,11... | collective-permute-start | bytes 3145736 | tf_op jit(solution)/shard_map/ppermute | solution.py:549
  173.2 1.0 copy-start.2
Sparse Core Ops, SparseCore 0:
  44.3 48.4 reduce-scatter.4
  95.1 31.5 reduce-scatter.2
  128.4 31.3 all-gather.2

commit v13 on v12

--- a/solution.py
+++ b/solution.py
@@ -603,11 +603,13 @@
             gathered = lax.all_gather(panel_1, "scen", axis_index_groups=groups)
             ahead, panel_1 = together((ahead, panel_1))
         ahead = [step(ahead[0], 1), step(ahead[1], -1)]
-        work = stages[d](work) if d < len(stages) else solve_rows(work, panel_0, panel_1)
+        if d < len(stages):
+            work = stages[d](work)
         ahead, work = together((ahead, work))
         shards += ahead
-    factor_rows, weight_0, weight_1 = work
-    shards += across(panel_0, ahead)
+    ahead, solved = together((across(panel_0, ahead), solve_rows(work, panel_0, panel_1)))
+    factor_rows, weight_0, weight_1 = solved
+    shards += ahead
     shards = shards + [swap(piece, 1) for piece in shards]
     updated = update_rows(update_table, parts, weight_0, prior_schur, shards)
     updated, gathered = together((updated, gathered))

time: 189 us -> 186 us (0.984)
  waiting for transfers between devices: 60.4 us -> 58 us
    ppermute x8, waiting for transfers between devices: 26.5 us -> 24 us  [step(): return lax.ppermute(values, 'scen', pairs)]
where the time goes in v13:
time: 186 us
  Pallas kernels  75 us (40%)
  waiting for transfers between devices  58 us (31%)
  starting transfers between devices  26.3 us (14%)
  between operations  14.6 us (8%)
  other arithmetic  8.89 us (5%)
  local copies, waits for them, and re-layouts  3.16 us (2%)
    ppermute x8, waiting for transfers between devices, step(): return lax.ppermute(values, 'scen', pairs)  24 us
    ppermute x16, waiting for transfers between devices, swap(): return lax.ppermute(values, 'scen', [(d, d ^ bit) for d in range(parts)])  21.5 us
    pallas_call x2, Pallas kernels, shards_on_ring(): work = stages[d](work)  19.2 us
    pallas_call x2, Pallas kernels, update_rows(): pl.pallas_call(lambda *refs: update_kernel(count, *refs), out_shape=jax.S...  18.2 us
    pallas_call x1, Pallas kernels, pick_columns(): pl.pallas_call(pick_kernel, grid=(depth // tall,), in_specs=[pl.BlockSpec...  14.7 us
    pallas_call x1, Pallas kernels, gram_blocks(): pl.pallas_call(gram_kernel, grid=(depth // tall,), in_specs=[pl.BlockSpec...  11.2 us
    ppermute x6, starting transfers between devices, shift(): lax.ppermute(values, 'scen', [(d, (d + 4 * by) % parts) for d in range(pa...  10.1 us
    ppermute x8, starting transfers between devices, step(): return lax.ppermute(values, 'scen', pairs)  8.58 us
  transfers between devices with their start and end apart: 33, of which 21 were waited for; matrix products, arithmetic and copies ran while one was open for 2% of the time, Pallas kernels for 28%

profile of v13, /device:TPU:0, one launch (start us, length us, event | category | flops | bytes accessed | tf_op | source)
XLA Modules:
  0.0 186.0 jit_solution(11564999962243080246)
XLA Ops:
  7.9 14.7 %pick_columns.1 = (bf16[512,1024]{1,0:T(8,128)(2,1)}, f32[384,256]{1,0:T(8,128)}, f32[128,256]{1,0:T(8,128)}, f32[128,640]{1,0:T(8,128)}, f32[128,640]{1,0:T(8,128)}) custom-call(s32[1]{0:T(128)S(6)} %copy.15.counts_ref, s32[1,512]{1,0:T(1,128)} %bitcast.38, f32[1,1024]{1,0:T(1,128)} %bitcast.37, f32[256,4096]{1,0:T(8,128)} %refs_2_.1, ...), custom_call_target="tpu_custom_call" | custom-call | flops 6442450944 | bytes 12582912 | tf_op jit(solution)/shard_map/pick_columns/pallas_call | solution.py:288
  22.6 0.5 collective-permute-start
  23.1 11.2 %gram_blocks.1 = (f32[8,384,256]{2,1,0:T(8,128)}, f32[8,128,256]{2,1,0:T(8,128)}, f32[8,384,256]{2,1,0:T(8,128)}, f32[8,128,256]{2,1,0:T(8,128)}) custom-call(s32[256]{0:T(256)} %constant.79.clone.table_ref, bf16[512,1024]{1,0:T(8,128)(2,1)} %get-tuple-element.65.scaled_ref, bf16[1024,4096]{1,0:T(8,128)(2,1)} %rows_ref.3), custom_call_target="tpu_custom_call" | custom-call | flops 4294967296 | bytes 16777216 | tf_op jit(solution)/shard_map/gram_blocks/pallas_call | solution.py:380
  34.3 0.1 collective-permute-start.1
  34.4 1.1 add.76
  35.5 0.7 dynamic-slice_bitcast_fusion
  36.2 4.0 %collective-permute-done.1 = f32[8,384,256]{2,1,0:T(8,128)S(1)} collective-permute-done((f32[8,384,256]{2,1,0:T(8,128)}, f32[8,384,256]{2,1,0:T(8,128)S(1)}, u32[]{:S(2)}, u32[]{:S(2)}) %collective-permute-start.1) | collective-permute-done | bytes 3145760 | tf_op jit(solution)/shard_map/ppermute | solution.py:549
  40.2 4.0 %add.95 = f32[8,384,256]{2,1,0:T(8,128)} add(f32[8,384,256]{2,1,0:T(8,128)} %get-tuple-element.78, f32[8,384,256]{2,1,0:T(8,128)S(1)} %collective-permute-done.1) | non-fusion elementwise | flops 786432 | bytes 9437184 | tf_op jit(solution)/shard_map/add | solution.py:579
  44.2 0.2 collective-permute-start.6
  44.4 2.9 %collective-permute-start.2 = (f32[4,16,640]{2,1,0:T(8,128)}, f32[4,16,640]{2,1,0:T(8,128)S(1)}, u32[]{:S(2)}, u32[]{:S(2)}) collective-permute-start(f32[4,16,640]{2,1,0:T(8,128)} %dynamic-slice_bitcast_fusion), channel_id=1, source_target_pairs={{0,2},{1,3},{2,0},{3,1},{4,6},{5,7},{6,4},{7,5},{8,10},{9,11},{10,... | collective-permute-start | bytes 491528 | tf_op jit(solution)/shard_map/ppermute | solution.py:549
  47.3 4.7 %collective-permute-done.2 = f32[4,16,640]{2,1,0:T(8,128)S(1)} collective-permute-done((f32[4,16,640]{2,1,0:T(8,128)}, f32[4,16,640]{2,1,0:T(8,128)S(1)}, u32[]{:S(2)}, u32[]{:S(2)}) %collective-permute-start.2) | collective-permute-done | bytes 163872 | tf_op jit(solution)/shard_map/ppermute | solution.py:549
  52.1 1.9 %collective-permute-start.3 = (f32[16,640]{1,0:T(8,128)S(1)}, f32[16,640]{1,0:T(8,128)S(1)}, u32[]{:S(2)}, u32[]{:S(2)}) collective-permute-start(f32[16,640]{1,0:T(8,128)S(1)} %get-tuple-element.122), channel_id=1, source_target_pairs={{0,4},{1,5},{2,6},{3,7},{4,8},{5,9},{6,10},{7,11},{8,12},{9,13},{1... | collective-permute-start | bytes 122888 | tf_op jit(solution)/shard_map/ppermute | solution.py:557
  54.0 2.6 %collective-permute-start.4 = (f32[16,640]{1,0:T(8,128)S(1)}, f32[16,640]{1,0:T(8,128)S(1)}, u32[]{:S(2)}, u32[]{:S(2)}) collective-permute-start(f32[16,640]{1,0:T(8,128)S(1)} %get-tuple-element.121), channel_id=1, source_target_pairs={{0,8},{1,9},{2,10},{3,11},{4,12},{5,13},{6,14},{7,15},{8,0},{9,1},... | collective-permute-start | bytes 122888 | tf_op jit(solution)/shard_map/ppermute | solution.py:557
  56.5 1.4 collective-permute-start.5
  57.9 1.0 collective-permute-done.3
  58.9 1.8 collective-permute-done.4
  60.7 0.8 collective-permute-done.5
  61.5 1.2 collective-permute-start.7
  62.7 2.7 %collective-permute-start.8 = (f32[16,640]{1,0:T(8,128)S(1)}, f32[16,640]{1,0:T(8,128)S(1)}, u32[]{:S(2)}, u32[]{:S(2)}) collective-permute-start(f32[16,640]{1,0:T(8,128)S(1)} %bitcast_add_fusion.1), channel_id=1, source_target_pairs={{0,8},{1,9},{2,10},{3,11},{4,12},{5,13},{6,14},{7,15},{8,0},{9,1},... | collective-permute-start | bytes 122888 | tf_op jit(solution)/shard_map/ppermute | solution.py:557
  65.4 0.4 collective-permute-start.9
  65.8 1.2 add.94
  67.0 1.9 collective-permute-done.7
  68.8 0.9 collective-permute-done.8
  69.7 0.9 collective-permute-done.9
  70.6 1.6 collective-permute-start.10
  72.3 7.1 %collective-permute-done.10 = f32[4,16,640]{2,1,0:T(8,128)S(1)} collective-permute-done((f32[4,16,640]{2,1,0:T(8,128)S(1)}, f32[4,16,640]{2,1,0:T(8,128)S(1)}, u32[]{:S(2)}, u32[]{:S(2)}) %collective-permute-start.10) | collective-permute-done | bytes 163872 | tf_op jit(solution)/shard_map/ppermute | solution.py:549
  79.5 1.5 collective-permute-done.11.refs_1_
  81.1 0.7 copy-done.18
  81.8 7.7 %factor_first.1.refs_0_ = f32[512,512]{1,0:T(8,128)} custom-call(s32[256]{0:T(256)} %constant.81.clone.table_ref, f32[1,512]{1,0:T(1,128)} %bitcast.39, f32[8,16,640]{2,1,0:T(8,128)} %copy-done.17, f32[8,16,640]{2,1,0:T(8,128)} %copy-done.18), custom_call_target="tpu_custom_call" | custom-call | flops 6710886400 | bytes 2097152 | tf_op jit(solution)/shard_map/factor_first/pallas_call | solution.py:146
  89.5 3.3 %reduce-scatter.5.cloned.1.call-done = f32[1,384,256]{2,1,0:T(8,128)} async-done(((f32[8,384,256]{2,1,0:T(8,128)}), f32[1,384,256]{2,1,0:T(8,128)}) %reduce-scatter.5.cloned.1.call-update) | async-done | bytes 393232 | tf_op jit(solution)/shard_map/reduce_scatter | solution.py:560
  92.8 1.0 add.96.first_ref.refs_3_
  93.9 1.0 collective-permute-start.12
  94.9 1.1 collective-permute-start.13
  95.9 12.3 %factor_1.1.refs_0_ = f32[512,512]{1,0:T(8,128)} custom-call(f32[512,512]{1,0:T(8,128)} %factor_first.1.refs_0_), custom_call_target="tpu_custom_call" | custom-call | flops 13421772800 | bytes 2097152 | tf_op jit(solution)/shard_map/factor_1/pallas_call | solution.py:607
  108.3 1.0 collective-permute-start.14
  109.3 1.1 collective-permute-start.15
  110.4 6.9 %factor_3.1.inverse_ref = f32[512,512]{1,0:T(8,128)} custom-call(f32[512,512]{1,0:T(8,128)} %factor_1.1.refs_0_), custom_call_target="tpu_custom_call" | custom-call | flops 6710886400 | bytes 2097152 | tf_op jit(solution)/shard_map/factor_3/pallas_call | solution.py:607
  117.2 7.1 %collective-permute-done.14.refs_6_ = f32[384,256]{1,0:T(8,128)S(1)} collective-permute-done((f32[384,256]{1,0:T(8,128)S(1)}, f32[384,256]{1,0:T(8,128)S(1)}, u32[]{:S(2)}, u32[]{:S(2)}) %collective-permute-start.14) | collective-permute-done | bytes 393248 | tf_op jit(solution)/shard_map/ppermute | solution.py:546
  124.3 0.5 collective-permute-done.15.refs_7_
  124.8 1.9 %reduce-scatter.3.cloned.1.call-done = f32[1,128,256]{2,1,0:T(8,128)} async-done(((f32[8,128,256]{2,1,0:T(8,128)}), f32[1,128,256]{2,1,0:T(8,128)}) %reduce-scatter.3.cloned.1.call-update) | async-done | bytes 131088 | tf_op jit(solution)/shard_map/reduce_scatter | solution.py:560
  126.7 1.6 add.97.second_ref
  128.3 0.9 collective-permute-start.16
  129.3 1.1 collective-permute-start.17
  130.4 0.5 collective-permute-start.21
  130.9 9.0 %collective-permute-done.16.refs_8_ = f32[384,256]{1,0:T(8,128)S(1)} collective-permute-done((f32[384,256]{1,0:T(8,128)S(1)}, f32[384,256]{1,0:T(8,128)S(1)}, u32[]{:S(2)}, u32[]{:S(2)}) %collective-permute-start.16) | collective-permute-done | bytes 393248 | tf_op jit(solution)/shard_map/ppermute | solution.py:546
  139.9 2.1 %collective-permute-done.17.refs_9_ = f32[384,256]{1,0:T(8,128)S(1)} collective-permute-done((f32[384,256]{1,0:T(8,128)S(1)}, f32[384,256]{1,0:T(8,128)S(1)}, u32[]{:S(2)}, u32[]{:S(2)}) %collective-permute-start.17) | collective-permute-done | bytes 393248 | tf_op jit(solution)/shard_map/ppermute | solution.py:546
  142.0 0.4 collective-permute-start.18
  142.5 1.9 %collective-permute-start.19 = (f32[192,256]{1,0:T(8,128)S(1)}, f32[192,256]{1,0:T(8,128)}, u32[]{:S(2)}, u32[]{:S(2)}) collective-permute-start(f32[192,256]{1,0:T(8,128)S(1)} %slice.7), channel_id=1, source_target_pairs={{0,2},{1,3},{4,0},{5,1},{8,4},{9,5},{12,8},{13,9},{14,12},{15,13},... | collective-permute-start | bytes 589832 | tf_op jit(solution)/shard_map/ppermute | solution.py:546
  144.4 0.5 collective-permute-start.23
  144.9 0.1 collective-permute-start.24
  145.0 4.1 %collective-permute-done.18.refs_10_ = f32[192,256]{1,0:T(8,128)} collective-permute-done((f32[192,256]{1,0:T(8,128)S(1)}, f32[192,256]{1,0:T(8,128)}, u32[]{:S(2)}, u32[]{:S(2)}) %collective-permute-start.18) | collective-permute-done | bytes 196640 | tf_op jit(solution)/shard_map/ppermute | solution.py:546
  149.2 1.2 collective-permute-done.19.refs_11_
  150.3 4.0 %solve_rows.1 = (f32[256,512]{1,0:T(8,128)}, f32[256,384]{1,0:T(8,128)}, f32[256,128]{1,0:T(8,128)}) custom-call(f32[512,512]{1,0:T(8,128)} %factor_3.1.inverse_ref, f32[384,256]{1,0:T(8,128)} %copy-done, f32[128,256]{1,0:T(8,128)} %add.97.second_ref), custom_call_target="tpu_custom_call" | custom-call | flops 5033164800 | bytes 2097152 | tf_op jit(solution)/shard_map/solve_rows/pallas_call | solution.py:183
  154.4 0.6 collective-permute-start.27
  155.0 0.1 collective-permute-start.28
  155.1 1.2 collective-permute-done.27.refs_19_
  156.2 0.4 collective-permute-done.28.refs_20_
  156.6 0.3 copy-done.14
  156.9 0.4 copy-done.15
  157.3 10.6 %update_rows.2.refs_2_ = f32[256,4096]{1,0:T(8,128)} custom-call(s32[384]{0:T(512)} %constant.80.clone.refs_0_, f32[256,384]{1,0:T(8,128)} %get-tuple-element.110.refs_1_, f32[256,4096]{1,0:T(8,128)} %refs_2_.1, f32[384,256]{1,0:T(8,128)} %copy-done, f32[384,256]{1,0:T(8,128)} %copy-done.6, f32[384,256]{1,0:T(8,128)} %copy-done.7, f32[384,256]{1,0:T(8,128)} %copy-done.8, ...), custom_call_target="tpu_custom_call" | custom-call | flops 2415919104 | bytes 14680064 | tf_op jit(solution)/shard_map/update_rows/pallas_call | solution.py:450
  168.0 0.3 collective-permute-start.29
  168.3 2.6 %collective-permute-done.29.refs_4_ = f32[8,128,256]{2,1,0:T(8,128)S(1)} collective-permute-done((f32[8,128,256]{2,1,0:T(8,128)}, f32[8,128,256]{2,1,0:T(8,128)S(1)}, u32[]{:S(2)}, u32[]{:S(2)}) %collective-permute-start.29) | collective-permute-done | bytes 1048608 | tf_op jit(solution)/shard_map/ppermute | solution.py:549
  170.9 1.0 copy-done.2
  171.9 7.5 %update_rows.3 = f32[256,4096]{1,0:T(8,128)} custom-call(s32[384]{0:T(512)} %constant.80.clone.refs_0_, f32[256,128]{1,0:T(8,128)} %get-tuple-element.109.refs_1_, f32[256,4096]{1,0:T(8,128)} %update_rows.2.refs_2_, f32[8,128,256]{2,1,0:T(8,128)} %bitcast.30, f32[8,128,256]{2,1,0:T(8,128)} %copy-done.2), custom_call_target="tpu_custom_call" | custom-call | flops 805306368 | bytes 10485760 | tf_op jit(solution)/shard_map/update_rows/pallas_call | solution.py:450
  (68 shorter events, 0.5 us)
Async XLA Ops:
  7.2 85.6 %reduce-scatter.5.cloned.1.call-start = ((), (), s32[]{:S(2)}) async-start(), calls=%async_computation.3 | async-start | bytes 3538944 | tf_op jit(solution)/shard_map/reduce_scatter | solution.py:560
  22.6 11.7 %collective-permute-start = (f32[128,640]{1,0:T(8,128)}, f32[128,640]{1,0:T(8,128)}, u32[]{:S(2)}, u32[]{:S(2)}) collective-permute-start(f32[128,640]{1,0:T(8,128)} %get-tuple-element.64), channel_id=1, source_target_pairs={{0,1},{1,0},{2,3},{3,2},{4,5},{5,4},{6,7},{7,6},{8,9},{9,8},{10,11... | collective-permute-start | bytes 983048 | tf_op jit(solution)/shard_map/ppermute | solution.py:549
  34.3 5.9 %collective-permute-start.1 = (f32[8,384,256]{2,1,0:T(8,128)}, f32[8,384,256]{2,1,0:T(8,128)S(1)}, u32[]{:S(2)}, u32[]{:S(2)}) collective-permute-start(f32[8,384,256]{2,1,0:T(8,128)} %get-tuple-element.69), channel_id=1, source_target_pairs={{0,1},{1,0},{2,3},{3,2},{4,5},{5,4},{6,7},{7,6},{8,9},{9,8},{10,11... | collective-permute-start | bytes 9437192 | tf_op jit(solution)/shard_map/ppermute | solution.py:549
  44.2 21.7 %copy-start.1 = (f32[8,128,256]{2,1,0:T(8,128)S(1)}, f32[8,128,256]{2,1,0:T(8,128)}, u32[]{:S(2)}) copy-start(f32[8,128,256]{2,1,0:T(8,128)} %get-tuple-element.75) | copy-start | bytes 3145732
  44.2 82.5 %reduce-scatter.3.cloned.1.call-start = ((), (), s32[]{:S(2)}) async-start(), calls=%async_computation.2 | async-start | bytes 1179648 | tf_op jit(solution)/shard_map/reduce_scatter | solution.py:560
  44.2 13.6 %collective-permute-start.6 = (f32[8,128,256]{2,1,0:T(8,128)}, f32[8,128,256]{2,1,0:T(8,128)S(1)}, u32[]{:S(2)}, u32[]{:S(2)}) collective-permute-start(f32[8,128,256]{2,1,0:T(8,128)} %get-tuple-element.71), channel_id=1, source_target_pairs={{0,1},{1,0},{2,3},{3,2},{4,5},{5,4},{6,7},{7,6},{8,9},{9,8},{10,11... | collective-permute-start | bytes 3145736 | tf_op jit(solution)/shard_map/ppermute | solution.py:549
  44.4 7.6 %collective-permute-start.2 = (f32[4,16,640]{2,1,0:T(8,128)}, f32[4,16,640]{2,1,0:T(8,128)S(1)}, u32[]{:S(2)}, u32[]{:S(2)}) collective-permute-start(f32[4,16,640]{2,1,0:T(8,128)} %dynamic-slice_bitcast_fusion), channel_id=1, source_target_pairs={{0,2},{1,3},{2,0},{3,1},{4,6},{5,7},{6,4},{7,5},{8,10},{9,11},{10,... | collective-permute-start | bytes 491528 | tf_op jit(solution)/shard_map/ppermute | solution.py:549
  52.1 6.8 %collective-permute-start.3 = (f32[16,640]{1,0:T(8,128)S(1)}, f32[16,640]{1,0:T(8,128)S(1)}, u32[]{:S(2)}, u32[]{:S(2)}) collective-permute-start(f32[16,640]{1,0:T(8,128)S(1)} %get-tuple-element.122), channel_id=1, source_target_pairs={{0,4},{1,5},{2,6},{3,7},{4,8},{5,9},{6,10},{7,11},{8,12},{9,13},{1... | collective-permute-start | bytes 122888 | tf_op jit(solution)/shard_map/ppermute | solution.py:557
  54.0 6.7 %collective-permute-start.4 = (f32[16,640]{1,0:T(8,128)S(1)}, f32[16,640]{1,0:T(8,128)S(1)}, u32[]{:S(2)}, u32[]{:S(2)}) collective-permute-start(f32[16,640]{1,0:T(8,128)S(1)} %get-tuple-element.121), channel_id=1, source_target_pairs={{0,8},{1,9},{2,10},{3,11},{4,12},{5,13},{6,14},{7,15},{8,0},{9,1},... | collective-permute-start | bytes 122888 | tf_op jit(solution)/shard_map/ppermute | solution.py:557
  56.5 5.0 %collective-permute-start.5 = (f32[16,640]{1,0:T(8,128)S(1)}, f32[16,640]{1,0:T(8,128)S(1)}, u32[]{:S(2)}, u32[]{:S(2)}) collective-permute-start(f32[16,640]{1,0:T(8,128)S(1)} %get-tuple-element.120), channel_id=1, source_target_pairs={{0,12},{1,13},{2,14},{3,15},{4,0},{5,1},{6,2},{7,3},{8,4},{9,5},{1... | collective-permute-start | bytes 122888 | tf_op jit(solution)/shard_map/ppermute | solution.py:557
  61.5 7.3 %collective-permute-start.7 = (f32[16,640]{1,0:T(8,128)S(1)}, f32[16,640]{1,0:T(8,128)S(1)}, u32[]{:S(2)}, u32[]{:S(2)}) collective-permute-start(f32[16,640]{1,0:T(8,128)S(1)} %bitcast_add_fusion.1), channel_id=1, source_target_pairs={{0,4},{1,5},{2,6},{3,7},{4,8},{5,9},{6,10},{7,11},{8,12},{9,13},{1... | collective-permute-start | bytes 122888 | tf_op jit(solution)/shard_map/ppermute | solution.py:557
  62.7 7.0 %collective-permute-start.8 = (f32[16,640]{1,0:T(8,128)S(1)}, f32[16,640]{1,0:T(8,128)S(1)}, u32[]{:S(2)}, u32[]{:S(2)}) collective-permute-start(f32[16,640]{1,0:T(8,128)S(1)} %bitcast_add_fusion.1), channel_id=1, source_target_pairs={{0,8},{1,9},{2,10},{3,11},{4,12},{5,13},{6,14},{7,15},{8,0},{9,1},... | collective-permute-start | bytes 122888 | tf_op jit(solution)/shard_map/ppermute | solution.py:557
  65.4 5.2 %collective-permute-start.9 = (f32[16,640]{1,0:T(8,128)S(1)}, f32[16,640]{1,0:T(8,128)S(1)}, u32[]{:S(2)}, u32[]{:S(2)}) collective-permute-start(f32[16,640]{1,0:T(8,128)S(1)} %bitcast_add_fusion.1), channel_id=1, source_target_pairs={{0,12},{1,13},{2,14},{3,15},{4,0},{5,1},{6,2},{7,3},{8,4},{9,5},{1... | collective-permute-start | bytes 122888 | tf_op jit(solution)/shard_map/ppermute | solution.py:557
  70.6 8.7 %collective-permute-start.10 = (f32[4,16,640]{2,1,0:T(8,128)S(1)}, f32[4,16,640]{2,1,0:T(8,128)S(1)}, u32[]{:S(2)}, u32[]{:S(2)}) collective-permute-start(f32[4,16,640]{2,1,0:T(8,128)S(1)} %pad_maximum_fusion), channel_id=1, source_target_pairs={{0,2},{1,3},{2,0},{3,1},{4,6},{5,7},{6,4},{7,5},{8,10},{9,11},{10,... | collective-permute-start | bytes 491528 | tf_op jit(solution)/shard_map/ppermute | solution.py:549
  79.4 1.7 copy-start.17
  79.4 1.7 collective-permute-start.11
  79.5 88.5 %all-gather.3.cloned.1.call-start = ((), (), s32[]{:S(2)}) async-start(), calls=%async_computation.4 | async-start | bytes 1179648 | tf_op jit(solution)/shard_map/all_gather | solution.py:603
  81.1 0.7 copy-start.18
  81.8 11.0 %copy-start.5 = (f32[384,256]{1,0:T(8,128)S(1)}, f32[384,256]{1,0:T(8,128)}, u32[]{:S(2)}) copy-start(f32[384,256]{1,0:T(8,128)} %get-tuple-element.85) | copy-start | bytes 1179652
  93.8 36.6 %copy-start = (f32[384,256]{1,0:T(8,128)}, f32[384,256]{1,0:T(8,128)S(1)}, u32[]{:S(2)}) copy-start(f32[384,256]{1,0:T(8,128)S(1)} %add.96.first_ref.refs_3_) | copy-start | bytes 1179652
  93.9 14.4 %collective-permute-start.12 = (f32[384,256]{1,0:T(8,128)S(1)}, f32[384,256]{1,0:T(8,128)S(1)}, u32[]{:S(2)}, u32[]{:S(2)}) collective-permute-start(f32[384,256]{1,0:T(8,128)S(1)} %add.96.first_ref.refs_3_), channel_id=1, source_target_pairs={{0,4},{1,5},{4,8},{5,9},{8,12},{9,13},{12,14},{13,15},{14,10},{15,... | collective-permute-start | bytes 1179656 | tf_op jit(solution)/shard_map/ppermute | solution.py:546
  94.9 13.4 %collective-permute-start.13 = (f32[384,256]{1,0:T(8,128)S(1)}, f32[384,256]{1,0:T(8,128)S(1)}, u32[]{:S(2)}, u32[]{:S(2)}) collective-permute-start(f32[384,256]{1,0:T(8,128)S(1)} %add.96.first_ref.refs_3_), channel_id=1, source_target_pairs={{0,2},{1,3},{4,0},{5,1},{8,4},{9,5},{12,8},{13,9},{14,12},{15,13},... | collective-permute-start | bytes 1179656 | tf_op jit(solution)/shard_map/ppermute | solution.py:546
  108.3 18.5 %copy-start.16 = (f32[128,256]{1,0:T(8,128)S(1)}, f32[128,256]{1,0:T(8,128)}, u32[]{:S(2)}) copy-start(f32[128,256]{1,0:T(8,128)} %get-tuple-element.98) | copy-start | bytes 393220
  108.3 22.2 %copy-start.6 = (f32[384,256]{1,0:T(8,128)}, f32[384,256]{1,0:T(8,128)S(1)}, u32[]{:S(2)}) copy-start(f32[384,256]{1,0:T(8,128)S(1)} %collective-permute-done.12.refs_4_) | copy-start | bytes 1179652
  108.3 36.1 %copy-start.7 = (f32[384,256]{1,0:T(8,128)}, f32[384,256]{1,0:T(8,128)S(1)}, u32[]{:S(2)}) copy-start(f32[384,256]{1,0:T(8,128)S(1)} %collective-permute-done.13.refs_5_) | copy-start | bytes 1179652
  108.3 16.1 %collective-permute-start.14 = (f32[384,256]{1,0:T(8,128)S(1)}, f32[384,256]{1,0:T(8,128)S(1)}, u32[]{:S(2)}, u32[]{:S(2)}) collective-permute-start(f32[384,256]{1,0:T(8,128)S(1)} %collective-permute-done.12.refs_4_), channel_id=1, source_target_pairs={{0,4},{1,5},{4,8},{5,9},{8,12},{9,13},{12,14},{13,15},{14,10},{15,... | collective-permute-start | bytes 1179656 | tf_op jit(solution)/shard_map/ppermute | solution.py:546
  109.3 15.5 %collective-permute-start.15 = (f32[384,256]{1,0:T(8,128)S(1)}, f32[384,256]{1,0:T(8,128)S(1)}, u32[]{:S(2)}, u32[]{:S(2)}) collective-permute-start(f32[384,256]{1,0:T(8,128)S(1)} %collective-permute-done.13.refs_5_), channel_id=1, source_target_pairs={{0,2},{1,3},{4,0},{5,1},{8,4},{9,5},{12,8},{13,9},{14,12},{15,13},... | collective-permute-start | bytes 1179656 | tf_op jit(solution)/shard_map/ppermute | solution.py:546
  124.3 30.0 %copy-start.8 = (f32[384,256]{1,0:T(8,128)}, f32[384,256]{1,0:T(8,128)S(1)}, u32[]{:S(2)}) copy-start(f32[384,256]{1,0:T(8,128)S(1)} %collective-permute-done.14.refs_6_) | copy-start | bytes 1179652
  124.8 29.5 %copy-start.9 = (f32[384,256]{1,0:T(8,128)}, f32[384,256]{1,0:T(8,128)S(1)}, u32[]{:S(2)}) copy-start(f32[384,256]{1,0:T(8,128)S(1)} %collective-permute-done.15.refs_7_) | copy-start | bytes 1179652
  128.3 11.6 %collective-permute-start.16 = (f32[384,256]{1,0:T(8,128)S(1)}, f32[384,256]{1,0:T(8,128)S(1)}, u32[]{:S(2)}, u32[]{:S(2)}) collective-permute-start(f32[384,256]{1,0:T(8,128)S(1)} %collective-permute-done.14.refs_6_), channel_id=1, source_target_pairs={{0,4},{1,5},{4,8},{5,9},{8,12},{9,13},{12,14},{13,15},{14,10},{15,... | collective-permute-start | bytes 1179656 | tf_op jit(solution)/shard_map/ppermute | solution.py:546
  129.3 12.8 %collective-permute-start.17 = (f32[384,256]{1,0:T(8,128)S(1)}, f32[384,256]{1,0:T(8,128)S(1)}, u32[]{:S(2)}, u32[]{:S(2)}) collective-permute-start(f32[384,256]{1,0:T(8,128)S(1)} %collective-permute-done.15.refs_7_), channel_id=1, source_target_pairs={{0,2},{1,3},{4,0},{5,1},{8,4},{9,5},{12,8},{13,9},{14,12},{15,13},... | collective-permute-start | bytes 1179656 | tf_op jit(solution)/shard_map/ppermute | solution.py:546
  130.4 14.0 %collective-permute-start.20 = (f32[384,256]{1,0:T(8,128)S(1)}, f32[384,256]{1,0:T(8,128)S(1)}, u32[]{:S(2)}, u32[]{:S(2)}) collective-permute-start(f32[384,256]{1,0:T(8,128)S(1)} %add.96.first_ref.refs_3_), channel_id=1, source_target_pairs={{0,1},{1,0},{2,3},{3,2},{4,5},{5,4},{6,7},{7,6},{8,9},{9,8},{10,11... | collective-permute-start | bytes 1179656 | tf_op jit(solution)/shard_map/ppermute | solution.py:549
  130.4 14.5 %collective-permute-start.21 = (f32[384,256]{1,0:T(8,128)S(1)}, f32[384,256]{1,0:T(8,128)S(1)}, u32[]{:S(2)}, u32[]{:S(2)}) collective-permute-start(f32[384,256]{1,0:T(8,128)S(1)} %collective-permute-done.12.refs_4_), channel_id=1, source_target_pairs={{0,1},{1,0},{2,3},{3,2},{4,5},{5,4},{6,7},{7,6},{8,9},{9,8},{10,11... | collective-permute-start | bytes 1179656 | tf_op jit(solution)/shard_map/ppermute | solution.py:549
  139.9 14.4 %copy-start.3 = (f32[384,256]{1,0:T(8,128)}, f32[384,256]{1,0:T(8,128)S(1)}, u32[]{:S(2)}) copy-start(f32[384,256]{1,0:T(8,128)S(1)} %collective-permute-done.16.refs_8_) | copy-start | bytes 1179652
  142.0 12.3 %copy-start.4 = (f32[384,256]{1,0:T(8,128)}, f32[384,256]{1,0:T(8,128)S(1)}, u32[]{:S(2)}) copy-start(f32[384,256]{1,0:T(8,128)S(1)} %collective-permute-done.17.refs_9_) | copy-start | bytes 1179652
  142.0 7.1 %collective-permute-start.18 = (f32[192,256]{1,0:T(8,128)S(1)}, f32[192,256]{1,0:T(8,128)}, u32[]{:S(2)}, u32[]{:S(2)}) collective-permute-start(f32[192,256]{1,0:T(8,128)S(1)} %slice.6), channel_id=1, source_target_pairs={{0,4},{1,5},{4,8},{5,9},{8,12},{9,13},{12,14},{13,15},{14,10},{15,... | collective-permute-start | bytes 589832 | tf_op jit(solution)/shard_map/ppermute | solution.py:546
  142.5 7.8 %collective-permute-start.19 = (f32[192,256]{1,0:T(8,128)S(1)}, f32[192,256]{1,0:T(8,128)}, u32[]{:S(2)}, u32[]{:S(2)}) collective-permute-start(f32[192,256]{1,0:T(8,128)S(1)} %slice.7), channel_id=1, source_target_pairs={{0,2},{1,3},{4,0},{5,1},{8,4},{9,5},{12,8},{13,9},{14,12},{15,13},... | collective-permute-start | bytes 589832 | tf_op jit(solution)/shard_map/ppermute | solution.py:546
  144.4 10.0 %collective-permute-start.22 = (f32[384,256]{1,0:T(8,128)S(1)}, f32[384,256]{1,0:T(8,128)}, u32[]{:S(2)}, u32[]{:S(2)}) collective-permute-start(f32[384,256]{1,0:T(8,128)S(1)} %collective-permute-done.13.refs_5_), channel_id=1, source_target_pairs={{0,1},{1,0},{2,3},{3,2},{4,5},{5,4},{6,7},{7,6},{8,9},{9,8},{10,11... | collective-permute-start | bytes 1179656 | tf_op jit(solution)/shard_map/ppermute | solution.py:549
  144.4 9.9 %copy-start.10 = (f32[384,256]{1,0:T(8,128)}, f32[384,256]{1,0:T(8,128)S(1)}, u32[]{:S(2)}) copy-start(f32[384,256]{1,0:T(8,128)S(1)} %collective-permute-done.20.refs_12_) | copy-start | bytes 1179652
  144.4 10.5 %collective-permute-start.23 = (f32[384,256]{1,0:T(8,128)S(1)}, f32[384,256]{1,0:T(8,128)S(1)}, u32[]{:S(2)}, u32[]{:S(2)}) collective-permute-start(f32[384,256]{1,0:T(8,128)S(1)} %collective-permute-done.14.refs_6_), channel_id=1, source_target_pairs={{0,1},{1,0},{2,3},{3,2},{4,5},{5,4},{6,7},{7,6},{8,9},{9,8},{10,11... | collective-permute-start | bytes 1179656 | tf_op jit(solution)/shard_map/ppermute | solution.py:549
  144.9 9.4 %copy-start.11 = (f32[384,256]{1,0:T(8,128)}, f32[384,256]{1,0:T(8,128)S(1)}, u32[]{:S(2)}) copy-start(f32[384,256]{1,0:T(8,128)S(1)} %collective-permute-done.21.refs_13_) | copy-start | bytes 1179652
  144.9 10.1 %collective-permute-start.24 = (f32[384,256]{1,0:T(8,128)S(1)}, f32[384,256]{1,0:T(8,128)S(1)}, u32[]{:S(2)}, u32[]{:S(2)}) collective-permute-start(f32[384,256]{1,0:T(8,128)S(1)} %collective-permute-done.15.refs_7_), channel_id=1, source_target_pairs={{0,1},{1,0},{2,3},{3,2},{4,5},{5,4},{6,7},{7,6},{8,9},{9,8},{10,11... | collective-permute-start | bytes 1179656 | tf_op jit(solution)/shard_map/ppermute | solution.py:549
  149.1 7.5 %collective-permute-start.25 = (f32[384,256]{1,0:T(8,128)S(1)}, f32[384,256]{1,0:T(8,128)}, u32[]{:S(2)}, u32[]{:S(2)}) collective-permute-start(f32[384,256]{1,0:T(8,128)S(1)} %collective-permute-done.16.refs_8_), channel_id=1, source_target_pairs={{0,1},{1,0},{2,3},{3,2},{4,5},{5,4},{6,7},{7,6},{8,9},{9,8},{10,11... | collective-permute-start | bytes 1179656 | tf_op jit(solution)/shard_map/ppermute | solution.py:549
  150.3 6.3 %collective-permute-start.26 = (f32[384,256]{1,0:T(8,128)S(1)}, f32[384,256]{1,0:T(8,128)}, u32[]{:S(2)}, u32[]{:S(2)}) collective-permute-start(f32[384,256]{1,0:T(8,128)S(1)} %collective-permute-done.17.refs_9_), channel_id=1, source_target_pairs={{0,1},{1,0},{2,3},{3,2},{4,5},{5,4},{6,7},{7,6},{8,9},{9,8},{10,11... | collective-permute-start | bytes 1179656 | tf_op jit(solution)/shard_map/ppermute | solution.py:549
  154.4 1.9 %collective-permute-start.27 = (f32[192,256]{1,0:T(8,128)}, f32[192,256]{1,0:T(8,128)S(1)}, u32[]{:S(2)}, u32[]{:S(2)}) collective-permute-start(f32[192,256]{1,0:T(8,128)} %collective-permute-done.18.refs_10_), channel_id=1, source_target_pairs={{0,1},{1,0},{2,3},{3,2},{4,5},{5,4},{6,7},{7,6},{8,9},{9,8},{10,11... | collective-permute-start | bytes 589832 | tf_op jit(solution)/shard_map/ppermute | solution.py:549
  155.0 1.7 copy-start.12
  155.0 1.7 collective-permute-start.28
  155.1 1.6 copy-start.13
  156.2 0.7 copy-start.14
  156.6 0.7 copy-start.15
  168.0 2.9 %collective-permute-start.29 = (f32[8,128,256]{2,1,0:T(8,128)}, f32[8,128,256]{2,1,0:T(8,128)S(1)}, u32[]{:S(2)}, u32[]{:S(2)}) collective-permute-start(f32[8,128,256]{2,1,0:T(8,128)} %bitcast.29), channel_id=1, source_target_pairs={{0,1},{1,0},{2,3},{3,2},{4,5},{5,4},{6,7},{7,6},{8,9},{9,8},{10,11... | collective-permute-start | bytes 3145736 | tf_op jit(solution)/shard_map/ppermute | solution.py:549
  170.9 1.0 copy-start.2
Sparse Core Ops, SparseCore 0:
  44.3 48.4 reduce-scatter.4
  95.1 31.5 reduce-scatter.2
  128.4 30.4 all-gather.2
